TPU v7x, 32 devices: a whole 2x2x4 slice. The times are simulated.
32 devices in a mesh: fsdp: 16 (over z, y, x), dp: 2 (over core).
Axes of the slice: x: 2, y: 2, z: 4, core: 2. Of those that a mesh axis runs over, the one named last changes fastest.
Arguments:
- inputs: bfloat16 [768, 256, 1024], P(('fsdp', 'dp')), may hold values from -6 to 6
- sides: int32 [768], P(('fsdp', 'dp')), may hold values from 0 to 2
- weight_one: bfloat16 [1024, 256], P('fsdp'), may hold values from -0.1875 to 0.1875
- weight_two: bfloat16 [1152, 512], P('fsdp'), may hold values from -0.1875 to 0.1875
- weight_three: bfloat16 [256, 1024], P('fsdp'), may hold values from -0.375 to 0.375
- fc_first: float32 [256, 128], replicated, may hold values from -0.375 to 0.375
- fc_second: float32 [128, 512], replicated, may hold values from -0.5 to 0.5
- fc_bias: float32 [512], replicated, may hold values from -3 to 3
- bn_gain: float32 [1920], replicated, may hold values from 0.25 to 1.75
- bn_shift: float32 [1920], replicated, may hold values from -3 to 3
- cotangent: bfloat16 [768, 256, 1024], P(('fsdp', 'dp')), may hold values from -6 to 6
Outputs:
- outputs: bfloat16 [768, 256, 1024], P(('fsdp', 'dp'))
- input_grad: bfloat16 [768, 256, 1024], P(('fsdp', 'dp'))
- weight_one_grad: float32 [1024, 256], P('fsdp')
- weight_two_grad: float32 [1152, 512], P('fsdp')
- weight_three_grad: float32 [256, 1024], P('fsdp')
- fc_first_grad: float32 [256, 128], replicated
- fc_second_grad: float32 [128, 512], replicated
- fc_bias_grad: float32 [512], replicated
- gain_grad: float32 [1920], replicated
- shift_grad: float32 [1920], replicated
All inputs are finite; a program needn't handle non-finite values.
Results may differ from a plain program's by a relative error of at most 0.017.
Values may be sent and summed in bfloat16 or wider, within the bound.
No kernel may reach another device: no remote copies, remote signals or barrier semaphores. Data moves between devices by JAX's collectives and lax.ppermute only.
A program may use at most 384 MiB of HBM per device.

v0:
```python
import jax
import jax.numpy as jnp
from jax import lax
from jax.sharding import PartitionSpec as P

C_IN = 1024
WIDTH = 256
INTER = 128
SIDE_MAX = 16


epsilon = 1e-05
highest = lax.Precision.HIGHEST


def image_mask(sides):
    image_side = SIDE_MAX - 2 * sides
    position = jnp.arange(SIDE_MAX * SIDE_MAX)
    inside = (position[None, :] // SIDE_MAX < image_side[:, None]) & (
        position[None, :] % SIDE_MAX < image_side[:, None]
    )
    return inside.astype(jnp.float32)


def silu_slope(values):
    sigmoid_value = jax.nn.sigmoid(values)
    return sigmoid_value * (1.0 + values * (1.0 - sigmoid_value))


def inner_rows(left, right):
    return lax.dot_general(
        left, right, (((0,), (0,)), ((), ())), preferred_element_type=jnp.float32
    )


def contract_last(left, right):
    return lax.dot_general(
        left, right, (((1,), (1,)), ((), ())), preferred_element_type=jnp.float32
    )


def normalize(values, weights_mask, norm_count, statistics):
    if statistics is None:
        totals = lax.psum(
            (
                jnp.sum(values * weights_mask, axis=0),
                jnp.sum(values * values * weights_mask, axis=0),
                norm_count,
            ),
            ("fsdp", "dp"),
        )
        mean_value = totals[0] / totals[2]
        variance = totals[1] / totals[2] - mean_value * mean_value
        statistics = (mean_value, lax.rsqrt(variance + epsilon), totals[2])
    return ((values - statistics[0]) * statistics[1], statistics)


def norm_backward(upstream, hat_values, statistics, norm_gain, weights_mask):
    shift_total, gain_total = lax.psum(
        (jnp.sum(upstream, axis=0), jnp.sum(upstream * hat_values, axis=0)), ("fsdp", "dp")
    )
    values_grad = statistics[1] * (
        upstream * norm_gain
        - weights_mask
        * (norm_gain * shift_total + hat_values * norm_gain * gain_total)
        / statistics[2]
    )
    return (values_grad, gain_total, shift_total)


def gather_taps(act_grid, radix_part):
    half_width = WIDTH // 2
    padded = jnp.pad(
        act_grid[..., radix_part * half_width : (radix_part + 1) * half_width],
        ((0, 0), (1, 1), (1, 1), (0, 0)),
    )
    pieces = [
        padded[:, row_off : row_off + SIDE_MAX, col_off : col_off + SIDE_MAX, :]
        for row_off in range(3)
        for col_off in range(3)
    ]
    return jnp.concatenate(pieces, axis=-1).reshape(-1, 9 * half_width)


def scatter_taps(tap_grads, images):
    half_width = WIDTH // 2
    shaped = tap_grads.reshape(images, SIDE_MAX, SIDE_MAX, 9, half_width)
    padded = jnp.zeros((images, SIDE_MAX + 2, SIDE_MAX + 2, half_width), jnp.float32)
    for row_off in range(3):
        for col_off in range(3):
            padded = padded.at[
                :, row_off : row_off + SIDE_MAX, col_off : col_off + SIDE_MAX, :
            ].add(shaped[:, :, :, 3 * row_off + col_off, :])
    return padded[:, 1 : SIDE_MAX + 1, 1 : SIDE_MAX + 1, :]


def front_part(
    flat_rows, rows_mask, pixel_count, weight_one, weight_two, bn_gain, bn_shift, stat_one, stat_two
):
    images = flat_rows.shape[0] // (SIDE_MAX * SIDE_MAX)
    first_conv = jnp.dot(flat_rows, weight_one, preferred_element_type=jnp.float32)
    first_hat, stat_one = normalize(first_conv, rows_mask, pixel_count, stat_one)
    first_pre = first_hat * bn_gain[:WIDTH] + bn_shift[:WIDTH]
    act_one = (rows_mask * jax.nn.silu(first_pre)).astype(jnp.bfloat16)
    act_grid = act_one.reshape(images, SIDE_MAX, SIDE_MAX, WIDTH)
    patches = [gather_taps(act_grid, radix_part) for radix_part in range(2)]
    second = jnp.concatenate(
        [
            jnp.dot(
                patches[radix_part],
                weight_two[:, radix_part * WIDTH : (radix_part + 1) * WIDTH],
                preferred_element_type=jnp.float32,
            )
            for radix_part in range(2)
        ],
        axis=1,
    )
    second_hat, stat_two = normalize(second, rows_mask, pixel_count, stat_two)
    second_pre = second_hat * bn_gain[WIDTH : 3 * WIDTH] + bn_shift[WIDTH : 3 * WIDTH]
    act_two = rows_mask * jax.nn.silu(second_pre)
    return (first_hat, first_pre, patches, second_hat, second_pre, act_two, stat_one, stat_two)


def attention_part(act_two, image_pixels, fc_first, fc_second, fc_bias, bn_gain, bn_shift):
    images = image_pixels.shape[0]
    halves = act_two[:, :WIDTH] + act_two[:, WIDTH:]
    pooled = jnp.sum(halves.reshape(images, SIDE_MAX * SIDE_MAX, WIDTH), axis=1) / image_pixels
    pre_hidden = jnp.dot(pooled, fc_first, precision=highest)
    hidden_hat, stat_att = normalize(
        pre_hidden,
        jnp.ones((images, 1), jnp.float32),
        jnp.full((), float(images), jnp.float32),
        None,
    )
    hidden_pre = (
        hidden_hat * bn_gain[3 * WIDTH : 3 * WIDTH + INTER]
        + bn_shift[3 * WIDTH : 3 * WIDTH + INTER]
    )
    hidden_act = jax.nn.silu(hidden_pre)
    logits = jnp.dot(hidden_act, fc_second, precision=highest) + fc_bias
    attention = jax.nn.softmax(logits.reshape(images, 2, WIDTH), axis=1)
    return (pooled, hidden_hat, hidden_pre, hidden_act, attention, stat_att)


def back_part(
    act_two,
    attention,
    weight_three,
    flat_rows,
    rows_mask,
    pixel_count,
    bn_gain,
    bn_shift,
    stat_three,
):
    images = attention.shape[0]
    split_act = act_two.reshape(images, SIDE_MAX * SIDE_MAX, 2, WIDTH)
    combined = (
        jnp.sum(attention[:, None, :, :] * split_act, axis=2)
        .reshape(-1, WIDTH)
        .astype(jnp.bfloat16)
    )
    third_conv = jnp.dot(combined, weight_three, preferred_element_type=jnp.float32)
    third_hat, stat_three = normalize(third_conv, rows_mask, pixel_count, stat_three)
    offset = 3 * WIDTH + INTER
    third_pre = third_hat * bn_gain[offset:] + bn_shift[offset:] + flat_rows.astype(jnp.float32)
    return (combined, third_hat, third_pre, stat_three)


def body(
    inputs,
    sides,
    weight_one,
    weight_two,
    weight_three,
    fc_first,
    fc_second,
    fc_bias,
    bn_gain,
    bn_shift,
    cotangent,
):
    images = inputs.shape[0]
    flat_rows = inputs.reshape(-1, C_IN)
    pixel_mask = image_mask(sides)
    rows_mask = pixel_mask.reshape(-1, 1)
    image_pixels = jnp.sum(pixel_mask, axis=1, keepdims=True)
    pixel_count = jnp.sum(pixel_mask)
    full_one, full_two, full_three = (
        lax.all_gather(weight_one, "fsdp", axis=0, tiled=True),
        lax.all_gather(weight_two, "fsdp", axis=0, tiled=True),
        lax.all_gather(weight_three, "fsdp", axis=0, tiled=True),
    )
    front_values = front_part(
        flat_rows, rows_mask, pixel_count, full_one, full_two, bn_gain, bn_shift, None, None
    )
    pooled, hidden_hat, hidden_pre, hidden_act, attention, stat_att = attention_part(
        front_values[5], image_pixels, fc_first, fc_second, fc_bias, bn_gain, bn_shift
    )
    back_values = back_part(
        front_values[5],
        attention,
        full_three,
        flat_rows,
        rows_mask,
        pixel_count,
        bn_gain,
        bn_shift,
        None,
    )
    outputs = (rows_mask * jax.nn.silu(back_values[2])).astype(jnp.bfloat16).reshape(inputs.shape)
    full_one, full_two, full_three = (
        lax.all_gather(weight_one, "fsdp", axis=0, tiled=True),
        lax.all_gather(weight_two, "fsdp", axis=0, tiled=True),
        lax.all_gather(weight_three, "fsdp", axis=0, tiled=True),
    )
    front_values = front_part(
        flat_rows,
        rows_mask,
        pixel_count,
        full_one,
        full_two,
        bn_gain,
        bn_shift,
        front_values[6],
        front_values[7],
    )
    back_values = back_part(
        front_values[5],
        attention,
        full_three,
        flat_rows,
        rows_mask,
        pixel_count,
        bn_gain,
        bn_shift,
        back_values[3],
    )
    first_hat, first_pre, patches, second_hat, second_pre, act_two, stat_one, stat_two = (
        front_values
    )
    combined, third_hat, third_pre, stat_three = back_values
    offset = 3 * WIDTH + INTER
    residual_grad = (
        cotangent.reshape(-1, C_IN).astype(jnp.float32) * rows_mask * silu_slope(third_pre)
    )
    third_grad, gain_three, shift_three = norm_backward(
        residual_grad, third_hat, stat_three, bn_gain[offset:], rows_mask
    )
    third_grad = third_grad.astype(jnp.bfloat16)
    weight_three_local = inner_rows(combined, third_grad)
    comb_grad = contract_last(third_grad, full_three)
    comb_split = comb_grad.reshape(images, SIDE_MAX * SIDE_MAX, 1, WIDTH)
    split_act = act_two.reshape(images, SIDE_MAX * SIDE_MAX, 2, WIDTH)
    attention_grad = jnp.sum(comb_split * split_act, axis=1)
    logits_grad = (
        attention * (attention_grad - jnp.sum(attention * attention_grad, axis=1, keepdims=True))
    ).reshape(images, 2 * WIDTH)
    fc_bias_local = jnp.sum(logits_grad, axis=0)
    fc_second_local = lax.dot_general(
        hidden_act, logits_grad, (((0,), (0,)), ((), ())), precision=highest
    )
    hidden_grad = lax.dot_general(
        logits_grad, fc_second, (((1,), (1,)), ((), ())), precision=highest
    ) * silu_slope(hidden_pre)
    pre_hidden_grad, gain_att, shift_att = norm_backward(
        hidden_grad, hidden_hat, stat_att, bn_gain[3 * WIDTH : 3 * WIDTH + INTER], 1.0
    )
    fc_first_local = lax.dot_general(
        pooled, pre_hidden_grad, (((0,), (0,)), ((), ())), precision=highest
    )
    pooled_grad = (
        lax.dot_general(pre_hidden_grad, fc_first, (((1,), (1,)), ((), ())), precision=highest)
        / image_pixels
    )
    act_two_grad = attention[:, None, :, :] * comb_split + pooled_grad[:, None, None, :]
    second_up = act_two_grad.reshape(-1, 2 * WIDTH) * rows_mask * silu_slope(second_pre)
    second_grad, gain_two, shift_two = norm_backward(
        second_up, second_hat, stat_two, bn_gain[WIDTH : 3 * WIDTH], rows_mask
    )
    second_grad = second_grad.astype(jnp.bfloat16)
    weight_two_parts = []
    act_one_parts = []
    for radix_part in range(2):
        part_grad = second_grad[:, radix_part * WIDTH : (radix_part + 1) * WIDTH]
        weight_two_parts.append(inner_rows(patches[radix_part], part_grad))
        act_one_parts.append(
            scatter_taps(
                contract_last(
                    part_grad, full_two[:, radix_part * WIDTH : (radix_part + 1) * WIDTH]
                ),
                images,
            )
        )
    weight_two_local = jnp.concatenate(weight_two_parts, axis=1)
    act_one_grad = jnp.concatenate(act_one_parts, axis=-1).reshape(-1, WIDTH)
    first_up = act_one_grad * rows_mask * silu_slope(first_pre)
    first_grad, gain_one, shift_one = norm_backward(
        first_up, first_hat, stat_one, bn_gain[:WIDTH], rows_mask
    )
    first_grad = first_grad.astype(jnp.bfloat16)
    weight_one_local = inner_rows(flat_rows, first_grad)
    input_grad = (
        (residual_grad + contract_last(first_grad, full_one))
        .astype(jnp.bfloat16)
        .reshape(inputs.shape)
    )
    fc_first_grad, fc_second_grad, fc_bias_grad = lax.psum(
        (fc_first_local, fc_second_local, fc_bias_local), ("fsdp", "dp")
    )
    summed = (
        lax.psum(weight_one_local.astype(jnp.bfloat16), "dp").astype(jnp.float32),
        lax.psum(weight_two_local.astype(jnp.bfloat16), "dp").astype(jnp.float32),
        lax.psum(weight_three_local.astype(jnp.bfloat16), "dp").astype(jnp.float32),
    )
    weight_one_grad, weight_two_grad, weight_three_grad = (
        lax.psum_scatter(summed[0], "fsdp", scatter_dimension=0, tiled=True),
        lax.psum_scatter(summed[1], "fsdp", scatter_dimension=0, tiled=True),
        lax.psum_scatter(summed[2], "fsdp", scatter_dimension=0, tiled=True),
    )
    gain_grad = jnp.concatenate([gain_one, gain_two, gain_att, gain_three])
    shift_grad = jnp.concatenate([shift_one, shift_two, shift_att, shift_three])
    return (
        outputs,
        input_grad,
        weight_one_grad,
        weight_two_grad,
        weight_three_grad,
        fc_first_grad,
        fc_second_grad,
        fc_bias_grad,
        gain_grad,
        shift_grad,
    )


def solution(mesh):
    return jax.shard_map(
        body,
        mesh=mesh,
        in_specs=(
            P(("fsdp", "dp"), None, None),
            P(("fsdp", "dp")),
            P("fsdp", None),
            P("fsdp", None),
            P("fsdp", None),
            P(),
            P(),
            P(),
            P(),
            P(),
            P(("fsdp", "dp"), None, None),
        ),
        out_specs=(
            P(("fsdp", "dp"), None, None),
            P(("fsdp", "dp"), None, None),
            P("fsdp", None),
            P("fsdp", None),
            P("fsdp", None),
            P(),
            P(),
            P(),
            P(),
            P(),
        ),
        check_vma=False,
    )
```

profile of v0, /device:TPU:9, one launch (start us, length us, event | category | flops | bytes accessed | tf_op | source)
XLA Modules:
  0.0 1751.7 jit_solution(13806621978240731664)
XLA Ops:
  15.6 32.3 %all_gather.12 = bf16[1024,256]{1,0:T(8,128)(2,1)S(1)} all-gather(bf16[64,256]{1,0:T(8,128)(2,1)} %param.49), channel_id=1, replica_groups=mesh['fsdp'=16,'dp'=2] {'fsdp'}, dimensions={0}, use_global_device_ids=true | all-gather | bytes 557056 | tf_op jit(solution)/shard_map/all_gather | solution.py:190
  47.9 8.5 multiply_reduce_fusion.9
  56.4 50.2 %all-reduce.11 = (f32[256]{0:T(256)S(1)}, f32[]{:T(128)}, f32[256]{0:T(256)S(1)}) all-reduce(f32[256]{0:T(256)S(1)} %get-tuple-element.275, f32[]{:T(128)} %get-tuple-element.283, f32[256]{0:T(256)S(1)} %get-tuple-element.274), channel_id=1, replica_groups=mesh['fsdp'=16,'dp'=2] {'fsdp','dp'}, use_global_device_ids=true, to_apply=%region_1.2 | all-reduce | flops 513 | bytes 4104 | tf_op jit(solution)/shard_map/psum | solution.py:44
  107.3 4.8 multiply_convert_fusion.4
  130.3 5.0 copy-done.33
  135.3 30.6 %all_gather.14 = bf16[256,1024]{1,0:T(8,128)(2,1)} all-gather(bf16[16,1024]{1,0:T(8,128)(2,1)S(1)} %copy-done.36), channel_id=1, replica_groups=mesh['fsdp'=16,'dp'=2] {'fsdp'}, dimensions={0}, use_global_device_ids=true | all-gather | bytes 557056 | tf_op jit(solution)/shard_map/all_gather | solution.py:192
  166.0 7.7 fusion.43
  173.7 14.3 fusion.40
  188.0 8.3 multiply_reduce_fusion.7
  196.3 50.5 %all-reduce.10 = (f32[512]{0:T(512)S(1)}, f32[512]{0:T(512)S(1)}) all-reduce(f32[512]{0:T(512)S(1)} %get-tuple-element.271, f32[512]{0:T(512)S(1)} %get-tuple-element.270), channel_id=1, replica_groups=mesh['fsdp'=16,'dp'=2] {'fsdp','dp'}, use_global_device_ids=true, to_apply=%region_9.10 | all-reduce | flops 1024 | bytes 8192 | tf_op jit(solution)/shard_map/psum | solution.py:44
  247.3 9.2 multiply_multiply_fusion.2
  257.5 5.3 copy.144
  266.9 39.2 %all-reduce.9 = (f32[128]{0:T(128)S(1)}, f32[]{:T(128)}, f32[128]{0:T(128)S(1)}) all-reduce(f32[128]{0:T(128)S(1)} %get-tuple-element.281, f32[]{:T(128)} %constant.511.clone.1, f32[128]{0:T(128)S(1)} %get-tuple-element.280), channel_id=1, replica_groups=mesh['fsdp'=16,'dp'=2] {'fsdp','dp'}, use_global_device_ids=true, to_apply=%region_13.14 | all-reduce | flops 257 | bytes 2056 | tf_op jit(solution)/shard_map/psum | solution.py:44
  307.5 14.9 copy.145
  322.4 10.7 multiply_reduce_fusion.5
  334.2 10.2 multiply_reduce_fusion.2
  344.4 42.2 %all-reduce.8 = (f32[1024]{0:T(1024)S(1)}, f32[1024]{0:T(1024)S(1)}) all-reduce(f32[1024]{0:T(1024)S(1)} %get-tuple-element.267, f32[1024]{0:T(1024)S(1)} %get-tuple-element.266), channel_id=1, replica_groups=mesh['fsdp'=16,'dp'=2] {'fsdp','dp'}, use_global_device_ids=true, to_apply=%region_23.24 | all-reduce | flops 2048 | bytes 16384 | tf_op jit(solution)/shard_map/psum | solution.py:44
  387.2 34.7 %fusion.57 = (f32[1024]{0:T(1024)S(1)}, f32[1024]{0:T(1024)S(1)}, f32[6144,1024]{1,0:T(8,128)}, bf16[6144,1024]{1,0:T(8,128)(2,1)}) fusion(f32[1024]{0:T(1024)S(1)} %get-tuple-element.342, f32[6144,1024]{1,0:T(8,128)} %get-tuple-element.353, f32[1024]{0:T(1024)S(1)} %get-tuple-element.341, bf16[24,256,1024]{2,1,0:T(8,128)(2,1)} %param.47, ...), kind=kLoop, calls=%fused_computation.163 | loop fusion | flops 138409984 | bytes 88129536 | tf_op jit(solution)/shard_map/reduce_sum | solution.py:60
  421.9 38.2 %all-reduce.7 = (f32[1024]{0:T(1024)S(1)}, f32[1024]{0:T(1024)S(1)}) all-reduce(f32[1024]{0:T(1024)S(1)} %get-tuple-element.269, f32[1024]{0:T(1024)S(1)} %get-tuple-element.268), channel_id=1, replica_groups=mesh['fsdp'=16,'dp'=2] {'fsdp','dp'}, use_global_device_ids=true, to_apply=%region_27.28 | all-reduce | flops 2048 | bytes 16384 | tf_op jit(solution)/shard_map/psum | solution.py:59
  460.1 18.4 %multiply_convert_fusion = bf16[6144,1024]{1,0:T(8,128)(2,1)S(1)} fusion(f32[6144,1024]{1,0:T(8,128)} %get-tuple-element.312, f32[6144,1024]{1,0:T(8,128)} %get-tuple-element.353, f32[]{:T(128)} %get-tuple-element.301, f32[1024]{0:T(1024)S(1)} %get-tuple-element.291, f32[1024]{0:T(1024)S(1)} %slice_multiply_fusion, f32[1024]{0:T(1024)S(1)} %slice.817, ...), kind=kLoop, calls=%fused_computation.3 | loop fusion | flops 69206016 | bytes 62959620 | tf_op jit(solution)/shard_map/convert_element_type | solution.py:250
  482.9 5.6 fusion.69
  488.7 6.7 copy.95
  495.4 8.8 multiply_reduce_fusion.4
  505.4 42.3 %all-reduce.6 = (f32[128]{0:T(128)S(1)}, f32[128]{0:T(128)S(1)}) all-reduce(f32[128]{0:T(128)S(1)} %get-tuple-element.279, f32[128]{0:T(128)S(1)} %get-tuple-element.278), channel_id=1, replica_groups=mesh['fsdp'=16,'dp'=2] {'fsdp','dp'}, use_global_device_ids=true, to_apply=%region_33.34 | all-reduce | flops 256 | bytes 2048 | tf_op jit(solution)/shard_map/psum | solution.py:59
  548.7 9.4 multiply_add_fusion
  558.1 15.1 copy.147
  573.2 15.9 fusion.58
  589.1 38.3 %all-reduce.5 = (f32[512]{0:T(512)S(1)}, f32[512]{0:T(512)S(1)}) all-reduce(f32[512]{0:T(512)S(1)} %get-tuple-element.273, f32[512]{0:T(512)S(1)} %get-tuple-element.272), channel_id=1, replica_groups=mesh['fsdp'=16,'dp'=2] {'fsdp','dp'}, use_global_device_ids=true, to_apply=%region_37.38 | all-reduce | flops 1024 | bytes 8192 | tf_op jit(solution)/shard_map/psum | solution.py:59
  627.4 22.8 %multiply_convert_fusion.2 = bf16[6144,512]{0,1:T(8,128)(2,1)S(1)} fusion(f32[6144,512]{0,1:T(8,128)} %get-tuple-element.311, f32[]{:T(128)} %get-tuple-element.301, f32[512]{0:T(512)S(1)} %get-tuple-element.287, f32[512]{0:T(512)S(1)} %slice_multiply_fusion.2, f32[512]{0:T(512)S(1)} %slice.811, f32[512]{0:T(512)S(1)} %get-tuple-element.346, ...), kind=kLoop, calls=%fused_computation.12 | loop fusion | flops 37748736 | bytes 31492100 | tf_op jit(solution)/shard_map/convert_element_type | solution.py:281
  650.2 10.6 fusion.16
  660.9 8.5 fusion.19
  669.4 11.5 fusion.14
  680.9 36.1 %reshape.1099 = f32[24,16,16,9,128]{4,3,2,1,0:T(8,128)} reshape(f32[6144,1152]{1,0:T(8,128)} %fusion.14) | data formatting | bytes 56623104 | tf_op jit(solution)/shard_map/reshape | solution.py:87
  717.0 75.6 %fusion.64 = (f32[24,16,16,1,128]{4,3,2,1,0:T(1,128)}, f32[24,16,16,1,128]{4,3,2,1,0:T(1,128)}, f32[24,16,16,1,128]{4,3,2,1,0:T(1,128)}, f32[24,16,16,1,128]{4,3...) fusion(f32[24,16,16,9,128]{4,3,2,1,0:T(8,128)} %reshape.1099), kind=kLoop, calls=%fused_computation.168 | loop fusion | bytes 56623104 | tf_op jit(solution)/shard_map/slice | solution.py:93
  799.0 20.1 %scatter-add.61 = f32[24,18,18,128]{3,2,1,0:T(8,128)} dynamic-update-slice(f32[24,18,18,128]{3,2,1,0:T(8,128)} %scatter-add.60, f32[24,16,16,128]{3,2,1,0:T(8,128)} %dynamic-slice_add_fusion.1, s32[]{:T(128)} %constant.502.clone.1, s32[]{:T(128)} %bitcast.11, s32[]{:T(128)} %bitcast.12, s32[]{:T(128)} %constant.502.clone.1) | dynamic-update-slice | bytes 6291460 | tf_op jit(solution)/shard_map/scatter-add | solution.py:93
  819.1 6.5 add_select_fusion.1
  825.7 20.4 %scatter-add.64 = f32[24,18,18,128]{3,2,1,0:T(8,128)} dynamic-update-slice(f32[24,18,18,128]{3,2,1,0:T(8,128)} %scatter-add.61, f32[24,16,16,128]{3,2,1,0:T(8,128)} %add_select_fusion.1, s32[]{:T(128)} %constant.502.clone.1, s32[]{:T(128)} %bitcast.14, s32[]{:T(128)} %bitcast.15, s32[]{:T(128)} %constant.502.clone.1) | dynamic-update-slice | bytes 6291460 | tf_op jit(solution)/shard_map/scatter-add | solution.py:93
  853.3 17.9 %scatter-add.66 = f32[24,18,18,128]{3,2,1,0:T(8,128)} dynamic-update-slice(f32[24,18,18,128]{3,2,1,0:T(8,128)} %fusion.7, f32[24,16,16,128]{3,2,1,0:T(8,128)S(1)} %slice_add_fusion.11, s32[]{:T(128)} %constant.502.clone.1, s32[]{:T(128)} %constant.500.clone.1, s32[]{:T(128)} %constant.500.clone.1, s32[]{:T(128)} %constant.502.clone.1) | dynamic-update-slice | bytes 6291460 | tf_op jit(solution)/shard_map/scatter-add | solution.py:93
  871.2 5.7 slice_add_fusion.10
  876.9 18.9 %scatter-add.69 = f32[24,18,18,128]{3,2,1,0:T(8,128)} dynamic-update-slice(f32[24,18,18,128]{3,2,1,0:T(8,128)} %scatter-add.66, f32[24,16,16,128]{3,2,1,0:T(8,128)} %slice_add_fusion.10, s32[]{:T(128)} %constant.502.clone.1, s32[]{:T(128)} %constant.500.clone.1, s32[]{:T(128)} %constant.506.clone.1, s32[]{:T(128)} %constant.502.clone.1) | dynamic-update-slice | bytes 6291460 | tf_op jit(solution)/shard_map/scatter-add | solution.py:93
  900.0 4.8 slice_add_fusion.8
  904.8 18.9 %scatter-add.71 = f32[24,18,18,128]{3,2,1,0:T(8,128)} dynamic-update-slice(f32[24,18,18,128]{3,2,1,0:T(8,128)} %fusion.6, f32[24,16,16,128]{3,2,1,0:T(8,128)} %slice_add_fusion.8, s32[]{:T(128)} %constant.502.clone.1, s32[]{:T(128)} %constant.506.clone.1, s32[]{:T(128)} %constant.500.clone.1, s32[]{:T(128)} %constant.502.clone.1) | dynamic-update-slice | bytes 6291460 | tf_op jit(solution)/shard_map/scatter-add | solution.py:93
  928.2 19.0 %scatter-add.74 = f32[24,18,18,128]{3,2,1,0:T(8,128)} dynamic-update-slice(f32[24,18,18,128]{3,2,1,0:T(8,128)} %scatter-add.71, f32[24,16,16,128]{3,2,1,0:T(8,128)} %slice_add_fusion.7, s32[]{:T(128)} %constant.502.clone.1, s32[]{:T(128)} %constant.506.clone.1, s32[]{:T(128)} %constant.506.clone.1, s32[]{:T(128)} %constant.502.clone.1) | dynamic-update-slice | bytes 6291460 | tf_op jit(solution)/shard_map/scatter-add | solution.py:93
  951.6 13.1 fusion.10
  964.7 36.1 %reshape.1112 = f32[24,16,16,9,128]{4,3,2,1,0:T(8,128)} reshape(f32[6144,1152]{1,0:T(8,128)} %fusion.10) | data formatting | bytes 56623104 | tf_op jit(solution)/shard_map/reshape | solution.py:87
  1000.9 75.8 %fusion.65 = (f32[24,16,16,1,128]{4,3,2,1,0:T(1,128)}, f32[24,16,16,1,128]{4,3,2,1,0:T(1,128)}, f32[24,16,16,1,128]{4,3,2,1,0:T(1,128)}, f32[24,16,16,1,128]{4,3...) fusion(f32[24,16,16,9,128]{4,3,2,1,0:T(8,128)} %reshape.1112), kind=kLoop, calls=%fused_computation.169 | loop fusion | bytes 56623104 | tf_op jit(solution)/shard_map/slice | solution.py:93
  1083.1 20.1 %scatter-add.76 = f32[24,18,18,128]{3,2,1,0:T(8,128)} dynamic-update-slice(f32[24,18,18,128]{3,2,1,0:T(8,128)} %scatter-add.75, f32[24,16,16,128]{3,2,1,0:T(8,128)} %dynamic-slice_add_fusion, s32[]{:T(128)} %constant.502.clone.1, s32[]{:T(128)} %bitcast.11, s32[]{:T(128)} %bitcast.12, s32[]{:T(128)} %constant.502.clone.1) | dynamic-update-slice | bytes 6291460 | tf_op jit(solution)/shard_map/scatter-add | solution.py:93
  1103.2 6.5 add_select_fusion
  1109.7 20.4 %scatter-add.79 = f32[24,18,18,128]{3,2,1,0:T(8,128)} dynamic-update-slice(f32[24,18,18,128]{3,2,1,0:T(8,128)} %scatter-add.76, f32[24,16,16,128]{3,2,1,0:T(8,128)} %add_select_fusion, s32[]{:T(128)} %constant.502.clone.1, s32[]{:T(128)} %bitcast.14, s32[]{:T(128)} %bitcast.15, s32[]{:T(128)} %constant.502.clone.1) | dynamic-update-slice | bytes 6291460 | tf_op jit(solution)/shard_map/scatter-add | solution.py:93
  1137.3 17.9 %scatter-add.81 = f32[24,18,18,128]{3,2,1,0:T(8,128)} dynamic-update-slice(f32[24,18,18,128]{3,2,1,0:T(8,128)} %fusion.5, f32[24,16,16,128]{3,2,1,0:T(8,128)S(1)} %slice_add_fusion.5, s32[]{:T(128)} %constant.502.clone.1, s32[]{:T(128)} %constant.500.clone.1, s32[]{:T(128)} %constant.500.clone.1, s32[]{:T(128)} %constant.502.clone.1) | dynamic-update-slice | bytes 6291460 | tf_op jit(solution)/shard_map/scatter-add | solution.py:93
  1155.2 5.7 slice_add_fusion.4
  1160.9 18.8 %scatter-add.84 = f32[24,18,18,128]{3,2,1,0:T(8,128)} dynamic-update-slice(f32[24,18,18,128]{3,2,1,0:T(8,128)} %scatter-add.81, f32[24,16,16,128]{3,2,1,0:T(8,128)} %slice_add_fusion.4, s32[]{:T(128)} %constant.502.clone.1, s32[]{:T(128)} %constant.500.clone.1, s32[]{:T(128)} %constant.506.clone.1, s32[]{:T(128)} %constant.502.clone.1) | dynamic-update-slice | bytes 6291460 | tf_op jit(solution)/shard_map/scatter-add | solution.py:93
  1188.7 18.8 %scatter-add.86 = f32[24,18,18,128]{3,2,1,0:T(8,128)} dynamic-update-slice(f32[24,18,18,128]{3,2,1,0:T(8,128)} %fusion.4, f32[24,16,16,128]{3,2,1,0:T(8,128)} %slice_add_fusion.2, s32[]{:T(128)} %constant.502.clone.1, s32[]{:T(128)} %constant.506.clone.1, s32[]{:T(128)} %constant.500.clone.1, s32[]{:T(128)} %constant.502.clone.1) | dynamic-update-slice | bytes 6291460 | tf_op jit(solution)/shard_map/scatter-add | solution.py:93
  1212.0 19.0 %scatter-add.89 = f32[24,18,18,128]{3,2,1,0:T(8,128)} dynamic-update-slice(f32[24,18,18,128]{3,2,1,0:T(8,128)} %scatter-add.86, f32[24,16,16,128]{3,2,1,0:T(8,128)} %slice_add_fusion.1, s32[]{:T(128)} %constant.502.clone.1, s32[]{:T(128)} %constant.506.clone.1, s32[]{:T(128)} %constant.506.clone.1, s32[]{:T(128)} %constant.502.clone.1) | dynamic-update-slice | bytes 6291460 | tf_op jit(solution)/shard_map/scatter-add | solution.py:93
  1235.7 5.6 fusion.59
  1241.3 42.3 %all-reduce.4 = (f32[256]{0:T(256)S(1)}, f32[256]{0:T(256)S(1)}, f32[512]{0:T(512)}) all-reduce(f32[256]{0:T(256)S(1)} %get-tuple-element.277, f32[256]{0:T(256)S(1)} %get-tuple-element.276, f32[512]{0:T(512)S(1)} %copy-done.58), channel_id=1, replica_groups=mesh['fsdp'=16,'dp'=2] {'fsdp','dp'}, use_global_device_ids=true, to_apply=%region_42.43 | all-reduce | flops 1024 | bytes 8192 | tf_op jit(solution)/shard_map/psum | solution.py:59
  1284.2 6.3 multiply_convert_fusion.3
  1290.7 7.4 fusion.38
  1302.4 19.2 %all-reduce.19.cloned.1.call-done = (bf16[1024,256]{0,1:T(8,128)(2,1)}, bf16[1152,512]{0,1:T(8,128)(2,1)}, bf16[256,1024]{1,0:T(8,128)(2,1)}) async-done(((bf16[1024,256]{0,1:T(8,128)(2,1)}, bf16[1152,512]{0,1:T(8,128)(2,1)}, bf16[256,1024]{1,0:T(8,128)(2,1)}), (bf16[1024,256]{0,1:T(8,128)(2,1)}, bf16[1152,512]{0,1:T(8,128)(2,1)}, bf16[256,1024]{1,0:T(8,128)(2,1)})) %all-reduce.19.cloned.1.call-update) | async-done | bytes 2228240 | tf_op jit(solution)/shard_map/psum | solution.py:312
  1330.2 15.2 add_convert_fusion
  1345.5 109.8 %all-reduce.17.cloned.1.call-done = (f32[256,128]{1,0:T(8,128)}, f32[128,512]{1,0:T(8,128)}) async-done(((f32[256,128]{1,0:T(8,128)}, f32[128,512]{1,0:T(8,128)}), (f32[256,128]{1,0:T(8,128)}, f32[128,512]{1,0:T(8,128)})) %all-reduce.17.cloned.1.call-update) | async-done | bytes 393232 | tf_op jit(solution)/shard_map/psum | solution.py:308
  1455.3 64.2 %reduce-scatter.10.cloned.1.call-done = f32[64,256]{1,0:T(8,128)} async-done(((f32[1024,256]{1,0:T(8,128)}), f32[64,256]{1,0:T(8,128)}) %reduce-scatter.10.cloned.1.call-update) | async-done | bytes 65552
  1519.5 76.8 %reduce-scatter.8.cloned.1.call-done = f32[16,1024]{1,0:T(8,128)} async-done(((f32[256,1024]{1,0:T(8,128)}), f32[16,1024]{1,0:T(8,128)}) %reduce-scatter.8.cloned.1.call-update) | async-done | bytes 65552 | tf_op jit(solution)/shard_map/reduce_scatter | solution.py:319
  1596.3 145.1 %reduce-scatter.12.cloned.1.call-done = f32[72,512]{1,0:T(8,128)} async-done(((f32[1152,512]{1,0:T(8,128)}), f32[72,512]{1,0:T(8,128)}) %reduce-scatter.12.cloned.1.call-update) | async-done | bytes 147472
  (266 shorter events, 117.2 us)
Async XLA Ops:
  7.2 299.6 %copy-start = (f32[128,512]{1,0:T(8,128)S(1)}, f32[128,512]{1,0:T(8,128)}, u32[]{:S(2)}) copy-start(f32[128,512]{1,0:T(8,128)} %param.53) | copy-start | bytes 786436
  7.2 158.8 %all-gather.2.cloned.1.call-start = ((), (), s32[]{:S(2)}) async-start(), calls=%async_computation.3 | async-start | bytes 1253376 | tf_op jit(solution)/shard_map/all_gather | solution.py:191
  7.9 1313.7 %all-reduce.19.cloned.1.call-start = ((), (), s32[]{:S(2)}) async-start(), calls=%async_computation.8 | async-start | bytes 4456448 | tf_op jit(solution)/shard_map/psum | solution.py:312
  8.7 539.0 %copy-start.52 = (f32[128]{0:T(128)}, f32[128]{0:T(128)S(1)}, u32[]{:S(2)}) copy-start(f32[128]{0:T(128)S(1)} %slice.815) | copy-start | bytes 1540
  9.4 97.9 %copy-start.42 = (f32[256]{0:T(256)}, f32[256]{0:T(256)S(1)}, u32[]{:S(2)}) copy-start(f32[256]{0:T(256)S(1)} %slice.789) | copy-start | bytes 3076
  10.1 495.0 %copy-start.63 = (f32[128]{0:T(128)}, f32[128]{0:T(128)S(1)}, u32[]{:S(2)}) copy-start(f32[128]{0:T(128)S(1)} %slice.816) | copy-start | bytes 1540
  10.8 96.5 %copy-start.54 = (f32[256]{0:T(256)}, f32[256]{0:T(256)S(1)}, u32[]{:S(2)}) copy-start(f32[256]{0:T(256)S(1)} %slice.790) | copy-start | bytes 3076
  14.9 532.8 %copy-start.56 = (f32[24]{0:T(128)}, f32[24]{0:T(128)S(1)}, u32[]{:S(2)}) copy-start(f32[24]{0:T(128)S(1)} %get-tuple-element.282) | copy-start | bytes 292
  15.6 611.8 %copy-start.17 = (f32[3,2,8,128]{3,1,2,0:T(2,128)}, f32[3,2,8,128]{3,1,2,0:T(2,128)S(1)}, u32[]{:S(2)}) copy-start(f32[3,2,8,128]{3,1,2,0:T(2,128)S(1)} %copy.143) | copy-start | bytes 73732
  47.9 8.5 copy-start.19
  125.3 10.0 copy-start.36
  173.7 14.3 copy-start.2
  262.8 44.0 %copy-start.67 = (f32[512]{0:T(512)S(1)}, f32[512]{0:T(512)}, u32[]{:S(2)}) copy-start(f32[512]{0:T(512)} %param.54) | copy-start | bytes 6148
  266.6 40.5 %copy-start.30 = (f32[24,256]{1,0:T(8,128)}, f32[24,256]{1,0:T(8,128)S(1)}, u32[]{:S(2)}) copy-start(f32[24,256]{1,0:T(8,128)S(1)} %copy.92) | copy-start | bytes 73732
  266.9 280.8 %copy-start.26 = (f32[24,128]{1,0:T(8,128)}, f32[24,128]{1,0:T(8,128)S(1)}, u32[]{:S(2)}) copy-start(f32[24,128]{1,0:T(8,128)S(1)} %get-tuple-element.352) | copy-start | bytes 36868
  306.8 241.0 %copy-start.38 = (f32[128]{0:T(128)}, f32[128]{0:T(128)S(1)}, u32[]{:S(2)}) copy-start(f32[128]{0:T(128)S(1)} %get-tuple-element.313) | copy-start | bytes 1540
  306.8 241.0 %copy-start.40 = (f32[128]{0:T(128)}, f32[128]{0:T(128)S(1)}, u32[]{:S(2)}) copy-start(f32[128]{0:T(128)S(1)} %get-tuple-element.314) | copy-start | bytes 1540
  334.1 10.2 copy-start.15
  387.2 72.9 %copy-start.37 = (f32[1920]{0:T(1024)S(1)}, f32[1920]{0:T(1024)}, u32[]{:S(2)}) copy-start(f32[1920]{0:T(1024)} %param.55) | copy-start | bytes 23044
  460.1 18.5 %copy-start.48 = (f32[1024]{0:T(1024)}, f32[1024]{0:T(1024)S(1)}, u32[]{:S(2)}) copy-start(f32[1024]{0:T(1024)S(1)} %get-tuple-element.291) | copy-start | bytes 12292
  460.1 18.5 %copy-start.50 = (f32[1024]{0:T(1024)}, f32[1024]{0:T(1024)S(1)}, u32[]{:S(2)}) copy-start(f32[1024]{0:T(1024)S(1)} %get-tuple-element.292) | copy-start | bytes 12292
  460.1 18.4 %copy-start.16 = (bf16[32,8,24,256]{3,1,2,0:T(8,128)(2,1)S(1)}, bf16[32,8,24,256]{3,1,2,0:T(8,128)(2,1)}, u32[]{:S(2)}) copy-start(bf16[32,8,24,256]{3,1,2,0:T(8,128)(2,1)} %copy-done.15) | copy-start | bytes 9437188
  505.0 53.1 %copy-start.28 = (f32[24,512]{1,0:T(8,128)}, f32[24,512]{1,0:T(8,128)S(1)}, u32[]{:S(2)}) copy-start(f32[24,512]{1,0:T(8,128)S(1)} %get-tuple-element.309) | copy-start | bytes 147460
  505.4 43.2 %copy-start.34 = (f32[24,128]{1,0:T(8,128)}, f32[24,128]{1,0:T(8,128)S(1)}, u32[]{:S(2)}) copy-start(f32[24,128]{1,0:T(8,128)S(1)} %get-tuple-element.354) | copy-start | bytes 36868
  547.7 10.4 copy-start.65
  547.7 10.4 copy-start.70
  547.7 10.4 copy-start.68
  548.7 24.5 %slice-start = ((s8[6291456]{0:T(1024)(128)(4,1)}), s8[4194304]{0:T(1024)(128)(4,1)S(1)}, s32[]{:S(2)}) async-start(s8[6291456]{0:T(1024)(128)(4,1)} %bitcast.127), calls=%async_computation.9 | async-start | bytes 8388608
  558.1 15.1 slice-start.1
  627.4 22.9 %copy-start.59 = (f32[512]{0:T(512)}, f32[512]{0:T(512)S(1)}, u32[]{:S(2)}) copy-start(f32[512]{0:T(512)S(1)} %get-tuple-element.287) | copy-start | bytes 6148
  627.4 22.9 %copy-start.61 = (f32[512]{0:T(512)}, f32[512]{0:T(512)S(1)}, u32[]{:S(2)}) copy-start(f32[512]{0:T(512)S(1)} %get-tuple-element.288) | copy-start | bytes 6148
  650.2 19.1 %copy-start.3 = (bf16[6144,512]{0,1:T(8,128)(2,1)}, bf16[6144,512]{0,1:T(8,128)(2,1)S(1)}, u32[]{:S(2)}) copy-start(bf16[6144,512]{0,1:T(8,128)(2,1)S(1)} %multiply_convert_fusion.2) | copy-start | bytes 18874372
  660.9 8.5 copy-start.20
  825.7 20.4 %copy-start.13 = (f32[24,16,16,1,128]{4,3,2,1,0:T(1,128)S(1)}, f32[24,16,16,1,128]{4,3,2,1,0:T(1,128)}, u32[]{:S(2)}) copy-start(f32[24,16,16,1,128]{4,3,2,1,0:T(1,128)} %get-tuple-element.321) | copy-start | bytes 9437188
  871.2 24.6 %copy-start.9 = (f32[24,16,16,1,128]{4,3,2,1,0:T(1,128)S(1)}, f32[24,16,16,1,128]{4,3,2,1,0:T(1,128)}, u32[]{:S(2)}) copy-start(f32[24,16,16,1,128]{4,3,2,1,0:T(1,128)} %get-tuple-element.318) | copy-start | bytes 9437188
  900.0 23.7 %copy-start.5 = (f32[24,16,16,1,128]{4,3,2,1,0:T(1,128)S(1)}, f32[24,16,16,1,128]{4,3,2,1,0:T(1,128)}, u32[]{:S(2)}) copy-start(f32[24,16,16,1,128]{4,3,2,1,0:T(1,128)} %get-tuple-element.317) | copy-start | bytes 9437188
  928.2 23.3 %copy-start.21 = (bf16[1152,512]{1,0:T(8,128)(2,1)S(1)}, bf16[1152,512]{1,0:T(8,128)(2,1)}, u32[]{:S(2)}) copy-start(bf16[1152,512]{1,0:T(8,128)(2,1)} %all-gather.2.cloned.1.call-done) | copy-start | bytes 3538948
  1109.7 20.4 %copy-start.11 = (f32[24,16,16,1,128]{4,3,2,1,0:T(1,128)S(1)}, f32[24,16,16,1,128]{4,3,2,1,0:T(1,128)}, u32[]{:S(2)}) copy-start(f32[24,16,16,1,128]{4,3,2,1,0:T(1,128)} %get-tuple-element.331) | copy-start | bytes 9437188
  1155.2 24.5 %copy-start.7 = (f32[24,16,16,1,128]{4,3,2,1,0:T(1,128)S(1)}, f32[24,16,16,1,128]{4,3,2,1,0:T(1,128)}, u32[]{:S(2)}) copy-start(f32[24,16,16,1,128]{4,3,2,1,0:T(1,128)} %get-tuple-element.328) | copy-start | bytes 9437188
  1183.9 23.7 %copy-start.4 = (f32[24,16,16,1,128]{4,3,2,1,0:T(1,128)S(1)}, f32[24,16,16,1,128]{4,3,2,1,0:T(1,128)}, u32[]{:S(2)}) copy-start(f32[24,16,16,1,128]{4,3,2,1,0:T(1,128)} %get-tuple-element.326) | copy-start | bytes 9437188
  1212.0 21.9 %copy-start.14 = (f32[24,16,16,128]{3,2,1,0:T(8,128)S(1)}, f32[24,16,16,128]{3,2,1,0:T(8,128)}, u32[]{:S(2)}) copy-start(f32[24,16,16,128]{3,2,1,0:T(8,128)} %slice.879) | copy-start | bytes 9437188
  1290.6 7.5 copy-start.22
  1290.6 7.5 copy-start.23
  1290.6 8.7 copy-start.27
  1290.6 8.7 copy-start.31
  1290.6 8.7 copy-start.35
  1290.6 8.7 copy-start.39
  1290.7 8.7 copy-start.41
  1290.7 8.7 copy-start.53
  1290.7 8.7 copy-start.57
  1290.7 8.7 copy-start.66
  1290.7 8.7 copy-start.69
  1290.7 10.5 copy-start.29
  1290.7 10.5 copy-start.64
  1299.2 29.8 %copy-start.49 = (f32[1024]{0:T(1024)S(1)}, f32[1024]{0:T(1024)}, u32[]{:S(2)}) copy-start(f32[1024]{0:T(1024)} %copy-done.48) | copy-start | bytes 12292
  1299.3 29.8 %copy-start.60 = (f32[512]{0:T(512)S(1)}, f32[512]{0:T(512)}, u32[]{:S(2)}) copy-start(f32[512]{0:T(512)} %copy-done.59) | copy-start | bytes 6148
  1299.3 30.4 %copy-start.51 = (f32[1024]{0:T(1024)S(1)}, f32[1024]{0:T(1024)}, u32[]{:S(2)}) copy-start(f32[1024]{0:T(1024)} %copy-done.50) | copy-start | bytes 12292
  1299.3 30.4 %copy-start.62 = (f32[512]{0:T(512)S(1)}, f32[512]{0:T(512)}, u32[]{:S(2)}) copy-start(f32[512]{0:T(512)} %copy-done.61) | copy-start | bytes 6148
  1299.3 30.3 %copy-start.71 = (f32[128]{0:T(128)S(1)}, f32[128]{0:T(128)}, u32[]{:S(2)}) copy-start(f32[128]{0:T(128)} %copy-done.70) | copy-start | bytes 1540
  1299.3 156.0 %all-reduce.17.cloned.1.call-start = ((), (), s32[]{:S(2)}) async-start(), calls=%async_computation.7 | async-start | bytes 786432 | tf_op jit(solution)/shard_map/psum | solution.py:308
  1302.3 217.2 %reduce-scatter.10.cloned.1.call-start = ((), (), s32[]{:S(2)}) async-start(), calls=%async_computation.5 | async-start | bytes 1114112
  1323.9 272.4 %reduce-scatter.8.cloned.1.call-start = ((), (), s32[]{:S(2)}) async-start(), calls=%async_computation.4 | async-start | bytes 1114112 | tf_op jit(solution)/shard_map/reduce_scatter | solution.py:319
  1326.1 415.3 %reduce-scatter.12.cloned.1.call-start = ((), (), s32[]{:S(2)}) async-start(), calls=%async_computation.6 | async-start | bytes 2506752
  1330.2 414.4 %copy-start.1 = (f32[128,512]{1,0:T(8,128)S(1)}, f32[128,512]{1,0:T(8,128)}, u32[]{:S(2)}) copy-start(f32[128,512]{1,0:T(8,128)} %param.53) | copy-start | bytes 786436
  (19 other events, 65.9 us)
Sparse Core Ops, SparseCore 0:
  10.8 55.7 all-gather.1
  1299.4 22.1 all-reduce.18
  1328.6 126.6 all-reduce.16
  1458.0 61.4 reduce-scatter.9
  1522.3 73.9 reduce-scatter.7
  1601.7 139.6 reduce-scatter.11
where the time goes:
time: 1770 us; the launch traced here: 1750 us
  local copies, waits for them, and re-layouts  549 us (31%)
  waiting for transfers between devices  416 us (24%)
  blocking collectives  406 us (23%)
  other arithmetic  244 us (14%)
  matrix products  122 us (7%)
    scatter-add x14, local copies, waits for them, and re-layouts, scatter_taps(): padded = padded.at[:, row_off:row_off + SIDE_MAX, col_off:col_off + SIDE_...  236 us
    unnamed x8, waiting for transfers between devices  210 us
    psum x4, blocking collectives, normalize(): lax.psum((jnp.sum(values * weights_mask, axis=0), jnp.sum(values * values...  182 us
    psum x4, blocking collectives, norm_backward(): lax.psum((jnp.sum(upstream, axis=0), jnp.sum(upstream * hat_values, axis=...  161 us
    slice x2, local copies, waits for them, and re-layouts, scatter_taps(): shaped[:, :, :, 3 * row_off + col_off, :]  151 us
    psum x1, waiting for transfers between devices, body(): lax.psum((fc_first_local, fc_second_local, fc_bias_local), ('fsdp', 'dp'))  110 us
    reduce_scatter x1, waiting for transfers between devices, body(): lax.psum_scatter(summed[2], 'fsdp', scatter_dimension=0, tiled=True)  76.8 us
    reshape x2, local copies, waits for them, and re-layouts, scatter_taps(): shaped = tap_grads.reshape(images, SIDE_MAX, SIDE_MAX, 9, half_width)  72.3 us
  transfers between devices with their start and end apart: 6, of which 5 were waited for; matrix products, arithmetic and copies ran while one was open for 4% of the time, Pallas kernels for 0%

commit v1 on v0

v1 whole, which is shorter than its diff:
```python
import functools

import jax
import jax.numpy as jnp
from jax import lax
from jax.experimental import pallas as pl
from jax.experimental.pallas import tpu as pltpu
from jax.sharding import PartitionSpec as P

C_IN = 1024
WIDTH = 256
INTER = 128
SIDE = 16
PIX = SIDE * SIDE
HALF = WIDTH // 2
EPS = 1e-05
AXES = ("fsdp", "dp")
HIGH = lax.Precision.HIGHEST
F32 = jnp.float32
BF16 = jnp.bfloat16
MIB = 1024 * 1024


def dot_f(left, right):
    return jnp.dot(left, right, preferred_element_type=F32)


def dot_rows(left, right):
    return lax.dot_general(left, right, (((0,), (0,)), ((), ())), preferred_element_type=F32)


def dot_last(left, right):
    return lax.dot_general(left, right, (((1,), (1,)), ((), ())), preferred_element_type=F32)


def high_f(left, right):
    return jnp.dot(left, right, preferred_element_type=F32, precision=HIGH)


def high_rows(left, right):
    return lax.dot_general(
        left, right, (((0,), (0,)), ((), ())), preferred_element_type=F32, precision=HIGH
    )


def high_last(left, right):
    return lax.dot_general(
        left, right, (((1,), (1,)), ((), ())), preferred_element_type=F32, precision=HIGH
    )


def pixel_mask(image_side, width):
    row = lax.broadcasted_iota(jnp.int32, (PIX, 128), 0)
    inside = ((row >> 4) < image_side) & ((row & 15) < image_side)
    return wide(jnp.where(inside, 1.0, 0.0).astype(F32), width)


def wide(mask, width):
    if width == 128:
        return mask
    return jnp.concatenate([mask] * (width // 128), axis=1)


def fold(values):
    rows, n = values.shape
    return jnp.sum(values.reshape(rows // 8, 8, n), axis=0)


def row_sum(values):
    return jnp.sum(values, axis=0, keepdims=True)


def total(payload_ref):
    return jnp.sum(payload_ref[...], axis=0)


def norm_terms(sums, count):
    mean = sums[0:1] / count
    variance = sums[1:2] / count - mean * mean
    return mean, lax.rsqrt(variance + EPS)


def send_rows(payload_ref, rows):
    block = jnp.concatenate(rows, axis=0)
    payload_ref[...] = jnp.broadcast_to(block[None], payload_ref.shape)


def silu_parts(half_pre):
    t = jnp.tanh(half_pre)
    a = 1.0 + t
    value = half_pre * a
    slope = 0.5 * a * (1.0 + half_pre * (1.0 - t))
    return value, slope


def whole(shape):
    zeros = (0,) * len(shape)
    return pl.BlockSpec(shape, lambda *_: zeros)


def rows_of(n_rows, width):
    return pl.BlockSpec((n_rows, width), lambda i: (i, 0))


SMEM_SPEC = pl.BlockSpec(memory_space=pltpu.SMEM)


def call(kernel, grid, ins, outs, scratch=(), vmem=48, flops=0, moved=0, name=None):
    return pl.pallas_call(
        kernel,
        grid=(grid,),
        in_specs=[spec for _, spec in ins],
        out_specs=[spec for _, _, spec in outs],
        out_shape=[jax.ShapeDtypeStruct(shape, dtype) for shape, dtype, _ in outs],
        scratch_shapes=list(scratch),
        compiler_params=pltpu.CompilerParams(
            dimension_semantics=("arbitrary",), vmem_limit_bytes=vmem * MIB
        ),
        cost_estimate=pl.CostEstimate(flops=flops, bytes_accessed=moved, transcendentals=0),
        name=name,
    )(*[array for array, _ in ins])


def conv_one_kernel(per, sides_ref, x_ref, w_ref, h_ref, send_ref, acc_ref, count_ref):
    step = pl.program_id(0)

    @pl.when(step == 0)
    def _():
        acc_ref[...] = jnp.zeros_like(acc_ref)
        count_ref[0] = 0.0

    h = dot_f(x_ref[...], w_ref[...])
    h_ref[...] = h
    for j in range(per):
        side = SIDE - 2 * sides_ref[step * per + j]
        mask = pixel_mask(side, WIDTH)
        one = h[j * PIX : (j + 1) * PIX]
        kept = one * mask
        acc_ref[0:8] += fold(kept)
        acc_ref[8:16] += fold(kept * one)
        count_ref[0] += (side * side).astype(F32)

    @pl.when(step == pl.num_programs(0) - 1)
    def _():
        count = jnp.full((1, WIDTH), count_ref[0], F32)
        send_rows(
            send_ref,
            [row_sum(acc_ref[0:8]), row_sum(acc_ref[8:16]), count, jnp.zeros((1, WIDTH), F32)],
        )


def conv_two_kernel(
    per, sides_ref, got_ref, h_ref, w_ref, gain_ref, shift_ref, hat_ref, h2_ref, send_ref,
    vec_ref, taps_ref, acc_ref,
):
    step = pl.program_id(0)

    @pl.when(step == 0)
    def _():
        sums = total(got_ref)
        mean, inv = norm_terms(sums, sums[2:3])
        vec_ref[0:1] = mean
        vec_ref[1:2] = inv
        acc_ref[...] = jnp.zeros_like(acc_ref)
        taps_ref[...] = jnp.zeros_like(taps_ref)

    gain = gain_ref[:, :WIDTH] * 0.5
    shift = shift_ref[:, :WIDTH] * 0.5
    column = lax.broadcasted_iota(jnp.int32, (PIX, 128), 0) & 15
    first = wide(jnp.where(column == 0, 0.0, 1.0).astype(F32), WIDTH)
    last = wide(jnp.where(column == 15, 0.0, 1.0).astype(F32), WIDTH)
    for j in range(per):
        side = SIDE - 2 * sides_ref[step * per + j]
        mask = pixel_mask(side, WIDTH)
        rows = pl.ds(j * PIX, PIX)
        hat = (h_ref[rows] - vec_ref[0:1]) * vec_ref[1:2]
        hat_ref[rows] = hat.astype(BF16)
        half_pre = hat * gain + shift
        act = half_pre * (1.0 + jnp.tanh(half_pre)) * mask
        shifted = (
            pltpu.roll(act, 1, 0) * first,
            act,
            pltpu.roll(act, PIX - 1, 0) * last,
        )
        for d in range(3):
            piece = shifted[d].astype(BF16)
            for q in range(2):
                taps_ref[j, pl.ds(SIDE, PIX), pl.ds(q * 384 + d * 128, 128)] = piece[
                    :, q * HALF : (q + 1) * HALF
                ]
    for q in range(2):
        cols = pl.ds(q * WIDTH, WIDTH)
        for j in range(per):
            patches = jnp.concatenate(
                [taps_ref[j, pl.ds(SIDE * d, PIX), pl.ds(q * 384, 384)] for d in range(3)], axis=1
            )
            h2 = dot_f(patches, w_ref[:, cols])
            h2_ref[pl.ds(j * PIX, PIX), cols] = h2
            side = SIDE - 2 * sides_ref[step * per + j]
            kept = h2 * pixel_mask(side, WIDTH)
            acc_ref[0:8, cols] += fold(kept)
            acc_ref[8:16, cols] += fold(kept * h2)

    @pl.when(step == pl.num_programs(0) - 1)
    def _():
        send_rows(send_ref, [row_sum(acc_ref[0:8]), row_sum(acc_ref[8:16])])


def act_two_kernel(
    per, sides_ref, one_ref, got_ref, h2_ref, gain_ref, shift_ref, fc_ref,
    a2_ref, hat_ref, slope_ref, pooled_ref, zin_ref, t2_ref, t4_ref, send_ref, vec_ref,
):
    step = pl.program_id(0)

    @pl.when(step == 0)
    def _():
        sums = total(got_ref)
        mean, inv = norm_terms(sums, jnp.concatenate([total(one_ref)[2:3]] * 2, axis=1))
        vec_ref[0:1] = mean
        vec_ref[1:2] = inv

    gain = gain_ref[:, WIDTH : 3 * WIDTH] * 0.5
    shift = shift_ref[:, WIDTH : 3 * WIDTH] * 0.5
    for j in range(per):
        side = SIDE - 2 * sides_ref[step * per + j]
        mask = pixel_mask(side, 2 * WIDTH)
        rows = pl.ds(j * PIX, PIX)
        hat = (h2_ref[rows] - vec_ref[0:1]) * vec_ref[1:2]
        half_pre = hat * gain + shift
        value, slope = silu_parts(half_pre)
        value = value * mask
        slope = slope * mask
        a2_ref[rows] = value.astype(BF16)
        hat_ref[rows] = hat.astype(BF16)
        slope_ref[rows] = slope.astype(BF16)
        sums = row_sum(fold(value))
        image = pl.ds(step * per + j, 1)
        pixels = (side * side).astype(F32)
        pooled_ref[image] = (sums[:, :WIDTH] + sums[:, WIDTH:]) / pixels
        t2_ref[image] = row_sum(fold(slope))
        t4_ref[image] = row_sum(fold(slope * hat))

    @pl.when(step == pl.num_programs(0) - 1)
    def _():
        z = high_f(pooled_ref[...], fc_ref[...])
        zin_ref[...] = z
        send_rows(send_ref, [row_sum(z), row_sum(z * z)])


def hidden_terms(zin, sums, n_images, gain_ref, shift_ref):
    mean, inv = norm_terms(sums, n_images)
    zhat = (zin - mean) * inv
    cols = slice(3 * WIDTH, 3 * WIDTH + INTER)
    half_z = (zhat * gain_ref[:, cols] + shift_ref[:, cols]) * 0.5
    value, slope = silu_parts(half_z)
    return zhat, inv, value, slope


def combine_kernel(
    per, n_images, got_ref, zin_ref, a2_ref, w3_ref, fc_ref, bias_ref, gain_ref, shift_ref,
    att_ref, comb_ref, gw_ref, csum_ref, send_ref, gram_ref, acc_ref,
):
    step = pl.program_id(0)

    @pl.when(step == 0)
    def _():
        _, _, hidden, _ = hidden_terms(zin_ref[...], total(got_ref), n_images, gain_ref, shift_ref)
        logits = high_f(hidden, fc_ref[...]) + bias_ref[...]
        left, right = logits[:, :WIDTH], logits[:, WIDTH:]
        top = jnp.maximum(left, right)
        left, right = jnp.exp(left - top), jnp.exp(right - top)
        both = left + right
        att_ref[:, :WIDTH] = left / both
        att_ref[:, WIDTH:] = right / both
        gram_ref[...] = jnp.zeros_like(gram_ref)
        acc_ref[...] = jnp.zeros_like(acc_ref)

    for j in range(per):
        rows = pl.ds(j * PIX, PIX)
        att = att_ref[pl.ds(step * per + j, 1)]
        a2 = a2_ref[rows].astype(F32)
        comb = (att[:, :WIDTH] * a2[:, :WIDTH] + att[:, WIDTH:] * a2[:, WIDTH:]).astype(BF16)
        comb_ref[rows] = comb
        acc_ref[...] += fold(comb.astype(F32))
    comb = comb_ref[...]
    gram_ref[...] += dot_rows(comb, comb)

    @pl.when(step == pl.num_programs(0) - 1)
    def _():
        w3 = w3_ref[...].astype(F32)
        csum = row_sum(acc_ref[...])
        csum_ref[...] = csum
        gw = high_f(gram_ref[...], w3)
        gw_ref[...] = gw
        send_rows(send_ref, [high_f(csum, w3), row_sum(w3 * gw)])


def norm_three(one_ref, got_ref, gain_ref):
    count = total(one_ref)[2:3]
    count = jnp.concatenate([count] * 4, axis=1)
    mean, inv = norm_terms(total(got_ref), count)
    offset = 3 * WIDTH + INTER
    return mean, inv, inv * gain_ref[:, offset:], count


def output_kernel(
    per, sides_ref, one_ref, got_ref, comb_ref, x_ref, cot_ref, w3_ref, gain_ref, shift_ref,
    out_ref, u3_ref, p_ref, cu_ref, send_ref, vec_ref, ones_ref,
):
    step = pl.program_id(0)

    @pl.when(step == 0)
    def _():
        mean, _, scale, _ = norm_three(one_ref, got_ref, gain_ref)
        vec_ref[0:1] = 0.5 * scale
        vec_ref[1:2] = 0.5 * (shift_ref[:, 3 * WIDTH + INTER :] - mean * scale)
        vec_ref[2:3] = scale
        cu_ref[...] = jnp.zeros_like(cu_ref)
        ones_ref[...] = jnp.zeros_like(ones_ref)

    w3 = w3_ref[...]
    chunk = 16
    for j in range(per):
        side = SIDE - 2 * sides_ref[step * per + j]
        mask = pixel_mask(side, 128)
        h3 = dot_f(comb_ref[pl.ds(j * PIX, PIX)], w3)
        for c in range(PIX // chunk):
            rows = pl.ds(j * PIX + c * chunk, chunk)
            m = wide(mask[c * chunk : (c + 1) * chunk], C_IN)
            half_pre = (
                h3[c * chunk : (c + 1) * chunk] * vec_ref[0:1]
                + vec_ref[1:2]
                + x_ref[rows].astype(F32) * 0.5
            )
            t = jnp.tanh(half_pre)
            a = (1.0 + t) * m
            out_ref[rows] = (half_pre * a).astype(BF16)
            slope = a * (1.0 + half_pre * (1.0 - t))
            u3_ref[rows] = (cot_ref[rows].astype(F32) * slope * vec_ref[0:1]).astype(BF16)
    u3 = u3_ref[...]
    p_ref[...] = dot_last(u3, w3)
    cu_ref[...] += dot_rows(comb_ref[...], u3)
    ones_ref[...] += dot_f(jnp.ones((8, per * PIX), BF16), u3)

    @pl.when(step == pl.num_programs(0) - 1)
    def _():
        scale = vec_ref[2:3]
        products = row_sum(w3_ref[...].astype(F32) * cu_ref[...]) / scale
        send_rows(send_ref, [ones_ref[0:1] / scale, products])


def back_three_kernel(
    per, n_images, one_ref, three_ref, got_ref, att_got_ref, comb_ref, p_ref, a2_ref, slope_ref,
    hat_ref, w3_ref, cu_ref, gw_ref, csum_ref, att_ref, zin_ref, fc_ref, gain_ref, shift_ref,
    dcomb_ref, t1_ref, t3_ref, duz_ref, w3g_ref, fcg_ref, biasg_ref, norm_ref, send_ref,
    s_ref, c_ref, datt_ref,
):
    step = pl.program_id(0)

    @pl.when(step == 0)
    def _():
        mean, inv, scale, count = norm_three(one_ref, three_ref, gain_ref)
        sums = total(got_ref)
        dshift = sums[0:1]
        dgain = (sums[1:2] - mean * dshift) * inv
        norm_ref[0:1] = dgain
        norm_ref[1:2] = dshift
        k2 = scale * inv * dgain / count
        k1 = scale * dshift / count - mean * k2
        w3 = w3_ref[...].astype(F32)
        s_ref[...] = dot_last((w3 * k2).astype(BF16), w3_ref[...]).astype(BF16)
        c_ref[...] = high_last(jnp.broadcast_to(k1, (8, C_IN)), w3)
        csum = jnp.broadcast_to(csum_ref[...], (8, WIDTH))
        outer = high_rows(csum, jnp.broadcast_to(k1, (8, C_IN))) * 0.125
        w3g_ref[...] = cu_ref[...] - outer - gw_ref[...] * k2

    corr = dot_f(comb_ref[...], s_ref[...])
    for j in range(per):
        rows = pl.ds(j * PIX, PIX)
        dcomb = p_ref[rows] - corr[j * PIX : (j + 1) * PIX] - c_ref[0:1]
        dcomb_ref[rows] = dcomb.astype(BF16)
        image = pl.ds(step * per + j, 1)
        for q in range(2):
            cols = pl.ds(q * WIDTH, WIDTH)
            datt_ref[image, cols] = row_sum(fold(dcomb * a2_ref[rows, cols].astype(F32)))
            u = dcomb * slope_ref[rows, cols].astype(F32)
            t1_ref[image, cols] = row_sum(fold(u))
            t3_ref[image, cols] = row_sum(fold(u * hat_ref[rows, cols].astype(F32)))

    @pl.when(step == pl.num_programs(0) - 1)
    def _():
        att = att_ref[...]
        datt = datt_ref[...]
        both = att * datt
        inner = both[:, :WIDTH] + both[:, WIDTH:]
        dlog = both - att * jnp.concatenate([inner, inner], axis=1)
        zhat, _, hidden, slope = hidden_terms(
            zin_ref[...], total(att_got_ref), n_images, gain_ref, shift_ref
        )
        biasg_ref[...] = row_sum(dlog)
        fcg_ref[...] = high_rows(hidden, dlog)
        duz = high_last(dlog, fc_ref[...]) * slope
        duz_ref[...] = duz
        send_rows(send_ref, [row_sum(duz), row_sum(duz * zhat)])


def back_att_kernel(
    n_images, got_ref, att_got_ref, zin_ref, duz_ref, pooled_ref, pixels_ref, fc_ref, att_ref,
    t1_ref, t2_ref, t3_ref, t4_ref, gain_ref, shift_ref, dpool_ref, fcg_ref, norm_ref, send_ref,
):
    zhat, inv, _, _ = hidden_terms(
        zin_ref[...], total(att_got_ref), n_images, gain_ref, shift_ref
    )
    sums = total(got_ref)
    norm_ref[0:1] = sums[1:2]
    norm_ref[1:2] = sums[0:1]
    scale = inv * gain_ref[:, 3 * WIDTH : 3 * WIDTH + INTER]
    dzin = scale * (duz_ref[...] - (sums[0:1] + zhat * sums[1:2]) / n_images)
    fcg_ref[...] = high_rows(pooled_ref[...], dzin)
    dpool = high_last(dzin, fc_ref[...]) / pixels_ref[...]
    dpool_ref[...] = dpool
    both = jnp.concatenate([dpool, dpool], axis=1)
    att = att_ref[...]
    send_rows(
        send_ref,
        [
            row_sum(att * t1_ref[...] + both * t2_ref[...]),
            row_sum(att * t3_ref[...] + both * t4_ref[...]),
        ],
    )


def back_two_kernel(
    per, sides_ref, one_ref, two_ref, got_ref, dcomb_ref, slope_ref, hat2_ref, hat1_ref, att_ref,
    dpool_ref, w_ref, gain_ref, shift_ref, dh2_ref, u1_ref, norm_ref, send_ref,
    vec_ref, pad_ref, acc_ref,
):
    step = pl.program_id(0)

    @pl.when(step == 0)
    def _():
        count = jnp.concatenate([total(one_ref)[2:3]] * 2, axis=1)
        _, inv = norm_terms(total(two_ref), count)
        scale = inv * gain_ref[:, WIDTH : 3 * WIDTH]
        sums = total(got_ref)
        norm_ref[0:1] = sums[1:2]
        norm_ref[1:2] = sums[0:1]
        vec_ref[0:1] = scale
        vec_ref[1:2] = scale * sums[0:1] / count
        vec_ref[2:3] = scale * sums[1:2] / count
        acc_ref[...] = jnp.zeros_like(acc_ref)
        pad_ref[...] = jnp.zeros_like(pad_ref)

    column = lax.broadcasted_iota(jnp.int32, (PIX, 128), 0) & 15
    first = jnp.where(column == 0, 0.0, 1.0).astype(F32)
    last = jnp.where(column == 15, 0.0, 1.0).astype(F32)
    for j in range(per):
        rows = pl.ds(j * PIX, PIX)
        side = SIDE - 2 * sides_ref[step * per + j]
        mask = pixel_mask(side, WIDTH)
        image = pl.ds(step * per + j, 1)
        dcomb = dcomb_ref[rows].astype(F32)
        dpool = dpool_ref[image]
        for q in range(2):
            cols = pl.ds(q * WIDTH, WIDTH)
            scale = vec_ref[0:1, cols]
            up = dcomb * (att_ref[image, cols] * scale) + dpool * scale
            dh2 = slope_ref[rows, cols].astype(F32) * up - mask * (
                vec_ref[1:2, cols] + hat2_ref[rows, cols].astype(F32) * vec_ref[2:3, cols]
            )
            dh2 = dh2.astype(BF16)
            dh2_ref[rows, cols] = dh2
            pad_ref[j, pl.ds(SIDE, PIX), cols] = dh2
    for j in range(per):
        rows = pl.ds(j * PIX, PIX)
        side = SIDE - 2 * sides_ref[step * per + j]
        mask = pixel_mask(side, 128)
        for q in range(2):
            lines = jnp.concatenate(
                [
                    pad_ref[j, pl.ds(SIDE * (2 - d), PIX), pl.ds(q * WIDTH, WIDTH)]
                    for d in range(3)
                ],
                axis=1,
            )
            y = dot_f(lines, w_ref[q])
            da1 = (
                y[:, HALF : 2 * HALF]
                + pltpu.roll(y[:, :HALF], PIX - 1, 0) * last
                + pltpu.roll(y[:, 2 * HALF :], 1, 0) * first
            )
            cols = pl.ds(q * HALF, HALF)
            hat = hat1_ref[rows, cols].astype(F32)
            half_pre = 0.5 * (hat * gain_ref[:, cols] + shift_ref[:, cols])
            _, slope = silu_parts(half_pre)
            u1 = da1 * slope * mask
            u1_ref[rows, cols] = u1.astype(BF16)
            acc_ref[0:8, cols] += fold(u1)
            acc_ref[8:16, cols] += fold(u1 * hat)

    @pl.when(step == pl.num_programs(0) - 1)
    def _():
        send_rows(send_ref, [row_sum(acc_ref[0:8]), row_sum(acc_ref[8:16])])


def weight_two_kernel(
    per, sides_ref, hat_ref, dh2_ref, gain_ref, shift_ref, out_ref, taps_ref, acc_ref
):
    step = pl.program_id(0)

    @pl.when(step == 0)
    def _():
        acc_ref[...] = jnp.zeros_like(acc_ref)
        taps_ref[...] = jnp.zeros_like(taps_ref)

    gain = gain_ref[:, :WIDTH] * 0.5
    shift = shift_ref[:, :WIDTH] * 0.5
    column = lax.broadcasted_iota(jnp.int32, (PIX, 128), 0) & 15
    first = wide(jnp.where(column == 0, 0.0, 1.0).astype(F32), WIDTH)
    last = wide(jnp.where(column == 15, 0.0, 1.0).astype(F32), WIDTH)
    for j in range(per):
        side = SIDE - 2 * sides_ref[step * per + j]
        mask = pixel_mask(side, WIDTH)
        rows = pl.ds(j * PIX, PIX)
        half_pre = hat_ref[rows].astype(F32) * gain + shift
        act = half_pre * (1.0 + jnp.tanh(half_pre)) * mask
        shifted = (
            pltpu.roll(act, 1, 0) * first,
            act,
            pltpu.roll(act, PIX - 1, 0) * last,
        )
        for d in range(3):
            piece = shifted[d].astype(BF16)
            for q in range(2):
                taps_ref[j, pl.ds(SIDE, PIX), pl.ds(q * 384 + d * 128, 128)] = piece[
                    :, q * HALF : (q + 1) * HALF
                ]
    for q in range(2):
        for j in range(per):
            patches = jnp.concatenate(
                [taps_ref[j, pl.ds(SIDE * d, PIX), pl.ds(q * 384, 384)] for d in range(3)], axis=1
            )
            acc_ref[q] += dot_rows(
                dh2_ref[pl.ds(j * PIX, PIX), pl.ds(q * WIDTH, WIDTH)], patches
            )

    @pl.when(step == pl.num_programs(0) - 1)
    def _():
        for q in range(2):
            out_ref[:, q * WIDTH : (q + 1) * WIDTH] = acc_ref[q].T


def back_one_kernel(
    per, sides_ref, one_ref, three_ref, got_ref, u1_ref, hat_ref, u3_ref, x_ref, w_ref, gain_ref,
    ig_ref, wg_ref, norm_ref, vec_ref, wide_ref, dh_ref, acc_ref,
):
    step = pl.program_id(0)

    @pl.when(step == 0)
    def _():
        one = total(one_ref)
        count = one[2:3]
        _, inv = norm_terms(one, count)
        scale = inv * gain_ref[:, :WIDTH]
        sums = total(got_ref)
        norm_ref[0:1] = sums[1:2]
        norm_ref[1:2] = sums[0:1]
        vec_ref[0:1] = scale
        vec_ref[1:2] = scale * sums[0:1] / count
        vec_ref[2:3] = scale * sums[1:2] / count
        _, _, scale_three, _ = norm_three(one_ref, three_ref, gain_ref)
        wide_ref[...] = 1.0 / scale_three
        acc_ref[...] = jnp.zeros_like(acc_ref)

    for j in range(per):
        rows = pl.ds(j * PIX, PIX)
        side = SIDE - 2 * sides_ref[step * per + j]
        mask = pixel_mask(side, WIDTH)
        dh_ref[rows] = (
            u1_ref[rows].astype(F32) * vec_ref[0:1]
            - mask * (vec_ref[1:2] + hat_ref[rows].astype(F32) * vec_ref[2:3])
        ).astype(BF16)
    dh = dh_ref[...]
    acc_ref[...] += dot_rows(dh, x_ref[...])
    dx = dot_last(dh, w_ref[...])
    ig_ref[...] = (u3_ref[...].astype(F32) * wide_ref[...] + dx).astype(BF16)

    @pl.when(step == pl.num_programs(0) - 1)
    def _():
        wg_ref[...] = acc_ref[...].T


def everyone(payload):
    return lax.all_to_all(payload, AXES, 0, 0, tiled=True)


def other_core(array):
    return lax.ppermute(array, "dp", [(0, 1), (1, 0)])


def gather_rows(weight):
    rows, cols = weight.shape
    core = lax.axis_index("dp")
    shards = lax.axis_size("fsdp")
    half = lax.dynamic_slice_in_dim(weight, core * (cols // 2), cols // 2, 1)
    half = jnp.broadcast_to(half[None], (shards, rows, cols // 2))
    mine = lax.all_to_all(half, "fsdp", 0, 0, tiled=True).reshape(shards * rows, cols // 2)
    other = other_core(mine)
    return jnp.where(
        core == 0,
        jnp.concatenate([mine, other], axis=1),
        jnp.concatenate([other, mine], axis=1),
    )


def scatter_rows(grad):
    rows, cols = grad.shape
    core = lax.axis_index("dp")
    shards = lax.axis_size("fsdp")
    keep = lax.dynamic_slice_in_dim(grad, core * (cols // 2), cols // 2, 1)
    give = lax.dynamic_slice_in_dim(grad, (1 - core) * (cols // 2), cols // 2, 1).astype(BF16)
    both = (keep + other_core(give).astype(F32)).astype(BF16)
    both = both.reshape(shards, rows // shards, cols // 2)
    mine = jnp.sum(lax.all_to_all(both, "fsdp", 0, 0, tiled=True).astype(F32), axis=0)
    other = other_core(mine)
    return jnp.where(
        core == 0,
        jnp.concatenate([mine, other], axis=1),
        jnp.concatenate([other, mine], axis=1),
    )


def sum_everywhere(array, devices):
    rows = array.shape[0]
    each = -(-rows // devices)
    padded = jnp.pad(array, ((0, each * devices - rows), (0, 0))).reshape(devices, each, 128)
    mine = jnp.sum(lax.all_to_all(padded, AXES, 0, 0, tiled=True), axis=0)
    spread = jnp.broadcast_to(mine[None], (devices, each, 128))
    return lax.all_to_all(spread, AXES, 0, 0, tiled=True).reshape(-1, 128)[:rows]


def body(
    inputs,
    sides,
    weight_one,
    weight_two,
    weight_three,
    fc_first,
    fc_second,
    fc_bias,
    bn_gain,
    bn_shift,
    cotangent,
):
    images = inputs.shape[0]
    rows = images * PIX
    devices = lax.axis_size("fsdp") * lax.axis_size("dp")
    n_images = float(images * devices)
    x = inputs.reshape(rows, C_IN)
    cot = cotangent.reshape(rows, C_IN)
    gain = bn_gain.reshape(1, -1)
    shift = bn_shift.reshape(1, -1)
    bias = fc_bias.reshape(1, -1)
    per = 2 if images % 2 == 0 else 1
    steps = images // per
    block = per * PIX
    n_ch = gain.shape[1]

    full_one = gather_rows(weight_one)
    full_one, weight_two, weight_three = lax.optimization_barrier(
        (full_one, weight_two, weight_three)
    )
    full_two = gather_rows(weight_two)
    back_weight = full_two.reshape(3, 3, HALF, 2, WIDTH).transpose(3, 0, 4, 1, 2)
    back_weight = back_weight.reshape(2, 3 * WIDTH, 3 * HALF)
    pixels = SIDE - 2 * sides
    pixels = (pixels * pixels).astype(F32).reshape(images, 1)

    sides_in = (sides, SMEM_SPEC)
    gain_in = (gain, whole((1, n_ch)))
    shift_in = (shift, whole((1, n_ch)))

    def payload(k, n):
        return ((devices, k, n), F32, whole((devices, k, n)))

    def full(array):
        return (array, whole(array.shape))

    def by_rows(array):
        return (array, rows_of(block, array.shape[1]))

    h1, send = call(
        functools.partial(conv_one_kernel, per),
        steps,
        [sides_in, by_rows(x), full(full_one)],
        [((rows, WIDTH), F32, rows_of(block, WIDTH)), payload(4, WIDTH)],
        [pltpu.VMEM((16, WIDTH), F32), pltpu.SMEM((1,), F32)],
        flops=2 * rows * C_IN * WIDTH,
        moved=rows * C_IN * 2 + rows * WIDTH * 4,
        name="conv_one",
    )
    got_one = everyone(send)
    full_two, weight_three = lax.optimization_barrier((full_two, weight_three))
    full_three = gather_rows(weight_three)

    hat1, h2, send = call(
        functools.partial(conv_two_kernel, per),
        steps,
        [sides_in, full(got_one), by_rows(h1), full(full_two), gain_in, shift_in],
        [
            ((rows, WIDTH), BF16, rows_of(block, WIDTH)),
            ((rows, 2 * WIDTH), F32, rows_of(block, 2 * WIDTH)),
            payload(2, 2 * WIDTH),
        ],
        [
            pltpu.VMEM((8, WIDTH), F32),
            pltpu.VMEM((per, PIX + 2 * SIDE, 6 * HALF), BF16),
            pltpu.VMEM((16, 2 * WIDTH), F32),
        ],
        flops=2 * rows * 9 * HALF * 2 * WIDTH,
        moved=rows * WIDTH * 14,
        name="conv_two",
    )
    got_two = everyone(send)

    a2, hat2, slope2, pooled, zin, t2, t4, send = call(
        functools.partial(act_two_kernel, per),
        steps,
        [
            sides_in,
            full(got_one),
            full(got_two),
            by_rows(h2),
            gain_in,
            shift_in,
            full(fc_first),
        ],
        [
            ((rows, 2 * WIDTH), BF16, rows_of(block, 2 * WIDTH)),
            ((rows, 2 * WIDTH), BF16, rows_of(block, 2 * WIDTH)),
            ((rows, 2 * WIDTH), BF16, rows_of(block, 2 * WIDTH)),
            ((images, WIDTH), F32, whole((images, WIDTH))),
            ((images, INTER), F32, whole((images, INTER))),
            ((images, 2 * WIDTH), F32, whole((images, 2 * WIDTH))),
            ((images, 2 * WIDTH), F32, whole((images, 2 * WIDTH))),
            payload(2, INTER),
        ],
        [pltpu.VMEM((8, 2 * WIDTH), F32)],
        flops=rows * 2 * WIDTH * 20,
        moved=rows * 2 * WIDTH * 10,
        name="act_two",
    )
    got_att = everyone(send)

    att, comb, gw, csum, send = call(
        functools.partial(combine_kernel, per, n_images),
        steps,
        [
            full(got_att),
            full(zin),
            by_rows(a2),
            full(full_three),
            full(fc_second),
            full(bias),
            gain_in,
            shift_in,
        ],
        [
            ((images, 2 * WIDTH), F32, whole((images, 2 * WIDTH))),
            ((rows, WIDTH), BF16, rows_of(block, WIDTH)),
            ((WIDTH, C_IN), F32, whole((WIDTH, C_IN))),
            ((1, WIDTH), F32, whole((1, WIDTH))),
            payload(2, C_IN),
        ],
        [pltpu.VMEM((WIDTH, WIDTH), F32), pltpu.VMEM((8, WIDTH), F32)],
        flops=2 * rows * WIDTH * WIDTH,
        moved=rows * WIDTH * 6,
        name="combine",
    )
    got_three = everyone(send)

    outputs, u3, p, cu, send = call(
        functools.partial(output_kernel, per),
        steps,
        [
            sides_in,
            full(got_one),
            full(got_three),
            by_rows(comb),
            by_rows(x),
            by_rows(cot),
            full(full_three),
            gain_in,
            shift_in,
        ],
        [
            ((rows, C_IN), BF16, rows_of(block, C_IN)),
            ((rows, C_IN), BF16, rows_of(block, C_IN)),
            ((rows, WIDTH), F32, rows_of(block, WIDTH)),
            ((WIDTH, C_IN), F32, whole((WIDTH, C_IN))),
            payload(2, C_IN),
        ],
        [pltpu.VMEM((8, C_IN), F32), pltpu.VMEM((8, C_IN), F32)],
        flops=6 * rows * WIDTH * C_IN,
        moved=rows * C_IN * 8,
        name="output",
    )
    got_back_three = everyone(send)

    dcomb, t1, t3, duz, w3_local, fc2_local, bias_local, norm3, send = call(
        functools.partial(back_three_kernel, per, n_images),
        steps,
        [
            full(got_one),
            full(got_three),
            full(got_back_three),
            full(got_att),
            by_rows(comb),
            by_rows(p),
            by_rows(a2),
            by_rows(slope2),
            by_rows(hat2),
            full(full_three),
            full(cu),
            full(gw),
            full(csum),
            full(att),
            full(zin),
            full(fc_second),
            gain_in,
            shift_in,
        ],
        [
            ((rows, WIDTH), BF16, rows_of(block, WIDTH)),
            ((images, 2 * WIDTH), F32, whole((images, 2 * WIDTH))),
            ((images, 2 * WIDTH), F32, whole((images, 2 * WIDTH))),
            ((images, INTER), F32, whole((images, INTER))),
            ((WIDTH, C_IN), F32, whole((WIDTH, C_IN))),
            ((INTER, 2 * WIDTH), F32, whole((INTER, 2 * WIDTH))),
            ((1, 2 * WIDTH), F32, whole((1, 2 * WIDTH))),
            ((2, C_IN), F32, whole((2, C_IN))),
            payload(2, INTER),
        ],
        [
            pltpu.VMEM((WIDTH, WIDTH), BF16),
            pltpu.VMEM((8, WIDTH), F32),
            pltpu.VMEM((images, 2 * WIDTH), F32),
        ],
        flops=2 * rows * WIDTH * WIDTH,
        moved=rows * WIDTH * 18,
        name="back_three",
    )
    got_back_att = everyone(send)

    dpool, fc1_local, norm_att, send = call(
        functools.partial(back_att_kernel, n_images),
        1,
        [
            full(got_back_att),
            full(got_att),
            full(zin),
            full(duz),
            full(pooled),
            full(pixels),
            full(fc_first),
            full(att),
            full(t1),
            full(t2),
            full(t3),
            full(t4),
            gain_in,
            shift_in,
        ],
        [
            ((images, WIDTH), F32, whole((images, WIDTH))),
            ((WIDTH, INTER), F32, whole((WIDTH, INTER))),
            ((2, INTER), F32, whole((2, INTER))),
            payload(2, 2 * WIDTH),
        ],
        flops=10000000,
        moved=1000000,
        name="back_att",
    )
    got_back_two = everyone(send)

    dh2, u1, norm2, send = call(
        functools.partial(back_two_kernel, per),
        steps,
        [
            sides_in,
            full(got_one),
            full(got_two),
            full(got_back_two),
            by_rows(dcomb),
            by_rows(slope2),
            by_rows(hat2),
            by_rows(hat1),
            full(att),
            full(dpool),
            full(back_weight),
            gain_in,
            shift_in,
        ],
        [
            ((rows, 2 * WIDTH), BF16, rows_of(block, 2 * WIDTH)),
            ((rows, WIDTH), BF16, rows_of(block, WIDTH)),
            ((2, 2 * WIDTH), F32, whole((2, 2 * WIDTH))),
            payload(2, WIDTH),
        ],
        [
            pltpu.VMEM((8, 2 * WIDTH), F32),
            pltpu.VMEM((per, PIX + 2 * SIDE, 2 * WIDTH), BF16),
            pltpu.VMEM((16, WIDTH), F32),
        ],
        flops=2 * rows * 9 * HALF * 2 * WIDTH,
        moved=rows * WIDTH * 18,
        name="back_two",
    )
    got_back_one = everyone(send)

    (w2_local,) = call(
        functools.partial(weight_two_kernel, per),
        steps,
        [sides_in, by_rows(hat1), by_rows(dh2), gain_in, shift_in],
        [((9 * HALF, 2 * WIDTH), F32, whole((9 * HALF, 2 * WIDTH)))],
        [
            pltpu.VMEM((per, PIX + 2 * SIDE, 6 * HALF), BF16),
            pltpu.VMEM((2, WIDTH, 9 * HALF), F32),
        ],
        flops=2 * rows * 9 * HALF * 2 * WIDTH,
        moved=rows * WIDTH * 6,
        name="weight_two",
    )
    w2_local, u1 = lax.optimization_barrier((w2_local, u1))

    input_grad, w1_local, norm1 = call(
        functools.partial(back_one_kernel, per),
        steps,
        [
            sides_in,
            full(got_one),
            full(got_three),
            full(got_back_one),
            by_rows(u1),
            by_rows(hat1),
            by_rows(u3),
            by_rows(x),
            full(full_one),
            gain_in,
        ],
        [
            ((rows, C_IN), BF16, rows_of(block, C_IN)),
            ((C_IN, WIDTH), F32, whole((C_IN, WIDTH))),
            ((2, WIDTH), F32, whole((2, WIDTH))),
        ],
        [
            pltpu.VMEM((8, WIDTH), F32),
            pltpu.VMEM((1, C_IN), F32),
            pltpu.VMEM((block, WIDTH), BF16),
            pltpu.VMEM((WIDTH, C_IN), F32),
        ],
        flops=4 * rows * WIDTH * C_IN,
        moved=rows * C_IN * 6,
        name="back_one",
    )

    packed = jnp.concatenate(
        [fc1_local, fc2_local.reshape(-1, 128), bias_local.reshape(-1, 128)], axis=0
    )
    summed = sum_everywhere(packed, devices)
    fc_first_grad = summed[:WIDTH]
    fc_second_grad = summed[WIDTH : WIDTH + INTER * 4].reshape(INTER, 2 * WIDTH)
    fc_bias_grad = summed[WIDTH + INTER * 4 :].reshape(2 * WIDTH)
    weight_three_grad = scatter_rows(w3_local)
    weight_two_grad = scatter_rows(w2_local)
    weight_one_grad = scatter_rows(w1_local)
    norms = jnp.concatenate([norm1, norm2, norm_att, norm3], axis=1)
    return (
        outputs.reshape(inputs.shape),
        input_grad.reshape(inputs.shape),
        weight_one_grad,
        weight_two_grad,
        weight_three_grad,
        fc_first_grad,
        fc_second_grad,
        fc_bias_grad,
        norms[0],
        norms[1],
    )


def solution(mesh):
    return jax.shard_map(
        body,
        mesh=mesh,
        in_specs=(
            P(("fsdp", "dp"), None, None),
            P(("fsdp", "dp")),
            P("fsdp", None),
            P("fsdp", None),
            P("fsdp", None),
            P(),
            P(),
            P(),
            P(),
            P(),
            P(("fsdp", "dp"), None, None),
        ),
        out_specs=(
            P(("fsdp", "dp"), None, None),
            P(("fsdp", "dp"), None, None),
            P("fsdp", None),
            P("fsdp", None),
            P("fsdp", None),
            P(),
            P(),
            P(),
            P(),
            P(),
        ),
        check_vma=False,
    )
```

time: 1770 us -> 399 us (0.23)
  local copies, waits for them, and re-layouts: 549 us -> 26.5 us
  waiting for transfers between devices: 416 us -> 49.4 us
  blocking collectives: 406 us -> 67.6 us
  other arithmetic: 244 us -> 14.2 us
  Pallas kernels: 0 us -> 166 us
  matrix products: 122 us -> 0 us
  starting transfers between devices: 0.24 us -> 69.5 us
    psum x8 -> x0, blocking collectives: 343 us -> none  [the longest x4 182 us: normalize(): lax.psum((jnp.sum(values * weights_mask, axis=0), jnp.sum(values * values...]
    scatter-add x14 -> x0, local copies, waits for them, and re-layouts: 236 us -> none  [scatter_taps(): padded = padded.at[:, row_off:row_off + SIDE_MAX, col_off:col_off + SIDE_...]
    unnamed x8 -> x0, waiting for transfers between devices: 210 us -> none
    pallas_call x0 -> x10, Pallas kernels: none -> 166 us  [call(): pl.pallas_call(kernel, grid=(grid,), in_specs=[spec for _, spec in ins],...]
    slice x13 -> x3, local copies, waits for them, and re-layouts: 165 us -> 1.32 us  [the longest x1 0.66 us: body(): fc_first_grad = summed[:WIDTH]]
    psum x2 -> x0, waiting for transfers between devices: 129 us -> none  [the longest x1 110 us: body(): lax.psum((fc_first_local, fc_second_local, fc_bias_local), ('fsdp', 'dp'))]
    dot_general x18 -> x0, matrix products: 122 us -> none  [the longest x4 45.5 us: contract_last(): lax.dot_general(left, right, (((1,), (1,)), ((), ())), preferred_element_...]
    reduce_sum x11 -> x4, other arithmetic: 89 us -> 3.16 us  [the longest x3 2.07 us: scatter_rows(): jnp.sum(lax.all_to_all(both, 'fsdp', 0, 0, tiled=True).astype(F32), axis=0)]
  transfers between devices with their start and end apart: 6 -> 20, of which waited for: 5 -> 11; matrix products, arithmetic and copies ran while one was open for 4% -> 7% of each run, Pallas kernels for 0% -> 27%
where the time goes in v1:
time: 399 us; the launch traced here: 394 us
  Pallas kernels  166 us (42%)
  starting transfers between devices  69.5 us (17%)
  blocking collectives  67.6 us (17%)
  waiting for transfers between devices  49.4 us (12%)
  local copies, waits for them, and re-layouts  26.5 us (7%)
  other arithmetic  14.2 us (4%)
    pallas_call x10, Pallas kernels, call(): pl.pallas_call(kernel, grid=(grid,), in_specs=[spec for _, spec in ins],...  166 us
    all_to_all x3, blocking collectives, everyone(): return lax.all_to_all(payload, AXES, 0, 0, tiled=True)  34.8 us
    all_to_all x2, blocking collectives, gather_rows(): lax.all_to_all(half, 'fsdp', 0, 0, tiled=True)  32.8 us
    all_to_all x5, starting transfers between devices, everyone(): return lax.all_to_all(payload, AXES, 0, 0, tiled=True)  25.6 us
    all_to_all x5, waiting for transfers between devices, everyone(): return lax.all_to_all(payload, AXES, 0, 0, tiled=True)  19.5 us
    all_to_all x3, starting transfers between devices, scatter_rows(): lax.all_to_all(both, 'fsdp', 0, 0, tiled=True).astype(F32)  16.6 us
    all_to_all x3, waiting for transfers between devices, scatter_rows(): lax.all_to_all(both, 'fsdp', 0, 0, tiled=True).astype(F32)  13.2 us
    all_to_all x1, waiting for transfers between devices, sum_everywhere(): lax.all_to_all(spread, AXES, 0, 0, tiled=True).reshape(-1, 128)[:rows]  12.2 us
  transfers between devices with their start and end apart: 20, of which 11 were waited for; matrix products, arithmetic and copies ran while one was open for 7% of the time, Pallas kernels for 27%

profile of v1, /device:TPU:9, one launch (start us, length us, event | category | flops | bytes accessed | tf_op | source)
XLA Modules:
  0.0 394.2 jit_solution(7721425148700749617)
XLA Ops:
  0.7 0.8 constant_dynamic-slice_fusion.2
  1.5 13.5 %all_to_all.80 = bf16[16,64,128]{2,1,0:T(8,128)(2,1)S(1)} all-to-all(bf16[16,64,128]{2,1,0:T(8,128)(2,1)S(1)} %broadcast_in_dim.8), channel_id=1, replica_groups=mesh['fsdp'=16,'dp'=2] {'fsdp'}, dimensions={0} | all-to-all | bytes 524288 | tf_op jit(solution)/shard_map/all_to_all | solution.py:607
  15.0 3.2 collective-permute-start
  18.2 1.2 collective-permute-done
  19.7 19.3 %all_to_all.81 = bf16[16,72,256]{2,1,0:T(8,128)(2,1)S(1)} all-to-all(bf16[16,72,256]{2,1,0:T(8,128)(2,1)S(1)} %broadcast_in_dim.9), channel_id=1, replica_groups=mesh['fsdp'=16,'dp'=2] {'fsdp'}, dimensions={0} | all-to-all | bytes 1179648 | tf_op jit(solution)/shard_map/all_to_all | solution.py:607
  39.0 1.7 collective-permute-start.1
  40.7 1.6 collective-permute-done.1
  42.7 0.7 broadcast_in_dim.10
  43.4 4.4 %all-to-all-start.5 = ((bf16[16,16,512]{2,1,0:T(8,128)(2,1)}), bf16[16,16,512]{2,1,0:T(8,128)(2,1)S(1)}, u32[]{:S(2)}, u32[]{:S(2)}) async-start(bf16[16,16,512]{2,1,0:T(8,128)(2,1)} %broadcast_in_dim.10), calls=%async_computation.5 | async-start | bytes 524288 | tf_op jit(solution)/shard_map/all_to_all | solution.py:607
  47.9 13.0 %conv_one.1 = (f32[6144,256]{1,0:T(8,128)}, f32[32,4,256]{2,1,0:T(4,128)}) custom-call(s32[24]{0:T(128)S(1)} %copy-done.15, bf16[6144,1024]{1,0:T(8,128)(2,1)} %bitcast.19, bf16[1024,256]{1,0:T(8,128)(2,1)S(1)} %maximum_select_fusion.1.w_ref), custom_call_target="tpu_custom_call" | custom-call | flops 3221225472 | bytes 18874368 | tf_op jit(solution)/shard_map/conv_one/pallas_call | solution.py:109
  60.8 6.1 %all-to-all-start.1 = ((f32[32,4,256]{2,1,0:T(4,128)}), f32[32,4,256]{2,1,0:T(4,128)S(1)}, u32[]{:S(2)}, u32[]{:S(2)}) async-start(f32[32,4,256]{2,1,0:T(4,128)} %get-tuple-element.61), calls=%async_computation.1 | async-start | bytes 262144 | tf_op jit(solution)/shard_map/all_to_all | solution.py:594
  67.4 5.7 %all-to-all-done.1.got_ref.one_ref = f32[32,4,256]{2,1,0:T(4,128)S(1)} async-done(((f32[32,4,256]{2,1,0:T(4,128)}), f32[32,4,256]{2,1,0:T(4,128)S(1)}, u32[]{:S(2)}, u32[]{:S(2)}) %all-to-all-start.1) | async-done | bytes 131104 | tf_op jit(solution)/shard_map/all_to_all | solution.py:594
  73.1 17.2 %conv_two.1 = (bf16[6144,256]{1,0:T(8,128)(2,1)S(1)}, f32[6144,512]{1,0:T(8,128)}, f32[32,2,512]{2,1,0:T(2,128)S(1)}) custom-call(s32[24]{0:T(128)S(1)} %copy-done.15, f32[32,4,256]{2,1,0:T(4,128)S(1)} %all-to-all-done.1.got_ref.one_ref, f32[6144,256]{1,0:T(8,128)} %get-tuple-element.62.h_ref, bf16[1152,512]{1,0:T(8,128)(2,1)S(1)} %maximum_select_fusion.w_ref, ...), custom_call_target="tpu_custom_call" | custom-call | flops 7247757312 | bytes 22020096 | tf_op jit(solution)/shard_map/conv_two/pallas_call | solution.py:109
  90.3 10.0 %all_to_all.82.got_ref.two_ref = f32[32,2,512]{2,1,0:T(2,128)S(1)} all-to-all(f32[32,2,512]{2,1,0:T(2,128)S(1)} %get-tuple-element.66), channel_id=1, replica_groups=mesh['fsdp'=16,'dp'=2] {'fsdp','dp'}, dimensions={0} | all-to-all | bytes 262144 | tf_op jit(solution)/shard_map/all_to_all | solution.py:594
  100.3 19.2 %act_two.1 = (bf16[6144,512]{1,0:T(8,128)(2,1)}, bf16[6144,512]{1,0:T(8,128)(2,1)}, bf16[6144,512]{1,0:T(8,128)(2,1)}, f32[24,256]{1,0:T(8,128)S(1)}, f32[24,128...) custom-call(s32[24]{0:T(128)S(1)} %copy-done.15, ...), custom_call_target="tpu_custom_call" | custom-call | flops 62914560 | bytes 31457280 | tf_op jit(solution)/shard_map/act_two/pallas_call | solution.py:109
  119.5 4.6 %all-to-all-start.4 = ((f32[32,2,128]{2,1,0:T(2,128)}), f32[32,2,128]{2,1,0:T(2,128)S(1)}, u32[]{:S(2)}, u32[]{:S(2)}) async-start(f32[32,2,128]{2,1,0:T(2,128)} %get-tuple-element.68), calls=%async_computation.4 | async-start | bytes 65536 | tf_op jit(solution)/shard_map/all_to_all | solution.py:594
  124.1 1.2 maximum_select_fusion.2.w3_ref
  125.3 4.4 %all-to-all-done.4.got_ref.att_got_ref = f32[32,2,128]{2,1,0:T(2,128)S(1)} async-done(((f32[32,2,128]{2,1,0:T(2,128)}), f32[32,2,128]{2,1,0:T(2,128)S(1)}, u32[]{:S(2)}, u32[]{:S(2)}) %all-to-all-start.4) | async-done | bytes 32800 | tf_op jit(solution)/shard_map/all_to_all | solution.py:594
  129.8 10.8 %combine.1 = (f32[24,512]{1,0:T(8,128)S(1)}, bf16[6144,256]{1,0:T(8,128)(2,1)S(1)}, f32[256,1024]{1,0:T(8,128)S(1)}, f32[1,256]{1,0:T(1,128)S(1)}, f32[32,2,1024]{2,1,0:T(2,128)S(1)}) custom-call(f32[32,2,128]{2,1,0:T(2,128)S(1)} %all-to-all-done.4.got_ref.att_got_ref, f32[24,128]{1,0:T(8,128)S(1)} %get-tuple-element.69.zin_ref, ...), custom_call_target="tpu_custom_call" | custom-call | flops 805306368 | bytes 9437184 | tf_op jit(solution)/shard_map/combine/pallas_call | solution.py:109
  140.6 12.1 %all_to_all.83.got_ref.three_ref = f32[32,2,1024]{2,1,0:T(2,128)S(1)} all-to-all(f32[32,2,1024]{2,1,0:T(2,128)S(1)} %get-tuple-element.72), channel_id=1, replica_groups=mesh['fsdp'=16,'dp'=2] {'fsdp','dp'}, dimensions={0} | all-to-all | bytes 524288 | tf_op jit(solution)/shard_map/all_to_all | solution.py:594
  152.7 30.7 %output.1 = (bf16[6144,1024]{1,0:T(8,128)(2,1)}, bf16[6144,1024]{1,0:T(8,128)(2,1)}, f32[6144,256]{1,0:T(8,128)}, f32[256,1024]{1,0:T(8,128)S(1)}, f32[32,2,1024]{2,1,0:T(2,128)S(1)}) custom-call(s32[24]{0:T(128)S(1)} %copy-done.15, f32[32,4,256]{2,1,0:T(4,128)S(1)} %all-to-all-done.1.got_ref.one_ref, f32[32,2,1024]{2,1,0:T(2,128)S(1)} %all_to_all.83.got_ref.three_ref, ...), custom_call_target="tpu_custom_call" | custom-call | flops 9663676416 | bytes 50331648 | tf_op jit(solution)/shard_map/output/pallas_call | solution.py:109
  183.4 12.7 %all_to_all.84.got_ref = f32[32,2,1024]{2,1,0:T(2,128)S(1)} all-to-all(f32[32,2,1024]{2,1,0:T(2,128)S(1)} %get-tuple-element.75), channel_id=1, replica_groups=mesh['fsdp'=16,'dp'=2] {'fsdp','dp'}, dimensions={0} | all-to-all | bytes 524288 | tf_op jit(solution)/shard_map/all_to_all | solution.py:594
  196.1 18.5 %back_three.1 = (bf16[6144,256]{1,0:T(8,128)(2,1)}, f32[24,512]{1,0:T(8,128)S(1)}, f32[24,512]{1,0:T(8,128)S(1)}, f32[24,128]{1,0:T(8,128)S(1)}, f32[256,1024]{1...) custom-call(f32[32,4,256]{2,1,0:T(4,128)S(1)} %all-to-all-done.1.got, ...), custom_call_target="tpu_custom_call" | custom-call | flops 805306368 | bytes 28311552 | tf_op jit(solution)/shard_map/back_three/pallas_call | solution.py:109
  214.6 1.0 copy-done.8
  216.3 4.4 %all-to-all-start.8 = ((f32[32,2,128]{2,1,0:T(2,128)}), f32[32,2,128]{2,1,0:T(2,128)S(1)}, u32[]{:S(2)}, u32[]{:S(2)}) async-start(f32[32,2,128]{2,1,0:T(2,128)} %get-tuple-element.83), calls=%async_computation.8 | async-start | bytes 65536 | tf_op jit(solution)/shard_map/all_to_all | solution.py:594
  220.8 5.6 %all-to-all-done.8.got_ref = f32[32,2,128]{2,1,0:T(2,128)S(1)} async-done(((f32[32,2,128]{2,1,0:T(2,128)}), f32[32,2,128]{2,1,0:T(2,128)S(1)}, u32[]{:S(2)}, u32[]{:S(2)}) %all-to-all-start.8) | async-done | bytes 32800 | tf_op jit(solution)/shard_map/all_to_all | solution.py:594
  226.4 1.0 back_att.1
  228.1 4.8 %all-to-all-start.9 = ((f32[32,2,512]{2,1,0:T(2,128)}), f32[32,2,512]{2,1,0:T(2,128)}, u32[]{:S(2)}, u32[]{:S(2)}) async-start(f32[32,2,512]{2,1,0:T(2,128)} %get-tuple-element.90), calls=%async_computation.9 | async-start | bytes 262144 | tf_op jit(solution)/shard_map/all_to_all | solution.py:594
  233.2 3.4 copy.24
  236.7 3.4 reshape.102.w_ref
  240.1 1.7 reshape.107
  241.8 0.7 dynamic-slice_convert_fusion.1
  242.9 1.7 select_maximum_fusion
  244.6 1.9 reshape.109
  246.5 19.7 %back_two.1 = (bf16[6144,512]{1,0:T(8,128)(2,1)}, bf16[6144,256]{1,0:T(8,128)(2,1)S(1)}, f32[2,512]{1,0:T(2,128)S(1)}, f32[32,2,256]{2,1,0:T(2,128)}) custom-call(s32[24]{0:T(128)S(1)} %copy-done.15, f32[32,4,256]{2,1,0:T(4,128)S(1)} %all-to-all-done.1.got_ref.one_ref, f32[32,2,512]{2,1,0:T(2,128)S(1)} %all_to_all.82.got_ref.two_ref, ...), custom_call_target="tpu_custom_call" | custom-call | flops 7247757312 | bytes 28311552 | tf_op jit(solution)/shard_map/back_two/pallas_call | solution.py:109
  266.2 1.6 copy-done.4
  267.8 5.7 %all-to-all-start.10 = ((f32[32,2,256]{2,1,0:T(2,128)}), f32[32,2,256]{2,1,0:T(2,128)S(1)}, u32[]{:S(2)}, u32[]{:S(2)}) async-start(f32[32,2,256]{2,1,0:T(2,128)} %get-tuple-element.94), calls=%async_computation.10 | async-start | bytes 131072 | tf_op jit(solution)/shard_map/all_to_all | solution.py:594
  273.6 1.7 add_convert_fusion.1
  275.3 3.8 all-to-all-done.10.got_ref
  279.1 5.7 %all-to-all-start.13 = ((bf16[16,16,512]{2,1,0:T(8,128)(2,1)}), bf16[16,16,512]{2,1,0:T(8,128)(2,1)}, u32[]{:S(2)}, u32[]{:S(2)}) async-start(bf16[16,16,512]{2,1,0:T(8,128)(2,1)} %bitcast.12), calls=%async_computation.13 | async-start | bytes 524288 | tf_op jit(solution)/shard_map/all_to_all | solution.py:624
  284.8 1.9 copy-done.3
  286.7 14.3 %weight_two.1 = f32[1152,512]{1,0:T(8,128)S(1)} custom-call(s32[24]{0:T(128)S(1)} %copy-done.15, bf16[6144,256]{1,0:T(8,128)(2,1)S(1)} %copy-done.3, bf16[6144,512]{1,0:T(8,128)(2,1)} %get-tuple-element.95.dh2_ref, f32[1,1920]{1,0:T(1,128)S(1)} %reshape.95.gain_ref, f32[1,1920]{1,0:T(1,128)S(1)} %reshape.96.shift_ref), custom_call_target="tpu_custom_call" | custom-call | flops 7247757312 | bytes 9437184 | tf_op jit(solution)/shard_map/weight_two/pallas_call | solution.py:109
  301.1 6.2 %all-to-all-start.14 = ((f32[32,25,128]{2,1,0:T(8,128)}), f32[32,25,128]{2,1,0:T(8,128)}, u32[]{:S(2)}, u32[]{:S(2)}) async-start(f32[32,25,128]{2,1,0:T(8,128)} %reshape.109), calls=%async_computation.14 | async-start | bytes 1048576 | tf_op jit(solution)/shard_map/all_to_all | solution.py:637
  307.3 1.9 copy-done.5
  309.1 21.4 %back_one.1 = (bf16[6144,1024]{1,0:T(8,128)(2,1)}, f32[1024,256]{1,0:T(8,128)S(1)}, f32[2,256]{1,0:T(2,128)S(1)}) custom-call(s32[24]{0:T(128)S(1)} %copy-done.15, f32[32,4,256]{2,1,0:T(4,128)S(1)} %all-to-all-done.1.got_ref.one_ref, f32[32,2,1024]{2,1,0:T(2,128)S(1)} %all_to_all.83.got_ref.three_ref, f32[32,2,256]{2,1,0:T(2,128)S(1)} %all-to-all-done.10.got_ref, ...), custom_call_target="tpu_custom_call" | custom-call | flops 6442450944 | bytes 37748736 | tf_op jit(solution)/shard_map/back_one/pallas_call | solution.py:109
  330.6 1.0 copy-done.10
  332.0 1.2 collective-permute-done.3
  333.2 1.8 add_convert_fusion.2
  335.0 6.5 %all-to-all-start.11 = ((bf16[16,64,128]{2,1,0:T(8,128)(2,1)}), bf16[16,64,128]{2,1,0:T(8,128)(2,1)S(1)}, u32[]{:S(2)}, u32[]{:S(2)}) async-start(bf16[16,64,128]{2,1,0:T(8,128)(2,1)} %bitcast.10), calls=%async_computation.11 | async-start | bytes 524288 | tf_op jit(solution)/shard_map/all_to_all | solution.py:624
  341.5 0.9 dynamic-slice_convert_fusion
  342.4 0.9 collective-permute-start.5
  343.3 1.1 reduce_sum.39
  344.4 4.4 %all-to-all-done.11 = bf16[16,64,128]{2,1,0:T(8,128)(2,1)S(1)} async-done(((bf16[16,64,128]{2,1,0:T(8,128)(2,1)}), bf16[16,64,128]{2,1,0:T(8,128)(2,1)S(1)}, u32[]{:S(2)}, u32[]{:S(2)}) %all-to-all-start.11) | async-done | bytes 262176 | tf_op jit(solution)/shard_map/all_to_all | solution.py:624
  348.8 0.9 broadcast_in_dim.11
  349.7 5.8 %all-to-all-start.15 = ((f32[32,25,128]{2,1,0:T(8,128)}), f32[32,25,128]{2,1,0:T(8,128)S(1)}, u32[]{:S(2)}, u32[]{:S(2)}) async-start(f32[32,25,128]{2,1,0:T(8,128)} %broadcast_in_dim.11), calls=%async_computation.15 | async-start | bytes 1048576 | tf_op jit(solution)/shard_map/all_to_all | solution.py:639
  355.5 2.1 add_convert_fusion
  357.6 12.2 %all-to-all-done.15 = f32[32,25,128]{2,1,0:T(8,128)S(1)} async-done(((f32[32,25,128]{2,1,0:T(8,128)}), f32[32,25,128]{2,1,0:T(8,128)S(1)}, u32[]{:S(2)}, u32[]{:S(2)}) %all-to-all-start.15) | async-done | bytes 409632 | tf_op jit(solution)/shard_map/all_to_all | solution.py:639
  369.8 4.5 %all-to-all-start.12 = ((bf16[16,72,256]{2,1,0:T(8,128)(2,1)}), bf16[16,72,256]{2,1,0:T(8,128)(2,1)S(1)}, u32[]{:S(2)}, u32[]{:S(2)}) async-start(bf16[16,72,256]{2,1,0:T(8,128)(2,1)} %bitcast.23), calls=%async_computation.12 | async-start | bytes 1179648 | tf_op jit(solution)/shard_map/all_to_all | solution.py:624
  374.9 1.0 convert_reduce_fusion.1
  375.9 1.5 collective-permute-start.8
  377.4 1.0 convert_reduce_fusion.2
  380.3 8.8 %all-to-all-done.12 = bf16[16,72,256]{2,1,0:T(8,128)(2,1)S(1)} async-done(((bf16[16,72,256]{2,1,0:T(8,128)(2,1)}), bf16[16,72,256]{2,1,0:T(8,128)(2,1)S(1)}, u32[]{:S(2)}, u32[]{:S(2)}) %all-to-all-start.12) | async-done | bytes 589856 | tf_op jit(solution)/shard_map/all_to_all | solution.py:624
  389.3 2.2 collective-permute-start.6
  392.8 0.7 reshape.111
  (80 shorter events, 8.4 us)
Async XLA Ops:
  0.6 18.9 %copy-start = (bf16[72,512]{1,0:T(8,128)(2,1)S(1)}, bf16[72,512]{1,0:T(8,128)(2,1)}, u32[]{:S(2)}) copy-start(bf16[72,512]{1,0:T(8,128)(2,1)} %param.14) | copy-start | bytes 221188
  15.0 4.4 %collective-permute-start = (bf16[1024,128]{1,0:T(8,128)(2,1)S(1)}, bf16[1024,128]{1,0:T(8,128)(2,1)S(1)}, u32[]{:S(2)}, u32[]{:S(2)}) collective-permute-start(bf16[1024,128]{1,0:T(8,128)(2,1)S(1)} %bitcast.28), channel_id=1, source_target_pairs={{0,1},{1,0},{2,3},{3,2},{4,5},{5,4},{6,7},{7,6},{8,9},{9,8},{10,11... | collective-permute-start | bytes 786440 | tf_op jit(solution)/shard_map/ppermute | solution.py:598
  19.6 23.1 %copy-start.20 = (bf16[16,1024]{1,0:T(8,128)(2,1)S(1)}, bf16[16,1024]{1,0:T(8,128)(2,1)}, u32[]{:S(2)}) copy-start(bf16[16,1024]{1,0:T(8,128)(2,1)} %param.15) | copy-start | bytes 98308
  19.6 28.2 %copy-start.15 = (s32[24]{0:T(128)S(1)}, s32[24]{0:T(128)}, u32[]{:S(2)}) copy-start(s32[24]{0:T(128)} %sides_ref.13) | copy-start | bytes 292
  39.0 3.4 collective-permute-start.1
  43.4 17.4 %all-to-all-start.5 = ((bf16[16,16,512]{2,1,0:T(8,128)(2,1)}), bf16[16,16,512]{2,1,0:T(8,128)(2,1)S(1)}, u32[]{:S(2)}, u32[]{:S(2)}) async-start(bf16[16,16,512]{2,1,0:T(8,128)(2,1)} %broadcast_in_dim.10), calls=%async_computation.5 | async-start | bytes 524288 | tf_op jit(solution)/shard_map/all_to_all | solution.py:607
  47.8 19.1 %copy-start.21 = (f32[1920]{0:T(1024)S(1)}, f32[1920]{0:T(1024)}, u32[]{:S(2)}) copy-start(f32[1920]{0:T(1024)} %param.19) | copy-start | bytes 23044
  47.8 19.1 %copy-start.22 = (f32[1920]{0:T(1024)S(1)}, f32[1920]{0:T(1024)}, u32[]{:S(2)}) copy-start(f32[1920]{0:T(1024)} %param.20) | copy-start | bytes 23044
  60.8 29.4 %copy-start.18 = (bf16[16,16,512]{2,1,0:T(8,128)(2,1)}, bf16[16,16,512]{2,1,0:T(8,128)(2,1)S(1)}, u32[]{:S(2)}) copy-start(bf16[16,16,512]{2,1,0:T(8,128)(2,1)S(1)} %all-to-all-done.5) | copy-start | bytes 786436
  60.8 12.2 %all-to-all-start.1 = ((f32[32,4,256]{2,1,0:T(4,128)}), f32[32,4,256]{2,1,0:T(4,128)S(1)}, u32[]{:S(2)}, u32[]{:S(2)}) async-start(f32[32,4,256]{2,1,0:T(4,128)} %get-tuple-element.61), calls=%async_computation.1 | async-start | bytes 262144 | tf_op jit(solution)/shard_map/all_to_all | solution.py:594
  67.0 57.1 %collective-permute-start.2 = (bf16[256,512]{1,0:T(8,128)(2,1)S(1)}, bf16[256,512]{1,0:T(8,128)(2,1)}, u32[]{:S(2)}, u32[]{:S(2)}) collective-permute-start(bf16[256,512]{1,0:T(8,128)(2,1)S(1)} %bitcast.26), channel_id=1, source_target_pairs={{0,1},{1,0},{2,3},{3,2},{4,5},{5,4},{6,7},{7,6},{8,9},{9,8},{10,11... | collective-permute-start | bytes 786440 | tf_op jit(solution)/shard_map/ppermute | solution.py:598
  73.1 27.2 %copy-start.11 = (f32[256,128]{1,0:T(8,128)S(1)}, f32[256,128]{1,0:T(8,128)}, u32[]{:S(2)}) copy-start(f32[256,128]{1,0:T(8,128)} %fc_ref.7) | copy-start | bytes 393220
  90.3 29.2 %copy-start.2 = (bf16[6144,256]{1,0:T(8,128)(2,1)}, bf16[6144,256]{1,0:T(8,128)(2,1)S(1)}, u32[]{:S(2)}) copy-start(bf16[6144,256]{1,0:T(8,128)(2,1)S(1)} %get-tuple-element.92.hat1_ref.hat_ref) | copy-start | bytes 9437188
  100.3 23.8 %copy-start.19 = (bf16[16,16,512]{2,1,0:T(8,128)(2,1)S(1)}, bf16[16,16,512]{2,1,0:T(8,128)(2,1)}, u32[]{:S(2)}) copy-start(bf16[16,16,512]{2,1,0:T(8,128)(2,1)} %copy-done.18) | copy-start | bytes 786436
  100.3 29.5 %copy-start.7 = (f32[128,512]{1,0:T(8,128)S(1)}, f32[128,512]{1,0:T(8,128)}, u32[]{:S(2)}) copy-start(f32[128,512]{1,0:T(8,128)} %fc_ref.6) | copy-start | bytes 786436
  100.3 29.5 %copy-start.16 = (f32[512]{0:T(512)S(1)}, f32[512]{0:T(512)}, u32[]{:S(2)}) copy-start(f32[512]{0:T(512)} %param.18) | copy-start | bytes 6148
  119.5 10.2 %all-to-all-start.4 = ((f32[32,2,128]{2,1,0:T(2,128)}), f32[32,2,128]{2,1,0:T(2,128)S(1)}, u32[]{:S(2)}, u32[]{:S(2)}) async-start(f32[32,2,128]{2,1,0:T(2,128)} %get-tuple-element.68), calls=%async_computation.4 | async-start | bytes 65536 | tf_op jit(solution)/shard_map/all_to_all | solution.py:594
  140.6 42.8 %copy-start.6 = (bf16[6144,256]{1,0:T(8,128)(2,1)}, bf16[6144,256]{1,0:T(8,128)(2,1)S(1)}, u32[]{:S(2)}) copy-start(bf16[6144,256]{1,0:T(8,128)(2,1)S(1)} %get-tuple-element.73.comb_ref) | copy-start | bytes 9437188
  214.6 1.0 copy-start.8
  215.6 0.7 copy-start.12
  216.3 10.1 %all-to-all-start.8 = ((f32[32,2,128]{2,1,0:T(2,128)}), f32[32,2,128]{2,1,0:T(2,128)S(1)}, u32[]{:S(2)}, u32[]{:S(2)}) async-start(f32[32,2,128]{2,1,0:T(2,128)} %get-tuple-element.83), calls=%async_computation.8 | async-start | bytes 65536 | tf_op jit(solution)/shard_map/all_to_all | solution.py:594
  227.4 0.7 copy-start.13
  228.1 18.4 %all-to-all-start.9 = ((f32[32,2,512]{2,1,0:T(2,128)}), f32[32,2,512]{2,1,0:T(2,128)}, u32[]{:S(2)}, u32[]{:S(2)}) async-start(f32[32,2,512]{2,1,0:T(2,128)} %get-tuple-element.90), calls=%async_computation.9 | async-start | bytes 262144 | tf_op jit(solution)/shard_map/all_to_all | solution.py:594
  233.2 8.5 %copy-start.9 = (f32[256,1024]{1,0:T(8,128)S(1)}, f32[256,1024]{1,0:T(8,128)}, u32[]{:S(2)}) copy-start(f32[256,1024]{1,0:T(8,128)} %copy-done.8) | copy-start | bytes 3145732
  236.7 6.2 %copy-start.14 = (f32[256,128]{1,0:T(8,128)S(1)}, f32[256,128]{1,0:T(8,128)}, u32[]{:S(2)}) copy-start(f32[256,128]{1,0:T(8,128)} %copy-done.13) | copy-start | bytes 393220
  242.5 31.1 %collective-permute-start.7 = (bf16[256,512]{1,0:T(8,128)(2,1)}, bf16[256,512]{1,0:T(8,128)(2,1)}, u32[]{:S(2)}, u32[]{:S(2)}) collective-permute-start(bf16[256,512]{1,0:T(8,128)(2,1)} %dynamic-slice_convert_fusion.1), channel_id=1, source_target_pairs={{0,1},{1,0},{2,3},{3,2},{4,5},{5,4},{6,7},{7,6},{8,9},{9,8},{10,11... | collective-permute-start | bytes 786440 | tf_op jit(solution)/shard_map/ppermute | solution.py:598
  266.2 1.6 copy-start.4
  267.8 11.3 %all-to-all-start.10 = ((f32[32,2,256]{2,1,0:T(2,128)}), f32[32,2,256]{2,1,0:T(2,128)S(1)}, u32[]{:S(2)}, u32[]{:S(2)}) async-start(f32[32,2,256]{2,1,0:T(2,128)} %get-tuple-element.94), calls=%async_computation.10 | async-start | bytes 131072 | tf_op jit(solution)/shard_map/all_to_all | solution.py:594
  279.1 21.9 %all-to-all-start.13 = ((bf16[16,16,512]{2,1,0:T(8,128)(2,1)}), bf16[16,16,512]{2,1,0:T(8,128)(2,1)}, u32[]{:S(2)}, u32[]{:S(2)}) async-start(bf16[16,16,512]{2,1,0:T(8,128)(2,1)} %bitcast.12), calls=%async_computation.13 | async-start | bytes 524288 | tf_op jit(solution)/shard_map/all_to_all | solution.py:624
  284.8 1.9 copy-start.3
  301.1 34.0 %all-to-all-start.14 = ((f32[32,25,128]{2,1,0:T(8,128)}), f32[32,25,128]{2,1,0:T(8,128)}, u32[]{:S(2)}, u32[]{:S(2)}) async-start(f32[32,25,128]{2,1,0:T(8,128)} %reshape.109), calls=%async_computation.14 | async-start | bytes 1048576 | tf_op jit(solution)/shard_map/all_to_all | solution.py:637
  307.2 1.9 copy-start.5
  330.6 1.0 copy-start.10
  331.6 1.6 collective-permute-start.3
  335.0 13.8 %all-to-all-start.11 = ((bf16[16,64,128]{2,1,0:T(8,128)(2,1)}), bf16[16,64,128]{2,1,0:T(8,128)(2,1)S(1)}, u32[]{:S(2)}, u32[]{:S(2)}) async-start(bf16[16,64,128]{2,1,0:T(8,128)(2,1)} %bitcast.10), calls=%async_computation.11 | async-start | bytes 524288 | tf_op jit(solution)/shard_map/all_to_all | solution.py:624
  342.4 13.1 %collective-permute-start.5 = (bf16[1152,256]{1,0:T(8,128)(2,1)}, bf16[1152,256]{1,0:T(8,128)(2,1)}, u32[]{:S(2)}, u32[]{:S(2)}) collective-permute-start(bf16[1152,256]{1,0:T(8,128)(2,1)} %dynamic-slice_convert_fusion), channel_id=1, source_target_pairs={{0,1},{1,0},{2,3},{3,2},{4,5},{5,4},{6,7},{7,6},{8,9},{9,8},{10,11... | collective-permute-start | bytes 1769480 | tf_op jit(solution)/shard_map/ppermute | solution.py:598
  348.8 21.0 %copy-start.17 = (bf16[16,64,128]{2,1,0:T(8,128)(2,1)}, bf16[16,64,128]{2,1,0:T(8,128)(2,1)S(1)}, u32[]{:S(2)}) copy-start(bf16[16,64,128]{2,1,0:T(8,128)(2,1)S(1)} %all-to-all-done.11) | copy-start | bytes 786436
  349.7 20.1 %all-to-all-start.15 = ((f32[32,25,128]{2,1,0:T(8,128)}), f32[32,25,128]{2,1,0:T(8,128)S(1)}, u32[]{:S(2)}, u32[]{:S(2)}) async-start(f32[32,25,128]{2,1,0:T(8,128)} %broadcast_in_dim.11), calls=%async_computation.15 | async-start | bytes 1048576 | tf_op jit(solution)/shard_map/all_to_all | solution.py:639
  369.8 19.4 %all-to-all-start.12 = ((bf16[16,72,256]{2,1,0:T(8,128)(2,1)}), bf16[16,72,256]{2,1,0:T(8,128)(2,1)S(1)}, u32[]{:S(2)}, u32[]{:S(2)}) async-start(bf16[16,72,256]{2,1,0:T(8,128)(2,1)} %bitcast.23), calls=%async_computation.12 | async-start | bytes 1179648 | tf_op jit(solution)/shard_map/all_to_all | solution.py:624
  374.2 19.9 %copy-start.1 = (bf16[72,512]{1,0:T(8,128)(2,1)S(1)}, bf16[72,512]{1,0:T(8,128)(2,1)}, u32[]{:S(2)}) copy-start(bf16[72,512]{1,0:T(8,128)(2,1)} %param.14) | copy-start | bytes 221188
  375.9 2.6 collective-permute-start.8
  378.4 1.3 collective-permute-start.4
  389.3 4.3 %collective-permute-start.6 = (f32[72,256]{1,0:T(8,128)S(1)}, f32[72,256]{1,0:T(8,128)S(1)}, u32[]{:S(2)}, u32[]{:S(2)}) collective-permute-start(f32[72,256]{1,0:T(8,128)S(1)} %convert_reduce_fusion), channel_id=1, source_target_pairs={{0,1},{1,0},{2,3},{3,2},{4,5},{5,4},{6,7},{7,6},{8,9},{9,8},{10,11... | collective-permute-start | bytes 221192 | tf_op jit(solution)/shard_map/ppermute | solution.py:598

commit v2 on v1

v2 whole, which is shorter than its diff:
```python
import functools

import jax
import jax.numpy as jnp
from jax import lax
from jax.experimental import pallas as pl
from jax.experimental.pallas import tpu as pltpu
from jax.sharding import PartitionSpec as P

C_IN = 1024
WIDTH = 256
INTER = 128
SIDE = 16
PIX = SIDE * SIDE
HALF = WIDTH // 2
EPS = 1e-05
AXES = ("fsdp", "dp")
HIGH = lax.Precision.HIGHEST
F32 = jnp.float32
BF16 = jnp.bfloat16
MIB = 1024 * 1024

PER_CONV_ONE = 4
PER_CONV_TWO = 4
PER_ACT_TWO = 4
PER_SLOPE_TWO = 4
PER_COMBINE = 4
PER_OUTPUT = 2
PER_PROJECT = 4
PER_BACK_THREE = 4
PER_BACK_TWO = 4
PER_WEIGHT_TWO = 2
PER_BACK_ONE = 2


def dot_f(left, right):
    return jnp.dot(left, right, preferred_element_type=F32)


def dot_rows(left, right):
    return lax.dot_general(left, right, (((0,), (0,)), ((), ())), preferred_element_type=F32)


def dot_last(left, right):
    return lax.dot_general(left, right, (((1,), (1,)), ((), ())), preferred_element_type=F32)


def high_f(left, right):
    return jnp.dot(left, right, preferred_element_type=F32, precision=HIGH)


def high_rows(left, right):
    return lax.dot_general(
        left, right, (((0,), (0,)), ((), ())), preferred_element_type=F32, precision=HIGH
    )


def high_last(left, right):
    return lax.dot_general(
        left, right, (((1,), (1,)), ((), ())), preferred_element_type=F32, precision=HIGH
    )


def pixel_mask(image_side, width):
    row = lax.broadcasted_iota(jnp.int32, (PIX, 128), 0)
    inside = ((row >> 4) < image_side) & ((row & 15) < image_side)
    return wide(jnp.where(inside, 1.0, 0.0).astype(F32), width)


def wide(mask, width):
    if width == 128:
        return mask
    return jnp.concatenate([mask] * (width // 128), axis=1)


def fold(values):
    rows, n = values.shape
    return jnp.sum(values.reshape(rows // 8, 8, n), axis=0)


def row_sum(values):
    return jnp.sum(values, axis=0, keepdims=True)


def total(payload_ref):
    return jnp.sum(payload_ref[...], axis=0)


def norm_terms(sums, count):
    mean = sums[0:1] / count
    variance = sums[1:2] / count - mean * mean
    return mean, lax.rsqrt(variance + EPS)


def send_rows(payload_ref, rows):
    block = jnp.concatenate(rows, axis=0)
    payload_ref[...] = jnp.broadcast_to(block[None], payload_ref.shape)


def silu_parts(half_pre):
    t = jnp.tanh(half_pre)
    a = 1.0 + t
    value = half_pre * a
    slope = 0.5 * a * (1.0 + half_pre * (1.0 - t))
    return value, slope


def whole(shape):
    zeros = (0,) * len(shape)
    return pl.BlockSpec(shape, lambda *_: zeros)


def rows_of(n_rows, width):
    return pl.BlockSpec((n_rows, width), lambda i: (i, 0))


SMEM_SPEC = pl.BlockSpec(memory_space=pltpu.SMEM)


def call(kernel, grid, ins, outs, scratch=(), vmem=32, flops=0, moved=0, name=None):
    arrays = [
        array
        if spec is SMEM_SPEC or near
        else pltpu.with_memory_space_constraint(array, pltpu.HBM)
        for array, spec, *near in ins
    ]
    shapes = [pltpu.HBM(shape, dtype) for shape, dtype, _ in outs]
    return pl.pallas_call(
        kernel,
        grid=(grid,),
        in_specs=[spec for _, spec, *_ in ins],
        out_specs=[spec for _, _, spec in outs],
        out_shape=shapes,
        scratch_shapes=list(scratch),
        compiler_params=pltpu.CompilerParams(
            dimension_semantics=("arbitrary",), vmem_limit_bytes=vmem * MIB
        ),
        cost_estimate=pl.CostEstimate(flops=flops, bytes_accessed=moved, transcendentals=0),
        name=name,
    )(*arrays)


def pack_kernel(core_ref, one_ref, two_ref, three_ref, first_ref, second_ref):
    def put(half):
        first_ref[...] = jnp.broadcast_to(
            one_ref[:, half * HALF : (half + 1) * HALF][None], first_ref.shape
        )
        at = 0
        for ref, blocks in ((two_ref, 2), (three_ref, 4)):
            rows = ref.shape[0]
            for b in range(blocks):
                low = (half * blocks + b) * 128
                piece = ref[:, low : low + 128]
                for f in range(second_ref.shape[0]):
                    second_ref[f, pl.ds(at, rows)] = piece
                at += rows

    for core in range(2):
        pl.when(core_ref[0] == core)(functools.partial(put, core))


def unpack_kernel(core_ref, mine_ref, other_ref, two_ref, three_ref, wide_ref):
    shards = mine_ref.shape[0]
    two_rows = two_ref.shape[0] // shards
    three_rows = three_ref.shape[0] // shards

    def put(half, source_ref):
        for f in range(shards):
            at = 0
            for b in range(2):
                piece = source_ref[f, pl.ds(at, two_rows)].astype(F32)
                wide_ref[pl.ds(f * two_rows, two_rows), pl.ds(half * WIDTH + b * 128, 128)] = piece
                at += two_rows
            for b in range(4):
                piece = source_ref[f, pl.ds(at, three_rows)]
                three_ref[pl.ds(f * three_rows, three_rows), pl.ds(half * 512 + b * 128, 128)] = piece
                at += three_rows

    for core in range(2):

        @pl.when(core_ref[0] == core)
        def _():
            put(core, mine_ref)
            put(1 - core, other_ref)

    two_ref[...] = wide_ref[...].astype(BF16)


def conv_one_kernel(
    per, core_ref, sides_ref, x_ref, mine_ref, other_ref, h_ref, w_out_ref, send_ref,
    acc_ref, count_ref,
):
    step = pl.program_id(0)

    @pl.when(step == 0)
    def _():
        acc_ref[...] = jnp.zeros_like(acc_ref)
        count_ref[0] = 0.0

        def put(core):
            for half, ref in ((core, mine_ref), (1 - core, other_ref)):
                w_out_ref[:, half * HALF : (half + 1) * HALF] = ref[...].reshape(C_IN, HALF)

        for core in range(2):
            pl.when(core_ref[0] == core)(functools.partial(put, core))

    h = dot_f(x_ref[...], w_out_ref[...])
    h_ref[...] = h
    for j in range(per):
        side = SIDE - 2 * sides_ref[step * per + j]
        mask = pixel_mask(side, WIDTH)
        one = h[j * PIX : (j + 1) * PIX]
        kept = one * mask
        acc_ref[0:8] += fold(kept)
        acc_ref[8:16] += fold(kept * one)
        count_ref[0] += (side * side).astype(F32)

    @pl.when(step == pl.num_programs(0) - 1)
    def _():
        count = jnp.full((1, WIDTH), count_ref[0], F32)
        send_rows(
            send_ref,
            [row_sum(acc_ref[0:8]), row_sum(acc_ref[8:16]), count, jnp.zeros((1, WIDTH), F32)],
        )


def edge_masks(width):
    column = lax.broadcasted_iota(jnp.int32, (PIX, 128), 0) & 15
    first = jnp.where(column == 0, 0.0, 1.0).astype(F32)
    last = jnp.where(column == 15, 0.0, 1.0).astype(F32)
    return wide(first, width), wide(last, width)


def put_taps(taps_ref, j, act, first, last):
    shifted = (pltpu.roll(act, 1, 0) * first, act, pltpu.roll(act, PIX - 1, 0) * last)
    for d in range(3):
        piece = shifted[d].astype(BF16)
        for q in range(2):
            taps_ref[pl.ds(SIDE + j * (PIX + SIDE), PIX), pl.ds(q * 384 + d * 128, 128)] = piece[
                :, q * HALF : (q + 1) * HALF
            ]


def conv_two_kernel(
    per, sides_ref, got_ref, h_ref, w_ref, gain_ref, shift_ref, hat_ref, h2_ref, vec_ref, send_ref,
    taps_ref, acc_ref,
):
    step = pl.program_id(0)

    @pl.when(step == 0)
    def _():
        sums = total(got_ref)
        mean, inv = norm_terms(sums, sums[2:3])
        vec_ref[0:1] = mean
        vec_ref[1:2] = inv
        vec_ref[2:3] = sums[2:3]
        acc_ref[...] = jnp.zeros_like(acc_ref)
        taps_ref[...] = jnp.zeros_like(taps_ref)

    gain = gain_ref[:, :WIDTH] * 0.5
    shift = shift_ref[:, :WIDTH] * 0.5
    first, last = edge_masks(WIDTH)
    for j in range(per):
        side = SIDE - 2 * sides_ref[step * per + j]
        mask = pixel_mask(side, WIDTH)
        rows = pl.ds(j * PIX, PIX)
        hat = (h_ref[rows] - vec_ref[0:1]) * vec_ref[1:2]
        hat_ref[pl.ds(j * PIX, PIX)] = hat.astype(BF16)
        half_pre = hat * gain + shift
        act = half_pre * (1.0 + jnp.tanh(half_pre)) * mask
        put_taps(taps_ref, j, act, first, last)
    height = per * (PIX + SIDE)
    for q in range(2):
        cols = pl.ds(q * WIDTH, WIDTH)
        patches = jnp.concatenate(
            [taps_ref[pl.ds(SIDE * d, height), pl.ds(q * 384, 384)] for d in range(3)], axis=1
        )
        both = dot_f(patches, w_ref[:, cols])
        for j in range(per):
            h2 = both[j * (PIX + SIDE) : j * (PIX + SIDE) + PIX]
            h2_ref[pl.ds(j * PIX, PIX), cols] = h2
            side = SIDE - 2 * sides_ref[step * per + j]
            kept = h2 * pixel_mask(side, WIDTH)
            acc_ref[0:8, cols] += fold(kept)
            acc_ref[8:16, cols] += fold(kept * h2)

    @pl.when(step == pl.num_programs(0) - 1)
    def _():
        send_rows(send_ref, [row_sum(acc_ref[0:8]), row_sum(acc_ref[8:16])])


def act_two_kernel(
    per, sides_ref, one_ref, got_ref, h2_ref, gain_ref, shift_ref, fc_ref,
    hat_ref, pooled_ref, zin_ref, vec_ref, send_ref,
):
    step = pl.program_id(0)

    @pl.when(step == 0)
    def _():
        sums = total(got_ref)
        mean, inv = norm_terms(sums, jnp.concatenate([one_ref[2:3]] * 2, axis=1))
        vec_ref[0:1] = mean
        vec_ref[1:2] = inv

    gain = gain_ref[:, WIDTH : 3 * WIDTH] * 0.5
    shift = shift_ref[:, WIDTH : 3 * WIDTH] * 0.5
    for j in range(per):
        side = SIDE - 2 * sides_ref[step * per + j]
        mask = pixel_mask(side, 2 * WIDTH)
        rows = pl.ds(j * PIX, PIX)
        hat = (h2_ref[rows] - vec_ref[0:1]) * vec_ref[1:2]
        hat_ref[rows] = hat.astype(BF16)
        half_pre = hat * gain + shift
        value = half_pre * ((1.0 + jnp.tanh(half_pre)) * mask)
        sums = row_sum(fold(value))
        image = pl.ds(step * per + j, 1)
        pixels = (side * side).astype(F32)
        pooled_ref[image] = (sums[:, :WIDTH] + sums[:, WIDTH:]) / pixels

    @pl.when(step == pl.num_programs(0) - 1)
    def _():
        z = high_f(pooled_ref[...], fc_ref[...])
        zin_ref[...] = z
        send_rows(send_ref, [row_sum(z), row_sum(z * z)])


def slope_two_kernel(
    per, sides_ref, hat_ref, gain_ref, shift_ref, a2_ref, slope_ref, t2_ref, t4_ref
):
    step = pl.program_id(0)
    gain = gain_ref[:, WIDTH : 3 * WIDTH] * 0.5
    shift = shift_ref[:, WIDTH : 3 * WIDTH] * 0.5
    for j in range(per):
        side = SIDE - 2 * sides_ref[step * per + j]
        mask = pixel_mask(side, 2 * WIDTH)
        rows = pl.ds(j * PIX, PIX)
        hat = hat_ref[rows].astype(F32)
        half_pre = hat * gain + shift
        a = (1.0 + jnp.tanh(half_pre)) * mask
        value = half_pre * a
        slope = (0.5 * a) * (1.0 + 2.0 * half_pre - value)
        a2_ref[rows] = value.astype(BF16)
        slope_ref[rows] = slope.astype(BF16)
        image = pl.ds(step * per + j, 1)
        t2_ref[image] = row_sum(fold(slope))
        t4_ref[image] = row_sum(fold(slope * hat))


def hidden_terms(zin, sums, n_images, gain_ref, shift_ref):
    mean, inv = norm_terms(sums, n_images)
    zhat = (zin - mean) * inv
    cols = slice(3 * WIDTH, 3 * WIDTH + INTER)
    half_z = (zhat * gain_ref[:, cols] + shift_ref[:, cols]) * 0.5
    value, slope = silu_parts(half_z)
    return zhat, inv, value, slope


def combine_kernel(
    per, n_images, got_ref, zin_ref, a2_ref, w3_ref, fc_ref, bias_ref, gain_ref, shift_ref,
    att_ref, comb_ref, gw_ref, csum_ref, hid_ref, send_ref, gram_ref, acc_ref,
):
    step = pl.program_id(0)

    @pl.when(step == 0)
    def _():
        zhat, inv, hidden, slope = hidden_terms(
            zin_ref[...], total(got_ref), n_images, gain_ref, shift_ref
        )
        hid_ref[0] = zhat
        hid_ref[1] = hidden
        hid_ref[2] = slope
        hid_ref[3] = jnp.broadcast_to(inv, slope.shape)
        logits = high_f(hidden, fc_ref[...]) + bias_ref[...]
        left, right = logits[:, :WIDTH], logits[:, WIDTH:]
        top = jnp.maximum(left, right)
        left, right = jnp.exp(left - top), jnp.exp(right - top)
        both = left + right
        att_ref[:, :WIDTH] = left / both
        att_ref[:, WIDTH:] = right / both
        gram_ref[...] = jnp.zeros_like(gram_ref)
        acc_ref[...] = jnp.zeros_like(acc_ref)

    for j in range(per):
        rows = pl.ds(j * PIX, PIX)
        att = att_ref[pl.ds(step * per + j, 1)]
        a2 = a2_ref[rows].astype(F32)
        comb = (att[:, :WIDTH] * a2[:, :WIDTH] + att[:, WIDTH:] * a2[:, WIDTH:]).astype(BF16)
        comb_ref[rows] = comb
        acc_ref[...] += fold(comb.astype(F32))
    comb = comb_ref[...]
    gram_ref[...] += dot_rows(comb, comb)

    @pl.when(step == pl.num_programs(0) - 1)
    def _():
        w3 = w3_ref[...].astype(F32)
        csum = row_sum(acc_ref[...])
        csum_ref[...] = csum
        gw = high_f(gram_ref[...], w3)
        gw_ref[...] = gw
        send_rows(send_ref, [high_f(csum, w3), row_sum(w3 * gw)])


def output_kernel(
    per, sides_ref, one_ref, got_ref, comb_ref, x_ref, cot_ref, w3_ref, gain_ref, shift_ref,
    out_ref, u3_ref, stat_ref, send_ref, vec_ref, acc_ref,
):
    step = pl.program_id(0)

    @pl.when(step == 0)
    def _():
        count = jnp.concatenate([one_ref[2:3]] * 4, axis=1)
        mean, inv = norm_terms(total(got_ref), count)
        scale = inv * gain_ref[:, 3 * WIDTH + INTER :]
        stat_ref[0:1] = mean
        stat_ref[1:2] = inv
        stat_ref[2:3] = scale
        stat_ref[3:4] = count
        vec_ref[0:1] = scale
        vec_ref[1:2] = shift_ref[:, 3 * WIDTH + INTER :] - mean * scale
        vec_ref[2:3] = 0.5 * scale
        acc_ref[...] = jnp.zeros_like(acc_ref)

    chunk = 16
    lanes = 512
    for j in range(per):
        side = SIDE - 2 * sides_ref[step * per + j]
        mask = pixel_mask(side, 128)
        h3 = dot_f(comb_ref[pl.ds(j * PIX, PIX)], w3_ref[...])
        for n in range(C_IN // lanes):
            cols = pl.ds(n * lanes, lanes)
            ups = jnp.zeros((8, lanes), F32)
            products = jnp.zeros((8, lanes), F32)
            for c in range(PIX // chunk):
                rows = pl.ds(j * PIX + c * chunk, chunk)
                scaled = (
                    h3[c * chunk : (c + 1) * chunk, n * lanes : (n + 1) * lanes] * vec_ref[0:1, cols]
                )
                pre = scaled + vec_ref[1:2, cols] + x_ref[rows, cols].astype(F32)
                half_pre = pre * 0.5
                a = (1.0 + jnp.tanh(half_pre)) * wide(mask[c * chunk : (c + 1) * chunk], lanes)
                value = half_pre * a
                out_ref[rows, cols] = value.astype(BF16)
                up = cot_ref[rows, cols].astype(F32) * (a * (1.0 + pre - value))
                u3_ref[rows, cols] = (up * vec_ref[2:3, cols]).astype(BF16)
                ups = ups + fold(up)
                products = products + fold(up * scaled)
            acc_ref[0:8, cols] += ups
            acc_ref[8:16, cols] += products

    @pl.when(step == pl.num_programs(0) - 1)
    def _():
        send_rows(
            send_ref,
            [0.5 * row_sum(acc_ref[0:8]), 0.5 * row_sum(acc_ref[8:16]) / vec_ref[0:1]],
        )


def project_kernel(comb_ref, u3_ref, w3_ref, p_ref, cu_ref):
    @pl.when(pl.program_id(0) == 0)
    def _():
        cu_ref[...] = jnp.zeros_like(cu_ref)

    u3 = u3_ref[...]
    p_ref[...] = dot_last(u3, w3_ref[...]).astype(BF16)
    cu_ref[...] += dot_rows(comb_ref[...], u3)


def back_three_kernel(
    per, three_ref, got_ref, hid_ref, comb_ref, p_ref, a2_ref, slope_ref,
    hat_ref, w3_ref, cu_ref, gw_ref, csum_ref, att_ref, fc_ref,
    t1_ref, t3_ref, duz_ref, w3g_ref, fcg_ref, norm_ref, s_ref, c_ref, send_ref, datt_ref,
):
    step = pl.program_id(0)

    @pl.when(step == 0)
    def _():
        mean, inv = three_ref[0:1], three_ref[1:2]
        scale, count = three_ref[2:3], three_ref[3:4]
        sums = total(got_ref)
        dshift = sums[0:1]
        dgain = (sums[1:2] - mean * dshift) * inv
        norm_ref[0:1] = dgain
        norm_ref[1:2] = dshift
        k2 = scale * inv * dgain / count
        k1 = scale * dshift / count - mean * k2
        w3 = w3_ref[...].astype(F32)
        s_ref[...] = dot_last((w3 * k2).astype(BF16), w3_ref[...]).astype(BF16)
        c_ref[...] = high_last(jnp.broadcast_to(k1, (8, C_IN)), w3)
        csum = jnp.broadcast_to(csum_ref[...], (8, WIDTH))
        outer = high_rows(csum, jnp.broadcast_to(k1, (8, C_IN))) * 0.125
        w3g_ref[...] = cu_ref[...] - outer - gw_ref[...] * k2

    corr = dot_f(comb_ref[...], s_ref[...])
    for j in range(per):
        rows = pl.ds(j * PIX, PIX)
        dcomb = p_ref[rows].astype(F32) - corr[j * PIX : (j + 1) * PIX] - c_ref[0:1]
        image = pl.ds(step * per + j, 1)
        for q in range(2):
            cols = pl.ds(q * WIDTH, WIDTH)
            datt_ref[image, cols] = row_sum(fold(dcomb * a2_ref[rows, cols].astype(F32)))
            u = dcomb * slope_ref[rows, cols].astype(F32)
            t1_ref[image, cols] = row_sum(fold(u))
            t3_ref[image, cols] = row_sum(fold(u * hat_ref[rows, cols].astype(F32)))

    @pl.when(step == pl.num_programs(0) - 1)
    def _():
        att = att_ref[...]
        datt = datt_ref[...]
        both = att * datt
        inner = both[:, :WIDTH] + both[:, WIDTH:]
        dlog = both - att * jnp.concatenate([inner, inner], axis=1)
        zhat, hidden, slope = hid_ref[0], hid_ref[1], hid_ref[2]
        fcg = high_rows(hidden, dlog)
        duz = high_last(dlog, fc_ref[...]) * slope
        duz_ref[...] = duz
        bias = row_sum(dlog)
        rows = [row_sum(duz), row_sum(duz * zhat)]
        for b in range(4):
            cols = slice(b * 128, (b + 1) * 128)
            fcg_ref[pl.ds(b * INTER, INTER)] = fcg[:, cols]
            rows.append(bias[:, cols])
        send_rows(send_ref, rows + [jnp.zeros((2, 128), F32)])


def back_att_kernel(
    n_images, got_ref, hid_ref, duz_ref, pooled_ref, sides_ref, fc_ref, att_ref,
    t1_ref, t2_ref, t3_ref, t4_ref, fcg_ref, gain_ref,
    dpool_ref, pack_ref, bias_ref, norm_ref, send_ref,
):
    zhat, inv = hid_ref[0], hid_ref[3, 0:1]
    sums = total(got_ref)
    norm_ref[0:1] = sums[1:2]
    norm_ref[1:2] = sums[0:1]
    for b in range(4):
        bias_ref[:, b * 128 : (b + 1) * 128] = sums[2 + b : 3 + b]
    scale = inv * gain_ref[:, 3 * WIDTH : 3 * WIDTH + INTER]
    dzin = scale * (duz_ref[...] - (sums[0:1] + zhat * sums[1:2]) / n_images)
    pack_ref[0:WIDTH] = high_rows(pooled_ref[...], dzin)
    pack_ref[WIDTH:] = fcg_ref[...]
    dpool_ref[...] = high_last(dzin, fc_ref[...])
    for i in range(dpool_ref.shape[0]):
        side = SIDE - 2 * sides_ref[i]
        dpool_ref[i : i + 1] = dpool_ref[i : i + 1] / (side * side).astype(F32)
    dpool = dpool_ref[...]
    both = jnp.concatenate([dpool, dpool], axis=1)
    att = att_ref[...]
    send_rows(
        send_ref,
        [
            row_sum(att * t1_ref[...] + both * t2_ref[...]),
            row_sum(att * t3_ref[...] + both * t4_ref[...]),
        ],
    )


def back_two_kernel(
    per, sides_ref, one_ref, two_ref, got_ref, comb_ref, p_ref, s_ref, c_ref, slope_ref, hat2_ref, hat1_ref, att_ref,
    dpool_ref, w_ref, gain_ref, shift_ref, dh2_ref, u1_ref, norm_ref, send_ref,
    vec_ref, pad_ref, acc_ref,
):
    step = pl.program_id(0)

    @pl.when(step == 0)
    def _():
        count = jnp.concatenate([one_ref[2:3]] * 2, axis=1)
        scale = two_ref[1:2] * gain_ref[:, WIDTH : 3 * WIDTH]
        sums = total(got_ref)
        norm_ref[0:1] = sums[1:2]
        norm_ref[1:2] = sums[0:1]
        vec_ref[0:1] = scale
        vec_ref[1:2] = scale * sums[0:1] / count
        vec_ref[2:3] = scale * sums[1:2] / count
        acc_ref[...] = jnp.zeros_like(acc_ref)
        pad_ref[...] = jnp.zeros_like(pad_ref)

    first, last = edge_masks(HALF)
    corr = dot_f(comb_ref[...], s_ref[...])
    for j in range(per):
        rows = pl.ds(j * PIX, PIX)
        side = SIDE - 2 * sides_ref[step * per + j]
        mask = pixel_mask(side, WIDTH)
        image = pl.ds(step * per + j, 1)
        dcomb = p_ref[rows].astype(F32) - corr[j * PIX : (j + 1) * PIX] - c_ref[0:1]
        dpool = dpool_ref[image]
        for q in range(2):
            cols = pl.ds(q * WIDTH, WIDTH)
            scale = vec_ref[0:1, cols]
            up = dcomb * (att_ref[image, cols] * scale) + dpool * scale
            dh2 = slope_ref[rows, cols].astype(F32) * up - mask * (
                vec_ref[1:2, cols] + hat2_ref[rows, cols].astype(F32) * vec_ref[2:3, cols]
            )
            dh2 = dh2.astype(BF16)
            dh2_ref[rows, cols] = dh2
            pad_ref[pl.ds(SIDE + j * (PIX + SIDE), PIX), cols] = dh2
    height = per * (PIX + SIDE)
    for q in range(2):
        lines = jnp.concatenate(
            [pad_ref[pl.ds(SIDE * (2 - d), height), pl.ds(q * WIDTH, WIDTH)] for d in range(3)],
            axis=1,
        )
        weight = jnp.concatenate(
            [
                jnp.concatenate(
                    [
                        w_ref[pl.ds((3 * r + d) * HALF, HALF), pl.ds(q * WIDTH, WIDTH)]
                        for r in range(3)
                    ],
                    axis=1,
                )
                for d in range(3)
            ],
            axis=0,
        )
        both = dot_last(lines, weight)
        for j in range(per):
            rows = pl.ds(j * PIX, PIX)
            side = SIDE - 2 * sides_ref[step * per + j]
            mask = pixel_mask(side, 128)
            y = both[j * (PIX + SIDE) : j * (PIX + SIDE) + PIX]
            da1 = (
                y[:, HALF : 2 * HALF]
                + pltpu.roll(y[:, :HALF], PIX - 1, 0) * last
                + pltpu.roll(y[:, 2 * HALF :], 1, 0) * first
            )
            cols = pl.ds(q * HALF, HALF)
            hat = hat1_ref[rows, cols].astype(F32)
            half_pre = 0.5 * (hat * gain_ref[:, cols] + shift_ref[:, cols])
            _, slope = silu_parts(half_pre)
            u1 = da1 * slope * mask
            u1_ref[rows, cols] = u1.astype(BF16)
            acc_ref[0:8, cols] += fold(u1)
            acc_ref[8:16, cols] += fold(u1 * hat)

    @pl.when(step == pl.num_programs(0) - 1)
    def _():
        send_rows(send_ref, [row_sum(acc_ref[0:8]), row_sum(acc_ref[8:16])])


def weight_two_kernel(
    per, core_ref, sides_ref, hat_ref, dh2_ref, gain_ref, shift_ref, keep_ref, give_ref,
    taps_ref, acc_ref,
):
    step = pl.program_id(0)

    @pl.when(step == 0)
    def _():
        acc_ref[...] = jnp.zeros_like(acc_ref)
        taps_ref[...] = jnp.zeros_like(taps_ref)

    gain = gain_ref[:, :WIDTH] * 0.5
    shift = shift_ref[:, :WIDTH] * 0.5
    first, last = edge_masks(WIDTH)
    height = PIX + SIDE
    for j in range(per):
        side = SIDE - 2 * sides_ref[step * per + j]
        mask = pixel_mask(side, WIDTH)
        rows = pl.ds(j * PIX, PIX)
        half_pre = hat_ref[rows].astype(F32) * gain + shift
        act = half_pre * (1.0 + jnp.tanh(half_pre)) * mask
        put_taps(taps_ref, j, act, first, last)
    for q in range(2):
        patches = jnp.concatenate(
            [
                jnp.concatenate(
                    [
                        taps_ref[pl.ds(SIDE * d + j * height, PIX), pl.ds(q * 384, 384)]
                        for d in range(3)
                    ],
                    axis=1,
                )
                for j in range(per)
            ],
            axis=0,
        )
        acc_ref[q] += dot_rows(dh2_ref[:, q * WIDTH : (q + 1) * WIDTH], patches)

    @pl.when(step == pl.num_programs(0) - 1)
    def _():
        def put(core):
            keep_ref[...] = acc_ref[core].T
            give_ref[...] = acc_ref[1 - core].T

        for core in range(2):
            pl.when(core_ref[0] == core)(functools.partial(put, core))


def back_one_kernel(
    per, core_ref, sides_ref, one_ref, three_ref, got_ref, u1_ref, hat_ref, u3_ref, x_ref, w_ref, gain_ref,
    norm2_ref, norm_att_ref, norm3_ref,
    ig_ref, keep_ref, give_ref, gain_out_ref, shift_out_ref, vec_ref, wide_ref, dh_ref, acc_ref,
):
    step = pl.program_id(0)

    @pl.when(step == 0)
    def _():
        count = one_ref[2:3]
        scale = one_ref[1:2] * gain_ref[:, :WIDTH]
        sums = total(got_ref)
        for row, out_ref in ((0, gain_out_ref), (1, shift_out_ref)):
            out_ref[:, :WIDTH] = sums[1 - row : 2 - row]
            out_ref[:, WIDTH : 3 * WIDTH] = norm2_ref[row : row + 1]
            out_ref[:, 3 * WIDTH : 3 * WIDTH + INTER] = norm_att_ref[row : row + 1]
            out_ref[:, 3 * WIDTH + INTER :] = norm3_ref[row : row + 1]
        vec_ref[0:1] = scale
        vec_ref[1:2] = scale * sums[0:1] / count
        vec_ref[2:3] = scale * sums[1:2] / count
        wide_ref[...] = 1.0 / three_ref[2:3]
        acc_ref[...] = jnp.zeros_like(acc_ref)

    for j in range(per):
        rows = pl.ds(j * PIX, PIX)
        side = SIDE - 2 * sides_ref[step * per + j]
        mask = pixel_mask(side, WIDTH)
        dh_ref[rows] = (
            u1_ref[rows].astype(F32) * vec_ref[0:1]
            - mask * (vec_ref[1:2] + hat_ref[rows].astype(F32) * vec_ref[2:3])
        ).astype(BF16)
    dh = dh_ref[...]
    acc_ref[...] += dot_rows(dh, x_ref[...])
    dx = dot_last(dh, w_ref[...])
    ig_ref[...] = (u3_ref[...].astype(F32) * wide_ref[...] + dx).astype(BF16)

    @pl.when(step == pl.num_programs(0) - 1)
    def _():
        def put(core):
            keep_ref[...] = acc_ref[core * HALF : (core + 1) * HALF].T
            give_ref[...] = acc_ref[(1 - core) * HALF : (2 - core) * HALF].T

        for core in range(2):
            pl.when(core_ref[0] == core)(functools.partial(put, core))


def round_up(value, multiple):
    return -(-value // multiple) * multiple


def pack_three_kernel(core_ref, w_ref, fc_ref, keep_ref, give_ref):
    shards = keep_ref.shape[0]
    w_rows = w_ref.shape[0] // shards
    fc_rows = fc_ref.shape[0] // (2 * shards)

    def put(half, out_ref):
        for f in range(shards):
            for b in range(4):
                low = (half * 4 + b) * 128
                out_ref[f, pl.ds(b * w_rows, w_rows)] = w_ref[
                    pl.ds(f * w_rows, w_rows), pl.ds(low, 128)
                ]
            out_ref[f, pl.ds(4 * w_rows, fc_rows)] = fc_ref[
                pl.ds((half * shards + f) * fc_rows, fc_rows)
            ]

    for core in range(2):

        @pl.when(core_ref[0] == core)
        def _():
            put(core, keep_ref)
            put(1 - core, give_ref)


def pack_two_kernel(keep_ref, other_ref, fc_ref, out_ref):
    shards, slot, _ = out_ref.shape
    rows = keep_ref.shape[0] // shards
    padded = round_up(rows, 16)
    fc = fc_ref[...]
    fc_half = (slot - padded) * 2 - fc.shape[0]
    if fc_half:
        fc = jnp.concatenate([fc, jnp.zeros((fc_half, 128), F32)], axis=0)
    fc = jnp.concatenate([fc[: slot - padded], fc[slot - padded :]], axis=1).astype(BF16)
    for f in range(shards):
        part = keep_ref[pl.ds(f * rows, rows)] + other_ref[pl.ds(f * rows, rows)]
        if padded > rows:
            part = jnp.concatenate([part, jnp.zeros((padded - rows, WIDTH), F32)], axis=0)
        out_ref[f, pl.ds(0, padded)] = part.astype(BF16)
        out_ref[f, pl.ds(padded, slot - padded)] = fc


def everyone(payload):
    return lax.all_to_all(payload, AXES, 0, 0, tiled=True)


def other_core(array):
    return lax.ppermute(array, "dp", [(0, 1), (1, 0)])


def both_halves(mine, axis=1):
    core = lax.axis_index("dp")
    other = other_core(mine)
    return jnp.where(
        core == 0,
        jnp.concatenate([mine, other], axis=axis),
        jnp.concatenate([other, mine], axis=axis),
    )


def gather_weights(core, weights):
    shards = lax.axis_size("fsdp")
    one, two, three = weights
    first = (shards, one.shape[0], HALF)
    second = (shards, 2 * two.shape[0] + 4 * three.shape[0], 128)
    spread_one, spread_two = call(
        pack_kernel,
        1,
        [(core, SMEM_SPEC)] + [(weight, whole(weight.shape)) for weight in weights],
        [(first, BF16, whole(first)), (second, BF16, whole(second))],
        flops=1000000,
        moved=4000000,
        name="pack",
    )
    mine = lax.all_to_all(spread_one, "fsdp", 0, 0, tiled=True)
    other = other_core(mine)
    spread_two, mine, other = lax.optimization_barrier((spread_two, mine, other))
    mine_two = lax.all_to_all(spread_two, "fsdp", 0, 0, tiled=True)

    def others(mine_two, after):
        mine_two, _ = lax.optimization_barrier((mine_two, after))
        other_two = other_core(mine_two)
        shapes = [(shards * weight.shape[0], weight.shape[1]) for weight in (two, three)]
        return call(
            unpack_kernel,
            1,
            [(core, SMEM_SPEC), (mine_two, whole(second), True), (other_two, whole(second), True)],
            [(shape, BF16, whole(shape)) for shape in shapes],
            [pltpu.VMEM(shapes[0], F32)],
            flops=1000000,
            moved=4000000,
            name="unpack",
        )

    return mine, other, functools.partial(others, mine_two)


def slots(parts):
    return lax.all_to_all(parts, "fsdp", 0, 0, tiled=True)


def body(
    inputs,
    sides,
    weight_one,
    weight_two,
    weight_three,
    fc_first,
    fc_second,
    fc_bias,
    bn_gain,
    bn_shift,
    cotangent,
):
    images = inputs.shape[0]
    rows = images * PIX
    devices = lax.axis_size("fsdp") * lax.axis_size("dp")
    n_images = float(images * devices)
    x = inputs.reshape(rows, C_IN)
    cot = cotangent.reshape(rows, C_IN)
    gain = bn_gain.reshape(1, -1)
    shift = bn_shift.reshape(1, -1)
    bias = fc_bias.reshape(1, -1)
    n_ch = gain.shape[1]
    core = lax.axis_index("dp").astype(jnp.int32).reshape(1)

    def split(most):
        per = max(n for n in range(1, most + 1) if images % n == 0)
        return per, images // per

    core_in = (core, SMEM_SPEC)
    sides_in = (sides, SMEM_SPEC)
    gain_in = (gain, whole((1, n_ch)))
    shift_in = (shift, whole((1, n_ch)))

    def payload(k, n):
        return ((devices, k, n), F32, whole((devices, k, n)))

    def small(*shape):
        return (shape, F32, whole(shape))

    def full(array):
        return (array, whole(array.shape))

    def near(array):
        return (array, whole(array.shape), True)

    def blocks(array):
        return (array, rows_of(per * PIX, array.shape[1]))

    def blocks_out(width, dtype=BF16):
        return ((rows, width), dtype, rows_of(per * PIX, width))

    mine, other, others = gather_weights(core, (weight_one, weight_two, weight_three))

    per, steps = split(PER_CONV_ONE)
    h1, full_one, send = call(
        functools.partial(conv_one_kernel, per),
        steps,
        [core_in, sides_in, blocks(x), near(mine), near(other)],
        [blocks_out(WIDTH, F32), ((C_IN, WIDTH), BF16, whole((C_IN, WIDTH))), payload(4, WIDTH)],
        [pltpu.VMEM((16, WIDTH), F32), pltpu.SMEM((1,), F32)],
        flops=2 * rows * C_IN * WIDTH,
        moved=rows * C_IN * 2 + rows * WIDTH * 4,
        name="conv_one",
    )
    got_one = everyone(send)
    full_two, full_three = others(send)

    per, steps = split(PER_CONV_TWO)
    hat1, h2, stat1, send = call(
        functools.partial(conv_two_kernel, per),
        steps,
        [sides_in, near(got_one), blocks(h1), full(full_two), gain_in, shift_in],
        [blocks_out(WIDTH), blocks_out(2 * WIDTH, F32), small(8, WIDTH), payload(2, 2 * WIDTH)],
        [
            pltpu.VMEM((per * (PIX + SIDE) + 2 * SIDE, 6 * HALF), BF16),
            pltpu.VMEM((16, 2 * WIDTH), F32),
        ],
        flops=2 * rows * 9 * HALF * 2 * WIDTH,
        moved=rows * WIDTH * 14,
        name="conv_two",
    )
    got_two = everyone(send)

    per, steps = split(PER_ACT_TWO)
    hat2, pooled, zin, stat2, send = call(
        functools.partial(act_two_kernel, per),
        steps,
        [
            sides_in,
            full(stat1),
            near(got_two),
            blocks(h2),
            gain_in,
            shift_in,
            full(fc_first),
        ],
        [
            blocks_out(2 * WIDTH),
            small(images, WIDTH),
            small(images, INTER),
            small(8, 2 * WIDTH),
            payload(2, INTER),
        ],
        flops=rows * 2 * WIDTH * 20,
        moved=rows * 2 * WIDTH * 10,
        name="act_two",
    )
    got_att = everyone(send)

    per, steps = split(PER_SLOPE_TWO)
    a2, slope2, t2, t4 = call(
        functools.partial(slope_two_kernel, per),
        steps,
        [sides_in, blocks(hat2), gain_in, shift_in],
        [
            blocks_out(2 * WIDTH),
            blocks_out(2 * WIDTH),
            small(images, 2 * WIDTH),
            small(images, 2 * WIDTH),
        ],
        flops=rows * 2 * WIDTH * 20,
        moved=rows * 2 * WIDTH * 6,
        name="slope_two",
    )

    per, steps = split(PER_COMBINE)
    att, comb, gw, csum, hid, send = call(
        functools.partial(combine_kernel, per, n_images),
        steps,
        [
            near(got_att),
            full(zin),
            blocks(a2),
            full(full_three),
            full(fc_second),
            full(bias),
            gain_in,
            shift_in,
        ],
        [
            small(images, 2 * WIDTH),
            blocks_out(WIDTH),
            small(WIDTH, C_IN),
            small(1, WIDTH),
            small(4, images, INTER),
            payload(2, C_IN),
        ],
        [pltpu.VMEM((WIDTH, WIDTH), F32), pltpu.VMEM((8, WIDTH), F32)],
        flops=2 * rows * WIDTH * WIDTH,
        moved=rows * WIDTH * 6,
        name="combine",
    )
    got_three = everyone(send)

    per, steps = split(PER_OUTPUT)
    outputs, u3, stat3, send = call(
        functools.partial(output_kernel, per),
        steps,
        [
            sides_in,
            full(stat1),
            near(got_three),
            blocks(comb),
            blocks(x),
            blocks(cot),
            full(full_three),
            gain_in,
            shift_in,
        ],
        [blocks_out(C_IN), blocks_out(C_IN), small(8, C_IN), payload(2, C_IN)],
        [pltpu.VMEM((8, C_IN), F32), pltpu.VMEM((16, C_IN), F32)],
        flops=2 * rows * WIDTH * C_IN,
        moved=rows * C_IN * 8,
        name="output",
    )
    got_back_three = everyone(send)

    per, steps = split(PER_PROJECT)
    p, cu = call(
        project_kernel,
        steps,
        [blocks(comb), blocks(u3), full(full_three)],
        [blocks_out(WIDTH), small(WIDTH, C_IN)],
        flops=4 * rows * WIDTH * C_IN,
        moved=rows * C_IN * 4,
        name="project",
    )

    per, steps = split(PER_BACK_THREE)
    t1, t3, duz, w3_local, fc2_local, norm3, corr_weight, corr_row, send = call(
        functools.partial(back_three_kernel, per),
        steps,
        [
            full(stat3),
            near(got_back_three),
            full(hid),
            blocks(comb),
            blocks(p),
            blocks(a2),
            blocks(slope2),
            blocks(hat2),
            full(full_three),
            full(cu),
            full(gw),
            full(csum),
            full(att),
            full(fc_second),
        ],
        [
            small(images, 2 * WIDTH),
            small(images, 2 * WIDTH),
            small(images, INTER),
            small(WIDTH, C_IN),
            small(4 * INTER, 128),
            small(2, C_IN),
            ((WIDTH, WIDTH), BF16, whole((WIDTH, WIDTH))),
            small(8, WIDTH),
            payload(8, INTER),
        ],
        [pltpu.VMEM((images, 2 * WIDTH), F32)],
        flops=2 * rows * WIDTH * WIDTH,
        moved=rows * WIDTH * 16,
        name="back_three",
    )
    got_back_att = everyone(send)

    dpool, packed, fc_bias_grad, norm_att, send = call(
        functools.partial(back_att_kernel, n_images),
        1,
        [
            near(got_back_att),
            full(hid),
            full(duz),
            full(pooled),
            sides_in,
            full(fc_first),
            full(att),
            full(t1),
            full(t2),
            full(t3),
            full(t4),
            full(fc2_local),
            gain_in,
        ],
        [
            small(images, WIDTH),
            small(WIDTH + 4 * INTER, 128),
            small(1, 2 * WIDTH),
            small(2, INTER),
            payload(2, 2 * WIDTH),
        ],
        flops=10000000,
        moved=1000000,
        name="back_att",
    )
    got_back_two = everyone(send)

    shards = lax.axis_size("fsdp")
    w3_rows = WIDTH // shards
    fc_rows = packed.shape[0] // (2 * shards)
    slot = (shards, 4 * w3_rows + fc_rows, 128)
    keep, give = call(
        pack_three_kernel,
        1,
        [core_in, full(w3_local), full(packed)],
        [(slot, F32, whole(slot)), (slot, F32, whole(slot))],
        flops=1000000,
        moved=3000000,
        name="pack_three",
    )
    got_back_two, three = lax.optimization_barrier((got_back_two, keep + other_core(give)))
    three = slots(three)

    per, steps = split(PER_BACK_TWO)
    dh2, u1, norm2, send = call(
        functools.partial(back_two_kernel, per),
        steps,
        [
            sides_in,
            full(stat1),
            full(stat2),
            near(got_back_two),
            blocks(comb),
            blocks(p),
            full(corr_weight),
            full(corr_row),
            blocks(slope2),
            blocks(hat2),
            blocks(hat1),
            full(att),
            full(dpool),
            full(full_two),
            gain_in,
            shift_in,
        ],
        [
            blocks_out(2 * WIDTH),
            blocks_out(WIDTH),
            small(2, 2 * WIDTH),
            payload(2, WIDTH),
        ],
        [
            pltpu.VMEM((8, 2 * WIDTH), F32),
            pltpu.VMEM((per * (PIX + SIDE) + 2 * SIDE, 2 * WIDTH), BF16),
            pltpu.VMEM((16, WIDTH), F32),
        ],
        flops=2 * rows * 9 * HALF * 2 * WIDTH,
        moved=rows * WIDTH * 20,
        name="back_two",
    )
    send, three, dh2 = lax.optimization_barrier((send, three, dh2))
    got_back_one = everyone(send)

    per, steps = split(PER_WEIGHT_TWO)
    half = (9 * HALF, WIDTH)
    keep, give = call(
        functools.partial(weight_two_kernel, per),
        steps,
        [core_in, sides_in, blocks(hat1), blocks(dh2), gain_in, shift_in],
        [(half, F32, whole(half)), (half, F32, whole(half))],
        [
            pltpu.VMEM((per * (PIX + SIDE) + 2 * SIDE, 6 * HALF), BF16),
            pltpu.VMEM((2, WIDTH, 9 * HALF), F32),
        ],
        flops=2 * rows * 9 * HALF * 2 * WIDTH,
        moved=rows * WIDTH * 6,
        name="weight_two",
    )
    got_back_one, keep, give = lax.optimization_barrier((got_back_one, keep, give))
    three = jnp.sum(three, axis=0)
    w2_rows = 9 * HALF // shards
    w2_padded = round_up(w2_rows, 16)
    slot = (shards, w2_padded + round_up(fc_rows, 32) // 2, WIDTH)
    (parts,) = call(
        pack_two_kernel,
        1,
        [full(keep), near(other_core(give)), near(three[4 * w3_rows :])],
        [(slot, BF16, whole(slot))],
        flops=1000000,
        moved=3000000,
        name="pack_two",
    )
    got_back_one, parts = lax.optimization_barrier((got_back_one, parts))
    two = slots(parts)

    per, steps = split(PER_BACK_ONE)
    half = (C_IN, HALF)
    input_grad, keep, give, gain_grad, shift_grad = call(
        functools.partial(back_one_kernel, per),
        steps,
        [
            core_in,
            sides_in,
            full(stat1),
            full(stat3),
            near(got_back_one),
            blocks(u1),
            blocks(hat1),
            blocks(u3),
            blocks(x),
            full(full_one),
            gain_in,
            full(norm2),
            full(norm_att),
            full(norm3),
        ],
        [blocks_out(C_IN), small(*half), small(*half), small(1, n_ch), small(1, n_ch)],
        [
            pltpu.VMEM((8, WIDTH), F32),
            pltpu.VMEM((1, C_IN), F32),
            pltpu.VMEM((per * PIX, WIDTH), BF16),
            pltpu.VMEM((WIDTH, C_IN), F32),
        ],
        flops=4 * rows * WIDTH * C_IN,
        moved=rows * C_IN * 6,
        name="back_one",
    )

    one = (keep + other_core(give)).astype(BF16).reshape(shards, -1, HALF)
    one, two = lax.optimization_barrier((one, two))
    weight_one_grad = both_halves(jnp.sum(slots(one).astype(F32), axis=0))
    weight_two_grad = both_halves(jnp.sum(two[:, :w2_rows].astype(F32), axis=0))
    weight_three_grad = both_halves(
        jnp.concatenate([three[b * w3_rows : (b + 1) * w3_rows] for b in range(4)], axis=1)
    )
    fc = two[:, w2_padded:].astype(F32)
    fc = jnp.concatenate([fc[:, :, :128], fc[:, :, 128:]], axis=1)[:, :fc_rows].reshape(-1, 128)
    summed = both_halves(fc, 0)
    fc_first_grad = summed[:WIDTH]
    fc_second_grad = jnp.concatenate(
        [summed[WIDTH + b * INTER : WIDTH + (b + 1) * INTER] for b in range(4)], axis=1
    )
    return (
        outputs.reshape(inputs.shape),
        input_grad.reshape(inputs.shape),
        weight_one_grad,
        weight_two_grad,
        weight_three_grad,
        fc_first_grad,
        fc_second_grad,
        fc_bias_grad.reshape(-1),
        gain_grad.reshape(-1),
        shift_grad.reshape(-1),
    )


def solution(mesh):
    return jax.shard_map(
        body,
        mesh=mesh,
        in_specs=(
            P(("fsdp", "dp"), None, None),
            P(("fsdp", "dp")),
            P("fsdp", None),
            P("fsdp", None),
            P("fsdp", None),
            P(),
            P(),
            P(),
            P(),
            P(),
            P(("fsdp", "dp"), None, None),
        ),
        out_specs=(
            P(("fsdp", "dp"), None, None),
            P(("fsdp", "dp"), None, None),
            P("fsdp", None),
            P("fsdp", None),
            P("fsdp", None),
            P(),
            P(),
            P(),
            P(),
            P(),
        ),
        check_vma=False,
    )
```

time: 399 us -> 339 us (0.85)
  waiting for transfers between devices: 49.4 us -> 24.5 us
  Pallas kernels: 166 us -> 190 us
  local copies, waits for them, and re-layouts: 26.5 us -> 2.59 us
  blocking collectives: 67.6 us -> 51.2 us
  starting transfers between devices: 69.5 us -> 56.5 us
  other arithmetic: 14.2 us -> 9.46 us
    pallas_call x10 -> x16, Pallas kernels: 166 us -> 190 us  [call(): pl.pallas_call(kernel, grid=(grid,), in_specs=[spec for _, spec, *_ in in...]
    all_to_all x2 -> x1, blocking collectives: 32.8 us -> 13.7 us  [gather_weights(): mine = lax.all_to_all(spread_one, 'fsdp', 0, 0, tiled=True)]
    all_to_all x6 -> x4, waiting for transfers between devices: 25.4 us -> 11.5 us  [the longest x1 9.27 us: gather_weights(): mine_two = lax.all_to_all(spread_two, 'fsdp', 0, 0, tiled=True)]
    all_to_all x5, waiting for transfers between devices: 19.5 us -> 7.58 us  [everyone(): return lax.all_to_all(payload, AXES, 0, 0, tiled=True)]
    all_to_all x6 -> x4, starting transfers between devices: 33 us -> 22.4 us  [the longest x3 18.3 us: slots(): return lax.all_to_all(parts, 'fsdp', 0, 0, tiled=True)]
    reshape x7 -> x0, local copies, waits for them, and re-layouts: 8.39 us -> none  [the longest x1 3.4 us: body(): back_weight = back_weight.reshape(2, 3 * WIDTH, 3 * HALF)]
    unnamed x49 -> x15, local copies, waits for them, and re-layouts: 8.84 us -> 0.67 us
  transfers between devices with their start and end apart: 20 -> 18, of which waited for: 11 -> 8; matrix products, arithmetic and copies ran while one was open for 7% -> 3% of each run, Pallas kernels for 27% -> 30%
where the time goes in v2:
time: 339 us; the launch traced here: 335 us
  Pallas kernels  190 us (56%)
  starting transfers between devices  56.5 us (17%)
  blocking collectives  51.2 us (15%)
  waiting for transfers between devices  24.5 us (7%)
  other arithmetic  9.46 us (3%)
    pallas_call x16, Pallas kernels, call(): pl.pallas_call(kernel, grid=(grid,), in_specs=[spec for _, spec, *_ in in...  190 us
    all_to_all x3, blocking collectives, everyone(): return lax.all_to_all(payload, AXES, 0, 0, tiled=True)  37.5 us
    all_to_all x5, starting transfers between devices, everyone(): return lax.all_to_all(payload, AXES, 0, 0, tiled=True)  21.9 us
    all_to_all x3, starting transfers between devices, slots(): return lax.all_to_all(parts, 'fsdp', 0, 0, tiled=True)  18.3 us
    all_to_all x1, blocking collectives, gather_weights(): mine = lax.all_to_all(spread_one, 'fsdp', 0, 0, tiled=True)  13.7 us
    ppermute x9, starting transfers between devices, other_core(): return lax.ppermute(array, 'dp', [(0, 1), (1, 0)])  12.2 us
    all_to_all x1, waiting for transfers between devices, gather_weights(): mine_two = lax.all_to_all(spread_two, 'fsdp', 0, 0, tiled=True)  9.27 us
    all_to_all x5, waiting for transfers between devices, everyone(): return lax.all_to_all(payload, AXES, 0, 0, tiled=True)  7.58 us
  transfers between devices with their start and end apart: 18, of which 8 were waited for; matrix products, arithmetic and copies ran while one was open for 3% of the time, Pallas kernels for 30%

profile of v2, /device:TPU:9, one launch (start us, length us, event | category | flops | bytes accessed | tf_op | source)
XLA Modules:
  0.0 334.6 jit_solution(4413450843760342266)
XLA Ops:
  0.6 2.0 pack.1
  2.7 13.7 %all_to_all.65.mine_ref = bf16[16,64,128]{2,1,0:T(8,128)(2,1)S(1)} all-to-all(bf16[16,64,128]{2,1,0:T(8,128)(2,1)} %get-tuple-element.86), channel_id=1, replica_groups=mesh['fsdp'=16,'dp'=2] {'fsdp'}, dimensions={0} | all-to-all | bytes 524288 | tf_op jit(solution)/shard_map/all_to_all | solution.py:810
  16.4 3.2 collective-permute-start
  19.6 1.2 collective-permute-done.other_ref
  20.8 4.1 %all-to-all-start.2 = ((bf16[16,208,128]{2,1,0:T(8,128)(2,1)}), bf16[16,208,128]{2,1,0:T(8,128)(2,1)S(1)}, u32[]{:S(2)}, u32[]{:S(2)}) async-start(bf16[16,208,128]{2,1,0:T(8,128)(2,1)} %get-tuple-element.91), calls=%async_computation.2 | async-start | bytes 1703936 | tf_op jit(solution)/shard_map/all_to_all | solution.py:813
  24.9 0.6 copy-done
  25.5 10.6 %conv_one.1 = (f32[6144,256]{1,0:T(8,128)}, bf16[1024,256]{1,0:T(8,128)(2,1)}, f32[32,4,256]{2,1,0:T(4,128)}) custom-call(s32[1]{0:T(128)} %bitcast.core_ref, s32[24]{0:T(128)S(1)} %copy-done, bf16[6144,1024]{1,0:T(8,128)(2,1)} %bitcast.9, bf16[16,64,128]{2,1,0:T(8,128)(2,1)S(1)} %all_to_all.65.mine_ref, bf16[16,64,128]{2,1,0:T(8,128)(2,1)S(1)} %collective-permute-done.other_ref), custom_call_target="tpu_custom_call" | custom-call | flops 3221225472 | bytes 18874368 | tf_op jit(solution)/shard_map/conv_one/pallas_call | solution.py:128
  36.1 9.3 %all-to-all-done.2.mine_ref = bf16[16,208,128]{2,1,0:T(8,128)(2,1)S(1)} async-done(((bf16[16,208,128]{2,1,0:T(8,128)(2,1)}), bf16[16,208,128]{2,1,0:T(8,128)(2,1)S(1)}, u32[]{:S(2)}, u32[]{:S(2)}) %all-to-all-start.2) | async-done | bytes 852000 | tf_op jit(solution)/shard_map/all_to_all | solution.py:813
  45.4 2.1 collective-permute-start.1
  47.5 3.4 %all-to-all-start.1 = ((f32[32,4,256]{2,1,0:T(4,128)}), f32[32,4,256]{2,1,0:T(4,128)S(1)}, u32[]{:S(2)}, u32[]{:S(2)}) async-start(f32[32,4,256]{2,1,0:T(4,128)} %get-tuple-element.89), calls=%async_computation.1 | async-start | bytes 262144 | tf_op jit(solution)/shard_map/all_to_all | solution.py:779
  50.9 0.6 reshape.61.gain_ref
  51.5 0.6 reshape.62.shift_ref
  52.1 1.5 unpack.1
  53.6 3.4 %all-to-all-done.1.got_ref = f32[32,4,256]{2,1,0:T(4,128)S(1)} async-done(((f32[32,4,256]{2,1,0:T(4,128)}), f32[32,4,256]{2,1,0:T(4,128)S(1)}, u32[]{:S(2)}, u32[]{:S(2)}) %all-to-all-start.1) | async-done | bytes 131104 | tf_op jit(solution)/shard_map/all_to_all | solution.py:779
  57.0 16.5 %conv_two.1 = (bf16[6144,256]{1,0:T(8,128)(2,1)}, f32[6144,512]{1,0:T(8,128)}, f32[8,256]{1,0:T(8,128)}, f32[32,2,512]{2,1,0:T(2,128)}) custom-call(s32[24]{0:T(128)S(1)} %copy-done.1, f32[32,4,256]{2,1,0:T(4,128)S(1)} %all-to-all-done.1.got_ref, f32[6144,256]{1,0:T(8,128)} %get-tuple-element.90.h_ref, bf16[1152,512]{1,0:T(8,128)(2,1)} %get-tuple-element.93.w_ref, ...), custom_call_target="tpu_custom_call" | custom-call | flops 7247757312 | bytes 22020096 | tf_op jit(solution)/shard_map/conv_two/pallas_call | solution.py:128
  73.5 10.8 %all_to_all.66.got_ref = f32[32,2,512]{2,1,0:T(2,128)S(1)} all-to-all(f32[32,2,512]{2,1,0:T(2,128)} %get-tuple-element.95), channel_id=1, replica_groups=mesh['fsdp'=16,'dp'=2] {'fsdp','dp'}, dimensions={0} | all-to-all | bytes 262144 | tf_op jit(solution)/shard_map/all_to_all | solution.py:779
  84.3 11.2 %act_two.1 = (bf16[6144,512]{1,0:T(8,128)(2,1)}, f32[24,256]{1,0:T(8,128)}, f32[24,128]{1,0:T(8,128)}, f32[8,512]{1,0:T(8,128)}, f32[32,2,128]{2,1,0:T(2,128)}) custom-call(s32[24]{0:T(128)S(1)} %copy-done.1, f32[8,256]{1,0:T(8,128)} %get-tuple-element.94.one_ref, f32[32,2,512]{2,1,0:T(2,128)S(1)} %all_to_all.66.got_ref, ...), custom_call_target="tpu_custom_call" | custom-call | flops 62914560 | bytes 31457280 | tf_op jit(solution)/shard_map/act_two/pallas_call | solution.py:128
  95.5 4.6 %all-to-all-start.4 = ((f32[32,2,128]{2,1,0:T(2,128)}), f32[32,2,128]{2,1,0:T(2,128)S(1)}, u32[]{:S(2)}, u32[]{:S(2)}) async-start(f32[32,2,128]{2,1,0:T(2,128)} %get-tuple-element.97), calls=%async_computation.4 | async-start | bytes 65536 | tf_op jit(solution)/shard_map/all_to_all | solution.py:779
  100.1 12.9 %slope_two.1 = (bf16[6144,512]{1,0:T(8,128)(2,1)}, bf16[6144,512]{1,0:T(8,128)(2,1)}, f32[24,512]{1,0:T(8,128)}, f32[24,512]{1,0:T(8,128)}) custom-call(s32[24]{0:T(128)S(1)} %copy-done.1, bf16[6144,512]{1,0:T(8,128)(2,1)} %get-tuple-element.99.hat_ref.hat2_ref, f32[1,1920]{1,0:T(1,128)} %reshape.61.gain_ref, f32[1,1920]{1,0:T(1,128)} %reshape.62.shift_ref), custom_call_target="tpu_custom_call" | custom-call | flops 62914560 | bytes 18874368 | tf_op jit(solution)/shard_map/slope_two/pallas_call | solution.py:128
  113.0 0.0 all-to-all-done.4.got_ref
  113.0 9.7 %combine.1 = (f32[24,512]{1,0:T(8,128)}, bf16[6144,256]{1,0:T(8,128)(2,1)}, f32[256,1024]{1,0:T(8,128)}, f32[1,256]{1,0:T(1,128)}, f32[4,24,128]{2,1,0:T(8,128)}, /*index=5*/f32[32,2,1024]{2,1,0:T(2,128)}) custom-call(f32[32,2,128]{2,1,0:T(2,128)S(1)} %all-to-all-done.4.got_ref, f32[24,128]{1,0:T(8,128)} %get-tuple-element.98.zin_ref, ...), custom_call_target="tpu_custom_call" | custom-call | flops 805306368 | bytes 9437184 | tf_op jit(solution)/shard_map/combine/pallas_call | solution.py:128
  122.7 14.6 %all_to_all.67.got_ref = f32[32,2,1024]{2,1,0:T(2,128)S(1)} all-to-all(f32[32,2,1024]{2,1,0:T(2,128)} %get-tuple-element.102), channel_id=1, replica_groups=mesh['fsdp'=16,'dp'=2] {'fsdp','dp'}, dimensions={0} | all-to-all | bytes 524288 | tf_op jit(solution)/shard_map/all_to_all | solution.py:779
  137.3 27.7 %output.1 = (bf16[6144,1024]{1,0:T(8,128)(2,1)}, bf16[6144,1024]{1,0:T(8,128)(2,1)}, f32[8,1024]{1,0:T(8,128)}, f32[32,2,1024]{2,1,0:T(2,128)}) custom-call(s32[24]{0:T(128)S(1)} %copy-done.1, f32[8,256]{1,0:T(8,128)} %get-tuple-element.94.one_ref, f32[32,2,1024]{2,1,0:T(2,128)S(1)} %all_to_all.67.got_ref, bf16[6144,256]{1,0:T(8,128)(2,1)} %get-tuple-element.103.comb_ref, ...), custom_call_target="tpu_custom_call" | custom-call | flops 3221225472 | bytes 50331648 | tf_op jit(solution)/shard_map/output/pallas_call | solution.py:128
  165.0 4.4 %all-to-all-start.6 = ((f32[32,2,1024]{2,1,0:T(2,128)}), f32[32,2,1024]{2,1,0:T(2,128)S(1)}, u32[]{:S(2)}, u32[]{:S(2)}) async-start(f32[32,2,1024]{2,1,0:T(2,128)} %get-tuple-element.107), calls=%async_computation.6 | async-start | bytes 524288 | tf_op jit(solution)/shard_map/all_to_all | solution.py:779
  169.5 12.4 %project.1 = (bf16[6144,256]{1,0:T(8,128)(2,1)}, f32[256,1024]{1,0:T(8,128)}) custom-call(bf16[6144,256]{1,0:T(8,128)(2,1)} %get-tuple-element.103.comb_ref, bf16[6144,1024]{1,0:T(8,128)(2,1)} %get-tuple-element.109.u3_ref, bf16[256,1024]{1,0:T(8,128)(2,1)} %get-tuple-element.101.w3_ref), custom_call_target="tpu_custom_call" | custom-call | flops 6442450944 | bytes 25165824 | tf_op jit(solution)/shard_map/project/pallas_call | solution.py:128
  181.9 16.2 %back_three.1 = (f32[24,512]{1,0:T(8,128)}, f32[24,512]{1,0:T(8,128)}, f32[24,128]{1,0:T(8,128)}, f32[256,1024]{1,0:T(8,128)}, f32[512,128]{1,0:T(8,128)}, /*ind...) custom-call(f32[8,1024]{1,0:T(8,128)} %get-tuple-element.105.three_ref, ...), custom_call_target="tpu_custom_call" | custom-call | flops 805306368 | bytes 25165824 | tf_op jit(solution)/shard_map/back_three/pallas_call | solution.py:128
  198.0 12.1 %all_to_all.68.got_ref = f32[32,8,128]{2,1,0:T(8,128)S(1)} all-to-all(f32[32,8,128]{2,1,0:T(8,128)} %get-tuple-element.116), channel_id=1, replica_groups=mesh['fsdp'=16,'dp'=2] {'fsdp','dp'}, dimensions={0} | all-to-all | bytes 262144 | tf_op jit(solution)/shard_map/all_to_all | solution.py:779
  210.1 2.3 back_att.1
  212.4 2.5 pack_three.1
  214.9 1.3 collective-permute-start.2
  216.2 3.5 %all-to-all-start.8 = ((f32[32,2,512]{2,1,0:T(2,128)}), f32[32,2,512]{2,1,0:T(2,128)S(1)}, u32[]{:S(2)}, u32[]{:S(2)}) async-start(f32[32,2,512]{2,1,0:T(2,128)} %get-tuple-element.124), calls=%async_computation.8 | async-start | bytes 262144 | tf_op jit(solution)/shard_map/all_to_all | solution.py:779
  219.7 2.1 add.6
  221.7 4.2 %all-to-all-done.8.got_ref = f32[32,2,512]{2,1,0:T(2,128)S(1)} async-done(((f32[32,2,512]{2,1,0:T(2,128)}), f32[32,2,512]{2,1,0:T(2,128)S(1)}, u32[]{:S(2)}, u32[]{:S(2)}) %all-to-all-start.8) | async-done | bytes 131104 | tf_op jit(solution)/shard_map/all_to_all | solution.py:779
  225.9 5.5 %all-to-all-start.9 = ((f32[16,88,128]{2,1,0:T(8,128)}), f32[16,88,128]{2,1,0:T(8,128)S(1)}, u32[]{:S(2)}, u32[]{:S(2)}) async-start(f32[16,88,128]{2,1,0:T(8,128)} %add.6), calls=%async_computation.9 | async-start | bytes 1441792 | tf_op jit(solution)/shard_map/all_to_all | solution.py:834
  231.4 22.9 %back_two.1 = (bf16[6144,512]{1,0:T(8,128)(2,1)}, bf16[6144,256]{1,0:T(8,128)(2,1)}, f32[2,512]{1,0:T(2,128)}, f32[32,2,256]{2,1,0:T(2,128)}) custom-call(s32[24]{0:T(128)S(1)} %copy-done.1, f32[8,256]{1,0:T(8,128)} %get-tuple-element.94.one_ref, f32[8,512]{1,0:T(8,128)} %get-tuple-element.106.two_ref, f32[32,2,512]{2,1,0:T(2,128)S(1)} %all-to-all-done.8.got_ref, ...), custom_call_target="tpu_custom_call" | custom-call | flops 7247757312 | bytes 31457280 | tf_op jit(solution)/shard_map/back_two/pallas_call | solution.py:128
  254.4 0.0 all-to-all-done.9
  254.4 6.0 %all-to-all-start.10 = ((f32[32,2,256]{2,1,0:T(2,128)}), f32[32,2,256]{2,1,0:T(2,128)S(1)}, u32[]{:S(2)}, u32[]{:S(2)}) async-start(f32[32,2,256]{2,1,0:T(2,128)} %get-tuple-element.137), calls=%async_computation.10 | async-start | bytes 131072 | tf_op jit(solution)/shard_map/all_to_all | solution.py:779
  260.4 16.4 %weight_two.1 = (f32[1152,256]{1,0:T(8,128)}, f32[1152,256]{1,0:T(8,128)}) custom-call(s32[1]{0:T(128)} %bitcast.core_ref, s32[24]{0:T(128)S(1)} %copy-done.1, bf16[6144,256]{1,0:T(8,128)(2,1)} %get-tuple-element.132.hat1_ref.hat_ref, bf16[6144,512]{1,0:T(8,128)(2,1)} %get-tuple-element.138.dh2_ref, f32[1,1920]{1,0:T(1,128)} %reshape.61.gain_ref, ...), custom_call_target="tpu_custom_call" | custom-call | flops 7247757312 | bytes 9437184 | tf_op jit(solution)/shard_map/weight_two/pallas_call | solution.py:128
  277.0 0.4 collective-permute-start.3
  277.4 0.2 collective-permute-start.7
  277.6 2.3 collective-permute-done.7
  279.9 0.1 collective-permute-done.3.other_ref
  280.1 2.3 pack_two.1
  282.4 6.5 %all-to-all-start.11 = ((bf16[16,96,256]{2,1,0:T(8,128)(2,1)}), bf16[16,96,256]{2,1,0:T(8,128)(2,1)S(1)}, u32[]{:S(2)}, u32[]{:S(2)}) async-start(bf16[16,96,256]{2,1,0:T(8,128)(2,1)} %pack_two.1), calls=%async_computation.11 | async-start | bytes 1572864 | tf_op jit(solution)/shard_map/all_to_all | solution.py:834
  288.8 22.4 %back_one.1 = (bf16[6144,1024]{1,0:T(8,128)(2,1)}, f32[1024,128]{1,0:T(8,128)}, f32[1024,128]{1,0:T(8,128)}, f32[1,1920]{1,0:T(1,128)}, f32[1,1920]{1,0:T(1,128)}) custom-call(s32[1]{0:T(128)} %bitcast.core_ref, s32[24]{0:T(128)S(1)} %copy-done.1, f32[8,256]{1,0:T(8,128)} %get-tuple-element.94.one_ref, f32[8,1024]{1,0:T(8,128)} %get-tuple-element.105.three_ref, ...), custom_call_target="tpu_custom_call" | custom-call | flops 6442450944 | bytes 37748736 | tf_op jit(solution)/shard_map/back_one/pallas_call | solution.py:128
  311.2 1.0 collective-permute-start.4
  312.2 1.7 collective-permute-done.4
  313.9 1.8 add_convert_fusion
  315.8 0.0 all-to-all-done.11
  315.8 0.1 convert_reduce_fusion
  315.9 6.3 %all-to-all-start.12 = ((bf16[16,64,128]{2,1,0:T(8,128)(2,1)}), bf16[16,64,128]{2,1,0:T(8,128)(2,1)S(1)}, u32[]{:S(2)}, u32[]{:S(2)}) async-start(bf16[16,64,128]{2,1,0:T(8,128)(2,1)} %bitcast.6), calls=%async_computation.12 | async-start | bytes 524288 | tf_op jit(solution)/shard_map/all_to_all | solution.py:834
  322.2 0.9 collective-permute-start.6
  323.2 0.1 collective-permute-start.8
  323.3 0.6 broadcast_select_fusion
  323.9 1.3 reduce
  325.2 1.3 reduce.1
  326.6 0.7 maximum_select_fusion.1
  327.2 0.0 collective-permute-done.8
  327.3 2.2 all-to-all-done.12
  329.6 3.0 collective-permute-start.5
  332.6 0.7 pad_maximum_fusion
  333.3 0.7 slice.67
  334.0 0.0 collective-permute-done.5
  334.0 0.6 maximum_select_fusion.2
  (31 shorter events, 0.3 us)
Async XLA Ops:
  16.4 4.4 %collective-permute-start = (bf16[16,64,128]{2,1,0:T(8,128)(2,1)S(1)}, bf16[16,64,128]{2,1,0:T(8,128)(2,1)S(1)}, u32[]{:S(2)}, u32[]{:S(2)}) collective-permute-start(bf16[16,64,128]{2,1,0:T(8,128)(2,1)S(1)} %all_to_all.65.mine_ref), channel_id=1, source_target_pairs={{0,1},{1,0},{2,3},{3,2},{4,5},{5,4},{6,7},{7,6},{8,9},{9,8},{10,11... | collective-permute-start | bytes 786440 | tf_op jit(solution)/shard_map/ppermute | solution.py:783
  20.8 24.6 %all-to-all-start.2 = ((bf16[16,208,128]{2,1,0:T(8,128)(2,1)}), bf16[16,208,128]{2,1,0:T(8,128)(2,1)S(1)}, u32[]{:S(2)}, u32[]{:S(2)}) async-start(bf16[16,208,128]{2,1,0:T(8,128)(2,1)} %get-tuple-element.91), calls=%async_computation.2 | async-start | bytes 1703936 | tf_op jit(solution)/shard_map/all_to_all | solution.py:813
  24.9 0.7 copy-start
  25.5 25.3 %copy-start.2 = (f32[1920]{0:T(1024)S(1)}, f32[1920]{0:T(1024)}, u32[]{:S(2)}) copy-start(f32[1920]{0:T(1024)} %param.19) | copy-start | bytes 23044
  25.5 26.0 %copy-start.3 = (f32[1920]{0:T(1024)S(1)}, f32[1920]{0:T(1024)}, u32[]{:S(2)}) copy-start(f32[1920]{0:T(1024)} %param.20) | copy-start | bytes 23044
  25.5 31.5 %copy-start.1 = (s32[24]{0:T(128)S(1)}, s32[24]{0:T(128)}, u32[]{:S(2)}) copy-start(s32[24]{0:T(128)} %sides_ref.17) | copy-start | bytes 292
  45.4 6.7 %collective-permute-start.1 = (bf16[16,208,128]{2,1,0:T(8,128)(2,1)S(1)}, bf16[16,208,128]{2,1,0:T(8,128)(2,1)S(1)}, u32[]{:S(2)}, u32[]{:S(2)}) collective-permute-start(bf16[16,208,128]{2,1,0:T(8,128)(2,1)S(1)} %all-to-all-done.2.mine_ref), channel_id=1, source_target_pairs={{0,1},{1,0},{2,3},{3,2},{4,5},{5,4},{6,7},{7,6},{8,9},{9,8},{10,11... | collective-permute-start | bytes 2555912 | tf_op jit(solution)/shard_map/ppermute | solution.py:783
  47.5 9.5 %all-to-all-start.1 = ((f32[32,4,256]{2,1,0:T(4,128)}), f32[32,4,256]{2,1,0:T(4,128)S(1)}, u32[]{:S(2)}, u32[]{:S(2)}) async-start(f32[32,4,256]{2,1,0:T(4,128)} %get-tuple-element.89), calls=%async_computation.1 | async-start | bytes 262144 | tf_op jit(solution)/shard_map/all_to_all | solution.py:779
  95.5 17.5 %all-to-all-start.4 = ((f32[32,2,128]{2,1,0:T(2,128)}), f32[32,2,128]{2,1,0:T(2,128)S(1)}, u32[]{:S(2)}, u32[]{:S(2)}) async-start(f32[32,2,128]{2,1,0:T(2,128)} %get-tuple-element.97), calls=%async_computation.4 | async-start | bytes 65536 | tf_op jit(solution)/shard_map/all_to_all | solution.py:779
  165.0 16.9 %all-to-all-start.6 = ((f32[32,2,1024]{2,1,0:T(2,128)}), f32[32,2,1024]{2,1,0:T(2,128)S(1)}, u32[]{:S(2)}, u32[]{:S(2)}) async-start(f32[32,2,1024]{2,1,0:T(2,128)} %get-tuple-element.107), calls=%async_computation.6 | async-start | bytes 524288 | tf_op jit(solution)/shard_map/all_to_all | solution.py:779
  214.9 4.8 %collective-permute-start.2 = (f32[16,88,128]{2,1,0:T(8,128)}, f32[16,88,128]{2,1,0:T(8,128)S(1)}, u32[]{:S(2)}, u32[]{:S(2)}) collective-permute-start(f32[16,88,128]{2,1,0:T(8,128)} %get-tuple-element.128), channel_id=1, source_target_pairs={{0,1},{1,0},{2,3},{3,2},{4,5},{5,4},{6,7},{7,6},{8,9},{9,8},{10,11... | collective-permute-start | bytes 2162696 | tf_op jit(solution)/shard_map/ppermute | solution.py:783
  216.2 9.7 %all-to-all-start.8 = ((f32[32,2,512]{2,1,0:T(2,128)}), f32[32,2,512]{2,1,0:T(2,128)S(1)}, u32[]{:S(2)}, u32[]{:S(2)}) async-start(f32[32,2,512]{2,1,0:T(2,128)} %get-tuple-element.124), calls=%async_computation.8 | async-start | bytes 262144 | tf_op jit(solution)/shard_map/all_to_all | solution.py:779
  225.9 28.5 %all-to-all-start.9 = ((f32[16,88,128]{2,1,0:T(8,128)}), f32[16,88,128]{2,1,0:T(8,128)S(1)}, u32[]{:S(2)}, u32[]{:S(2)}) async-start(f32[16,88,128]{2,1,0:T(8,128)} %add.6), calls=%async_computation.9 | async-start | bytes 1441792 | tf_op jit(solution)/shard_map/all_to_all | solution.py:834
  254.4 22.5 %all-to-all-start.10 = ((f32[32,2,256]{2,1,0:T(2,128)}), f32[32,2,256]{2,1,0:T(2,128)S(1)}, u32[]{:S(2)}, u32[]{:S(2)}) async-start(f32[32,2,256]{2,1,0:T(2,128)} %get-tuple-element.137), calls=%async_computation.10 | async-start | bytes 131072 | tf_op jit(solution)/shard_map/all_to_all | solution.py:779
  277.0 3.1 collective-permute-start.3
  277.4 2.5 collective-permute-start.7
  282.4 33.4 %all-to-all-start.11 = ((bf16[16,96,256]{2,1,0:T(8,128)(2,1)}), bf16[16,96,256]{2,1,0:T(8,128)(2,1)S(1)}, u32[]{:S(2)}, u32[]{:S(2)}) async-start(bf16[16,96,256]{2,1,0:T(8,128)(2,1)} %pack_two.1), calls=%async_computation.11 | async-start | bytes 1572864 | tf_op jit(solution)/shard_map/all_to_all | solution.py:834
  311.2 2.7 collective-permute-start.4
  315.9 13.7 %all-to-all-start.12 = ((bf16[16,64,128]{2,1,0:T(8,128)(2,1)}), bf16[16,64,128]{2,1,0:T(8,128)(2,1)S(1)}, u32[]{:S(2)}, u32[]{:S(2)}) async-start(bf16[16,64,128]{2,1,0:T(8,128)(2,1)} %bitcast.6), calls=%async_computation.12 | async-start | bytes 524288 | tf_op jit(solution)/shard_map/all_to_all | solution.py:834
  322.2 4.3 %collective-permute-start.6 = (f32[72,256]{1,0:T(8,128)S(1)}, f32[72,256]{1,0:T(8,128)S(1)}, u32[]{:S(2)}, u32[]{:S(2)}) collective-permute-start(f32[72,256]{1,0:T(8,128)S(1)} %convert_reduce_fusion), channel_id=1, source_target_pairs={{0,1},{1,0},{2,3},{3,2},{4,5},{5,4},{6,7},{7,6},{8,9},{9,8},{10,11... | collective-permute-start | bytes 221192 | tf_op jit(solution)/shard_map/ppermute | solution.py:783
  323.2 4.0 %collective-permute-start.8 = (f32[384,128]{1,0:T(8,128)S(1)}, f32[384,128]{1,0:T(8,128)S(1)}, u32[]{:S(2)}, u32[]{:S(2)}) collective-permute-start(f32[384,128]{1,0:T(8,128)S(1)} %bitcast.13), channel_id=1, source_target_pairs={{0,1},{1,0},{2,3},{3,2},{4,5},{5,4},{6,7},{7,6},{8,9},{9,8},{10,11... | collective-permute-start | bytes 589832 | tf_op jit(solution)/shard_map/ppermute | solution.py:783
  329.6 4.4 %collective-permute-start.5 = (f32[64,128]{1,0:T(8,128)S(1)}, f32[64,128]{1,0:T(8,128)S(1)}, u32[]{:S(2)}, u32[]{:S(2)}) collective-permute-start(f32[64,128]{1,0:T(8,128)S(1)} %convert_reduce_fusion.1), channel_id=1, source_target_pairs={{0,1},{1,0},{2,3},{3,2},{4,5},{5,4},{6,7},{7,6},{8,9},{9,8},{10,11... | collective-permute-start | bytes 98312 | tf_op jit(solution)/shard_map/ppermute | solution.py:783

commit v3 on v2

--- a/solution.py
+++ b/solution.py
@@ -20,16 +20,17 @@
 BF16 = jnp.bfloat16
 MIB = 1024 * 1024
 
+AHEAD = 4
 PER_CONV_ONE = 4
-PER_CONV_TWO = 4
+PER_CONV_TWO = 3
 PER_ACT_TWO = 4
-PER_SLOPE_TWO = 4
-PER_COMBINE = 4
+PER_SLOPE_TWO = 3
+PER_COMBINE = 6
 PER_OUTPUT = 2
 PER_PROJECT = 4
 PER_BACK_THREE = 4
-PER_BACK_TWO = 4
-PER_WEIGHT_TWO = 2
+PER_BACK_TWO = 2
+PER_WEIGHT_TWO = 4
 PER_BACK_ONE = 2
 
 
@@ -110,31 +111,153 @@
     return pl.BlockSpec(shape, lambda *_: zeros)
 
 
-def rows_of(n_rows, width):
-    return pl.BlockSpec((n_rows, width), lambda i: (i, 0))
-
-
 SMEM_SPEC = pl.BlockSpec(memory_space=pltpu.SMEM)
 
 
-def call(kernel, grid, ins, outs, scratch=(), vmem=32, flops=0, moved=0, name=None):
+def call(kernel, grid, ins, outs, scratch=(), vmem=56, flops=0, moved=0, name=None):
     arrays = [
         array
         if spec is SMEM_SPEC or near
         else pltpu.with_memory_space_constraint(array, pltpu.HBM)
         for array, spec, *near in ins
     ]
-    shapes = [pltpu.HBM(shape, dtype) for shape, dtype, _ in outs]
+    shapes = [
+        jax.ShapeDtypeStruct(shape, dtype) if near else pltpu.HBM(shape, dtype)
+        for shape, dtype, _, *near in outs
+    ]
     return pl.pallas_call(
         kernel,
         grid=(grid,),
         in_specs=[spec for _, spec, *_ in ins],
-        out_specs=[spec for _, _, spec in outs],
+        out_specs=[spec for _, _, spec, *_ in outs],
         out_shape=shapes,
         scratch_shapes=list(scratch),
         compiler_params=pltpu.CompilerParams(
             dimension_semantics=("arbitrary",), vmem_limit_bytes=vmem * MIB
         ),
+        cost_estimate=pl.CostEstimate(flops=flops, bytes_accessed=moved, transcendentals=0),
+        name=name,
+    )(*arrays)
+
+
+class Stream:
+    def __init__(self, over=None):
+        self.over = over
+
+
+BEGIN, END = "begin", "end"
+
+
+def stream_call(kernel, per, steps, ins, outs, scratch=(), vmem=56, flops=0, moved=0, name=None):
+    block = per * PIX
+    in_specs, out_specs, arrays, shapes, rooms = [], [], [], [], []
+    in_streams, out_streams, room_of = [], [], {}
+    for at, (array, spec, *near) in enumerate(ins):
+        if isinstance(spec, Stream):
+            in_streams.append(at)
+            room_of[at] = len(rooms)
+            rooms.append(pltpu.VMEM(array.shape, array.dtype))
+            spec = pl.BlockSpec(memory_space=pltpu.HBM)
+        elif near:
+            arrays.append(array)
+            in_specs.append(spec)
+            continue
+        in_specs.append(spec)
+        arrays.append(
+            array if spec is SMEM_SPEC else pltpu.with_memory_space_constraint(array, pltpu.HBM)
+        )
+    for at, (shape, dtype, spec, *near) in enumerate(outs):
+        shapes.append(jax.ShapeDtypeStruct(shape, dtype) if near else pltpu.HBM(shape, dtype))
+        if isinstance(spec, Stream):
+            out_streams.append(at)
+            if spec.over is None:
+                room_of[len(ins) + at] = len(rooms)
+                rooms.append(pltpu.VMEM(shape, dtype))
+            else:
+                room_of[len(ins) + at] = room_of[spec.over]
+            spec = pl.BlockSpec(memory_space=pltpu.HBM)
+        out_specs.append(spec)
+    n_in, n_out, n_rooms = len(ins), len(outs), len(rooms)
+
+    def whole_kernel(*refs):
+        in_refs, out_refs = refs[:n_in], refs[n_in : n_in + n_out]
+        room_refs = refs[n_in + n_out : n_in + n_out + n_rooms]
+        own_refs = refs[n_in + n_out + n_rooms : -2]
+        in_sems, out_sems = refs[-2:]
+
+        def rows(step):
+            return pl.ds(pl.multiple_of(step * block, block), block)
+
+        def copies_in(step):
+            return [
+                pltpu.make_async_copy(
+                    in_refs[at].at[rows(step)],
+                    room_refs[room_of[at]].at[rows(step)],
+                    in_sems.at[k, step],
+                )
+                for k, at in enumerate(in_streams)
+            ]
+
+        def copies_out(step):
+            return [
+                pltpu.make_async_copy(
+                    room_refs[room_of[n_in + at]].at[rows(step)],
+                    out_refs[at].at[rows(step)],
+                    out_sems.at[k, step],
+                )
+                for k, at in enumerate(out_streams)
+            ]
+
+        def views(step):
+            both = []
+            for at, ref in enumerate(in_refs + out_refs):
+                if at in room_of:
+                    ref = room_refs[room_of[at]].at[rows(step)]
+                both.append(ref)
+            return both + list(own_refs)
+
+        ahead = min(AHEAD, steps)
+        for step in range(ahead):
+            for copy in copies_in(step):
+                copy.start()
+        kernel(BEGIN, *views(0))
+
+        def one(step, carry):
+            for copy in copies_in(step):
+                copy.wait()
+
+            @pl.when(step + ahead < steps)
+            def _():
+                for copy in copies_in(step + ahead):
+                    copy.start()
+
+            kernel(step, *views(step))
+            for copy in copies_out(step):
+                copy.start()
+            return carry
+
+        lax.fori_loop(0, steps, one, 0)
+        kernel(END, *views(0))
+
+        def last(step, carry):
+            for copy in copies_out(step):
+                copy.wait()
+            return carry
+
+        lax.fori_loop(0, steps, last, 0)
+
+    return pl.pallas_call(
+        whole_kernel,
+        in_specs=in_specs,
+        out_specs=out_specs,
+        out_shape=shapes,
+        scratch_shapes=rooms
+        + list(scratch)
+        + [
+            pltpu.SemaphoreType.DMA((max(len(in_streams), 1), steps)),
+            pltpu.SemaphoreType.DMA((max(len(out_streams), 1), steps)),
+        ],
+        compiler_params=pltpu.CompilerParams(vmem_limit_bytes=vmem * MIB),
         cost_estimate=pl.CostEstimate(flops=flops, bytes_accessed=moved, transcendentals=0),
         name=name,
     )(*arrays)
@@ -187,13 +310,10 @@
 
 
 def conv_one_kernel(
-    per, core_ref, sides_ref, x_ref, mine_ref, other_ref, h_ref, w_out_ref, send_ref,
+    step, per, core_ref, sides_ref, x_ref, mine_ref, other_ref, h_ref, w_out_ref, send_ref,
     acc_ref, count_ref,
 ):
-    step = pl.program_id(0)
-
-    @pl.when(step == 0)
-    def _():
+    if step is BEGIN:
         acc_ref[...] = jnp.zeros_like(acc_ref)
         count_ref[0] = 0.0
 
@@ -203,6 +323,15 @@
 
         for core in range(2):
             pl.when(core_ref[0] == core)(functools.partial(put, core))
+        return
+
+    if step is END:
+        count = jnp.full((1, WIDTH), count_ref[0], F32)
+        send_rows(
+            send_ref,
+            [row_sum(acc_ref[0:8]), row_sum(acc_ref[8:16]), count, jnp.zeros((1, WIDTH), F32)],
+        )
+        return
 
     h = dot_f(x_ref[...], w_out_ref[...])
     h_ref[...] = h
@@ -215,14 +344,6 @@
         acc_ref[8:16] += fold(kept * one)
         count_ref[0] += (side * side).astype(F32)
 
-    @pl.when(step == pl.num_programs(0) - 1)
-    def _():
-        count = jnp.full((1, WIDTH), count_ref[0], F32)
-        send_rows(
-            send_ref,
-            [row_sum(acc_ref[0:8]), row_sum(acc_ref[8:16]), count, jnp.zeros((1, WIDTH), F32)],
-        )
-
 
 def edge_masks(width):
     column = lax.broadcasted_iota(jnp.int32, (PIX, 128), 0) & 15
@@ -242,13 +363,10 @@
 
 
 def conv_two_kernel(
-    per, sides_ref, got_ref, h_ref, w_ref, gain_ref, shift_ref, hat_ref, h2_ref, vec_ref, send_ref,
+    step, per, sides_ref, got_ref, h_ref, w_ref, gain_ref, shift_ref, hat_ref, h2_ref, vec_ref, send_ref,
     taps_ref, acc_ref,
 ):
-    step = pl.program_id(0)
-
-    @pl.when(step == 0)
-    def _():
+    if step is BEGIN:
         sums = total(got_ref)
         mean, inv = norm_terms(sums, sums[2:3])
         vec_ref[0:1] = mean
@@ -256,6 +374,11 @@
         vec_ref[2:3] = sums[2:3]
         acc_ref[...] = jnp.zeros_like(acc_ref)
         taps_ref[...] = jnp.zeros_like(taps_ref)
+        return
+
+    if step is END:
+        send_rows(send_ref, [row_sum(acc_ref[0:8]), row_sum(acc_ref[8:16])])
+        return
 
     gain = gain_ref[:, :WIDTH] * 0.5
     shift = shift_ref[:, :WIDTH] * 0.5
@@ -284,23 +407,23 @@
             acc_ref[0:8, cols] += fold(kept)
             acc_ref[8:16, cols] += fold(kept * h2)
 
-    @pl.when(step == pl.num_programs(0) - 1)
-    def _():
-        send_rows(send_ref, [row_sum(acc_ref[0:8]), row_sum(acc_ref[8:16])])
-
 
 def act_two_kernel(
-    per, sides_ref, one_ref, got_ref, h2_ref, gain_ref, shift_ref, fc_ref,
+    step, per, sides_ref, one_ref, got_ref, h2_ref, gain_ref, shift_ref, fc_ref,
     hat_ref, pooled_ref, zin_ref, vec_ref, send_ref,
 ):
-    step = pl.program_id(0)
-
-    @pl.when(step == 0)
-    def _():
+    if step is BEGIN:
         sums = total(got_ref)
         mean, inv = norm_terms(sums, jnp.concatenate([one_ref[2:3]] * 2, axis=1))
         vec_ref[0:1] = mean
         vec_ref[1:2] = inv
+        return
+
+    if step is END:
+        z = high_f(pooled_ref[...], fc_ref[...])
+        zin_ref[...] = z
+        send_rows(send_ref, [row_sum(z), row_sum(z * z)])
+        return
 
     gain = gain_ref[:, WIDTH : 3 * WIDTH] * 0.5
     shift = shift_ref[:, WIDTH : 3 * WIDTH] * 0.5
@@ -317,17 +440,16 @@
         pixels = (side * side).astype(F32)
         pooled_ref[image] = (sums[:, :WIDTH] + sums[:, WIDTH:]) / pixels
 
-    @pl.when(step == pl.num_programs(0) - 1)
-    def _():
-        z = high_f(pooled_ref[...], fc_ref[...])
-        zin_ref[...] = z
-        send_rows(send_ref, [row_sum(z), row_sum(z * z)])
-
 
 def slope_two_kernel(
-    per, sides_ref, hat_ref, gain_ref, shift_ref, a2_ref, slope_ref, t2_ref, t4_ref
+    step, per, sides_ref, hat_ref, gain_ref, shift_ref, a2_ref, slope_ref, t2_ref, t4_ref
 ):
-    step = pl.program_id(0)
+    if step is BEGIN:
+        return
+
+    if step is END:
+        return
+
     gain = gain_ref[:, WIDTH : 3 * WIDTH] * 0.5
     shift = shift_ref[:, WIDTH : 3 * WIDTH] * 0.5
     for j in range(per):
@@ -356,13 +478,10 @@
 
 
 def combine_kernel(
-    per, n_images, got_ref, zin_ref, a2_ref, w3_ref, fc_ref, bias_ref, gain_ref, shift_ref,
+    step, per, n_images, got_ref, zin_ref, a2_ref, w3_ref, fc_ref, bias_ref, gain_ref, shift_ref,
     att_ref, comb_ref, gw_ref, csum_ref, hid_ref, send_ref, gram_ref, acc_ref,
 ):
-    step = pl.program_id(0)
-
-    @pl.when(step == 0)
-    def _():
+    if step is BEGIN:
         zhat, inv, hidden, slope = hidden_terms(
             zin_ref[...], total(got_ref), n_images, gain_ref, shift_ref
         )
@@ -379,6 +498,16 @@
         att_ref[:, WIDTH:] = right / both
         gram_ref[...] = jnp.zeros_like(gram_ref)
         acc_ref[...] = jnp.zeros_like(acc_ref)
+        return
+
+    if step is END:
+        w3 = w3_ref[...].astype(F32)
+        csum = row_sum(acc_ref[...])
+        csum_ref[...] = csum
+        gw = high_f(gram_ref[...], w3)
+        gw_ref[...] = gw
+        send_rows(send_ref, [high_f(csum, w3), row_sum(w3 * gw)])
+        return
 
     for j in range(per):
         rows = pl.ds(j * PIX, PIX)
@@ -390,24 +519,12 @@
     comb = comb_ref[...]
     gram_ref[...] += dot_rows(comb, comb)
 
-    @pl.when(step == pl.num_programs(0) - 1)
-    def _():
-        w3 = w3_ref[...].astype(F32)
-        csum = row_sum(acc_ref[...])
-        csum_ref[...] = csum
-        gw = high_f(gram_ref[...], w3)
-        gw_ref[...] = gw
-        send_rows(send_ref, [high_f(csum, w3), row_sum(w3 * gw)])
-
 
 def output_kernel(
-    per, sides_ref, one_ref, got_ref, comb_ref, x_ref, cot_ref, w3_ref, gain_ref, shift_ref,
+    step, per, sides_ref, one_ref, got_ref, comb_ref, x_ref, cot_ref, w3_ref, gain_ref, shift_ref,
     out_ref, u3_ref, stat_ref, send_ref, vec_ref, acc_ref,
 ):
-    step = pl.program_id(0)
-
-    @pl.when(step == 0)
-    def _():
+    if step is BEGIN:
         count = jnp.concatenate([one_ref[2:3]] * 4, axis=1)
         mean, inv = norm_terms(total(got_ref), count)
         scale = inv * gain_ref[:, 3 * WIDTH + INTER :]
@@ -419,6 +536,14 @@
         vec_ref[1:2] = shift_ref[:, 3 * WIDTH + INTER :] - mean * scale
         vec_ref[2:3] = 0.5 * scale
         acc_ref[...] = jnp.zeros_like(acc_ref)
+        return
+
+    if step is END:
+        send_rows(
+            send_ref,
+            [0.5 * row_sum(acc_ref[0:8]), 0.5 * row_sum(acc_ref[8:16]) / vec_ref[0:1]],
+        )
+        return
 
     chunk = 16
     lanes = 512
@@ -447,18 +572,14 @@
             acc_ref[0:8, cols] += ups
             acc_ref[8:16, cols] += products
 
-    @pl.when(step == pl.num_programs(0) - 1)
-    def _():
-        send_rows(
-            send_ref,
-            [0.5 * row_sum(acc_ref[0:8]), 0.5 * row_sum(acc_ref[8:16]) / vec_ref[0:1]],
-        )
-
-
-def project_kernel(comb_ref, u3_ref, w3_ref, p_ref, cu_ref):
-    @pl.when(pl.program_id(0) == 0)
-    def _():
+
+def project_kernel(step, comb_ref, u3_ref, w3_ref, p_ref, cu_ref):
+    if step is BEGIN:
         cu_ref[...] = jnp.zeros_like(cu_ref)
+        return
+
+    if step is END:
+        return
 
     u3 = u3_ref[...]
     p_ref[...] = dot_last(u3, w3_ref[...]).astype(BF16)
@@ -466,14 +587,11 @@
 
 
 def back_three_kernel(
-    per, three_ref, got_ref, hid_ref, comb_ref, p_ref, a2_ref, slope_ref,
+    step, per, three_ref, got_ref, hid_ref, comb_ref, p_ref, a2_ref, slope_ref,
     hat_ref, w3_ref, cu_ref, gw_ref, csum_ref, att_ref, fc_ref,
     t1_ref, t3_ref, duz_ref, w3g_ref, fcg_ref, norm_ref, s_ref, c_ref, send_ref, datt_ref,
 ):
-    step = pl.program_id(0)
-
-    @pl.when(step == 0)
-    def _():
+    if step is BEGIN:
         mean, inv = three_ref[0:1], three_ref[1:2]
         scale, count = three_ref[2:3], three_ref[3:4]
         sums = total(got_ref)
@@ -489,21 +607,9 @@
         csum = jnp.broadcast_to(csum_ref[...], (8, WIDTH))
         outer = high_rows(csum, jnp.broadcast_to(k1, (8, C_IN))) * 0.125
         w3g_ref[...] = cu_ref[...] - outer - gw_ref[...] * k2
-
-    corr = dot_f(comb_ref[...], s_ref[...])
-    for j in range(per):
-        rows = pl.ds(j * PIX, PIX)
-        dcomb = p_ref[rows].astype(F32) - corr[j * PIX : (j + 1) * PIX] - c_ref[0:1]
-        image = pl.ds(step * per + j, 1)
-        for q in range(2):
-            cols = pl.ds(q * WIDTH, WIDTH)
-            datt_ref[image, cols] = row_sum(fold(dcomb * a2_ref[rows, cols].astype(F32)))
-            u = dcomb * slope_ref[rows, cols].astype(F32)
-            t1_ref[image, cols] = row_sum(fold(u))
-            t3_ref[image, cols] = row_sum(fold(u * hat_ref[rows, cols].astype(F32)))
-
-    @pl.when(step == pl.num_programs(0) - 1)
-    def _():
+        return
+
+    if step is END:
         att = att_ref[...]
         datt = datt_ref[...]
         both = att * datt
@@ -520,6 +626,19 @@
             fcg_ref[pl.ds(b * INTER, INTER)] = fcg[:, cols]
             rows.append(bias[:, cols])
         send_rows(send_ref, rows + [jnp.zeros((2, 128), F32)])
+        return
+
+    corr = dot_f(comb_ref[...], s_ref[...])
+    for j in range(per):
+        rows = pl.ds(j * PIX, PIX)
+        dcomb = p_ref[rows].astype(F32) - corr[j * PIX : (j + 1) * PIX] - c_ref[0:1]
+        image = pl.ds(step * per + j, 1)
+        for q in range(2):
+            cols = pl.ds(q * WIDTH, WIDTH)
+            datt_ref[image, cols] = row_sum(fold(dcomb * a2_ref[rows, cols].astype(F32)))
+            u = dcomb * slope_ref[rows, cols].astype(F32)
+            t1_ref[image, cols] = row_sum(fold(u))
+            t3_ref[image, cols] = row_sum(fold(u * hat_ref[rows, cols].astype(F32)))
 
 
 def back_att_kernel(
@@ -554,14 +673,11 @@
 
 
 def back_two_kernel(
-    per, sides_ref, one_ref, two_ref, got_ref, comb_ref, p_ref, s_ref, c_ref, slope_ref, hat2_ref, hat1_ref, att_ref,
+    step, per, sides_ref, one_ref, two_ref, got_ref, comb_ref, p_ref, s_ref, c_ref, slope_ref, hat2_ref, hat1_ref, att_ref,
     dpool_ref, w_ref, gain_ref, shift_ref, dh2_ref, u1_ref, norm_ref, send_ref,
     vec_ref, pad_ref, acc_ref,
 ):
-    step = pl.program_id(0)
-
-    @pl.when(step == 0)
-    def _():
+    if step is BEGIN:
         count = jnp.concatenate([one_ref[2:3]] * 2, axis=1)
         scale = two_ref[1:2] * gain_ref[:, WIDTH : 3 * WIDTH]
         sums = total(got_ref)
@@ -572,6 +688,11 @@
         vec_ref[2:3] = scale * sums[1:2] / count
         acc_ref[...] = jnp.zeros_like(acc_ref)
         pad_ref[...] = jnp.zeros_like(pad_ref)
+        return
+
+    if step is END:
+        send_rows(send_ref, [row_sum(acc_ref[0:8]), row_sum(acc_ref[8:16])])
+        return
 
     first, last = edge_masks(HALF)
     corr = dot_f(comb_ref[...], s_ref[...])
@@ -631,21 +752,24 @@
             acc_ref[0:8, cols] += fold(u1)
             acc_ref[8:16, cols] += fold(u1 * hat)
 
-    @pl.when(step == pl.num_programs(0) - 1)
-    def _():
-        send_rows(send_ref, [row_sum(acc_ref[0:8]), row_sum(acc_ref[8:16])])
-
 
 def weight_two_kernel(
-    per, core_ref, sides_ref, hat_ref, dh2_ref, gain_ref, shift_ref, keep_ref, give_ref,
+    step, per, core_ref, sides_ref, hat_ref, dh2_ref, gain_ref, shift_ref, keep_ref, give_ref,
     taps_ref, acc_ref,
 ):
-    step = pl.program_id(0)
-
-    @pl.when(step == 0)
-    def _():
+    if step is BEGIN:
         acc_ref[...] = jnp.zeros_like(acc_ref)
         taps_ref[...] = jnp.zeros_like(taps_ref)
+        return
+
+    if step is END:
+        def put(core):
+            keep_ref[...] = acc_ref[core].T
+            give_ref[...] = acc_ref[1 - core].T
+
+        for core in range(2):
+            pl.when(core_ref[0] == core)(functools.partial(put, core))
+        return
 
     gain = gain_ref[:, :WIDTH] * 0.5
     shift = shift_ref[:, :WIDTH] * 0.5
@@ -674,25 +798,13 @@
         )
         acc_ref[q] += dot_rows(dh2_ref[:, q * WIDTH : (q + 1) * WIDTH], patches)
 
-    @pl.when(step == pl.num_programs(0) - 1)
-    def _():
-        def put(core):
-            keep_ref[...] = acc_ref[core].T
-            give_ref[...] = acc_ref[1 - core].T
-
-        for core in range(2):
-            pl.when(core_ref[0] == core)(functools.partial(put, core))
-
 
 def back_one_kernel(
-    per, core_ref, sides_ref, one_ref, three_ref, got_ref, u1_ref, hat_ref, u3_ref, x_ref, w_ref, gain_ref,
+    step, per, core_ref, sides_ref, one_ref, three_ref, got_ref, u1_ref, hat_ref, u3_ref, x_ref, w_ref, gain_ref,
     norm2_ref, norm_att_ref, norm3_ref,
     ig_ref, keep_ref, give_ref, gain_out_ref, shift_out_ref, vec_ref, wide_ref, dh_ref, acc_ref,
 ):
-    step = pl.program_id(0)
-
-    @pl.when(step == 0)
-    def _():
+    if step is BEGIN:
         count = one_ref[2:3]
         scale = one_ref[1:2] * gain_ref[:, :WIDTH]
         sums = total(got_ref)
@@ -706,6 +818,16 @@
         vec_ref[2:3] = scale * sums[1:2] / count
         wide_ref[...] = 1.0 / three_ref[2:3]
         acc_ref[...] = jnp.zeros_like(acc_ref)
+        return
+
+    if step is END:
+        def put(core):
+            keep_ref[...] = acc_ref[core * HALF : (core + 1) * HALF].T
+            give_ref[...] = acc_ref[(1 - core) * HALF : (2 - core) * HALF].T
+
+        for core in range(2):
+            pl.when(core_ref[0] == core)(functools.partial(put, core))
+        return
 
     for j in range(per):
         rows = pl.ds(j * PIX, PIX)
@@ -719,15 +841,6 @@
     acc_ref[...] += dot_rows(dh, x_ref[...])
     dx = dot_last(dh, w_ref[...])
     ig_ref[...] = (u3_ref[...].astype(F32) * wide_ref[...] + dx).astype(BF16)
-
-    @pl.when(step == pl.num_programs(0) - 1)
-    def _():
-        def put(core):
-            keep_ref[...] = acc_ref[core * HALF : (core + 1) * HALF].T
-            give_ref[...] = acc_ref[(1 - core) * HALF : (2 - core) * HALF].T
-
-        for core in range(2):
-            pl.when(core_ref[0] == core)(functools.partial(put, core))
 
 
 def round_up(value, multiple):
@@ -802,7 +915,7 @@
         pack_kernel,
         1,
         [(core, SMEM_SPEC)] + [(weight, whole(weight.shape)) for weight in weights],
-        [(first, BF16, whole(first)), (second, BF16, whole(second))],
+        [(first, BF16, whole(first), True), (second, BF16, whole(second), True)],
         flops=1000000,
         moved=4000000,
         name="pack",
@@ -869,7 +982,7 @@
     shift_in = (shift, whole((1, n_ch)))
 
     def payload(k, n):
-        return ((devices, k, n), F32, whole((devices, k, n)))
+        return ((devices, k, n), F32, whole((devices, k, n)), True)
 
     def small(*shape):
         return (shape, F32, whole(shape))
@@ -881,16 +994,17 @@
         return (array, whole(array.shape), True)
 
     def blocks(array):
-        return (array, rows_of(per * PIX, array.shape[1]))
-
-    def blocks_out(width, dtype=BF16):
-        return ((rows, width), dtype, rows_of(per * PIX, width))
+        return (array, Stream())
+
+    def blocks_out(width, dtype=BF16, over=None):
+        return ((rows, width), dtype, Stream(over))
 
     mine, other, others = gather_weights(core, (weight_one, weight_two, weight_three))
 
     per, steps = split(PER_CONV_ONE)
-    h1, full_one, send = call(
-        functools.partial(conv_one_kernel, per),
+    h1, full_one, send = stream_call(
+        lambda step, *refs, per=per: conv_one_kernel(step, per, *refs),
+        per,
         steps,
         [core_in, sides_in, blocks(x), near(mine), near(other)],
         [blocks_out(WIDTH, F32), ((C_IN, WIDTH), BF16, whole((C_IN, WIDTH))), payload(4, WIDTH)],
@@ -903,8 +1017,9 @@
     full_two, full_three = others(send)
 
     per, steps = split(PER_CONV_TWO)
-    hat1, h2, stat1, send = call(
-        functools.partial(conv_two_kernel, per),
+    hat1, h2, stat1, send = stream_call(
+        lambda step, *refs, per=per: conv_two_kernel(step, per, *refs),
+        per,
         steps,
         [sides_in, near(got_one), blocks(h1), full(full_two), gain_in, shift_in],
         [blocks_out(WIDTH), blocks_out(2 * WIDTH, F32), small(8, WIDTH), payload(2, 2 * WIDTH)],
@@ -919,8 +1034,9 @@
     got_two = everyone(send)
 
     per, steps = split(PER_ACT_TWO)
-    hat2, pooled, zin, stat2, send = call(
-        functools.partial(act_two_kernel, per),
+    hat2, pooled, zin, stat2, send = stream_call(
+        lambda step, *refs, per=per: act_two_kernel(step, per, *refs),
+        per,
         steps,
         [
             sides_in,
@@ -945,8 +1061,9 @@
     got_att = everyone(send)
 
     per, steps = split(PER_SLOPE_TWO)
-    a2, slope2, t2, t4 = call(
-        functools.partial(slope_two_kernel, per),
+    a2, slope2, t2, t4 = stream_call(
+        lambda step, *refs, per=per: slope_two_kernel(step, per, *refs),
+        per,
         steps,
         [sides_in, blocks(hat2), gain_in, shift_in],
         [
@@ -961,8 +1078,9 @@
     )
 
     per, steps = split(PER_COMBINE)
-    att, comb, gw, csum, hid, send = call(
-        functools.partial(combine_kernel, per, n_images),
+    att, comb, gw, csum, hid, send = stream_call(
+        lambda step, *refs, per=per: combine_kernel(step, per, n_images, *refs),
+        per,
         steps,
         [
             near(got_att),
@@ -990,8 +1108,9 @@
     got_three = everyone(send)
 
     per, steps = split(PER_OUTPUT)
-    outputs, u3, stat3, send = call(
-        functools.partial(output_kernel, per),
+    outputs, u3, stat3, send = stream_call(
+        lambda step, *refs, per=per: output_kernel(step, per, *refs),
+        per,
         steps,
         [
             sides_in,
@@ -1004,7 +1123,12 @@
             gain_in,
             shift_in,
         ],
-        [blocks_out(C_IN), blocks_out(C_IN), small(8, C_IN), payload(2, C_IN)],
+        [
+            blocks_out(C_IN, over=4),
+            blocks_out(C_IN, over=5),
+            small(8, C_IN),
+            payload(2, C_IN),
+        ],
         [pltpu.VMEM((8, C_IN), F32), pltpu.VMEM((16, C_IN), F32)],
         flops=2 * rows * WIDTH * C_IN,
         moved=rows * C_IN * 8,
@@ -1013,8 +1137,9 @@
     got_back_three = everyone(send)
 
     per, steps = split(PER_PROJECT)
-    p, cu = call(
+    p, cu = stream_call(
         project_kernel,
+        per,
         steps,
         [blocks(comb), blocks(u3), full(full_three)],
         [blocks_out(WIDTH), small(WIDTH, C_IN)],
@@ -1024,8 +1149,9 @@
     )
 
     per, steps = split(PER_BACK_THREE)
-    t1, t3, duz, w3_local, fc2_local, norm3, corr_weight, corr_row, send = call(
-        functools.partial(back_three_kernel, per),
+    t1, t3, duz, w3_local, fc2_local, norm3, corr_weight, corr_row, send = stream_call(
+        lambda step, *refs, per=per: back_three_kernel(step, per, *refs),
+        per,
         steps,
         [
             full(stat3),
@@ -1109,8 +1235,9 @@
     three = slots(three)
 
     per, steps = split(PER_BACK_TWO)
-    dh2, u1, norm2, send = call(
-        functools.partial(back_two_kernel, per),
+    dh2, u1, norm2, send = stream_call(
+        lambda step, *refs, per=per: back_two_kernel(step, per, *refs),
+        per,
         steps,
         [
             sides_in,
@@ -1150,8 +1277,9 @@
 
     per, steps = split(PER_WEIGHT_TWO)
     half = (9 * HALF, WIDTH)
-    keep, give = call(
-        functools.partial(weight_two_kernel, per),
+    keep, give = stream_call(
+        lambda step, *refs, per=per: weight_two_kernel(step, per, *refs),
+        per,
         steps,
         [core_in, sides_in, blocks(hat1), blocks(dh2), gain_in, shift_in],
         [(half, F32, whole(half)), (half, F32, whole(half))],
@@ -1182,8 +1310,9 @@
 
     per, steps = split(PER_BACK_ONE)
     half = (C_IN, HALF)
-    input_grad, keep, give, gain_grad, shift_grad = call(
-        functools.partial(back_one_kernel, per),
+    input_grad, keep, give, gain_grad, shift_grad = stream_call(
+        lambda step, *refs, per=per: back_one_kernel(step, per, *refs),
+        per,
         steps,
         [
             core_in,

time: 339 us -> 327 us (0.965)
  Pallas kernels: 190 us -> 175 us
  local copies, waits for them, and re-layouts: 2.59 us -> 6.46 us
    pallas_call x16 -> x5, Pallas kernels: 190 us -> 12.5 us  [call(): pl.pallas_call(kernel, grid=(grid,), in_specs=[spec for _, spec, *_ in in...]
    pallas_call x0 -> x11, Pallas kernels: none -> 163 us  [stream_call(): pl.pallas_call(whole_kernel, in_specs=in_specs, out_specs=out_specs, out_...]
  transfers between devices with their start and end apart: 18 -> 18, of which waited for: 8 -> 8; matrix products, arithmetic and copies ran while one was open for 3% -> 3% of each run, Pallas kernels for 30% -> 29%
where the time goes in v3:
time: 327 us; the launch traced here: 324 us
  Pallas kernels  175 us (54%)
  starting transfers between devices  56.6 us (17%)
  blocking collectives  52.1 us (16%)
  waiting for transfers between devices  22.8 us (7%)
  other arithmetic  9.46 us (3%)
  local copies, waits for them, and re-layouts  6.46 us (2%)
    pallas_call x11, Pallas kernels, stream_call(): pl.pallas_call(whole_kernel, in_specs=in_specs, out_specs=out_specs, out_...  163 us
    all_to_all x3, blocking collectives, everyone(): return lax.all_to_all(payload, AXES, 0, 0, tiled=True)  38.4 us
    all_to_all x5, starting transfers between devices, everyone(): return lax.all_to_all(payload, AXES, 0, 0, tiled=True)  21.9 us
    all_to_all x3, starting transfers between devices, slots(): return lax.all_to_all(parts, 'fsdp', 0, 0, tiled=True)  18.4 us
    all_to_all x1, blocking collectives, gather_weights(): mine = lax.all_to_all(spread_one, 'fsdp', 0, 0, tiled=True)  13.7 us
    pallas_call x5, Pallas kernels, call(): pl.pallas_call(kernel, grid=(grid,), in_specs=[spec for _, spec, *_ in in...  12.5 us
    ppermute x9, starting transfers between devices, other_core(): return lax.ppermute(array, 'dp', [(0, 1), (1, 0)])  12.2 us
    all_to_all x1, waiting for transfers between devices, gather_weights(): mine_two = lax.all_to_all(spread_two, 'fsdp', 0, 0, tiled=True)  10.5 us
  transfers between devices with their start and end apart: 18, of which 8 were waited for; matrix products, arithmetic and copies ran while one was open for 3% of the time, Pallas kernels for 29%

profile of v3, /device:TPU:9, one launch (start us, length us, event | category | flops | bytes accessed | tf_op | source)
XLA Modules:
  0.0 323.8 jit_solution(7006257867721962027)
XLA Ops:
  0.6 2.0 pack.1
  2.7 13.7 %all_to_all.65.refs_3_ = bf16[16,64,128]{2,1,0:T(8,128)(2,1)S(1)} all-to-all(bf16[16,64,128]{2,1,0:T(8,128)(2,1)} %get-tuple-element.86), channel_id=1, replica_groups=mesh['fsdp'=16,'dp'=2] {'fsdp'}, dimensions={0} | all-to-all | bytes 524288 | tf_op jit(solution)/shard_map/all_to_all | solution.py:923
  16.4 3.2 collective-permute-start
  19.6 1.2 collective-permute-done.refs_4_
  20.8 4.1 %all-to-all-start.2 = ((bf16[16,208,128]{2,1,0:T(8,128)(2,1)}), bf16[16,208,128]{2,1,0:T(8,128)(2,1)S(1)}, u32[]{:S(2)}, u32[]{:S(2)}) async-start(bf16[16,208,128]{2,1,0:T(8,128)(2,1)} %get-tuple-element.91), calls=%async_computation.2 | async-start | bytes 1703936 | tf_op jit(solution)/shard_map/all_to_all | solution.py:926
  24.9 10.0 %conv_one.1 = (f32[6144,256]{1,0:T(8,128)}, bf16[1024,256]{1,0:T(8,128)(2,1)}, f32[32,4,256]{2,1,0:T(4,128)}) custom-call(s32[1]{0:T(128)} %bitcast.core_ref.refs_0_, s32[24]{0:T(128)} %refs_1_.5, bf16[6144,1024]{1,0:T(8,128)(2,1)} %bitcast.9, bf16[16,64,128]{2,1,0:T(8,128)(2,1)} %copy-done.3, bf16[16,64,128]{2,1,0:T(8,128)(2,1)} %copy-done.6), custom_call_target="tpu_custom_call" | custom-call | flops 3221225472 | bytes 18874368 | tf_op jit(solution)/shard_map/conv_one/pallas_call | solution.py:249
  34.9 10.5 %all-to-all-done.2.mine_ref = bf16[16,208,128]{2,1,0:T(8,128)(2,1)S(1)} async-done(((bf16[16,208,128]{2,1,0:T(8,128)(2,1)}), bf16[16,208,128]{2,1,0:T(8,128)(2,1)S(1)}, u32[]{:S(2)}, u32[]{:S(2)}) %all-to-all-start.2) | async-done | bytes 852000 | tf_op jit(solution)/shard_map/all_to_all | solution.py:926
  45.4 2.1 collective-permute-start.1
  47.5 3.4 %all-to-all-start.1 = ((f32[32,4,256]{2,1,0:T(4,128)}), f32[32,4,256]{2,1,0:T(4,128)S(1)}, u32[]{:S(2)}, u32[]{:S(2)}) async-start(f32[32,4,256]{2,1,0:T(4,128)} %get-tuple-element.89), calls=%async_computation.1 | async-start | bytes 262144 | tf_op jit(solution)/shard_map/all_to_all | solution.py:892
  50.9 0.6 reshape.61.refs_4_.refs_2_.refs_6_.refs_7_.gain_ref.refs_14_.refs_10_
  51.5 0.6 reshape.62.refs_5_.refs_3_.refs_7_.refs_8_.refs_15_
  52.1 0.9 copy-done.4
  53.0 2.9 unpack.1
  55.9 1.1 all-to-all-done.1.refs_1_
  57.0 0.7 copy-done.9
  57.7 17.2 %conv_two.1 = (bf16[6144,256]{1,0:T(8,128)(2,1)}, f32[6144,512]{1,0:T(8,128)}, f32[8,256]{1,0:T(8,128)}, f32[32,2,512]{2,1,0:T(2,128)}) custom-call(s32[24]{0:T(128)} %refs_1_.5, f32[32,4,256]{2,1,0:T(4,128)} %copy-done.9, f32[6144,256]{1,0:T(8,128)} %get-tuple-element.90.refs_2_, bf16[1152,512]{1,0:T(8,128)(2,1)} %get-tuple-element.93.refs_3_.refs_13_, ...), custom_call_target="tpu_custom_call" | custom-call | flops 7247757312 | bytes 22020096 | tf_op jit(solution)/shard_map/conv_two/pallas_call | solution.py:249
  74.9 11.5 %all_to_all.66.refs_2_ = f32[32,2,512]{2,1,0:T(2,128)} all-to-all(f32[32,2,512]{2,1,0:T(2,128)} %get-tuple-element.95), channel_id=1, replica_groups=mesh['fsdp'=16,'dp'=2] {'fsdp','dp'}, dimensions={0} | all-to-all | bytes 262144 | tf_op jit(solution)/shard_map/all_to_all | solution.py:892
  86.4 9.6 %act_two.1 = (bf16[6144,512]{1,0:T(8,128)(2,1)}, f32[24,256]{1,0:T(8,128)}, f32[24,128]{1,0:T(8,128)}, f32[8,512]{1,0:T(8,128)}, f32[32,2,128]{2,1,0:T(2,128)}) custom-call(s32[24]{0:T(128)} %refs_1_.5, f32[8,256]{1,0:T(8,128)} %get-tuple-element.94.refs_1_.refs_2_, f32[32,2,512]{2,1,0:T(2,128)} %all_to_all.66.refs_2_, ...), custom_call_target="tpu_custom_call" | custom-call | flops 62914560 | bytes 31457280 | tf_op jit(solution)/shard_map/act_two/pallas_call | solution.py:249
  96.0 4.6 %all-to-all-start.4 = ((f32[32,2,128]{2,1,0:T(2,128)}), f32[32,2,128]{2,1,0:T(2,128)S(1)}, u32[]{:S(2)}, u32[]{:S(2)}) async-start(f32[32,2,128]{2,1,0:T(2,128)} %get-tuple-element.97), calls=%async_computation.4 | async-start | bytes 65536 | tf_op jit(solution)/shard_map/all_to_all | solution.py:892
  100.6 11.3 %slope_two.1 = (bf16[6144,512]{1,0:T(8,128)(2,1)}, bf16[6144,512]{1,0:T(8,128)(2,1)}, f32[24,512]{1,0:T(8,128)}, f32[24,512]{1,0:T(8,128)}) custom-call(s32[24]{0:T(128)} %refs_1_.5, bf16[6144,512]{1,0:T(8,128)(2,1)} %get-tuple-element.99.refs_1_.refs_7_.refs_9_, f32[1,1920]{1,0:T(1,128)} %reshape.61.refs_4_.refs_2_.refs_6_.refs_7_.gain_ref.refs_14_.refs_10_, ...), custom_call_target="tpu_custom_call" | custom-call | flops 62914560 | bytes 18874368 | tf_op jit(solution)/shard_map/slope_two/pallas_call | solution.py:249
  111.9 0.6 copy-done.7
  112.5 8.0 %combine.1 = (f32[24,512]{1,0:T(8,128)}, bf16[6144,256]{1,0:T(8,128)(2,1)}, f32[256,1024]{1,0:T(8,128)}, f32[1,256]{1,0:T(1,128)}, f32[4,24,128]{2,1,0:T(8,128)}, /*index=5*/f32[32,2,1024]{2,1,0:T(2,128)}) custom-call(f32[32,2,128]{2,1,0:T(2,128)} %copy-done.7, f32[24,128]{1,0:T(8,128)} %get-tuple-element.98.refs_1_, ...), custom_call_target="tpu_custom_call" | custom-call | flops 805306368 | bytes 9437184 | tf_op jit(solution)/shard_map/combine/pallas_call | solution.py:249
  120.5 14.7 %all_to_all.67.refs_2_ = f32[32,2,1024]{2,1,0:T(2,128)} all-to-all(f32[32,2,1024]{2,1,0:T(2,128)} %get-tuple-element.102), channel_id=1, replica_groups=mesh['fsdp'=16,'dp'=2] {'fsdp','dp'}, dimensions={0} | all-to-all | bytes 524288 | tf_op jit(solution)/shard_map/all_to_all | solution.py:892
  135.3 24.9 %output.1 = (bf16[6144,1024]{1,0:T(8,128)(2,1)}, bf16[6144,1024]{1,0:T(8,128)(2,1)}, f32[8,1024]{1,0:T(8,128)}, f32[32,2,1024]{2,1,0:T(2,128)}) custom-call(s32[24]{0:T(128)} %refs_1_.5, f32[8,256]{1,0:T(8,128)} %get-tuple-element.94.refs_1_.refs_2_, f32[32,2,1024]{2,1,0:T(2,128)} %all_to_all.67.refs_2_, ...), custom_call_target="tpu_custom_call" | custom-call | flops 3221225472 | bytes 50331648 | tf_op jit(solution)/shard_map/output/pallas_call | solution.py:249
  160.2 4.5 %all-to-all-start.6 = ((f32[32,2,1024]{2,1,0:T(2,128)}), f32[32,2,1024]{2,1,0:T(2,128)S(1)}, u32[]{:S(2)}, u32[]{:S(2)}) async-start(f32[32,2,1024]{2,1,0:T(2,128)} %get-tuple-element.107), calls=%async_computation.6 | async-start | bytes 524288 | tf_op jit(solution)/shard_map/all_to_all | solution.py:892
  164.7 12.5 %project.1 = (bf16[6144,256]{1,0:T(8,128)(2,1)}, f32[256,1024]{1,0:T(8,128)}) custom-call(bf16[6144,256]{1,0:T(8,128)(2,1)} %get-tuple-element.103.refs_3_.refs_0_.refs_4_, bf16[6144,1024]{1,0:T(8,128)(2,1)} %get-tuple-element.109.refs_1_.refs_7_, bf16[256,1024]{1,0:T(8,128)(2,1)} %get-tuple-element.101.refs_3_.refs_6_.refs_2_.refs_8_), custom_call_target="tpu_custom_call" | custom-call | flops 6442450944 | bytes 25165824 | tf_op jit(solution)/shard_map/project/pallas_call | solution.py:249
  177.2 0.7 copy-done.2
  177.9 12.8 %back_three.1 = (f32[24,512]{1,0:T(8,128)}, f32[24,512]{1,0:T(8,128)}, f32[24,128]{1,0:T(8,128)}, f32[256,1024]{1,0:T(8,128)}, f32[512,128]{1,0:T(8,128)}, /*ind...) custom-call(f32[8,1024]{1,0:T(8,128)} %get-tuple-element.105.refs_0_.refs_3_, ...), custom_call_target="tpu_custom_call" | custom-call | flops 805306368 | bytes 25165824 | tf_op jit(solution)/shard_map/back_three/pallas_call | solution.py:249
  190.7 12.2 %all_to_all.68.got_ref = f32[32,8,128]{2,1,0:T(8,128)} all-to-all(f32[32,8,128]{2,1,0:T(8,128)} %get-tuple-element.116), channel_id=1, replica_groups=mesh['fsdp'=16,'dp'=2] {'fsdp','dp'}, dimensions={0} | all-to-all | bytes 262144 | tf_op jit(solution)/shard_map/all_to_all | solution.py:892
  202.9 2.5 back_att.1
  205.4 2.5 pack_three.1
  207.9 1.3 collective-permute-start.2
  209.2 3.5 %all-to-all-start.8 = ((f32[32,2,512]{2,1,0:T(2,128)}), f32[32,2,512]{2,1,0:T(2,128)S(1)}, u32[]{:S(2)}, u32[]{:S(2)}) async-start(f32[32,2,512]{2,1,0:T(2,128)} %get-tuple-element.124), calls=%async_computation.8 | async-start | bytes 262144 | tf_op jit(solution)/shard_map/all_to_all | solution.py:892
  212.7 2.1 add.6
  214.8 4.1 %all-to-all-done.8.refs_3_ = f32[32,2,512]{2,1,0:T(2,128)S(1)} async-done(((f32[32,2,512]{2,1,0:T(2,128)}), f32[32,2,512]{2,1,0:T(2,128)S(1)}, u32[]{:S(2)}, u32[]{:S(2)}) %all-to-all-start.8) | async-done | bytes 131104 | tf_op jit(solution)/shard_map/all_to_all | solution.py:892
  218.9 5.5 %all-to-all-start.9 = ((f32[16,88,128]{2,1,0:T(8,128)}), f32[16,88,128]{2,1,0:T(8,128)S(1)}, u32[]{:S(2)}, u32[]{:S(2)}) async-start(f32[16,88,128]{2,1,0:T(8,128)} %add.6), calls=%async_computation.9 | async-start | bytes 1441792 | tf_op jit(solution)/shard_map/all_to_all | solution.py:947
  224.5 23.0 %back_two.1 = (bf16[6144,512]{1,0:T(8,128)(2,1)}, bf16[6144,256]{1,0:T(8,128)(2,1)}, f32[2,512]{1,0:T(2,128)}, f32[32,2,256]{2,1,0:T(2,128)}) custom-call(s32[24]{0:T(128)} %refs_1_.5, f32[8,256]{1,0:T(8,128)} %get-tuple-element.94.refs_1_.refs_2_, f32[8,512]{1,0:T(8,128)} %get-tuple-element.106.refs_2_, f32[32,2,512]{2,1,0:T(2,128)} %copy-done.8, ...), custom_call_target="tpu_custom_call" | custom-call | flops 7247757312 | bytes 31457280 | tf_op jit(solution)/shard_map/back_two/pallas_call | solution.py:249
  247.5 6.0 %all-to-all-start.10 = ((f32[32,2,256]{2,1,0:T(2,128)}), f32[32,2,256]{2,1,0:T(2,128)S(1)}, u32[]{:S(2)}, u32[]{:S(2)}) async-start(f32[32,2,256]{2,1,0:T(2,128)} %get-tuple-element.137), calls=%async_computation.10 | async-start | bytes 131072 | tf_op jit(solution)/shard_map/all_to_all | solution.py:892
  253.6 15.5 %weight_two.1 = (f32[1152,256]{1,0:T(8,128)}, f32[1152,256]{1,0:T(8,128)}) custom-call(s32[1]{0:T(128)} %bitcast.core_ref.refs_0_, s32[24]{0:T(128)} %refs_1_.5, bf16[6144,256]{1,0:T(8,128)(2,1)} %get-tuple-element.132.refs_10_.refs_2_.refs_6_, bf16[6144,512]{1,0:T(8,128)(2,1)} %get-tuple-element.138.refs_3_, ...), custom_call_target="tpu_custom_call" | custom-call | flops 7247757312 | bytes 9437184 | tf_op jit(solution)/shard_map/weight_two/pallas_call | solution.py:249
  269.2 0.4 collective-permute-start.3
  269.6 0.2 collective-permute-start.7
  269.8 0.6 slice.60.fc_ref
  270.4 1.7 collective-permute-done.7
  272.1 0.1 collective-permute-done.3.other_ref
  272.3 1.0 copy-done.1
  273.3 2.6 pack_two.1
  275.9 6.5 %all-to-all-start.11 = ((bf16[16,96,256]{2,1,0:T(8,128)(2,1)}), bf16[16,96,256]{2,1,0:T(8,128)(2,1)S(1)}, u32[]{:S(2)}, u32[]{:S(2)}) async-start(bf16[16,96,256]{2,1,0:T(8,128)(2,1)} %pack_two.1), calls=%async_computation.11 | async-start | bytes 1572864 | tf_op jit(solution)/shard_map/all_to_all | solution.py:947
  282.4 17.9 %back_one.1 = (bf16[6144,1024]{1,0:T(8,128)(2,1)}, f32[1024,128]{1,0:T(8,128)}, f32[1024,128]{1,0:T(8,128)}, f32[1,1920]{1,0:T(1,128)}, f32[1,1920]{1,0:T(1,128)}) custom-call(s32[1]{0:T(128)} %bitcast.core_ref.refs_0_, s32[24]{0:T(128)} %refs_1_.5, f32[8,256]{1,0:T(8,128)} %get-tuple-element.94.refs_1_.refs_2_, ...), custom_call_target="tpu_custom_call" | custom-call | flops 6442450944 | bytes 37748736 | tf_op jit(solution)/shard_map/back_one/pallas_call | solution.py:249
  300.3 1.0 collective-permute-start.4
  301.3 1.7 collective-permute-done.4
  303.1 1.8 add_convert_fusion
  304.9 0.1 convert_reduce_fusion
  305.0 6.4 %all-to-all-start.12 = ((bf16[16,64,128]{2,1,0:T(8,128)(2,1)}), bf16[16,64,128]{2,1,0:T(8,128)(2,1)S(1)}, u32[]{:S(2)}, u32[]{:S(2)}) async-start(bf16[16,64,128]{2,1,0:T(8,128)(2,1)} %bitcast.6), calls=%async_computation.12 | async-start | bytes 524288 | tf_op jit(solution)/shard_map/all_to_all | solution.py:947
  311.4 0.9 collective-permute-start.6
  312.3 0.1 collective-permute-start.8
  312.4 0.6 broadcast_select_fusion
  313.1 1.3 reduce
  314.4 1.3 reduce.1
  315.7 0.7 maximum_select_fusion.1
  316.5 2.2 all-to-all-done.12
  318.7 3.0 collective-permute-start.5
  321.7 0.7 pad_maximum_fusion
  322.5 0.7 slice.67
  323.1 0.6 maximum_select_fusion.2
  (47 shorter events, 0.3 us)
Async XLA Ops:
  16.4 8.5 %copy-start.3 = (bf16[16,64,128]{2,1,0:T(8,128)(2,1)}, bf16[16,64,128]{2,1,0:T(8,128)(2,1)S(1)}, u32[]{:S(2)}) copy-start(bf16[16,64,128]{2,1,0:T(8,128)(2,1)S(1)} %all_to_all.65.refs_3_) | copy-start | bytes 786436
  16.4 4.4 %collective-permute-start = (bf16[16,64,128]{2,1,0:T(8,128)(2,1)S(1)}, bf16[16,64,128]{2,1,0:T(8,128)(2,1)S(1)}, u32[]{:S(2)}, u32[]{:S(2)}) collective-permute-start(bf16[16,64,128]{2,1,0:T(8,128)(2,1)S(1)} %all_to_all.65.refs_3_), channel_id=1, source_target_pairs={{0,1},{1,0},{2,3},{3,2},{4,5},{5,4},{6,7},{7,6},{8,9},{9,8},{10,11... | collective-permute-start | bytes 786440 | tf_op jit(solution)/shard_map/ppermute | solution.py:896
  20.8 4.1 %copy-start.6 = (bf16[16,64,128]{2,1,0:T(8,128)(2,1)}, bf16[16,64,128]{2,1,0:T(8,128)(2,1)S(1)}, u32[]{:S(2)}) copy-start(bf16[16,64,128]{2,1,0:T(8,128)(2,1)S(1)} %collective-permute-done.refs_4_) | copy-start | bytes 786436
  20.8 24.6 %all-to-all-start.2 = ((bf16[16,208,128]{2,1,0:T(8,128)(2,1)}), bf16[16,208,128]{2,1,0:T(8,128)(2,1)S(1)}, u32[]{:S(2)}, u32[]{:S(2)}) async-start(bf16[16,208,128]{2,1,0:T(8,128)(2,1)} %get-tuple-element.91), calls=%async_computation.2 | async-start | bytes 1703936 | tf_op jit(solution)/shard_map/all_to_all | solution.py:926
  24.9 26.0 %copy-start.10 = (f32[1920]{0:T(1024)S(1)}, f32[1920]{0:T(1024)}, u32[]{:S(2)}) copy-start(f32[1920]{0:T(1024)} %param.19) | copy-start | bytes 23044
  24.9 26.6 %copy-start.11 = (f32[1920]{0:T(1024)S(1)}, f32[1920]{0:T(1024)}, u32[]{:S(2)}) copy-start(f32[1920]{0:T(1024)} %param.20) | copy-start | bytes 23044
  45.4 6.7 %copy-start = (bf16[16,208,128]{2,1,0:T(8,128)(2,1)}, bf16[16,208,128]{2,1,0:T(8,128)(2,1)S(1)}, u32[]{:S(2)}) copy-start(bf16[16,208,128]{2,1,0:T(8,128)(2,1)S(1)} %all-to-all-done.2.mine_ref) | copy-start | bytes 2555908
  45.4 6.7 %collective-permute-start.1 = (bf16[16,208,128]{2,1,0:T(8,128)(2,1)S(1)}, bf16[16,208,128]{2,1,0:T(8,128)(2,1)S(1)}, u32[]{:S(2)}, u32[]{:S(2)}) collective-permute-start(bf16[16,208,128]{2,1,0:T(8,128)(2,1)S(1)} %all-to-all-done.2.mine_ref), channel_id=1, source_target_pairs={{0,1},{1,0},{2,3},{3,2},{4,5},{5,4},{6,7},{7,6},{8,9},{9,8},{10,11... | collective-permute-start | bytes 2555912 | tf_op jit(solution)/shard_map/ppermute | solution.py:896
  47.5 9.5 %all-to-all-start.1 = ((f32[32,4,256]{2,1,0:T(4,128)}), f32[32,4,256]{2,1,0:T(4,128)S(1)}, u32[]{:S(2)}, u32[]{:S(2)}) async-start(f32[32,4,256]{2,1,0:T(4,128)} %get-tuple-element.89), calls=%async_computation.1 | async-start | bytes 262144 | tf_op jit(solution)/shard_map/all_to_all | solution.py:892
  52.1 0.9 copy-start.4
  57.0 0.7 copy-start.9
  96.0 15.9 %all-to-all-start.4 = ((f32[32,2,128]{2,1,0:T(2,128)}), f32[32,2,128]{2,1,0:T(2,128)S(1)}, u32[]{:S(2)}, u32[]{:S(2)}) async-start(f32[32,2,128]{2,1,0:T(2,128)} %get-tuple-element.97), calls=%async_computation.4 | async-start | bytes 65536 | tf_op jit(solution)/shard_map/all_to_all | solution.py:892
  111.9 0.6 copy-start.7
  160.2 17.0 %all-to-all-start.6 = ((f32[32,2,1024]{2,1,0:T(2,128)}), f32[32,2,1024]{2,1,0:T(2,128)S(1)}, u32[]{:S(2)}, u32[]{:S(2)}) async-start(f32[32,2,1024]{2,1,0:T(2,128)} %get-tuple-element.107), calls=%async_computation.6 | async-start | bytes 524288 | tf_op jit(solution)/shard_map/all_to_all | solution.py:892
  177.2 0.7 copy-start.2
  207.9 4.8 %collective-permute-start.2 = (f32[16,88,128]{2,1,0:T(8,128)}, f32[16,88,128]{2,1,0:T(8,128)S(1)}, u32[]{:S(2)}, u32[]{:S(2)}) collective-permute-start(f32[16,88,128]{2,1,0:T(8,128)} %get-tuple-element.128), channel_id=1, source_target_pairs={{0,1},{1,0},{2,3},{3,2},{4,5},{5,4},{6,7},{7,6},{8,9},{9,8},{10,11... | collective-permute-start | bytes 2162696 | tf_op jit(solution)/shard_map/ppermute | solution.py:896
  209.2 9.7 %all-to-all-start.8 = ((f32[32,2,512]{2,1,0:T(2,128)}), f32[32,2,512]{2,1,0:T(2,128)S(1)}, u32[]{:S(2)}, u32[]{:S(2)}) async-start(f32[32,2,512]{2,1,0:T(2,128)} %get-tuple-element.124), calls=%async_computation.8 | async-start | bytes 262144 | tf_op jit(solution)/shard_map/all_to_all | solution.py:892
  218.9 5.5 %copy-start.8 = (f32[32,2,512]{2,1,0:T(2,128)}, f32[32,2,512]{2,1,0:T(2,128)S(1)}, u32[]{:S(2)}) copy-start(f32[32,2,512]{2,1,0:T(2,128)S(1)} %all-to-all-done.8.refs_3_) | copy-start | bytes 393220
  218.9 28.6 %all-to-all-start.9 = ((f32[16,88,128]{2,1,0:T(8,128)}), f32[16,88,128]{2,1,0:T(8,128)S(1)}, u32[]{:S(2)}, u32[]{:S(2)}) async-start(f32[16,88,128]{2,1,0:T(8,128)} %add.6), calls=%async_computation.9 | async-start | bytes 1441792 | tf_op jit(solution)/shard_map/all_to_all | solution.py:947
  247.5 21.6 %all-to-all-start.10 = ((f32[32,2,256]{2,1,0:T(2,128)}), f32[32,2,256]{2,1,0:T(2,128)S(1)}, u32[]{:S(2)}, u32[]{:S(2)}) async-start(f32[32,2,256]{2,1,0:T(2,128)} %get-tuple-element.137), calls=%async_computation.10 | async-start | bytes 131072 | tf_op jit(solution)/shard_map/all_to_all | solution.py:892
  269.1 13.2 %copy-start.5 = (f32[32,2,256]{2,1,0:T(2,128)}, f32[32,2,256]{2,1,0:T(2,128)S(1)}, u32[]{:S(2)}) copy-start(f32[32,2,256]{2,1,0:T(2,128)S(1)} %all-to-all-done.10.refs_4_) | copy-start | bytes 196612
  269.2 3.1 collective-permute-start.3
  269.6 2.5 collective-permute-start.7
  272.3 1.0 copy-start.1
  275.9 29.0 %all-to-all-start.11 = ((bf16[16,96,256]{2,1,0:T(8,128)(2,1)}), bf16[16,96,256]{2,1,0:T(8,128)(2,1)S(1)}, u32[]{:S(2)}, u32[]{:S(2)}) async-start(bf16[16,96,256]{2,1,0:T(8,128)(2,1)} %pack_two.1), calls=%async_computation.11 | async-start | bytes 1572864 | tf_op jit(solution)/shard_map/all_to_all | solution.py:947
  300.3 2.7 collective-permute-start.4
  305.0 13.7 %all-to-all-start.12 = ((bf16[16,64,128]{2,1,0:T(8,128)(2,1)}), bf16[16,64,128]{2,1,0:T(8,128)(2,1)S(1)}, u32[]{:S(2)}, u32[]{:S(2)}) async-start(bf16[16,64,128]{2,1,0:T(8,128)(2,1)} %bitcast.6), calls=%async_computation.12 | async-start | bytes 524288 | tf_op jit(solution)/shard_map/all_to_all | solution.py:947
  311.4 4.3 %collective-permute-start.6 = (f32[72,256]{1,0:T(8,128)S(1)}, f32[72,256]{1,0:T(8,128)S(1)}, u32[]{:S(2)}, u32[]{:S(2)}) collective-permute-start(f32[72,256]{1,0:T(8,128)S(1)} %convert_reduce_fusion), channel_id=1, source_target_pairs={{0,1},{1,0},{2,3},{3,2},{4,5},{5,4},{6,7},{7,6},{8,9},{9,8},{10,11... | collective-permute-start | bytes 221192 | tf_op jit(solution)/shard_map/ppermute | solution.py:896
  312.3 4.0 %collective-permute-start.8 = (f32[384,128]{1,0:T(8,128)S(1)}, f32[384,128]{1,0:T(8,128)S(1)}, u32[]{:S(2)}, u32[]{:S(2)}) collective-permute-start(f32[384,128]{1,0:T(8,128)S(1)} %bitcast.13), channel_id=1, source_target_pairs={{0,1},{1,0},{2,3},{3,2},{4,5},{5,4},{6,7},{7,6},{8,9},{9,8},{10,11... | collective-permute-start | bytes 589832 | tf_op jit(solution)/shard_map/ppermute | solution.py:896
  318.7 4.4 %collective-permute-start.5 = (f32[64,128]{1,0:T(8,128)S(1)}, f32[64,128]{1,0:T(8,128)S(1)}, u32[]{:S(2)}, u32[]{:S(2)}) collective-permute-start(f32[64,128]{1,0:T(8,128)S(1)} %convert_reduce_fusion.1), channel_id=1, source_target_pairs={{0,1},{1,0},{2,3},{3,2},{4,5},{5,4},{6,7},{7,6},{8,9},{9,8},{10,11... | collective-permute-start | bytes 98312 | tf_op jit(solution)/shard_map/ppermute | solution.py:896

commit v4 on v3

--- a/solution.py
+++ b/solution.py
@@ -21,6 +21,8 @@
 MIB = 1024 * 1024
 
 AHEAD = 4
+VMEM = 44
+CHUNK = 32
 PER_CONV_ONE = 4
 PER_CONV_TWO = 3
 PER_ACT_TWO = 4
@@ -32,6 +34,7 @@
 PER_BACK_TWO = 2
 PER_WEIGHT_TWO = 4
 PER_BACK_ONE = 2
+PER_INPUT_GRAD = 2
 
 
 def dot_f(left, right):
@@ -60,6 +63,16 @@
     return lax.dot_general(
         left, right, (((1,), (1,)), ((), ())), preferred_element_type=F32, precision=HIGH
     )
+
+
+def exact_f(left, right):
+    total_product = None
+    for _ in range(3):
+        piece = left.astype(BF16)
+        product = dot_f(piece, right)
+        total_product = product if total_product is None else total_product + product
+        left = left - piece.astype(F32)
+    return total_product
 
 
 def pixel_mask(image_side, width):
@@ -77,6 +90,11 @@
 def fold(values):
     rows, n = values.shape
     return jnp.sum(values.reshape(rows // 8, 8, n), axis=0)
+
+
+def chunks(j=0):
+    for low in range(0, PIX, CHUNK):
+        yield pl.ds(j * PIX + low, CHUNK), slice(low, low + CHUNK)
 
 
 def row_sum(values):
@@ -114,7 +132,7 @@
 SMEM_SPEC = pl.BlockSpec(memory_space=pltpu.SMEM)
 
 
-def call(kernel, grid, ins, outs, scratch=(), vmem=56, flops=0, moved=0, name=None):
+def call(kernel, grid, ins, outs, scratch=(), vmem=VMEM, flops=0, moved=0, name=None):
     arrays = [
         array
         if spec is SMEM_SPEC or near
@@ -148,7 +166,7 @@
 BEGIN, END = "begin", "end"
 
 
-def stream_call(kernel, per, steps, ins, outs, scratch=(), vmem=56, flops=0, moved=0, name=None):
+def stream_call(kernel, per, steps, ins, outs, scratch=(), vmem=VMEM, flops=0, moved=0, name=None):
     block = per * PIX
     in_specs, out_specs, arrays, shapes, rooms = [], [], [], [], []
     in_streams, out_streams, room_of = [], [], {}
@@ -263,41 +281,35 @@
     )(*arrays)
 
 
-def pack_kernel(core_ref, one_ref, two_ref, three_ref, first_ref, second_ref):
+def pack_kernel(core_ref, *refs):
+    count = len(refs) // 2
+
     def put(half):
-        first_ref[...] = jnp.broadcast_to(
-            one_ref[:, half * HALF : (half + 1) * HALF][None], first_ref.shape
-        )
-        at = 0
-        for ref, blocks in ((two_ref, 2), (three_ref, 4)):
-            rows = ref.shape[0]
-            for b in range(blocks):
-                low = (half * blocks + b) * 128
+        for ref, out_ref in zip(refs[:count], refs[count:]):
+            rows, cols = ref.shape
+            for b in range(cols // 256):
+                low = half * (cols // 2) + b * 128
                 piece = ref[:, low : low + 128]
-                for f in range(second_ref.shape[0]):
-                    second_ref[f, pl.ds(at, rows)] = piece
-                at += rows
+                for f in range(out_ref.shape[0]):
+                    out_ref[f, pl.ds(b * rows, rows)] = piece
 
     for core in range(2):
         pl.when(core_ref[0] == core)(functools.partial(put, core))
 
 
-def unpack_kernel(core_ref, mine_ref, other_ref, two_ref, three_ref, wide_ref):
+def unpack_kernel(core_ref, mine_ref, other_ref, out_ref, *wide_refs):
     shards = mine_ref.shape[0]
-    two_rows = two_ref.shape[0] // shards
-    three_rows = three_ref.shape[0] // shards
+    rows, cols = out_ref.shape[0] // shards, out_ref.shape[1]
 
     def put(half, source_ref):
         for f in range(shards):
-            at = 0
-            for b in range(2):
-                piece = source_ref[f, pl.ds(at, two_rows)].astype(F32)
-                wide_ref[pl.ds(f * two_rows, two_rows), pl.ds(half * WIDTH + b * 128, 128)] = piece
-                at += two_rows
-            for b in range(4):
-                piece = source_ref[f, pl.ds(at, three_rows)]
-                three_ref[pl.ds(f * three_rows, three_rows), pl.ds(half * 512 + b * 128, 128)] = piece
-                at += three_rows
+            for b in range(cols // 256):
+                piece = source_ref[f, pl.ds(b * rows, rows)]
+                at = (pl.ds(f * rows, rows), pl.ds(half * (cols // 2) + b * 128, 128))
+                if wide_refs:
+                    wide_refs[0][at] = piece.astype(F32)
+                else:
+                    out_ref[at] = piece
 
     for core in range(2):
 
@@ -306,7 +318,8 @@
             put(core, mine_ref)
             put(1 - core, other_ref)
 
-    two_ref[...] = wide_ref[...].astype(BF16)
+    if wide_refs:
+        out_ref[...] = wide_refs[0][...].astype(BF16)
 
 
 def conv_one_kernel(
@@ -337,27 +350,33 @@
     h_ref[...] = h
     for j in range(per):
         side = SIDE - 2 * sides_ref[step * per + j]
-        mask = pixel_mask(side, WIDTH)
-        one = h[j * PIX : (j + 1) * PIX]
-        kept = one * mask
-        acc_ref[0:8] += fold(kept)
-        acc_ref[8:16] += fold(kept * one)
+        mask = pixel_mask(side, 128)
+        sums = jnp.zeros((8, WIDTH), F32)
+        squares = jnp.zeros((8, WIDTH), F32)
+        for rows, part in chunks():
+            one = h[j * PIX + part.start : j * PIX + part.stop]
+            kept = one * wide(mask[part], WIDTH)
+            sums = sums + fold(kept)
+            squares = squares + fold(kept * one)
+        acc_ref[0:8] += sums
+        acc_ref[8:16] += squares
         count_ref[0] += (side * side).astype(F32)
 
 
 def edge_masks(width):
-    column = lax.broadcasted_iota(jnp.int32, (PIX, 128), 0) & 15
+    column = lax.broadcasted_iota(jnp.int32, (CHUNK, 128), 0) & 15
     first = jnp.where(column == 0, 0.0, 1.0).astype(F32)
     last = jnp.where(column == 15, 0.0, 1.0).astype(F32)
     return wide(first, width), wide(last, width)
 
 
-def put_taps(taps_ref, j, act, first, last):
-    shifted = (pltpu.roll(act, 1, 0) * first, act, pltpu.roll(act, PIX - 1, 0) * last)
+def put_taps(taps_ref, j, part, act, first, last):
+    shifted = (pltpu.roll(act, 1, 0) * first, act, pltpu.roll(act, CHUNK - 1, 0) * last)
+    low = SIDE + j * (PIX + SIDE) + part.start
     for d in range(3):
         piece = shifted[d].astype(BF16)
         for q in range(2):
-            taps_ref[pl.ds(SIDE + j * (PIX + SIDE), PIX), pl.ds(q * 384 + d * 128, 128)] = piece[
+            taps_ref[pl.ds(low, CHUNK), pl.ds(q * 384 + d * 128, 128)] = piece[
                 :, q * HALF : (q + 1) * HALF
             ]
 
@@ -385,13 +404,13 @@
     first, last = edge_masks(WIDTH)
     for j in range(per):
         side = SIDE - 2 * sides_ref[step * per + j]
-        mask = pixel_mask(side, WIDTH)
-        rows = pl.ds(j * PIX, PIX)
-        hat = (h_ref[rows] - vec_ref[0:1]) * vec_ref[1:2]
-        hat_ref[pl.ds(j * PIX, PIX)] = hat.astype(BF16)
-        half_pre = hat * gain + shift
-        act = half_pre * (1.0 + jnp.tanh(half_pre)) * mask
-        put_taps(taps_ref, j, act, first, last)
+        mask = pixel_mask(side, 128)
+        for rows, part in chunks(j):
+            hat = (h_ref[rows] - vec_ref[0:1]) * vec_ref[1:2]
+            hat_ref[rows] = hat.astype(BF16)
+            half_pre = hat * gain + shift
+            act = half_pre * ((1.0 + jnp.tanh(half_pre)) * wide(mask[part], WIDTH))
+            put_taps(taps_ref, j, part, act, first, last)
     height = per * (PIX + SIDE)
     for q in range(2):
         cols = pl.ds(q * WIDTH, WIDTH)
@@ -400,12 +419,19 @@
         )
         both = dot_f(patches, w_ref[:, cols])
         for j in range(per):
-            h2 = both[j * (PIX + SIDE) : j * (PIX + SIDE) + PIX]
-            h2_ref[pl.ds(j * PIX, PIX), cols] = h2
             side = SIDE - 2 * sides_ref[step * per + j]
-            kept = h2 * pixel_mask(side, WIDTH)
-            acc_ref[0:8, cols] += fold(kept)
-            acc_ref[8:16, cols] += fold(kept * h2)
+            mask = pixel_mask(side, 128)
+            sums = jnp.zeros((8, WIDTH), F32)
+            squares = jnp.zeros((8, WIDTH), F32)
+            for rows, part in chunks(j):
+                low = j * (PIX + SIDE) + part.start
+                h2 = both[low : low + CHUNK]
+                h2_ref[rows, cols] = h2
+                kept = h2 * wide(mask[part], WIDTH)
+                sums = sums + fold(kept)
+                squares = squares + fold(kept * h2)
+            acc_ref[0:8, cols] += sums
+            acc_ref[8:16, cols] += squares
 
 
 def act_two_kernel(
@@ -429,16 +455,19 @@
     shift = shift_ref[:, WIDTH : 3 * WIDTH] * 0.5
     for j in range(per):
         side = SIDE - 2 * sides_ref[step * per + j]
-        mask = pixel_mask(side, 2 * WIDTH)
-        rows = pl.ds(j * PIX, PIX)
-        hat = (h2_ref[rows] - vec_ref[0:1]) * vec_ref[1:2]
-        hat_ref[rows] = hat.astype(BF16)
-        half_pre = hat * gain + shift
-        value = half_pre * ((1.0 + jnp.tanh(half_pre)) * mask)
-        sums = row_sum(fold(value))
+        mask = pixel_mask(side, 128)
+        sums = jnp.zeros((8, WIDTH), F32)
+        for q in range(2):
+            cols = slice(q * WIDTH, (q + 1) * WIDTH)
+            for rows, part in chunks(j):
+                hat = (h2_ref[rows, cols] - vec_ref[0:1, cols]) * vec_ref[1:2, cols]
+                hat_ref[rows, cols] = hat.astype(BF16)
+                half_pre = hat * gain[:, cols] + shift[:, cols]
+                value = half_pre * ((1.0 + jnp.tanh(half_pre)) * wide(mask[part], WIDTH))
+                sums = sums + fold(value)
         image = pl.ds(step * per + j, 1)
         pixels = (side * side).astype(F32)
-        pooled_ref[image] = (sums[:, :WIDTH] + sums[:, WIDTH:]) / pixels
+        pooled_ref[image] = row_sum(sums) / pixels
 
 
 def slope_two_kernel(
@@ -454,18 +483,24 @@
     shift = shift_ref[:, WIDTH : 3 * WIDTH] * 0.5
     for j in range(per):
         side = SIDE - 2 * sides_ref[step * per + j]
-        mask = pixel_mask(side, 2 * WIDTH)
-        rows = pl.ds(j * PIX, PIX)
-        hat = hat_ref[rows].astype(F32)
-        half_pre = hat * gain + shift
-        a = (1.0 + jnp.tanh(half_pre)) * mask
-        value = half_pre * a
-        slope = (0.5 * a) * (1.0 + 2.0 * half_pre - value)
-        a2_ref[rows] = value.astype(BF16)
-        slope_ref[rows] = slope.astype(BF16)
+        mask = pixel_mask(side, 128)
         image = pl.ds(step * per + j, 1)
-        t2_ref[image] = row_sum(fold(slope))
-        t4_ref[image] = row_sum(fold(slope * hat))
+        for q in range(2):
+            cols = slice(q * WIDTH, (q + 1) * WIDTH)
+            sums = jnp.zeros((8, WIDTH), F32)
+            products = jnp.zeros((8, WIDTH), F32)
+            for rows, part in chunks(j):
+                hat = hat_ref[rows, cols].astype(F32)
+                half_pre = hat * gain[:, cols] + shift[:, cols]
+                a = (1.0 + jnp.tanh(half_pre)) * wide(mask[part], WIDTH)
+                value = half_pre * a
+                slope = a * (0.5 + half_pre - 0.5 * value)
+                a2_ref[rows, cols] = value.astype(BF16)
+                slope_ref[rows, cols] = slope.astype(BF16)
+                sums = sums + fold(slope)
+                products = products + fold(slope * hat)
+            t2_ref[image, cols] = row_sum(sums)
+            t4_ref[image, cols] = row_sum(products)
 
 
 def hidden_terms(zin, sums, n_images, gain_ref, shift_ref):
@@ -501,21 +536,24 @@
         return
 
     if step is END:
-        w3 = w3_ref[...].astype(F32)
         csum = row_sum(acc_ref[...])
         csum_ref[...] = csum
-        gw = high_f(gram_ref[...], w3)
+        both = jnp.concatenate([gram_ref[...], jnp.broadcast_to(csum, (8, WIDTH))], axis=0)
+        both = exact_f(both, w3_ref[...])
+        gw = both[:WIDTH]
         gw_ref[...] = gw
-        send_rows(send_ref, [high_f(csum, w3), row_sum(w3 * gw)])
+        send_rows(send_ref, [both[WIDTH : WIDTH + 1], row_sum(w3_ref[...].astype(F32) * gw)])
         return
 
     for j in range(per):
-        rows = pl.ds(j * PIX, PIX)
         att = att_ref[pl.ds(step * per + j, 1)]
-        a2 = a2_ref[rows].astype(F32)
-        comb = (att[:, :WIDTH] * a2[:, :WIDTH] + att[:, WIDTH:] * a2[:, WIDTH:]).astype(BF16)
-        comb_ref[rows] = comb
-        acc_ref[...] += fold(comb.astype(F32))
+        sums = jnp.zeros((8, WIDTH), F32)
+        for rows, _ in chunks(j):
+            left = att[:, :WIDTH] * a2_ref[rows, :WIDTH].astype(F32)
+            comb = (left + att[:, WIDTH:] * a2_ref[rows, WIDTH:].astype(F32)).astype(BF16)
+            comb_ref[rows] = comb
+            sums = sums + fold(comb.astype(F32))
+        acc_ref[...] += sums
     comb = comb_ref[...]
     gram_ref[...] += dot_rows(comb, comb)
 
@@ -630,15 +668,20 @@
 
     corr = dot_f(comb_ref[...], s_ref[...])
     for j in range(per):
-        rows = pl.ds(j * PIX, PIX)
-        dcomb = p_ref[rows].astype(F32) - corr[j * PIX : (j + 1) * PIX] - c_ref[0:1]
         image = pl.ds(step * per + j, 1)
-        for q in range(2):
-            cols = pl.ds(q * WIDTH, WIDTH)
-            datt_ref[image, cols] = row_sum(fold(dcomb * a2_ref[rows, cols].astype(F32)))
-            u = dcomb * slope_ref[rows, cols].astype(F32)
-            t1_ref[image, cols] = row_sum(fold(u))
-            t3_ref[image, cols] = row_sum(fold(u * hat_ref[rows, cols].astype(F32)))
+        sums = [jnp.zeros((8, WIDTH), F32)] * 6
+        for rows, part in chunks(j):
+            low = j * PIX + part.start
+            dcomb = p_ref[rows].astype(F32) - corr[low : low + CHUNK] - c_ref[0:1]
+            for q in range(2):
+                cols = slice(q * WIDTH, (q + 1) * WIDTH)
+                u = dcomb * slope_ref[rows, cols].astype(F32)
+                sums[q] = sums[q] + fold(dcomb * a2_ref[rows, cols].astype(F32))
+                sums[2 + q] = sums[2 + q] + fold(u)
+                sums[4 + q] = sums[4 + q] + fold(u * hat_ref[rows, cols].astype(F32))
+        for k, ref in enumerate((datt_ref, t1_ref, t3_ref)):
+            for q in range(2):
+                ref[image, q * WIDTH : (q + 1) * WIDTH] = row_sum(sums[2 * k + q])
 
 
 def back_att_kernel(
@@ -697,22 +740,23 @@
     first, last = edge_masks(HALF)
     corr = dot_f(comb_ref[...], s_ref[...])
     for j in range(per):
-        rows = pl.ds(j * PIX, PIX)
         side = SIDE - 2 * sides_ref[step * per + j]
-        mask = pixel_mask(side, WIDTH)
+        mask = pixel_mask(side, 128)
         image = pl.ds(step * per + j, 1)
-        dcomb = p_ref[rows].astype(F32) - corr[j * PIX : (j + 1) * PIX] - c_ref[0:1]
         dpool = dpool_ref[image]
-        for q in range(2):
-            cols = pl.ds(q * WIDTH, WIDTH)
-            scale = vec_ref[0:1, cols]
-            up = dcomb * (att_ref[image, cols] * scale) + dpool * scale
-            dh2 = slope_ref[rows, cols].astype(F32) * up - mask * (
-                vec_ref[1:2, cols] + hat2_ref[rows, cols].astype(F32) * vec_ref[2:3, cols]
-            )
-            dh2 = dh2.astype(BF16)
-            dh2_ref[rows, cols] = dh2
-            pad_ref[pl.ds(SIDE + j * (PIX + SIDE), PIX), cols] = dh2
+        for rows, part in chunks(j):
+            low = j * PIX + part.start
+            dcomb = p_ref[rows].astype(F32) - corr[low : low + CHUNK] - c_ref[0:1]
+            for q in range(2):
+                cols = slice(q * WIDTH, (q + 1) * WIDTH)
+                scale = vec_ref[0:1, cols]
+                up = dcomb * (att_ref[image, cols] * scale) + dpool * scale
+                dh2 = slope_ref[rows, cols].astype(F32) * up - wide(mask[part], WIDTH) * (
+                    vec_ref[1:2, cols] + hat2_ref[rows, cols].astype(F32) * vec_ref[2:3, cols]
+                )
+                dh2 = dh2.astype(BF16)
+                dh2_ref[rows, cols] = dh2
+                pad_ref[pl.ds(SIDE + j * (PIX + SIDE) + part.start, CHUNK), cols] = dh2
     height = per * (PIX + SIDE)
     for q in range(2):
         lines = jnp.concatenate(
@@ -734,23 +778,30 @@
         )
         both = dot_last(lines, weight)
         for j in range(per):
-            rows = pl.ds(j * PIX, PIX)
             side = SIDE - 2 * sides_ref[step * per + j]
             mask = pixel_mask(side, 128)
-            y = both[j * (PIX + SIDE) : j * (PIX + SIDE) + PIX]
-            da1 = (
-                y[:, HALF : 2 * HALF]
-                + pltpu.roll(y[:, :HALF], PIX - 1, 0) * last
-                + pltpu.roll(y[:, 2 * HALF :], 1, 0) * first
-            )
-            cols = pl.ds(q * HALF, HALF)
-            hat = hat1_ref[rows, cols].astype(F32)
-            half_pre = 0.5 * (hat * gain_ref[:, cols] + shift_ref[:, cols])
-            _, slope = silu_parts(half_pre)
-            u1 = da1 * slope * mask
-            u1_ref[rows, cols] = u1.astype(BF16)
-            acc_ref[0:8, cols] += fold(u1)
-            acc_ref[8:16, cols] += fold(u1 * hat)
+            cols = slice(q * HALF, (q + 1) * HALF)
+            gain = gain_ref[:, cols] * 0.5
+            shift = shift_ref[:, cols] * 0.5
+            sums = jnp.zeros((8, HALF), F32)
+            products = jnp.zeros((8, HALF), F32)
+            for rows, part in chunks(j):
+                low = j * (PIX + SIDE) + part.start
+                y = both[low : low + CHUNK]
+                da1 = (
+                    y[:, HALF : 2 * HALF]
+                    + pltpu.roll(y[:, :HALF], CHUNK - 1, 0) * last
+                    + pltpu.roll(y[:, 2 * HALF :], 1, 0) * first
+                )
+                hat = hat1_ref[rows, cols].astype(F32)
+                half_pre = hat * gain + shift
+                a = (1.0 + jnp.tanh(half_pre)) * mask[part]
+                u1 = da1 * (a * (0.5 + half_pre - 0.5 * half_pre * a))
+                u1_ref[rows, cols] = u1.astype(BF16)
+                sums = sums + fold(u1)
+                products = products + fold(u1 * hat)
+            acc_ref[0:8, cols] += sums
+            acc_ref[8:16, cols] += products
 
 
 def weight_two_kernel(
@@ -777,11 +828,11 @@
     height = PIX + SIDE
     for j in range(per):
         side = SIDE - 2 * sides_ref[step * per + j]
-        mask = pixel_mask(side, WIDTH)
-        rows = pl.ds(j * PIX, PIX)
-        half_pre = hat_ref[rows].astype(F32) * gain + shift
-        act = half_pre * (1.0 + jnp.tanh(half_pre)) * mask
-        put_taps(taps_ref, j, act, first, last)
+        mask = pixel_mask(side, 128)
+        for rows, part in chunks(j):
+            half_pre = hat_ref[rows].astype(F32) * gain + shift
+            act = half_pre * ((1.0 + jnp.tanh(half_pre)) * wide(mask[part], WIDTH))
+            put_taps(taps_ref, j, part, act, first, last)
     for q in range(2):
         patches = jnp.concatenate(
             [
@@ -800,9 +851,8 @@
 
 
 def back_one_kernel(
-    step, per, core_ref, sides_ref, one_ref, three_ref, got_ref, u1_ref, hat_ref, u3_ref, x_ref, w_ref, gain_ref,
-    norm2_ref, norm_att_ref, norm3_ref,
-    ig_ref, keep_ref, give_ref, gain_out_ref, shift_out_ref, vec_ref, wide_ref, dh_ref, acc_ref,
+    step, per, core_ref, sides_ref, one_ref, got_ref, u1_ref, hat_ref, x_ref, gain_ref, norm2_ref,
+    norm_att_ref, norm3_ref, dh_ref, keep_ref, give_ref, gain_out_ref, shift_out_ref, vec_ref, acc_ref,
 ):
     if step is BEGIN:
         count = one_ref[2:3]
@@ -816,11 +866,11 @@
         vec_ref[0:1] = scale
         vec_ref[1:2] = scale * sums[0:1] / count
         vec_ref[2:3] = scale * sums[1:2] / count
-        wide_ref[...] = 1.0 / three_ref[2:3]
         acc_ref[...] = jnp.zeros_like(acc_ref)
         return
 
     if step is END:
+
         def put(core):
             keep_ref[...] = acc_ref[core * HALF : (core + 1) * HALF].T
             give_ref[...] = acc_ref[(1 - core) * HALF : (2 - core) * HALF].T
@@ -830,17 +880,28 @@
         return
 
     for j in range(per):
-        rows = pl.ds(j * PIX, PIX)
         side = SIDE - 2 * sides_ref[step * per + j]
-        mask = pixel_mask(side, WIDTH)
-        dh_ref[rows] = (
-            u1_ref[rows].astype(F32) * vec_ref[0:1]
-            - mask * (vec_ref[1:2] + hat_ref[rows].astype(F32) * vec_ref[2:3])
-        ).astype(BF16)
-    dh = dh_ref[...]
-    acc_ref[...] += dot_rows(dh, x_ref[...])
-    dx = dot_last(dh, w_ref[...])
-    ig_ref[...] = (u3_ref[...].astype(F32) * wide_ref[...] + dx).astype(BF16)
+        mask = pixel_mask(side, 128)
+        for rows, part in chunks(j):
+            dh_ref[rows] = (
+                u1_ref[rows].astype(F32) * vec_ref[0:1]
+                - wide(mask[part], WIDTH) * (vec_ref[1:2] + hat_ref[rows].astype(F32) * vec_ref[2:3])
+            ).astype(BF16)
+    acc_ref[...] += dot_rows(dh_ref[...], x_ref[...])
+
+
+def input_grad_kernel(step, dh_ref, u3_ref, three_ref, w_ref, ig_ref, wide_ref):
+    if step is BEGIN:
+        wide_ref[...] = 1.0 / three_ref[2:3]
+        return
+
+    if step is END:
+        return
+
+    dx = dot_last(dh_ref[...], w_ref[...])
+    for low in range(0, dx.shape[0], 16):
+        rows = pl.ds(low, 16)
+        ig_ref[rows] = (u3_ref[rows].astype(F32) * wide_ref[...] + dx[low : low + 16]).astype(BF16)
 
 
 def round_up(value, multiple):
@@ -871,21 +932,98 @@
             put(1 - core, give_ref)
 
 
-def pack_two_kernel(keep_ref, other_ref, fc_ref, out_ref):
-    shards, slot, _ = out_ref.shape
-    rows = keep_ref.shape[0] // shards
-    padded = round_up(rows, 16)
-    fc = fc_ref[...]
-    fc_half = (slot - padded) * 2 - fc.shape[0]
-    if fc_half:
-        fc = jnp.concatenate([fc, jnp.zeros((fc_half, 128), F32)], axis=0)
-    fc = jnp.concatenate([fc[: slot - padded], fc[slot - padded :]], axis=1).astype(BF16)
+def two_wide(part, rows):
+    missing = 2 * rows - part.shape[0]
+    if missing:
+        part = jnp.concatenate([part, jnp.zeros((missing, 128), F32)], axis=0)
+    return jnp.concatenate([part[:rows], part[rows:]], axis=1)
+
+
+def slot_rows(two_rows, fc_rows, one_rows):
+    return round_up(two_rows, 16), round_up(fc_rows, 32) // 2, round_up(one_rows, 32) // 2
+
+
+def add_slots(ref, at, rows):
+    rows = pl.ds(at, rows)
+    both = ref[0, rows].astype(F32)
+    for f in range(1, ref.shape[0]):
+        both = both + ref[f, rows].astype(F32)
+    return both
+
+
+def pack_last_kernel(
+    fc_rows, keep2_ref, other2_ref, keep1_ref, other1_ref, three_ref, out_ref
+):
+    shards = out_ref.shape[0]
+    two_rows = keep2_ref.shape[0] // shards
+    one_rows = keep1_ref.shape[0] // shards
+    two_slot, fc_slot, one_slot = slot_rows(two_rows, fc_rows, one_rows)
+    fc = add_slots(three_ref, three_ref.shape[1] - fc_rows, fc_rows)
+    fc = two_wide(fc, fc_slot).astype(BF16)
     for f in range(shards):
-        part = keep_ref[pl.ds(f * rows, rows)] + other_ref[pl.ds(f * rows, rows)]
-        if padded > rows:
-            part = jnp.concatenate([part, jnp.zeros((padded - rows, WIDTH), F32)], axis=0)
-        out_ref[f, pl.ds(0, padded)] = part.astype(BF16)
-        out_ref[f, pl.ds(padded, slot - padded)] = fc
+        rows = pl.ds(f * two_rows, two_rows)
+        part = keep2_ref[rows] + other2_ref[rows]
+        if two_slot > two_rows:
+            part = jnp.concatenate([part, jnp.zeros((two_slot - two_rows, WIDTH), F32)], axis=0)
+        out_ref[f, pl.ds(0, two_slot)] = part.astype(BF16)
+        out_ref[f, pl.ds(two_slot, fc_slot)] = fc
+        rows = pl.ds(f * one_rows, one_rows)
+        part = two_wide(keep1_ref[rows] + other1_ref[rows], one_slot)
+        out_ref[f, pl.ds(two_slot + fc_slot, one_slot)] = part.astype(BF16)
+
+
+def sum_last_kernel(two_rows, fc_rows, one_rows, parts_ref, three_ref, out_ref):
+    shards = parts_ref.shape[0]
+    two_slot, fc_slot, one_slot = slot_rows(two_rows, fc_rows, one_rows)
+    out_ref[pl.ds(0, two_slot)] = add_slots(parts_ref, 0, two_slot)
+    out_ref[pl.ds(two_slot, one_slot)] = add_slots(parts_ref, two_slot + fc_slot, one_slot)
+    at = two_slot + one_slot
+    three_half = (three_ref.shape[1] - fc_rows) // 2
+    three = add_slots(three_ref, 0, 2 * three_half)
+    out_ref[pl.ds(at, three_half)] = two_wide(three, three_half)
+    at += three_half
+    for f in range(shards):
+        out_ref[pl.ds(at + f * fc_slot, fc_slot)] = parts_ref[f, pl.ds(two_slot, fc_slot)].astype(F32)
+
+
+def finish_kernel(
+    two_rows, fc_rows, one_rows, three_rows, core_ref, mine_ref, other_ref,
+    one_ref, two_ref, three_ref, fc1_ref, fc2_ref, pack_ref,
+):
+    two_slot, fc_slot, one_slot = slot_rows(two_rows, fc_rows, one_rows)
+    three_half = 2 * three_rows
+    at_three = two_slot + one_slot
+    at_fc = at_three + three_half
+    shards = (mine_ref.shape[0] - at_fc) // fc_slot
+
+    def tall(ref, at, half_rows, rows):
+        both = jnp.concatenate(
+            [ref[pl.ds(at, half_rows), :128], ref[pl.ds(at, half_rows), 128:]], axis=0
+        )
+        return both[:rows]
+
+    def put(half, ref):
+        two_ref[:, half * WIDTH : (half + 1) * WIDTH] = ref[pl.ds(0, two_rows)]
+        one_ref[:, half * HALF : (half + 1) * HALF] = tall(ref, two_slot, one_slot, one_rows)
+        three = tall(ref, at_three, three_half, 4 * three_rows)
+        for b in range(4):
+            low = half * 512 + b * 128
+            three_ref[:, low : low + 128] = three[b * three_rows : (b + 1) * three_rows]
+        for f in range(shards):
+            pack_ref[pl.ds((half * shards + f) * fc_rows, fc_rows)] = tall(
+                ref, at_fc + f * fc_slot, fc_slot, fc_rows
+            )
+
+    for core in range(2):
+
+        @pl.when(core_ref[0] == core)
+        def _():
+            put(core, mine_ref)
+            put(1 - core, other_ref)
+
+    fc1_ref[...] = pack_ref[0:WIDTH]
+    for b in range(4):
+        fc2_ref[:, b * 128 : (b + 1) * 128] = pack_ref[pl.ds(WIDTH + b * INTER, INTER)]
 
 
 def everyone(payload):
@@ -896,51 +1034,33 @@
     return lax.ppermute(array, "dp", [(0, 1), (1, 0)])
 
 
-def both_halves(mine, axis=1):
-    core = lax.axis_index("dp")
-    other = other_core(mine)
-    return jnp.where(
-        core == 0,
-        jnp.concatenate([mine, other], axis=axis),
-        jnp.concatenate([other, mine], axis=axis),
-    )
-
-
-def gather_weights(core, weights):
+def spread_weights(core, weights):
     shards = lax.axis_size("fsdp")
-    one, two, three = weights
-    first = (shards, one.shape[0], HALF)
-    second = (shards, 2 * two.shape[0] + 4 * three.shape[0], 128)
-    spread_one, spread_two = call(
+    shapes = [(shards, w.shape[0] * w.shape[1] // 256, 128) for w in weights]
+    return call(
         pack_kernel,
         1,
         [(core, SMEM_SPEC)] + [(weight, whole(weight.shape)) for weight in weights],
-        [(first, BF16, whole(first), True), (second, BF16, whole(second), True)],
+        [(shape, BF16, whole(shape), True) for shape in shapes],
         flops=1000000,
         moved=4000000,
         name="pack",
     )
-    mine = lax.all_to_all(spread_one, "fsdp", 0, 0, tiled=True)
+
+
+def join_weight(core, mine, shape):
     other = other_core(mine)
-    spread_two, mine, other = lax.optimization_barrier((spread_two, mine, other))
-    mine_two = lax.all_to_all(spread_two, "fsdp", 0, 0, tiled=True)
-
-    def others(mine_two, after):
-        mine_two, _ = lax.optimization_barrier((mine_two, after))
-        other_two = other_core(mine_two)
-        shapes = [(shards * weight.shape[0], weight.shape[1]) for weight in (two, three)]
-        return call(
-            unpack_kernel,
-            1,
-            [(core, SMEM_SPEC), (mine_two, whole(second), True), (other_two, whole(second), True)],
-            [(shape, BF16, whole(shape)) for shape in shapes],
-            [pltpu.VMEM(shapes[0], F32)],
-            flops=1000000,
-            moved=4000000,
-            name="unpack",
-        )
-
-    return mine, other, functools.partial(others, mine_two)
+    rows = shape[0] // mine.shape[0]
+    return call(
+        unpack_kernel,
+        1,
+        [(core, SMEM_SPEC), (mine, whole(mine.shape), True), (other, whole(mine.shape), True)],
+        [(shape, BF16, whole(shape))],
+        [] if rows % 16 == 0 else [pltpu.VMEM(shape, F32)],
+        flops=1000000,
+        moved=4000000,
+        name="unpack",
+    )[0]
 
 
 def slots(parts):
@@ -999,7 +1119,13 @@
     def blocks_out(width, dtype=BF16, over=None):
         return ((rows, width), dtype, Stream(over))
 
-    mine, other, others = gather_weights(core, (weight_one, weight_two, weight_three))
+    spread_one, spread_two, spread_three = spread_weights(
+        core, (weight_one, weight_two, weight_three)
+    )
+    mine = slots(spread_one)
+    other = other_core(mine)
+    spread_two, mine, other = lax.optimization_barrier((spread_two, mine, other))
+    mine_two = slots(spread_two)
 
     per, steps = split(PER_CONV_ONE)
     h1, full_one, send = stream_call(
@@ -1013,8 +1139,11 @@
         moved=rows * C_IN * 2 + rows * WIDTH * 4,
         name="conv_one",
     )
+    send, mine_two = lax.optimization_barrier((send, mine_two))
     got_one = everyone(send)
-    full_two, full_three = others(send)
+    full_two = join_weight(core, mine_two, (9 * HALF, 2 * WIDTH))
+    got_one, spread_three, full_two = lax.optimization_barrier((got_one, spread_three, full_two))
+    mine_three = slots(spread_three)
 
     per, steps = split(PER_CONV_TWO)
     hat1, h2, stat1, send = stream_call(
@@ -1031,7 +1160,9 @@
         moved=rows * WIDTH * 14,
         name="conv_two",
     )
+    send, mine_three = lax.optimization_barrier((send, mine_three))
     got_two = everyone(send)
+    full_three = join_weight(core, mine_three, (WIDTH, C_IN))
 
     per, steps = split(PER_ACT_TWO)
     hat2, pooled, zin, stat2, send = stream_call(
@@ -1231,8 +1362,7 @@
         moved=3000000,
         name="pack_three",
     )
-    got_back_two, three = lax.optimization_barrier((got_back_two, keep + other_core(give)))
-    three = slots(three)
+    three = slots(keep + other_core(give))
 
     per, steps = split(PER_BACK_TWO)
     dh2, u1, norm2, send = stream_call(
@@ -1292,25 +1422,9 @@
         name="weight_two",
     )
     got_back_one, keep, give = lax.optimization_barrier((got_back_one, keep, give))
-    three = jnp.sum(three, axis=0)
-    w2_rows = 9 * HALF // shards
-    w2_padded = round_up(w2_rows, 16)
-    slot = (shards, w2_padded + round_up(fc_rows, 32) // 2, WIDTH)
-    (parts,) = call(
-        pack_two_kernel,
-        1,
-        [full(keep), near(other_core(give)), near(three[4 * w3_rows :])],
-        [(slot, BF16, whole(slot))],
-        flops=1000000,
-        moved=3000000,
-        name="pack_two",
-    )
-    got_back_one, parts = lax.optimization_barrier((got_back_one, parts))
-    two = slots(parts)
-
     per, steps = split(PER_BACK_ONE)
-    half = (C_IN, HALF)
-    input_grad, keep, give, gain_grad, shift_grad = stream_call(
+    half_one = (C_IN, HALF)
+    dh1, keep_one, give_one, gain_grad, shift_grad = stream_call(
         lambda step, *refs, per=per: back_one_kernel(step, per, *refs),
         per,
         steps,
@@ -1318,43 +1432,88 @@
             core_in,
             sides_in,
             full(stat1),
-            full(stat3),
             near(got_back_one),
             blocks(u1),
             blocks(hat1),
-            blocks(u3),
             blocks(x),
-            full(full_one),
             gain_in,
             full(norm2),
             full(norm_att),
             full(norm3),
         ],
-        [blocks_out(C_IN), small(*half), small(*half), small(1, n_ch), small(1, n_ch)],
-        [
-            pltpu.VMEM((8, WIDTH), F32),
-            pltpu.VMEM((1, C_IN), F32),
-            pltpu.VMEM((per * PIX, WIDTH), BF16),
-            pltpu.VMEM((WIDTH, C_IN), F32),
-        ],
-        flops=4 * rows * WIDTH * C_IN,
-        moved=rows * C_IN * 6,
+        [
+            blocks_out(WIDTH),
+            small(*half_one),
+            small(*half_one),
+            small(1, n_ch),
+            small(1, n_ch),
+        ],
+        [pltpu.VMEM((8, WIDTH), F32), pltpu.VMEM((WIDTH, C_IN), F32)],
+        flops=2 * rows * WIDTH * C_IN,
+        moved=rows * C_IN * 4,
         name="back_one",
     )
 
-    one = (keep + other_core(give)).astype(BF16).reshape(shards, -1, HALF)
-    one, two = lax.optimization_barrier((one, two))
-    weight_one_grad = both_halves(jnp.sum(slots(one).astype(F32), axis=0))
-    weight_two_grad = both_halves(jnp.sum(two[:, :w2_rows].astype(F32), axis=0))
-    weight_three_grad = both_halves(
-        jnp.concatenate([three[b * w3_rows : (b + 1) * w3_rows] for b in range(4)], axis=1)
-    )
-    fc = two[:, w2_padded:].astype(F32)
-    fc = jnp.concatenate([fc[:, :, :128], fc[:, :, 128:]], axis=1)[:, :fc_rows].reshape(-1, 128)
-    summed = both_halves(fc, 0)
-    fc_first_grad = summed[:WIDTH]
-    fc_second_grad = jnp.concatenate(
-        [summed[WIDTH + b * INTER : WIDTH + (b + 1) * INTER] for b in range(4)], axis=1
+    two_rows, one_rows = 9 * HALF // shards, C_IN // shards
+    two_slot, fc_slot, one_slot = slot_rows(two_rows, fc_rows, one_rows)
+    slot = (shards, two_slot + fc_slot + one_slot, WIDTH)
+    (parts,) = call(
+        functools.partial(pack_last_kernel, fc_rows),
+        1,
+        [
+            full(keep),
+            near(other_core(give)),
+            full(keep_one),
+            near(other_core(give_one)),
+            near(three),
+        ],
+        [(slot, BF16, whole(slot))],
+        flops=1000000,
+        moved=5000000,
+        name="pack_last",
+    )
+    dh1, parts = lax.optimization_barrier((dh1, parts))
+    parts = slots(parts)
+
+    per, steps = split(PER_INPUT_GRAD)
+    (input_grad,) = stream_call(
+        input_grad_kernel,
+        per,
+        steps,
+        [blocks(dh1), blocks(u3), full(stat3), full(full_one)],
+        [blocks_out(C_IN, over=1)],
+        [pltpu.VMEM((1, C_IN), F32)],
+        flops=2 * rows * WIDTH * C_IN,
+        moved=rows * C_IN * 5,
+        name="input_grad",
+    )
+
+    parts, input_grad = lax.optimization_barrier((parts, input_grad))
+    sums = (two_slot + one_slot + 2 * w3_rows + shards * fc_slot, WIDTH)
+    (mine,) = call(
+        functools.partial(sum_last_kernel, two_rows, fc_rows, one_rows),
+        1,
+        [near(parts), near(three)],
+        [(sums, F32, whole(sums), True)],
+        flops=1000000,
+        moved=2000000,
+        name="sum_last",
+    )
+    (weight_one_grad, weight_two_grad, weight_three_grad, fc_first_grad, fc_second_grad) = call(
+        functools.partial(finish_kernel, two_rows, fc_rows, one_rows, w3_rows),
+        1,
+        [core_in, near(mine), near(other_core(mine))],
+        [
+            small(one_rows, WIDTH),
+            small(two_rows, 2 * WIDTH),
+            small(w3_rows, C_IN),
+            small(WIDTH, INTER),
+            small(INTER, 2 * WIDTH),
+        ],
+        [pltpu.VMEM((2 * shards * fc_rows, 128), F32)],
+        flops=1000000,
+        moved=2000000,
+        name="finish",
     )
     return (
         outputs.reshape(inputs.shape),

time: 327 us -> 319 us (0.976)
  blocking collectives: 52.1 us -> 39.8 us
  waiting for transfers between devices: 22.8 us -> 33.8 us
  other arithmetic: 9.46 us -> 3.32 us
  local copies, waits for them, and re-layouts: 6.46 us -> 1.87 us
  Pallas kernels: 175 us -> 179 us
    all_to_all x3 -> x4, waiting for transfers between devices: 2.25 us -> 17.2 us  [slots(): return lax.all_to_all(parts, 'fsdp', 0, 0, tiled=True)]
    all_to_all x3 -> x2, blocking collectives: 38.4 us -> 26.3 us  [everyone(): return lax.all_to_all(payload, AXES, 0, 0, tiled=True)]
    all_to_all x1 -> x0, waiting for transfers between devices: 10.5 us -> none  [gather_weights(): mine_two = lax.all_to_all(spread_two, 'fsdp', 0, 0, tiled=True)]
    all_to_all x5 -> x6, waiting for transfers between devices: 5.21 us -> 13.4 us  [everyone(): return lax.all_to_all(payload, AXES, 0, 0, tiled=True)]
    all_to_all x5 -> x6, starting transfers between devices: 21.9 us -> 27.7 us  [everyone(): return lax.all_to_all(payload, AXES, 0, 0, tiled=True)]
    all_to_all x1 -> x0, starting transfers between devices: 4.09 us -> none  [gather_weights(): mine_two = lax.all_to_all(spread_two, 'fsdp', 0, 0, tiled=True)]
    pallas_call x11 -> x12, Pallas kernels: 163 us -> 167 us  [stream_call(): pl.pallas_call(whole_kernel, in_specs=in_specs, out_specs=out_specs, out_...]
    unnamed x31 -> x12, local copies, waits for them, and re-layouts: 3.95 us -> 0.67 us
  transfers between devices with their start and end apart: 18 -> 17, of which waited for: 8 -> 8; matrix products, arithmetic and copies ran while one was open for 3% -> 1% of each run, Pallas kernels for 29% -> 39%
where the time goes in v4:
time: 319 us; the launch traced here: 318 us
  Pallas kernels  179 us (56%)
  starting transfers between devices  59.1 us (19%)
  blocking collectives  39.8 us (12%)
  waiting for transfers between devices  33.8 us (11%)
  other arithmetic  3.32 us (1%)
    pallas_call x12, Pallas kernels, stream_call(): pl.pallas_call(whole_kernel, in_specs=in_specs, out_specs=out_specs, out_...  167 us
    all_to_all x6, starting transfers between devices, everyone(): return lax.all_to_all(payload, AXES, 0, 0, tiled=True)  27.7 us
    all_to_all x2, blocking collectives, everyone(): return lax.all_to_all(payload, AXES, 0, 0, tiled=True)  26.3 us
    all_to_all x4, starting transfers between devices, slots(): return lax.all_to_all(parts, 'fsdp', 0, 0, tiled=True)  21.6 us
    all_to_all x4, waiting for transfers between devices, slots(): return lax.all_to_all(parts, 'fsdp', 0, 0, tiled=True)  17.2 us
    all_to_all x1, blocking collectives, slots(): return lax.all_to_all(parts, 'fsdp', 0, 0, tiled=True)  13.5 us
    all_to_all x6, waiting for transfers between devices, everyone(): return lax.all_to_all(payload, AXES, 0, 0, tiled=True)  13.4 us
    pallas_call x8, Pallas kernels, call(): pl.pallas_call(kernel, grid=(grid,), in_specs=[spec for _, spec, *_ in in...  12.6 us
  transfers between devices with their start and end apart: 17, of which 8 were waited for; matrix products, arithmetic and copies ran while one was open for 1% of the time, Pallas kernels for 39%

profile of v4, /device:TPU:9, one launch (start us, length us, event | category | flops | bytes accessed | tf_op | source)
XLA Modules:
  0.0 318.0 jit_solution(2932540676013979835)
XLA Ops:
  0.6 2.0 pack.1
  2.6 13.5 %all_to_all.65.refs_3_ = bf16[16,64,128]{2,1,0:T(8,128)(2,1)S(1)} all-to-all(bf16[16,64,128]{2,1,0:T(8,128)(2,1)S(1)} %get-tuple-element.94), channel_id=1, replica_groups=mesh['fsdp'=16,'dp'=2] {'fsdp'}, dimensions={0} | all-to-all | bytes 524288 | tf_op jit(solution)/shard_map/all_to_all | solution.py:1067
  16.1 3.2 %collective-permute-start = (bf16[16,64,128]{2,1,0:T(8,128)(2,1)S(1)}, bf16[16,64,128]{2,1,0:T(8,128)(2,1)S(1)}, u32[]{:S(2)}, u32[]{:S(2)}) collective-permute-start(bf16[16,64,128]{2,1,0:T(8,128)(2,1)S(1)} %all_to_all.65.refs_3_), channel_id=1, source_target_pairs={{0,1},{1,0},{2,3},{3,2},{4,5},{5,4},{6,7},{7,6},{8,9},{9,8},{10,11... | collective-permute-start | bytes 786440 | tf_op jit(solution)/shard_map/ppermute | solution.py:1034
  19.3 1.2 collective-permute-done.refs_4_
  20.5 4.0 %all-to-all-start.1 = ((bf16[16,144,128]{2,1,0:T(8,128)(2,1)}), bf16[16,144,128]{2,1,0:T(8,128)(2,1)S(1)}, u32[]{:S(2)}, u32[]{:S(2)}) async-start(bf16[16,144,128]{2,1,0:T(8,128)(2,1)} %get-tuple-element.98), calls=%async_computation.1 | async-start | bytes 1179648 | tf_op jit(solution)/shard_map/all_to_all | solution.py:1067
  24.5 0.6 copy-done
  25.2 9.5 %conv_one.1 = (f32[6144,256]{1,0:T(8,128)}, bf16[1024,256]{1,0:T(8,128)(2,1)}, f32[32,4,256]{2,1,0:T(4,128)}) custom-call(s32[1]{0:T(128)} %bitcast.core_ref.refs_0_, s32[24]{0:T(128)S(1)} %copy-done, bf16[6144,1024]{1,0:T(8,128)(2,1)} %bitcast.7, bf16[16,64,128]{2,1,0:T(8,128)(2,1)S(1)} %all_to_all.65.refs_3_, ...), custom_call_target="tpu_custom_call" | custom-call | flops 3221225472 | bytes 18874368 | tf_op jit(solution)/shard_map/conv_one/pallas_call | solution.py:267
  34.7 5.1 %all-to-all-done.1.mine_ref = bf16[16,144,128]{2,1,0:T(8,128)(2,1)S(1)} async-done(((bf16[16,144,128]{2,1,0:T(8,128)(2,1)}), bf16[16,144,128]{2,1,0:T(8,128)(2,1)S(1)}, u32[]{:S(2)}, u32[]{:S(2)}) %all-to-all-start.1) | async-done | bytes 589856 | tf_op jit(solution)/shard_map/all_to_all | solution.py:1067
  39.7 1.9 collective-permute-start.1
  41.6 3.1 all-to-all-start.2
  44.8 0.6 reshape.55.refs_4_.refs_2_.refs_6_.refs_7_.gain_ref.refs_14_
  45.4 0.6 reshape.56.refs_5_.refs_3_.refs_7_.refs_8_.refs_15_
  46.0 0.0 collective-permute-done.1.other_ref
  46.0 1.3 unpack.2.refs_3_.refs_13_
  47.4 3.6 %all-to-all-done.2.refs_1_ = f32[32,4,256]{2,1,0:T(4,128)S(1)} async-done(((f32[32,4,256]{2,1,0:T(4,128)}), f32[32,4,256]{2,1,0:T(4,128)S(1)}, u32[]{:S(2)}, u32[]{:S(2)}) %all-to-all-start.2) | async-done | bytes 131104 | tf_op jit(solution)/shard_map/all_to_all | solution.py:1030
  50.9 5.5 %all-to-all-start.3 = ((bf16[16,64,128]{2,1,0:T(8,128)(2,1)}), bf16[16,64,128]{2,1,0:T(8,128)(2,1)S(1)}, u32[]{:S(2)}, u32[]{:S(2)}) async-start(bf16[16,64,128]{2,1,0:T(8,128)(2,1)} %get-tuple-element.107), calls=%async_computation.3 | async-start | bytes 524288 | tf_op jit(solution)/shard_map/all_to_all | solution.py:1067
  56.4 17.3 %conv_two.1 = (bf16[6144,256]{1,0:T(8,128)(2,1)}, f32[6144,512]{1,0:T(8,128)}, f32[8,256]{1,0:T(8,128)}, f32[32,2,512]{2,1,0:T(2,128)}) custom-call(s32[24]{0:T(128)S(1)} %copy-done.1, f32[32,4,256]{2,1,0:T(4,128)S(1)} %all-to-all-done.2.refs_1_, f32[6144,256]{1,0:T(8,128)} %get-tuple-element.103.refs_2_, bf16[1152,512]{1,0:T(8,128)(2,1)} %unpack.2.refs_3_.refs_13_, ...), custom_call_target="tpu_custom_call" | custom-call | flops 7247757312 | bytes 22020096 | tf_op jit(solution)/shard_map/conv_two/pallas_call | solution.py:267
  73.7 0.0 all-to-all-done.3.mine_ref
  73.7 6.0 %all-to-all-start.4 = ((f32[32,2,512]{2,1,0:T(2,128)}), f32[32,2,512]{2,1,0:T(2,128)S(1)}, u32[]{:S(2)}, u32[]{:S(2)}) async-start(f32[32,2,512]{2,1,0:T(2,128)} %get-tuple-element.108), calls=%async_computation.4 | async-start | bytes 262144 | tf_op jit(solution)/shard_map/all_to_all | solution.py:1030
  79.7 0.4 collective-permute-start.2
  80.1 5.7 %all-to-all-done.4.refs_2_ = f32[32,2,512]{2,1,0:T(2,128)S(1)} async-done(((f32[32,2,512]{2,1,0:T(2,128)}), f32[32,2,512]{2,1,0:T(2,128)S(1)}, u32[]{:S(2)}, u32[]{:S(2)}) %all-to-all-start.4) | async-done | bytes 131104 | tf_op jit(solution)/shard_map/all_to_all | solution.py:1030
  85.8 9.6 %act_two.1 = (bf16[6144,512]{1,0:T(8,128)(2,1)}, f32[24,256]{1,0:T(8,128)}, f32[24,128]{1,0:T(8,128)}, f32[8,512]{1,0:T(8,128)}, f32[32,2,128]{2,1,0:T(2,128)}) custom-call(s32[24]{0:T(128)S(1)} %copy-done.1, f32[8,256]{1,0:T(8,128)} %get-tuple-element.105.refs_1_.refs_2_, f32[32,2,512]{2,1,0:T(2,128)S(1)} %all-to-all-done.4.refs_2_, ...), custom_call_target="tpu_custom_call" | custom-call | flops 62914560 | bytes 31457280 | tf_op jit(solution)/shard_map/act_two/pallas_call | solution.py:267
  95.4 4.6 %all-to-all-start.5 = ((f32[32,2,128]{2,1,0:T(2,128)}), f32[32,2,128]{2,1,0:T(2,128)S(1)}, u32[]{:S(2)}, u32[]{:S(2)}) async-start(f32[32,2,128]{2,1,0:T(2,128)} %get-tuple-element.110), calls=%async_computation.5 | async-start | bytes 65536 | tf_op jit(solution)/shard_map/all_to_all | solution.py:1030
  100.0 10.8 %slope_two.1 = (bf16[6144,512]{1,0:T(8,128)(2,1)}, bf16[6144,512]{1,0:T(8,128)(2,1)}, f32[24,512]{1,0:T(8,128)}, f32[24,512]{1,0:T(8,128)}) custom-call(s32[24]{0:T(128)S(1)} %copy-done.1, bf16[6144,512]{1,0:T(8,128)(2,1)} %get-tuple-element.112.refs_1_.refs_7_.refs_9_, f32[1,1920]{1,0:T(1,128)} %reshape.55.refs_4_.refs_2_.refs_6_.refs_7_.gain_ref.refs_14_, ...), custom_call_target="tpu_custom_call" | custom-call | flops 62914560 | bytes 18874368 | tf_op jit(solution)/shard_map/slope_two/pallas_call | solution.py:267
  110.8 0.0 collective-permute-done.2.other_ref
  110.8 0.9 unpack.3.refs_3_.refs_6_.refs_2_.refs_8_
  111.7 0.0 all-to-all-done.5.refs_0_
  111.7 7.2 %combine.1 = (f32[24,512]{1,0:T(8,128)}, bf16[6144,256]{1,0:T(8,128)(2,1)}, f32[256,1024]{1,0:T(8,128)}, f32[1,256]{1,0:T(1,128)}, f32[4,24,128]{2,1,0:T(8,128)}, /*index=5*/f32[32,2,1024]{2,1,0:T(2,128)S(1)}) custom-call(f32[32,2,128]{2,1,0:T(2,128)S(1)} %all-to-all-done.5.refs_0_, f32[24,128]{1,0:T(8,128)} %get-tuple-element.111.refs_1_, ...), custom_call_target="tpu_custom_call" | custom-call | flops 805306368 | bytes 9437184 | tf_op jit(solution)/shard_map/combine/pallas_call | solution.py:267
  118.9 14.4 %all_to_all.66.refs_2_ = f32[32,2,1024]{2,1,0:T(2,128)S(1)} all-to-all(f32[32,2,1024]{2,1,0:T(2,128)S(1)} %get-tuple-element.115), channel_id=1, replica_groups=mesh['fsdp'=16,'dp'=2] {'fsdp','dp'}, dimensions={0} | all-to-all | bytes 524288 | tf_op jit(solution)/shard_map/all_to_all | solution.py:1030
  133.3 24.8 %output.1 = (bf16[6144,1024]{1,0:T(8,128)(2,1)}, bf16[6144,1024]{1,0:T(8,128)(2,1)}, f32[8,1024]{1,0:T(8,128)}, f32[32,2,1024]{2,1,0:T(2,128)}) custom-call(s32[24]{0:T(128)S(1)} %copy-done.1, f32[8,256]{1,0:T(8,128)} %get-tuple-element.105.refs_1_.refs_2_, f32[32,2,1024]{2,1,0:T(2,128)S(1)} %all_to_all.66.refs_2_, ...), custom_call_target="tpu_custom_call" | custom-call | flops 3221225472 | bytes 50331648 | tf_op jit(solution)/shard_map/output/pallas_call | solution.py:267
  158.1 4.5 %all-to-all-start.7 = ((f32[32,2,1024]{2,1,0:T(2,128)}), f32[32,2,1024]{2,1,0:T(2,128)S(1)}, u32[]{:S(2)}, u32[]{:S(2)}) async-start(f32[32,2,1024]{2,1,0:T(2,128)} %get-tuple-element.120), calls=%async_computation.7 | async-start | bytes 524288 | tf_op jit(solution)/shard_map/all_to_all | solution.py:1030
  162.6 12.5 %project.1 = (bf16[6144,256]{1,0:T(8,128)(2,1)}, f32[256,1024]{1,0:T(8,128)}) custom-call(bf16[6144,256]{1,0:T(8,128)(2,1)} %get-tuple-element.116.refs_3_.refs_0_.refs_4_, bf16[6144,1024]{1,0:T(8,128)(2,1)} %get-tuple-element.122.refs_1_, bf16[256,1024]{1,0:T(8,128)(2,1)} %unpack.3.refs_3_.refs_6_.refs_2_.refs_8_), custom_call_target="tpu_custom_call" | custom-call | flops 6442450944 | bytes 25165824 | tf_op jit(solution)/shard_map/project/pallas_call | solution.py:267
  175.2 0.0 all-to-all-done.7.refs_1_
  175.2 12.8 %back_three.1 = (f32[24,512]{1,0:T(8,128)}, f32[24,512]{1,0:T(8,128)}, f32[24,128]{1,0:T(8,128)}, f32[256,1024]{1,0:T(8,128)}, f32[512,128]{1,0:T(8,128)}, /*ind...) custom-call(f32[8,1024]{1,0:T(8,128)} %get-tuple-element.119.refs_0_.refs_2_, ...), custom_call_target="tpu_custom_call" | custom-call | flops 805306368 | bytes 25165824 | tf_op jit(solution)/shard_map/back_three/pallas_call | solution.py:267
  188.0 11.9 %all_to_all.67.got_ref = f32[32,8,128]{2,1,0:T(8,128)S(1)} all-to-all(f32[32,8,128]{2,1,0:T(8,128)S(1)} %get-tuple-element.129), channel_id=1, replica_groups=mesh['fsdp'=16,'dp'=2] {'fsdp','dp'}, dimensions={0} | all-to-all | bytes 262144 | tf_op jit(solution)/shard_map/all_to_all | solution.py:1030
  199.8 2.3 back_att.1
  202.1 2.5 pack_three.1
  204.6 1.3 collective-permute-start.3
  205.9 3.5 %all-to-all-start.9 = ((f32[32,2,512]{2,1,0:T(2,128)}), f32[32,2,512]{2,1,0:T(2,128)S(1)}, u32[]{:S(2)}, u32[]{:S(2)}) async-start(f32[32,2,512]{2,1,0:T(2,128)} %get-tuple-element.137), calls=%async_computation.9 | async-start | bytes 262144 | tf_op jit(solution)/shard_map/all_to_all | solution.py:1030
  209.4 0.0 collective-permute-done.3
  209.4 2.1 add.3
  211.5 4.1 %all-to-all-done.9.refs_3_ = f32[32,2,512]{2,1,0:T(2,128)S(1)} async-done(((f32[32,2,512]{2,1,0:T(2,128)}), f32[32,2,512]{2,1,0:T(2,128)S(1)}, u32[]{:S(2)}, u32[]{:S(2)}) %all-to-all-start.9) | async-done | bytes 131104 | tf_op jit(solution)/shard_map/all_to_all | solution.py:1030
  215.6 5.5 %all-to-all-start.10 = ((f32[16,88,128]{2,1,0:T(8,128)}), f32[16,88,128]{2,1,0:T(8,128)S(1)}, u32[]{:S(2)}, u32[]{:S(2)}) async-start(f32[16,88,128]{2,1,0:T(8,128)} %add.3), calls=%async_computation.10 | async-start | bytes 1441792 | tf_op jit(solution)/shard_map/all_to_all | solution.py:1067
  221.2 23.4 %back_two.1 = (bf16[6144,512]{1,0:T(8,128)(2,1)}, bf16[6144,256]{1,0:T(8,128)(2,1)}, f32[2,512]{1,0:T(2,128)}, f32[32,2,256]{2,1,0:T(2,128)}) custom-call(s32[24]{0:T(128)S(1)} %copy-done.1, f32[8,256]{1,0:T(8,128)} %get-tuple-element.105.refs_1_.refs_2_, f32[8,512]{1,0:T(8,128)} %get-tuple-element.118.refs_2_, f32[32,2,512]{2,1,0:T(2,128)S(1)} %all-to-all-done.9.refs_3_, ...), custom_call_target="tpu_custom_call" | custom-call | flops 7247757312 | bytes 31457280 | tf_op jit(solution)/shard_map/back_two/pallas_call | solution.py:267
  244.6 0.0 all-to-all-done.10.three_ref
  244.6 6.0 %all-to-all-start.11 = ((f32[32,2,256]{2,1,0:T(2,128)}), f32[32,2,256]{2,1,0:T(2,128)S(1)}, u32[]{:S(2)}, u32[]{:S(2)}) async-start(f32[32,2,256]{2,1,0:T(2,128)} %get-tuple-element.148), calls=%async_computation.11 | async-start | bytes 131072 | tf_op jit(solution)/shard_map/all_to_all | solution.py:1030
  250.7 15.2 %weight_two.1 = (f32[1152,256]{1,0:T(8,128)}, f32[1152,256]{1,0:T(8,128)}) custom-call(s32[1]{0:T(128)} %bitcast.core_ref.refs_0_, s32[24]{0:T(128)S(1)} %copy-done.1, bf16[6144,256]{1,0:T(8,128)(2,1)} %get-tuple-element.140.refs_10_.refs_2_.refs_5_, bf16[6144,512]{1,0:T(8,128)(2,1)} %get-tuple-element.149.refs_3_, ...), custom_call_target="tpu_custom_call" | custom-call | flops 7247757312 | bytes 9437184 | tf_op jit(solution)/shard_map/weight_two/pallas_call | solution.py:267
  265.9 0.0 all-to-all-done.11.refs_3_
  265.9 0.4 collective-permute-start.4
  266.3 11.3 %back_one.1 = (bf16[6144,256]{1,0:T(8,128)(2,1)}, f32[1024,128]{1,0:T(8,128)}, f32[1024,128]{1,0:T(8,128)}, f32[1,1920]{1,0:T(1,128)}, f32[1,1920]{1,0:T(1,128)}) custom-call(s32[1]{0:T(128)} %bitcast.core_ref.refs_0_, s32[24]{0:T(128)S(1)} %copy-done.1, f32[8,256]{1,0:T(8,128)} %get-tuple-element.105.refs_1_.refs_2_, ...), custom_call_target="tpu_custom_call" | custom-call | flops 3221225472 | bytes 25165824 | tf_op jit(solution)/shard_map/back_one/pallas_call | solution.py:267
  277.6 0.3 collective-permute-start.5
  277.9 1.9 collective-permute-done.5.other1_ref
  279.8 0.0 collective-permute-done.4.other2_ref
  279.8 2.6 pack_last.1
  282.4 6.5 %all-to-all-start.12 = ((bf16[16,128,256]{2,1,0:T(8,128)(2,1)}), bf16[16,128,256]{2,1,0:T(8,128)(2,1)S(1)}, u32[]{:S(2)}, u32[]{:S(2)}) async-start(bf16[16,128,256]{2,1,0:T(8,128)(2,1)} %pack_last.1), calls=%async_computation.12 | async-start | bytes 2097152 | tf_op jit(solution)/shard_map/all_to_all | solution.py:1067
  288.9 0.0 copy-start.4
  288.9 12.3 %input_grad.1 = bf16[6144,1024]{1,0:T(8,128)(2,1)} custom-call(bf16[6144,256]{1,0:T(8,128)(2,1)} %get-tuple-element.164.refs_0_, bf16[6144,1024]{1,0:T(8,128)(2,1)} %get-tuple-element.122.refs_1_, f32[8,1024]{1,0:T(8,128)} %get-tuple-element.119.refs_0_.refs_2_, bf16[1024,256]{1,0:T(8,128)(2,1)} %get-tuple-element.165.refs_3_), custom_call_target="tpu_custom_call" | custom-call | flops 3221225472 | bytes 31457280 | tf_op jit(solution)/shard_map/input_grad/pallas_call | solution.py:267
  301.2 12.1 %all-to-all-done.12.parts_ref = bf16[16,128,256]{2,1,0:T(8,128)(2,1)S(1)} async-done(((bf16[16,128,256]{2,1,0:T(8,128)(2,1)}), bf16[16,128,256]{2,1,0:T(8,128)(2,1)S(1)}, u32[]{:S(2)}, u32[]{:S(2)}) %all-to-all-start.12) | async-done | bytes 1048608 | tf_op jit(solution)/shard_map/all_to_all | solution.py:1067
  313.3 0.1 sum_last.1.mine_ref
  313.4 2.3 collective-permute-start.6
  315.8 0.6 reduce
  316.4 0.6 reduce.1
  317.0 0.1 collective-permute-done.6.other_ref
  317.1 0.9 finish.1
  (10 shorter events, 0.0 us)
Async XLA Ops:
  16.1 4.4 %collective-permute-start = (bf16[16,64,128]{2,1,0:T(8,128)(2,1)S(1)}, bf16[16,64,128]{2,1,0:T(8,128)(2,1)S(1)}, u32[]{:S(2)}, u32[]{:S(2)}) collective-permute-start(bf16[16,64,128]{2,1,0:T(8,128)(2,1)S(1)} %all_to_all.65.refs_3_), channel_id=1, source_target_pairs={{0,1},{1,0},{2,3},{3,2},{4,5},{5,4},{6,7},{7,6},{8,9},{9,8},{10,11... | collective-permute-start | bytes 786440 | tf_op jit(solution)/shard_map/ppermute | solution.py:1034
  20.5 19.2 %all-to-all-start.1 = ((bf16[16,144,128]{2,1,0:T(8,128)(2,1)}), bf16[16,144,128]{2,1,0:T(8,128)(2,1)S(1)}, u32[]{:S(2)}, u32[]{:S(2)}) async-start(bf16[16,144,128]{2,1,0:T(8,128)(2,1)} %get-tuple-element.98), calls=%async_computation.1 | async-start | bytes 1179648 | tf_op jit(solution)/shard_map/all_to_all | solution.py:1067
  24.5 0.7 copy-start
  25.2 19.6 %copy-start.2 = (f32[1920]{0:T(1024)S(1)}, f32[1920]{0:T(1024)}, u32[]{:S(2)}) copy-start(f32[1920]{0:T(1024)} %param.19) | copy-start | bytes 23044
  25.2 20.2 %copy-start.3 = (f32[1920]{0:T(1024)S(1)}, f32[1920]{0:T(1024)}, u32[]{:S(2)}) copy-start(f32[1920]{0:T(1024)} %param.20) | copy-start | bytes 23044
  25.2 31.2 %copy-start.1 = (s32[24]{0:T(128)S(1)}, s32[24]{0:T(128)}, u32[]{:S(2)}) copy-start(s32[24]{0:T(128)} %refs_1_.7) | copy-start | bytes 292
  39.7 6.3 %collective-permute-start.1 = (bf16[16,144,128]{2,1,0:T(8,128)(2,1)S(1)}, bf16[16,144,128]{2,1,0:T(8,128)(2,1)S(1)}, u32[]{:S(2)}, u32[]{:S(2)}) collective-permute-start(bf16[16,144,128]{2,1,0:T(8,128)(2,1)S(1)} %all-to-all-done.1.mine_ref), channel_id=1, source_target_pairs={{0,1},{1,0},{2,3},{3,2},{4,5},{5,4},{6,7},{7,6},{8,9},{9,8},{10,11... | collective-permute-start | bytes 1769480 | tf_op jit(solution)/shard_map/ppermute | solution.py:1034
  41.6 9.3 %all-to-all-start.2 = ((f32[32,4,256]{2,1,0:T(4,128)}), f32[32,4,256]{2,1,0:T(4,128)S(1)}, u32[]{:S(2)}, u32[]{:S(2)}) async-start(f32[32,4,256]{2,1,0:T(4,128)} %get-tuple-element.99), calls=%async_computation.2 | async-start | bytes 262144 | tf_op jit(solution)/shard_map/all_to_all | solution.py:1030
  50.9 22.8 %all-to-all-start.3 = ((bf16[16,64,128]{2,1,0:T(8,128)(2,1)}), bf16[16,64,128]{2,1,0:T(8,128)(2,1)S(1)}, u32[]{:S(2)}, u32[]{:S(2)}) async-start(bf16[16,64,128]{2,1,0:T(8,128)(2,1)} %get-tuple-element.107), calls=%async_computation.3 | async-start | bytes 524288 | tf_op jit(solution)/shard_map/all_to_all | solution.py:1067
  73.7 12.1 %all-to-all-start.4 = ((f32[32,2,512]{2,1,0:T(2,128)}), f32[32,2,512]{2,1,0:T(2,128)S(1)}, u32[]{:S(2)}, u32[]{:S(2)}) async-start(f32[32,2,512]{2,1,0:T(2,128)} %get-tuple-element.108), calls=%async_computation.4 | async-start | bytes 262144 | tf_op jit(solution)/shard_map/all_to_all | solution.py:1030
  79.7 31.1 %collective-permute-start.2 = (bf16[16,64,128]{2,1,0:T(8,128)(2,1)S(1)}, bf16[16,64,128]{2,1,0:T(8,128)(2,1)S(1)}, u32[]{:S(2)}, u32[]{:S(2)}) collective-permute-start(bf16[16,64,128]{2,1,0:T(8,128)(2,1)S(1)} %all-to-all-done.3.mine_ref), channel_id=1, source_target_pairs={{0,1},{1,0},{2,3},{3,2},{4,5},{5,4},{6,7},{7,6},{8,9},{9,8},{10,11... | collective-permute-start | bytes 786440 | tf_op jit(solution)/shard_map/ppermute | solution.py:1034
  95.4 16.3 %all-to-all-start.5 = ((f32[32,2,128]{2,1,0:T(2,128)}), f32[32,2,128]{2,1,0:T(2,128)S(1)}, u32[]{:S(2)}, u32[]{:S(2)}) async-start(f32[32,2,128]{2,1,0:T(2,128)} %get-tuple-element.110), calls=%async_computation.5 | async-start | bytes 65536 | tf_op jit(solution)/shard_map/all_to_all | solution.py:1030
  158.1 17.0 %all-to-all-start.7 = ((f32[32,2,1024]{2,1,0:T(2,128)}), f32[32,2,1024]{2,1,0:T(2,128)S(1)}, u32[]{:S(2)}, u32[]{:S(2)}) async-start(f32[32,2,1024]{2,1,0:T(2,128)} %get-tuple-element.120), calls=%async_computation.7 | async-start | bytes 524288 | tf_op jit(solution)/shard_map/all_to_all | solution.py:1030
  204.6 4.8 %collective-permute-start.3 = (f32[16,88,128]{2,1,0:T(8,128)}, f32[16,88,128]{2,1,0:T(8,128)S(1)}, u32[]{:S(2)}, u32[]{:S(2)}) collective-permute-start(f32[16,88,128]{2,1,0:T(8,128)} %get-tuple-element.146), channel_id=1, source_target_pairs={{0,1},{1,0},{2,3},{3,2},{4,5},{5,4},{6,7},{7,6},{8,9},{9,8},{10,11... | collective-permute-start | bytes 2162696 | tf_op jit(solution)/shard_map/ppermute | solution.py:1034
  205.9 9.7 %all-to-all-start.9 = ((f32[32,2,512]{2,1,0:T(2,128)}), f32[32,2,512]{2,1,0:T(2,128)S(1)}, u32[]{:S(2)}, u32[]{:S(2)}) async-start(f32[32,2,512]{2,1,0:T(2,128)} %get-tuple-element.137), calls=%async_computation.9 | async-start | bytes 262144 | tf_op jit(solution)/shard_map/all_to_all | solution.py:1030
  215.6 29.0 %all-to-all-start.10 = ((f32[16,88,128]{2,1,0:T(8,128)}), f32[16,88,128]{2,1,0:T(8,128)S(1)}, u32[]{:S(2)}, u32[]{:S(2)}) async-start(f32[16,88,128]{2,1,0:T(8,128)} %add.3), calls=%async_computation.10 | async-start | bytes 1441792 | tf_op jit(solution)/shard_map/all_to_all | solution.py:1067
  244.6 21.2 %all-to-all-start.11 = ((f32[32,2,256]{2,1,0:T(2,128)}), f32[32,2,256]{2,1,0:T(2,128)S(1)}, u32[]{:S(2)}, u32[]{:S(2)}) async-start(f32[32,2,256]{2,1,0:T(2,128)} %get-tuple-element.148), calls=%async_computation.11 | async-start | bytes 131072 | tf_op jit(solution)/shard_map/all_to_all | solution.py:1030
  265.9 13.9 %collective-permute-start.4 = (f32[1152,256]{1,0:T(8,128)}, f32[1152,256]{1,0:T(8,128)S(1)}, u32[]{:S(2)}, u32[]{:S(2)}) collective-permute-start(f32[1152,256]{1,0:T(8,128)} %get-tuple-element.159), channel_id=1, source_target_pairs={{0,1},{1,0},{2,3},{3,2},{4,5},{5,4},{6,7},{7,6},{8,9},{9,8},{10,11... | collective-permute-start | bytes 3538952 | tf_op jit(solution)/shard_map/ppermute | solution.py:1034
  277.6 2.2 collective-permute-start.5
  282.4 30.9 %all-to-all-start.12 = ((bf16[16,128,256]{2,1,0:T(8,128)(2,1)}), bf16[16,128,256]{2,1,0:T(8,128)(2,1)S(1)}, u32[]{:S(2)}, u32[]{:S(2)}) async-start(bf16[16,128,256]{2,1,0:T(8,128)(2,1)} %pack_last.1), calls=%async_computation.12 | async-start | bytes 2097152 | tf_op jit(solution)/shard_map/all_to_all | solution.py:1067
  288.9 26.9 %copy-start.5 = (f32[1,1920]{1,0:T(1,128)S(1)}, f32[1,1920]{1,0:T(1,128)}, u32[]{:S(2)}) copy-start(f32[1,1920]{1,0:T(1,128)} %get-tuple-element.174) | copy-start | bytes 23044
  288.9 27.5 %copy-start.4 = (f32[1,1920]{1,0:T(1,128)S(1)}, f32[1,1920]{1,0:T(1,128)}, u32[]{:S(2)}) copy-start(f32[1,1920]{1,0:T(1,128)} %get-tuple-element.175) | copy-start | bytes 23044
  313.4 3.7 %collective-permute-start.6 = (f32[400,256]{1,0:T(8,128)S(1)}, f32[400,256]{1,0:T(8,128)S(1)}, u32[]{:S(2)}, u32[]{:S(2)}) collective-permute-start(f32[400,256]{1,0:T(8,128)S(1)} %sum_last.1.mine_ref), channel_id=1, source_target_pairs={{0,1},{1,0},{2,3},{3,2},{4,5},{5,4},{6,7},{7,6},{8,9},{9,8},{10,11... | collective-permute-start | bytes 1228808 | tf_op jit(solution)/shard_map/ppermute | solution.py:1034

commit v5 on v4

--- a/solution.py
+++ b/solution.py
@@ -26,15 +26,14 @@
 PER_CONV_ONE = 4
 PER_CONV_TWO = 3
 PER_ACT_TWO = 4
-PER_SLOPE_TWO = 3
 PER_COMBINE = 6
 PER_OUTPUT = 2
-PER_PROJECT = 4
-PER_BACK_THREE = 4
+PER_OUTER_THREE = 4
+PER_BACK_THREE = 3
 PER_BACK_TWO = 2
 PER_WEIGHT_TWO = 4
-PER_BACK_ONE = 2
-PER_INPUT_GRAD = 2
+PER_BACK_ONE = 3
+PER_INPUT_GRAD = 3
 
 
 def dot_f(left, right):
@@ -436,7 +435,7 @@
 
 def act_two_kernel(
     step, per, sides_ref, one_ref, got_ref, h2_ref, gain_ref, shift_ref, fc_ref,
-    hat_ref, pooled_ref, zin_ref, vec_ref, send_ref,
+    hat_ref, a2_ref, slope_ref, pooled_ref, zin_ref, t2_ref, t4_ref, vec_ref, send_ref,
 ):
     if step is BEGIN:
         sums = total(got_ref)
@@ -456,51 +455,27 @@
     for j in range(per):
         side = SIDE - 2 * sides_ref[step * per + j]
         mask = pixel_mask(side, 128)
-        sums = jnp.zeros((8, WIDTH), F32)
-        for q in range(2):
-            cols = slice(q * WIDTH, (q + 1) * WIDTH)
-            for rows, part in chunks(j):
-                hat = (h2_ref[rows, cols] - vec_ref[0:1, cols]) * vec_ref[1:2, cols]
-                hat_ref[rows, cols] = hat.astype(BF16)
-                half_pre = hat * gain[:, cols] + shift[:, cols]
-                value = half_pre * ((1.0 + jnp.tanh(half_pre)) * wide(mask[part], WIDTH))
-                sums = sums + fold(value)
         image = pl.ds(step * per + j, 1)
-        pixels = (side * side).astype(F32)
-        pooled_ref[image] = row_sum(sums) / pixels
-
-
-def slope_two_kernel(
-    step, per, sides_ref, hat_ref, gain_ref, shift_ref, a2_ref, slope_ref, t2_ref, t4_ref
-):
-    if step is BEGIN:
-        return
-
-    if step is END:
-        return
-
-    gain = gain_ref[:, WIDTH : 3 * WIDTH] * 0.5
-    shift = shift_ref[:, WIDTH : 3 * WIDTH] * 0.5
-    for j in range(per):
-        side = SIDE - 2 * sides_ref[step * per + j]
-        mask = pixel_mask(side, 128)
-        image = pl.ds(step * per + j, 1)
+        values = jnp.zeros((8, WIDTH), F32)
         for q in range(2):
             cols = slice(q * WIDTH, (q + 1) * WIDTH)
             sums = jnp.zeros((8, WIDTH), F32)
             products = jnp.zeros((8, WIDTH), F32)
             for rows, part in chunks(j):
-                hat = hat_ref[rows, cols].astype(F32)
+                hat = (h2_ref[rows, cols] - vec_ref[0:1, cols]) * vec_ref[1:2, cols]
+                hat_ref[rows, cols] = hat.astype(BF16)
                 half_pre = hat * gain[:, cols] + shift[:, cols]
                 a = (1.0 + jnp.tanh(half_pre)) * wide(mask[part], WIDTH)
                 value = half_pre * a
                 slope = a * (0.5 + half_pre - 0.5 * value)
                 a2_ref[rows, cols] = value.astype(BF16)
                 slope_ref[rows, cols] = slope.astype(BF16)
+                values = values + fold(value)
                 sums = sums + fold(slope)
                 products = products + fold(slope * hat)
             t2_ref[image, cols] = row_sum(sums)
             t4_ref[image, cols] = row_sum(products)
+        pooled_ref[image] = row_sum(values) / (side * side).astype(F32)
 
 
 def hidden_terms(zin, sums, n_images, gain_ref, shift_ref):
@@ -611,7 +586,7 @@
             acc_ref[8:16, cols] += products
 
 
-def project_kernel(step, comb_ref, u3_ref, w3_ref, p_ref, cu_ref):
+def outer_three_kernel(step, comb_ref, u3_ref, cu_ref):
     if step is BEGIN:
         cu_ref[...] = jnp.zeros_like(cu_ref)
         return
@@ -619,15 +594,13 @@
     if step is END:
         return
 
-    u3 = u3_ref[...]
-    p_ref[...] = dot_last(u3, w3_ref[...]).astype(BF16)
-    cu_ref[...] += dot_rows(comb_ref[...], u3)
+    cu_ref[...] += dot_rows(comb_ref[...], u3_ref[...])
 
 
 def back_three_kernel(
-    step, per, three_ref, got_ref, hid_ref, comb_ref, p_ref, a2_ref, slope_ref,
+    step, per, three_ref, got_ref, hid_ref, comb_ref, u3_ref, a2_ref, slope_ref,
     hat_ref, w3_ref, cu_ref, gw_ref, csum_ref, att_ref, fc_ref,
-    t1_ref, t3_ref, duz_ref, w3g_ref, fcg_ref, norm_ref, s_ref, c_ref, send_ref, datt_ref,
+    p_ref, t1_ref, t3_ref, duz_ref, w3g_ref, fcg_ref, norm_ref, s_ref, c_ref, send_ref, datt_ref, k_ref,
 ):
     if step is BEGIN:
         mean, inv = three_ref[0:1], three_ref[1:2]
@@ -642,12 +615,14 @@
         w3 = w3_ref[...].astype(F32)
         s_ref[...] = dot_last((w3 * k2).astype(BF16), w3_ref[...]).astype(BF16)
         c_ref[...] = high_last(jnp.broadcast_to(k1, (8, C_IN)), w3)
+        k_ref[0:1] = k1
+        k_ref[1:2] = k2
+        return
+
+    if step is END:
         csum = jnp.broadcast_to(csum_ref[...], (8, WIDTH))
-        outer = high_rows(csum, jnp.broadcast_to(k1, (8, C_IN))) * 0.125
-        w3g_ref[...] = cu_ref[...] - outer - gw_ref[...] * k2
-        return
-
-    if step is END:
+        outer = high_rows(csum, jnp.broadcast_to(k_ref[0:1], (8, C_IN))) * 0.125
+        w3g_ref[...] = cu_ref[...] - outer - gw_ref[...] * k_ref[1:2]
         att = att_ref[...]
         datt = datt_ref[...]
         both = att * datt
@@ -667,6 +642,7 @@
         return
 
     corr = dot_f(comb_ref[...], s_ref[...])
+    p_ref[...] = dot_last(u3_ref[...], w3_ref[...]).astype(BF16)
     for j in range(per):
         image = pl.ds(step * per + j, 1)
         sums = [jnp.zeros((8, WIDTH), F32)] * 6
@@ -1165,7 +1141,7 @@
     full_three = join_weight(core, mine_three, (WIDTH, C_IN))
 
     per, steps = split(PER_ACT_TWO)
-    hat2, pooled, zin, stat2, send = stream_call(
+    hat2, a2, slope2, pooled, zin, t2, t4, stat2, send = stream_call(
         lambda step, *refs, per=per: act_two_kernel(step, per, *refs),
         per,
         steps,
@@ -1180,8 +1156,12 @@
         ],
         [
             blocks_out(2 * WIDTH),
+            blocks_out(2 * WIDTH),
+            blocks_out(2 * WIDTH),
             small(images, WIDTH),
             small(images, INTER),
+            small(images, 2 * WIDTH),
+            small(images, 2 * WIDTH),
             small(8, 2 * WIDTH),
             payload(2, INTER),
         ],
@@ -1190,23 +1170,6 @@
         name="act_two",
     )
     got_att = everyone(send)
-
-    per, steps = split(PER_SLOPE_TWO)
-    a2, slope2, t2, t4 = stream_call(
-        lambda step, *refs, per=per: slope_two_kernel(step, per, *refs),
-        per,
-        steps,
-        [sides_in, blocks(hat2), gain_in, shift_in],
-        [
-            blocks_out(2 * WIDTH),
-            blocks_out(2 * WIDTH),
-            small(images, 2 * WIDTH),
-            small(images, 2 * WIDTH),
-        ],
-        flops=rows * 2 * WIDTH * 20,
-        moved=rows * 2 * WIDTH * 6,
-        name="slope_two",
-    )
 
     per, steps = split(PER_COMBINE)
     att, comb, gw, csum, hid, send = stream_call(
@@ -1267,20 +1230,20 @@
     )
     got_back_three = everyone(send)
 
-    per, steps = split(PER_PROJECT)
-    p, cu = stream_call(
-        project_kernel,
+    per, steps = split(PER_OUTER_THREE)
+    (cu,) = stream_call(
+        outer_three_kernel,
         per,
         steps,
-        [blocks(comb), blocks(u3), full(full_three)],
-        [blocks_out(WIDTH), small(WIDTH, C_IN)],
-        flops=4 * rows * WIDTH * C_IN,
-        moved=rows * C_IN * 4,
-        name="project",
+        [blocks(comb), blocks(u3)],
+        [small(WIDTH, C_IN)],
+        flops=2 * rows * WIDTH * C_IN,
+        moved=rows * C_IN * 3,
+        name="outer_three",
     )
 
     per, steps = split(PER_BACK_THREE)
-    t1, t3, duz, w3_local, fc2_local, norm3, corr_weight, corr_row, send = stream_call(
+    p, t1, t3, duz, w3_local, fc2_local, norm3, corr_weight, corr_row, send = stream_call(
         lambda step, *refs, per=per: back_three_kernel(step, per, *refs),
         per,
         steps,
@@ -1289,7 +1252,7 @@
             near(got_back_three),
             full(hid),
             blocks(comb),
-            blocks(p),
+            blocks(u3),
             blocks(a2),
             blocks(slope2),
             blocks(hat2),
@@ -1301,6 +1264,7 @@
             full(fc_second),
         ],
         [
+            blocks_out(WIDTH, over=3),
             small(images, 2 * WIDTH),
             small(images, 2 * WIDTH),
             small(images, INTER),
@@ -1311,8 +1275,8 @@
             small(8, WIDTH),
             payload(8, INTER),
         ],
-        [pltpu.VMEM((images, 2 * WIDTH), F32)],
-        flops=2 * rows * WIDTH * WIDTH,
+        [pltpu.VMEM((images, 2 * WIDTH), F32), pltpu.VMEM((2, C_IN), F32)],
+        flops=4 * rows * WIDTH * C_IN,
         moved=rows * WIDTH * 16,
         name="back_three",
     )

time: 319 us -> 314 us (0.984)
  Pallas kernels: 179 us -> 171 us
  waiting for transfers between devices: 33.8 us -> 40.5 us
  blocking collectives: 39.8 us -> 36.3 us
    pallas_call x12 -> x11, Pallas kernels: 167 us -> 158 us  [stream_call(): pl.pallas_call(whole_kernel, in_specs=in_specs, out_specs=out_specs, out_...]
    all_to_all x6, waiting for transfers between devices: 13.4 us -> 19.2 us  [everyone(): return lax.all_to_all(payload, AXES, 0, 0, tiled=True)]
    all_to_all x2, blocking collectives: 26.3 us -> 22.8 us  [everyone(): return lax.all_to_all(payload, AXES, 0, 0, tiled=True)]
  transfers between devices with their start and end apart: 17 -> 17, of which waited for: 8 -> 10; matrix products, arithmetic and copies ran while one was open for 1% -> 1% of each run, Pallas kernels for 39% -> 35%
where the time goes in v5:
time: 314 us; the launch traced here: 313 us
  Pallas kernels  171 us (54%)
  starting transfers between devices  59 us (19%)
  waiting for transfers between devices  40.5 us (13%)
  blocking collectives  36.3 us (12%)
  other arithmetic  3.31 us (1%)
    pallas_call x11, Pallas kernels, stream_call(): pl.pallas_call(whole_kernel, in_specs=in_specs, out_specs=out_specs, out_...  158 us
    all_to_all x6, starting transfers between devices, everyone(): return lax.all_to_all(payload, AXES, 0, 0, tiled=True)  27.7 us
    all_to_all x2, blocking collectives, everyone(): return lax.all_to_all(payload, AXES, 0, 0, tiled=True)  22.8 us
    all_to_all x4, starting transfers between devices, slots(): return lax.all_to_all(parts, 'fsdp', 0, 0, tiled=True)  21.5 us
    all_to_all x6, waiting for transfers between devices, everyone(): return lax.all_to_all(payload, AXES, 0, 0, tiled=True)  19.2 us
    all_to_all x4, waiting for transfers between devices, slots(): return lax.all_to_all(parts, 'fsdp', 0, 0, tiled=True)  18.1 us
    all_to_all x1, blocking collectives, slots(): return lax.all_to_all(parts, 'fsdp', 0, 0, tiled=True)  13.5 us
    pallas_call x8, Pallas kernels, call(): pl.pallas_call(kernel, grid=(grid,), in_specs=[spec for _, spec, *_ in in...  12.7 us
  transfers between devices with their start and end apart: 17, of which 10 were waited for; matrix products, arithmetic and copies ran while one was open for 1% of the time, Pallas kernels for 35%

profile of v5, /device:TPU:9, one launch (start us, length us, event | category | flops | bytes accessed | tf_op | source)
XLA Modules:
  0.0 312.8 jit_solution(17655638054938272465)
XLA Ops:
  0.6 2.0 pack.1
  2.6 13.5 %all_to_all.65.refs_3_ = bf16[16,64,128]{2,1,0:T(8,128)(2,1)S(1)} all-to-all(bf16[16,64,128]{2,1,0:T(8,128)(2,1)S(1)} %get-tuple-element.93), channel_id=1, replica_groups=mesh['fsdp'=16,'dp'=2] {'fsdp'}, dimensions={0} | all-to-all | bytes 524288 | tf_op jit(solution)/shard_map/all_to_all | solution.py:1043
  16.1 3.2 %collective-permute-start = (bf16[16,64,128]{2,1,0:T(8,128)(2,1)S(1)}, bf16[16,64,128]{2,1,0:T(8,128)(2,1)S(1)}, u32[]{:S(2)}, u32[]{:S(2)}) collective-permute-start(bf16[16,64,128]{2,1,0:T(8,128)(2,1)S(1)} %all_to_all.65.refs_3_), channel_id=1, source_target_pairs={{0,1},{1,0},{2,3},{3,2},{4,5},{5,4},{6,7},{7,6},{8,9},{9,8},{10,11... | collective-permute-start | bytes 786440 | tf_op jit(solution)/shard_map/ppermute | solution.py:1010
  19.3 1.2 collective-permute-done.refs_4_
  20.5 4.0 %all-to-all-start.1 = ((bf16[16,144,128]{2,1,0:T(8,128)(2,1)}), bf16[16,144,128]{2,1,0:T(8,128)(2,1)S(1)}, u32[]{:S(2)}, u32[]{:S(2)}) async-start(bf16[16,144,128]{2,1,0:T(8,128)(2,1)} %get-tuple-element.97), calls=%async_computation.1 | async-start | bytes 1179648 | tf_op jit(solution)/shard_map/all_to_all | solution.py:1043
  24.5 0.6 copy-done
  25.2 9.5 %conv_one.1 = (f32[6144,256]{1,0:T(8,128)}, bf16[1024,256]{1,0:T(8,128)(2,1)}, f32[32,4,256]{2,1,0:T(4,128)}) custom-call(s32[1]{0:T(128)} %bitcast.core_ref.refs_0_, s32[24]{0:T(128)S(1)} %copy-done, bf16[6144,1024]{1,0:T(8,128)(2,1)} %bitcast.7, bf16[16,64,128]{2,1,0:T(8,128)(2,1)S(1)} %all_to_all.65.refs_3_, ...), custom_call_target="tpu_custom_call" | custom-call | flops 3221225472 | bytes 18874368 | tf_op jit(solution)/shard_map/conv_one/pallas_call | solution.py:266
  34.7 5.1 %all-to-all-done.1.mine_ref = bf16[16,144,128]{2,1,0:T(8,128)(2,1)S(1)} async-done(((bf16[16,144,128]{2,1,0:T(8,128)(2,1)}), bf16[16,144,128]{2,1,0:T(8,128)(2,1)S(1)}, u32[]{:S(2)}, u32[]{:S(2)}) %all-to-all-start.1) | async-done | bytes 589856 | tf_op jit(solution)/shard_map/all_to_all | solution.py:1043
  39.7 1.9 collective-permute-start.1
  41.6 3.1 %all-to-all-start.2 = ((f32[32,4,256]{2,1,0:T(4,128)}), f32[32,4,256]{2,1,0:T(4,128)S(1)}, u32[]{:S(2)}, u32[]{:S(2)}) async-start(f32[32,4,256]{2,1,0:T(4,128)} %get-tuple-element.98), calls=%async_computation.2 | async-start | bytes 262144 | tf_op jit(solution)/shard_map/all_to_all | solution.py:1006
  44.8 0.6 reshape.55.refs_4_.refs_6_.refs_7_.gain_ref.refs_14_
  45.4 0.0 copy-done.3
  45.4 0.6 reshape.56.refs_5_.refs_7_.refs_8_.refs_15_
  46.0 0.0 collective-permute-done.1.other_ref
  46.0 1.4 unpack.2.refs_3_.refs_13_
  47.4 3.5 %all-to-all-done.2.refs_1_ = f32[32,4,256]{2,1,0:T(4,128)S(1)} async-done(((f32[32,4,256]{2,1,0:T(4,128)}), f32[32,4,256]{2,1,0:T(4,128)S(1)}, u32[]{:S(2)}, u32[]{:S(2)}) %all-to-all-start.2) | async-done | bytes 131104 | tf_op jit(solution)/shard_map/all_to_all | solution.py:1006
  50.9 5.5 %all-to-all-start.3 = ((bf16[16,64,128]{2,1,0:T(8,128)(2,1)}), bf16[16,64,128]{2,1,0:T(8,128)(2,1)S(1)}, u32[]{:S(2)}, u32[]{:S(2)}) async-start(bf16[16,64,128]{2,1,0:T(8,128)(2,1)} %get-tuple-element.106), calls=%async_computation.3 | async-start | bytes 524288 | tf_op jit(solution)/shard_map/all_to_all | solution.py:1043
  56.4 17.3 %conv_two.1 = (bf16[6144,256]{1,0:T(8,128)(2,1)}, f32[6144,512]{1,0:T(8,128)}, f32[8,256]{1,0:T(8,128)}, f32[32,2,512]{2,1,0:T(2,128)}) custom-call(s32[24]{0:T(128)S(1)} %copy-done.1, f32[32,4,256]{2,1,0:T(4,128)S(1)} %all-to-all-done.2.refs_1_, f32[6144,256]{1,0:T(8,128)} %get-tuple-element.102.refs_2_, bf16[1152,512]{1,0:T(8,128)(2,1)} %unpack.2.refs_3_.refs_13_, ...), custom_call_target="tpu_custom_call" | custom-call | flops 7247757312 | bytes 22020096 | tf_op jit(solution)/shard_map/conv_two/pallas_call | solution.py:266
  73.7 0.0 all-to-all-done.3.mine_ref
  73.7 6.0 %all-to-all-start.4 = ((f32[32,2,512]{2,1,0:T(2,128)}), f32[32,2,512]{2,1,0:T(2,128)S(1)}, u32[]{:S(2)}, u32[]{:S(2)}) async-start(f32[32,2,512]{2,1,0:T(2,128)} %get-tuple-element.107), calls=%async_computation.4 | async-start | bytes 262144 | tf_op jit(solution)/shard_map/all_to_all | solution.py:1006
  79.7 0.4 collective-permute-start.2
  80.1 5.7 %all-to-all-done.4.refs_2_ = f32[32,2,512]{2,1,0:T(2,128)S(1)} async-done(((f32[32,2,512]{2,1,0:T(2,128)}), f32[32,2,512]{2,1,0:T(2,128)S(1)}, u32[]{:S(2)}, u32[]{:S(2)}) %all-to-all-start.4) | async-done | bytes 131104 | tf_op jit(solution)/shard_map/all_to_all | solution.py:1006
  85.8 13.2 %act_two.1 = (bf16[6144,512]{1,0:T(8,128)(2,1)}, bf16[6144,512]{1,0:T(8,128)(2,1)}, bf16[6144,512]{1,0:T(8,128)(2,1)}, f32[24,256]{1,0:T(8,128)}, f32[24,128]{1,...) custom-call(s32[24]{0:T(128)S(1)} %copy-done.1, ...), custom_call_target="tpu_custom_call" | custom-call | flops 62914560 | bytes 31457280 | tf_op jit(solution)/shard_map/act_two/pallas_call | solution.py:266
  99.1 4.6 %all-to-all-start.5 = ((f32[32,2,128]{2,1,0:T(2,128)}), f32[32,2,128]{2,1,0:T(2,128)S(1)}, u32[]{:S(2)}, u32[]{:S(2)}) async-start(f32[32,2,128]{2,1,0:T(2,128)} %get-tuple-element.109), calls=%async_computation.5 | async-start | bytes 65536 | tf_op jit(solution)/shard_map/all_to_all | solution.py:1006
  103.7 0.0 collective-permute-done.2.other_ref
  103.7 0.9 unpack.3.refs_3_.refs_6_.refs_8_
  104.6 4.7 %all-to-all-done.5.refs_0_ = f32[32,2,128]{2,1,0:T(2,128)S(1)} async-done(((f32[32,2,128]{2,1,0:T(2,128)}), f32[32,2,128]{2,1,0:T(2,128)S(1)}, u32[]{:S(2)}, u32[]{:S(2)}) %all-to-all-start.5) | async-done | bytes 32800 | tf_op jit(solution)/shard_map/all_to_all | solution.py:1006
  109.3 7.2 %combine.1 = (f32[24,512]{1,0:T(8,128)}, bf16[6144,256]{1,0:T(8,128)(2,1)}, f32[256,1024]{1,0:T(8,128)}, f32[1,256]{1,0:T(1,128)}, f32[4,24,128]{2,1,0:T(8,128)}, /*index=5*/f32[32,2,1024]{2,1,0:T(2,128)S(1)}) custom-call(f32[32,2,128]{2,1,0:T(2,128)S(1)} %all-to-all-done.5.refs_0_, f32[24,128]{1,0:T(8,128)} %get-tuple-element.110.refs_1_, ...), custom_call_target="tpu_custom_call" | custom-call | flops 805306368 | bytes 9437184 | tf_op jit(solution)/shard_map/combine/pallas_call | solution.py:266
  116.5 12.1 %all_to_all.66.refs_2_ = f32[32,2,1024]{2,1,0:T(2,128)S(1)} all-to-all(f32[32,2,1024]{2,1,0:T(2,128)S(1)} %get-tuple-element.113), channel_id=1, replica_groups=mesh['fsdp'=16,'dp'=2] {'fsdp','dp'}, dimensions={0} | all-to-all | bytes 524288 | tf_op jit(solution)/shard_map/all_to_all | solution.py:1006
  128.6 24.8 %output.1 = (bf16[6144,1024]{1,0:T(8,128)(2,1)}, bf16[6144,1024]{1,0:T(8,128)(2,1)}, f32[8,1024]{1,0:T(8,128)}, f32[32,2,1024]{2,1,0:T(2,128)}) custom-call(s32[24]{0:T(128)S(1)} %copy-done.1, f32[8,256]{1,0:T(8,128)} %get-tuple-element.104.refs_1_.refs_2_, f32[32,2,1024]{2,1,0:T(2,128)S(1)} %all_to_all.66.refs_2_, ...), custom_call_target="tpu_custom_call" | custom-call | flops 3221225472 | bytes 50331648 | tf_op jit(solution)/shard_map/output/pallas_call | solution.py:266
  153.4 4.5 %all-to-all-start.7 = ((f32[32,2,1024]{2,1,0:T(2,128)}), f32[32,2,1024]{2,1,0:T(2,128)S(1)}, u32[]{:S(2)}, u32[]{:S(2)}) async-start(f32[32,2,1024]{2,1,0:T(2,128)} %get-tuple-element.118), calls=%async_computation.7 | async-start | bytes 524288 | tf_op jit(solution)/shard_map/all_to_all | solution.py:1006
  157.9 7.6 %outer_three.1.refs_9_ = f32[256,1024]{1,0:T(8,128)} custom-call(bf16[6144,256]{1,0:T(8,128)(2,1)} %get-tuple-element.114.refs_3_.refs_0_.refs_4_, bf16[6144,1024]{1,0:T(8,128)(2,1)} %get-tuple-element.120.refs_1_.refs_4_), custom_call_target="tpu_custom_call" | custom-call | flops 3221225472 | bytes 18874368 | tf_op jit(solution)/shard_map/outer_three/pallas_call | solution.py:266
  165.5 1.1 all-to-all-done.7.refs_1_
  166.6 17.9 %back_three.1 = (bf16[6144,256]{1,0:T(8,128)(2,1)}, f32[24,512]{1,0:T(8,128)}, f32[24,512]{1,0:T(8,128)}, f32[24,128]{1,0:T(8,128)}, f32[256,1024]{1,0:T(8,128)}...) custom-call(f32[8,1024]{1,0:T(8,128)} %get-tuple-element.117.refs_0_, ...), custom_call_target="tpu_custom_call" | custom-call | flops 6442450944 | bytes 25165824 | tf_op jit(solution)/shard_map/back_three/pallas_call | solution.py:266
  184.5 10.8 %all_to_all.67.got_ref = f32[32,8,128]{2,1,0:T(8,128)S(1)} all-to-all(f32[32,8,128]{2,1,0:T(8,128)S(1)} %get-tuple-element.126), channel_id=1, replica_groups=mesh['fsdp'=16,'dp'=2] {'fsdp','dp'}, dimensions={0} | all-to-all | bytes 262144 | tf_op jit(solution)/shard_map/all_to_all | solution.py:1006
  195.3 2.3 back_att.1
  197.6 2.6 pack_three.1
  200.1 1.3 collective-permute-start.3
  201.5 3.5 %all-to-all-start.9 = ((f32[32,2,512]{2,1,0:T(2,128)}), f32[32,2,512]{2,1,0:T(2,128)S(1)}, u32[]{:S(2)}, u32[]{:S(2)}) async-start(f32[32,2,512]{2,1,0:T(2,128)} %get-tuple-element.134), calls=%async_computation.9 | async-start | bytes 262144 | tf_op jit(solution)/shard_map/all_to_all | solution.py:1006
  205.0 0.0 collective-permute-done.3
  205.0 2.1 add.3
  207.0 4.1 %all-to-all-done.9.refs_3_ = f32[32,2,512]{2,1,0:T(2,128)S(1)} async-done(((f32[32,2,512]{2,1,0:T(2,128)}), f32[32,2,512]{2,1,0:T(2,128)S(1)}, u32[]{:S(2)}, u32[]{:S(2)}) %all-to-all-start.9) | async-done | bytes 131104 | tf_op jit(solution)/shard_map/all_to_all | solution.py:1006
  211.2 5.5 %all-to-all-start.10 = ((f32[16,88,128]{2,1,0:T(8,128)}), f32[16,88,128]{2,1,0:T(8,128)S(1)}, u32[]{:S(2)}, u32[]{:S(2)}) async-start(f32[16,88,128]{2,1,0:T(8,128)} %add.3), calls=%async_computation.10 | async-start | bytes 1441792 | tf_op jit(solution)/shard_map/all_to_all | solution.py:1043
  216.7 23.4 %back_two.1 = (bf16[6144,512]{1,0:T(8,128)(2,1)}, bf16[6144,256]{1,0:T(8,128)(2,1)}, f32[2,512]{1,0:T(2,128)}, f32[32,2,256]{2,1,0:T(2,128)}) custom-call(s32[24]{0:T(128)S(1)} %copy-done.1, f32[8,256]{1,0:T(8,128)} %get-tuple-element.104.refs_1_.refs_2_, f32[8,512]{1,0:T(8,128)} %get-tuple-element.116.refs_2_, f32[32,2,512]{2,1,0:T(2,128)S(1)} %all-to-all-done.9.refs_3_, ...), custom_call_target="tpu_custom_call" | custom-call | flops 7247757312 | bytes 31457280 | tf_op jit(solution)/shard_map/back_two/pallas_call | solution.py:266
  240.2 0.0 all-to-all-done.10.three_ref
  240.2 6.0 %all-to-all-start.11 = ((f32[32,2,256]{2,1,0:T(2,128)}), f32[32,2,256]{2,1,0:T(2,128)S(1)}, u32[]{:S(2)}, u32[]{:S(2)}) async-start(f32[32,2,256]{2,1,0:T(2,128)} %get-tuple-element.146), calls=%async_computation.11 | async-start | bytes 131072 | tf_op jit(solution)/shard_map/all_to_all | solution.py:1006
  246.2 15.2 %weight_two.1 = (f32[1152,256]{1,0:T(8,128)}, f32[1152,256]{1,0:T(8,128)}) custom-call(s32[1]{0:T(128)} %bitcast.core_ref.refs_0_, s32[24]{0:T(128)S(1)} %copy-done.1, bf16[6144,256]{1,0:T(8,128)(2,1)} %get-tuple-element.138.refs_10_.refs_2_.refs_5_, bf16[6144,512]{1,0:T(8,128)(2,1)} %get-tuple-element.147.refs_3_, ...), custom_call_target="tpu_custom_call" | custom-call | flops 7247757312 | bytes 9437184 | tf_op jit(solution)/shard_map/weight_two/pallas_call | solution.py:266
  261.4 0.0 all-to-all-done.11.refs_3_
  261.4 0.4 collective-permute-start.4
  261.8 10.7 %back_one.1 = (bf16[6144,256]{1,0:T(8,128)(2,1)}, f32[1024,128]{1,0:T(8,128)}, f32[1024,128]{1,0:T(8,128)}, f32[1,1920]{1,0:T(1,128)}, f32[1,1920]{1,0:T(1,128)}) custom-call(s32[1]{0:T(128)} %bitcast.core_ref.refs_0_, s32[24]{0:T(128)S(1)} %copy-done.1, f32[8,256]{1,0:T(8,128)} %get-tuple-element.104.refs_1_.refs_2_, ...), custom_call_target="tpu_custom_call" | custom-call | flops 3221225472 | bytes 25165824 | tf_op jit(solution)/shard_map/back_one/pallas_call | solution.py:266
  272.5 0.2 collective-permute-start.5
  272.7 2.0 collective-permute-done.5.other1_ref
  274.7 0.0 collective-permute-done.4.other2_ref
  274.7 2.6 pack_last.1
  277.2 6.5 %all-to-all-start.12 = ((bf16[16,128,256]{2,1,0:T(8,128)(2,1)}), bf16[16,128,256]{2,1,0:T(8,128)(2,1)S(1)}, u32[]{:S(2)}, u32[]{:S(2)}) async-start(bf16[16,128,256]{2,1,0:T(8,128)(2,1)} %pack_last.1), calls=%async_computation.12 | async-start | bytes 2097152 | tf_op jit(solution)/shard_map/all_to_all | solution.py:1043
  283.7 0.0 copy-start.4
  283.7 11.4 %input_grad.1 = bf16[6144,1024]{1,0:T(8,128)(2,1)} custom-call(bf16[6144,256]{1,0:T(8,128)(2,1)} %get-tuple-element.162.refs_0_, bf16[6144,1024]{1,0:T(8,128)(2,1)} %get-tuple-element.120.refs_1_.refs_4_, f32[8,1024]{1,0:T(8,128)} %get-tuple-element.117.refs_0_.refs_2_, bf16[1024,256]{1,0:T(8,128)(2,1)} %get-tuple-element.163.refs_3_), custom_call_target="tpu_custom_call" | custom-call | flops 3221225472 | bytes 31457280 | tf_op jit(solution)/shard_map/input_grad/pallas_call | solution.py:266
  295.1 13.0 %all-to-all-done.12.parts_ref = bf16[16,128,256]{2,1,0:T(8,128)(2,1)S(1)} async-done(((bf16[16,128,256]{2,1,0:T(8,128)(2,1)}), bf16[16,128,256]{2,1,0:T(8,128)(2,1)S(1)}, u32[]{:S(2)}, u32[]{:S(2)}) %all-to-all-start.12) | async-done | bytes 1048608 | tf_op jit(solution)/shard_map/all_to_all | solution.py:1043
  308.1 0.1 sum_last.1.mine_ref
  308.2 2.3 collective-permute-start.6
  310.6 0.6 reduce
  311.2 0.6 reduce.1
  311.8 0.1 collective-permute-done.6.other_ref
  312.0 0.9 finish.1
  (9 shorter events, 0.0 us)
Async XLA Ops:
  16.1 4.4 %collective-permute-start = (bf16[16,64,128]{2,1,0:T(8,128)(2,1)S(1)}, bf16[16,64,128]{2,1,0:T(8,128)(2,1)S(1)}, u32[]{:S(2)}, u32[]{:S(2)}) collective-permute-start(bf16[16,64,128]{2,1,0:T(8,128)(2,1)S(1)} %all_to_all.65.refs_3_), channel_id=1, source_target_pairs={{0,1},{1,0},{2,3},{3,2},{4,5},{5,4},{6,7},{7,6},{8,9},{9,8},{10,11... | collective-permute-start | bytes 786440 | tf_op jit(solution)/shard_map/ppermute | solution.py:1010
  20.5 19.2 %all-to-all-start.1 = ((bf16[16,144,128]{2,1,0:T(8,128)(2,1)}), bf16[16,144,128]{2,1,0:T(8,128)(2,1)S(1)}, u32[]{:S(2)}, u32[]{:S(2)}) async-start(bf16[16,144,128]{2,1,0:T(8,128)(2,1)} %get-tuple-element.97), calls=%async_computation.1 | async-start | bytes 1179648 | tf_op jit(solution)/shard_map/all_to_all | solution.py:1043
  24.5 0.7 copy-start
  25.2 19.6 %copy-start.2 = (f32[1920]{0:T(1024)S(1)}, f32[1920]{0:T(1024)}, u32[]{:S(2)}) copy-start(f32[1920]{0:T(1024)} %param.19) | copy-start | bytes 23044
  25.2 20.2 %copy-start.3 = (f32[1920]{0:T(1024)S(1)}, f32[1920]{0:T(1024)}, u32[]{:S(2)}) copy-start(f32[1920]{0:T(1024)} %param.20) | copy-start | bytes 23044
  25.2 31.2 %copy-start.1 = (s32[24]{0:T(128)S(1)}, s32[24]{0:T(128)}, u32[]{:S(2)}) copy-start(s32[24]{0:T(128)} %refs_1_.7) | copy-start | bytes 292
  39.7 6.3 %collective-permute-start.1 = (bf16[16,144,128]{2,1,0:T(8,128)(2,1)S(1)}, bf16[16,144,128]{2,1,0:T(8,128)(2,1)S(1)}, u32[]{:S(2)}, u32[]{:S(2)}) collective-permute-start(bf16[16,144,128]{2,1,0:T(8,128)(2,1)S(1)} %all-to-all-done.1.mine_ref), channel_id=1, source_target_pairs={{0,1},{1,0},{2,3},{3,2},{4,5},{5,4},{6,7},{7,6},{8,9},{9,8},{10,11... | collective-permute-start | bytes 1769480 | tf_op jit(solution)/shard_map/ppermute | solution.py:1010
  41.6 9.3 %all-to-all-start.2 = ((f32[32,4,256]{2,1,0:T(4,128)}), f32[32,4,256]{2,1,0:T(4,128)S(1)}, u32[]{:S(2)}, u32[]{:S(2)}) async-start(f32[32,4,256]{2,1,0:T(4,128)} %get-tuple-element.98), calls=%async_computation.2 | async-start | bytes 262144 | tf_op jit(solution)/shard_map/all_to_all | solution.py:1006
  50.9 22.8 %all-to-all-start.3 = ((bf16[16,64,128]{2,1,0:T(8,128)(2,1)}), bf16[16,64,128]{2,1,0:T(8,128)(2,1)S(1)}, u32[]{:S(2)}, u32[]{:S(2)}) async-start(bf16[16,64,128]{2,1,0:T(8,128)(2,1)} %get-tuple-element.106), calls=%async_computation.3 | async-start | bytes 524288 | tf_op jit(solution)/shard_map/all_to_all | solution.py:1043
  73.7 12.1 %all-to-all-start.4 = ((f32[32,2,512]{2,1,0:T(2,128)}), f32[32,2,512]{2,1,0:T(2,128)S(1)}, u32[]{:S(2)}, u32[]{:S(2)}) async-start(f32[32,2,512]{2,1,0:T(2,128)} %get-tuple-element.107), calls=%async_computation.4 | async-start | bytes 262144 | tf_op jit(solution)/shard_map/all_to_all | solution.py:1006
  79.7 24.0 %collective-permute-start.2 = (bf16[16,64,128]{2,1,0:T(8,128)(2,1)S(1)}, bf16[16,64,128]{2,1,0:T(8,128)(2,1)S(1)}, u32[]{:S(2)}, u32[]{:S(2)}) collective-permute-start(bf16[16,64,128]{2,1,0:T(8,128)(2,1)S(1)} %all-to-all-done.3.mine_ref), channel_id=1, source_target_pairs={{0,1},{1,0},{2,3},{3,2},{4,5},{5,4},{6,7},{7,6},{8,9},{9,8},{10,11... | collective-permute-start | bytes 786440 | tf_op jit(solution)/shard_map/ppermute | solution.py:1010
  99.1 10.3 %all-to-all-start.5 = ((f32[32,2,128]{2,1,0:T(2,128)}), f32[32,2,128]{2,1,0:T(2,128)S(1)}, u32[]{:S(2)}, u32[]{:S(2)}) async-start(f32[32,2,128]{2,1,0:T(2,128)} %get-tuple-element.109), calls=%async_computation.5 | async-start | bytes 65536 | tf_op jit(solution)/shard_map/all_to_all | solution.py:1006
  153.4 13.2 %all-to-all-start.7 = ((f32[32,2,1024]{2,1,0:T(2,128)}), f32[32,2,1024]{2,1,0:T(2,128)S(1)}, u32[]{:S(2)}, u32[]{:S(2)}) async-start(f32[32,2,1024]{2,1,0:T(2,128)} %get-tuple-element.118), calls=%async_computation.7 | async-start | bytes 524288 | tf_op jit(solution)/shard_map/all_to_all | solution.py:1006
  200.1 4.8 %collective-permute-start.3 = (f32[16,88,128]{2,1,0:T(8,128)}, f32[16,88,128]{2,1,0:T(8,128)S(1)}, u32[]{:S(2)}, u32[]{:S(2)}) collective-permute-start(f32[16,88,128]{2,1,0:T(8,128)} %get-tuple-element.144), channel_id=1, source_target_pairs={{0,1},{1,0},{2,3},{3,2},{4,5},{5,4},{6,7},{7,6},{8,9},{9,8},{10,11... | collective-permute-start | bytes 2162696 | tf_op jit(solution)/shard_map/ppermute | solution.py:1010
  201.5 9.7 %all-to-all-start.9 = ((f32[32,2,512]{2,1,0:T(2,128)}), f32[32,2,512]{2,1,0:T(2,128)S(1)}, u32[]{:S(2)}, u32[]{:S(2)}) async-start(f32[32,2,512]{2,1,0:T(2,128)} %get-tuple-element.134), calls=%async_computation.9 | async-start | bytes 262144 | tf_op jit(solution)/shard_map/all_to_all | solution.py:1006
  211.2 29.0 %all-to-all-start.10 = ((f32[16,88,128]{2,1,0:T(8,128)}), f32[16,88,128]{2,1,0:T(8,128)S(1)}, u32[]{:S(2)}, u32[]{:S(2)}) async-start(f32[16,88,128]{2,1,0:T(8,128)} %add.3), calls=%async_computation.10 | async-start | bytes 1441792 | tf_op jit(solution)/shard_map/all_to_all | solution.py:1043
  240.2 21.2 %all-to-all-start.11 = ((f32[32,2,256]{2,1,0:T(2,128)}), f32[32,2,256]{2,1,0:T(2,128)S(1)}, u32[]{:S(2)}, u32[]{:S(2)}) async-start(f32[32,2,256]{2,1,0:T(2,128)} %get-tuple-element.146), calls=%async_computation.11 | async-start | bytes 131072 | tf_op jit(solution)/shard_map/all_to_all | solution.py:1006
  261.4 13.3 %collective-permute-start.4 = (f32[1152,256]{1,0:T(8,128)}, f32[1152,256]{1,0:T(8,128)S(1)}, u32[]{:S(2)}, u32[]{:S(2)}) collective-permute-start(f32[1152,256]{1,0:T(8,128)} %get-tuple-element.157), channel_id=1, source_target_pairs={{0,1},{1,0},{2,3},{3,2},{4,5},{5,4},{6,7},{7,6},{8,9},{9,8},{10,11... | collective-permute-start | bytes 3538952 | tf_op jit(solution)/shard_map/ppermute | solution.py:1010
  272.5 2.2 collective-permute-start.5
  277.2 30.8 %all-to-all-start.12 = ((bf16[16,128,256]{2,1,0:T(8,128)(2,1)}), bf16[16,128,256]{2,1,0:T(8,128)(2,1)S(1)}, u32[]{:S(2)}, u32[]{:S(2)}) async-start(bf16[16,128,256]{2,1,0:T(8,128)(2,1)} %pack_last.1), calls=%async_computation.12 | async-start | bytes 2097152 | tf_op jit(solution)/shard_map/all_to_all | solution.py:1043
  283.7 26.9 %copy-start.5 = (f32[1,1920]{1,0:T(1,128)S(1)}, f32[1,1920]{1,0:T(1,128)}, u32[]{:S(2)}) copy-start(f32[1,1920]{1,0:T(1,128)} %get-tuple-element.172) | copy-start | bytes 23044
  283.7 27.5 %copy-start.4 = (f32[1,1920]{1,0:T(1,128)S(1)}, f32[1,1920]{1,0:T(1,128)}, u32[]{:S(2)}) copy-start(f32[1,1920]{1,0:T(1,128)} %get-tuple-element.173) | copy-start | bytes 23044
  308.2 3.7 %collective-permute-start.6 = (f32[400,256]{1,0:T(8,128)S(1)}, f32[400,256]{1,0:T(8,128)S(1)}, u32[]{:S(2)}, u32[]{:S(2)}) collective-permute-start(f32[400,256]{1,0:T(8,128)S(1)} %sum_last.1.mine_ref), channel_id=1, source_target_pairs={{0,1},{1,0},{2,3},{3,2},{4,5},{5,4},{6,7},{7,6},{8,9},{9,8},{10,11... | collective-permute-start | bytes 1228808 | tf_op jit(solution)/shard_map/ppermute | solution.py:1010

commit v6 on v5

--- a/solution.py
+++ b/solution.py
@@ -599,8 +599,8 @@
 
 def back_three_kernel(
     step, per, three_ref, got_ref, hid_ref, comb_ref, u3_ref, a2_ref, slope_ref,
-    hat_ref, w3_ref, cu_ref, gw_ref, csum_ref, att_ref, fc_ref,
-    p_ref, t1_ref, t3_ref, duz_ref, w3g_ref, fcg_ref, norm_ref, s_ref, c_ref, send_ref, datt_ref, k_ref,
+    hat_ref, w3_ref, cu_ref, gw_ref, csum_ref, att_ref, fc_ref, core_ref,
+    p_ref, t1_ref, t3_ref, duz_ref, keep_ref, give_ref, fcg_ref, norm_ref, s_ref, c_ref, send_ref, datt_ref, k_ref,
 ):
     if step is BEGIN:
         mean, inv = three_ref[0:1], three_ref[1:2]
@@ -622,7 +622,14 @@
     if step is END:
         csum = jnp.broadcast_to(csum_ref[...], (8, WIDTH))
         outer = high_rows(csum, jnp.broadcast_to(k_ref[0:1], (8, C_IN))) * 0.125
-        w3g_ref[...] = cu_ref[...] - outer - gw_ref[...] * k_ref[1:2]
+        w3g = cu_ref[...] - outer - gw_ref[...] * k_ref[1:2]
+
+        def put(core):
+            keep_ref[...] = w3g[:, core * 512 : (core + 1) * 512]
+            give_ref[...] = w3g[:, (1 - core) * 512 : (2 - core) * 512]
+
+        for core in range(2):
+            pl.when(core_ref[0] == core)(functools.partial(put, core))
         att = att_ref[...]
         datt = datt_ref[...]
         both = att * datt
@@ -693,7 +700,7 @@
 
 def back_two_kernel(
     step, per, sides_ref, one_ref, two_ref, got_ref, comb_ref, p_ref, s_ref, c_ref, slope_ref, hat2_ref, hat1_ref, att_ref,
-    dpool_ref, w_ref, gain_ref, shift_ref, dh2_ref, u1_ref, norm_ref, send_ref,
+    dpool_ref, w_ref, gain_ref, shift_ref, fc_ref, dh2_ref, u1_ref, norm_ref, send_ref,
     vec_ref, pad_ref, acc_ref,
 ):
     if step is BEGIN:
@@ -710,7 +717,15 @@
         return
 
     if step is END:
-        send_rows(send_ref, [row_sum(acc_ref[0:8]), row_sum(acc_ref[8:16])])
+        rows = []
+        for k in range(2):
+            both = row_sum(acc_ref[8 * k : 8 * k + 8])
+            rows += [both[:, :HALF], both[:, HALF:]]
+        sums = jnp.concatenate(rows, axis=0)
+        devices, height, _ = send_ref.shape
+        for d in range(devices):
+            send_ref[d, pl.ds(0, 4)] = sums
+            send_ref[d, pl.ds(4, height - 4)] = fc_ref[pl.ds(d * (height - 4), height - 4)]
         return
 
     first, last = edge_masks(HALF)
@@ -834,14 +849,15 @@
         count = one_ref[2:3]
         scale = one_ref[1:2] * gain_ref[:, :WIDTH]
         sums = total(got_ref)
+        sums = [jnp.concatenate([sums[k : k + 1], sums[k + 1 : k + 2]], axis=1) for k in (0, 2)]
         for row, out_ref in ((0, gain_out_ref), (1, shift_out_ref)):
-            out_ref[:, :WIDTH] = sums[1 - row : 2 - row]
+            out_ref[:, :WIDTH] = sums[1 - row]
             out_ref[:, WIDTH : 3 * WIDTH] = norm2_ref[row : row + 1]
             out_ref[:, 3 * WIDTH : 3 * WIDTH + INTER] = norm_att_ref[row : row + 1]
             out_ref[:, 3 * WIDTH + INTER :] = norm3_ref[row : row + 1]
         vec_ref[0:1] = scale
-        vec_ref[1:2] = scale * sums[0:1] / count
-        vec_ref[2:3] = scale * sums[1:2] / count
+        vec_ref[1:2] = scale * sums[0] / count
+        vec_ref[2:3] = scale * sums[1] / count
         acc_ref[...] = jnp.zeros_like(acc_ref)
         return
 
@@ -884,30 +900,6 @@
     return -(-value // multiple) * multiple
 
 
-def pack_three_kernel(core_ref, w_ref, fc_ref, keep_ref, give_ref):
-    shards = keep_ref.shape[0]
-    w_rows = w_ref.shape[0] // shards
-    fc_rows = fc_ref.shape[0] // (2 * shards)
-
-    def put(half, out_ref):
-        for f in range(shards):
-            for b in range(4):
-                low = (half * 4 + b) * 128
-                out_ref[f, pl.ds(b * w_rows, w_rows)] = w_ref[
-                    pl.ds(f * w_rows, w_rows), pl.ds(low, 128)
-                ]
-            out_ref[f, pl.ds(4 * w_rows, fc_rows)] = fc_ref[
-                pl.ds((half * shards + f) * fc_rows, fc_rows)
-            ]
-
-    for core in range(2):
-
-        @pl.when(core_ref[0] == core)
-        def _():
-            put(core, keep_ref)
-            put(1 - core, give_ref)
-
-
 def two_wide(part, rows):
     missing = 2 * rows - part.shape[0]
     if missing:
@@ -915,8 +907,13 @@
     return jnp.concatenate([part[:rows], part[rows:]], axis=1)
 
 
-def slot_rows(two_rows, fc_rows, one_rows):
-    return round_up(two_rows, 16), round_up(fc_rows, 32) // 2, round_up(one_rows, 32) // 2
+def slot_rows(two_rows, fc_rows, one_rows, three_rows):
+    return (
+        round_up(two_rows, 16),
+        round_up(fc_rows, 32) // 2,
+        round_up(one_rows, 32) // 2,
+        round_up(2 * three_rows, 16),
+    )
 
 
 def add_slots(ref, at, rows):
@@ -927,37 +924,47 @@
     return both
 
 
+def lengthen(part, rows):
+    if rows == part.shape[0]:
+        return part
+    return jnp.concatenate([part, jnp.zeros((rows - part.shape[0], part.shape[1]), F32)], axis=0)
+
+
 def pack_last_kernel(
-    fc_rows, keep2_ref, other2_ref, keep1_ref, other1_ref, three_ref, out_ref
+    fc_rows, keep2_ref, other2_ref, keep1_ref, other1_ref, keep3_ref, other3_ref, got_ref, out_ref
 ):
     shards = out_ref.shape[0]
     two_rows = keep2_ref.shape[0] // shards
     one_rows = keep1_ref.shape[0] // shards
-    two_slot, fc_slot, one_slot = slot_rows(two_rows, fc_rows, one_rows)
-    fc = add_slots(three_ref, three_ref.shape[1] - fc_rows, fc_rows)
-    fc = two_wide(fc, fc_slot).astype(BF16)
+    three_rows = keep3_ref.shape[0] // shards
+    two_slot, fc_slot, one_slot, three_slot = slot_rows(two_rows, fc_rows, one_rows, three_rows)
+    fc = two_wide(add_slots(got_ref, 4, fc_rows), fc_slot).astype(BF16)
     for f in range(shards):
         rows = pl.ds(f * two_rows, two_rows)
-        part = keep2_ref[rows] + other2_ref[rows]
-        if two_slot > two_rows:
-            part = jnp.concatenate([part, jnp.zeros((two_slot - two_rows, WIDTH), F32)], axis=0)
+        part = lengthen(keep2_ref[rows] + other2_ref[rows], two_slot)
         out_ref[f, pl.ds(0, two_slot)] = part.astype(BF16)
-        out_ref[f, pl.ds(two_slot, fc_slot)] = fc
+        at = two_slot
+        out_ref[f, pl.ds(at, fc_slot)] = fc
+        at += fc_slot
         rows = pl.ds(f * one_rows, one_rows)
         part = two_wide(keep1_ref[rows] + other1_ref[rows], one_slot)
-        out_ref[f, pl.ds(two_slot + fc_slot, one_slot)] = part.astype(BF16)
-
-
-def sum_last_kernel(two_rows, fc_rows, one_rows, parts_ref, three_ref, out_ref):
+        out_ref[f, pl.ds(at, one_slot)] = part.astype(BF16)
+        at += one_slot
+        rows = pl.ds(f * three_rows, three_rows)
+        part = keep3_ref[rows] + other3_ref[rows]
+        part = jnp.concatenate([part[:, :WIDTH], part[:, WIDTH:]], axis=0)
+        out_ref[f, pl.ds(at, three_slot)] = lengthen(part, three_slot).astype(BF16)
+
+
+def sum_last_kernel(two_rows, fc_rows, one_rows, three_rows, parts_ref, out_ref):
     shards = parts_ref.shape[0]
-    two_slot, fc_slot, one_slot = slot_rows(two_rows, fc_rows, one_rows)
+    two_slot, fc_slot, one_slot, three_slot = slot_rows(two_rows, fc_rows, one_rows, three_rows)
     out_ref[pl.ds(0, two_slot)] = add_slots(parts_ref, 0, two_slot)
-    out_ref[pl.ds(two_slot, one_slot)] = add_slots(parts_ref, two_slot + fc_slot, one_slot)
-    at = two_slot + one_slot
-    three_half = (three_ref.shape[1] - fc_rows) // 2
-    three = add_slots(three_ref, 0, 2 * three_half)
-    out_ref[pl.ds(at, three_half)] = two_wide(three, three_half)
-    at += three_half
+    after = two_slot + fc_slot
+    out_ref[pl.ds(two_slot, one_slot + three_slot)] = add_slots(
+        parts_ref, after, one_slot + three_slot
+    )
+    at = two_slot + one_slot + three_slot
     for f in range(shards):
         out_ref[pl.ds(at + f * fc_slot, fc_slot)] = parts_ref[f, pl.ds(two_slot, fc_slot)].astype(F32)
 
@@ -966,10 +973,9 @@
     two_rows, fc_rows, one_rows, three_rows, core_ref, mine_ref, other_ref,
     one_ref, two_ref, three_ref, fc1_ref, fc2_ref, pack_ref,
 ):
-    two_slot, fc_slot, one_slot = slot_rows(two_rows, fc_rows, one_rows)
-    three_half = 2 * three_rows
+    two_slot, fc_slot, one_slot, three_slot = slot_rows(two_rows, fc_rows, one_rows, three_rows)
     at_three = two_slot + one_slot
-    at_fc = at_three + three_half
+    at_fc = at_three + three_slot
     shards = (mine_ref.shape[0] - at_fc) // fc_slot
 
     def tall(ref, at, half_rows, rows):
@@ -981,12 +987,11 @@
     def put(half, ref):
         two_ref[:, half * WIDTH : (half + 1) * WIDTH] = ref[pl.ds(0, two_rows)]
         one_ref[:, half * HALF : (half + 1) * HALF] = tall(ref, two_slot, one_slot, one_rows)
-        three = tall(ref, at_three, three_half, 4 * three_rows)
-        for b in range(4):
-            low = half * 512 + b * 128
-            three_ref[:, low : low + 128] = three[b * three_rows : (b + 1) * three_rows]
+        for b in range(2):
+            low = (half * 2 + b) * WIDTH
+            three_ref[:, low : low + WIDTH] = ref[pl.ds(at_three + b * three_rows, three_rows)]
         for f in range(shards):
-            pack_ref[pl.ds((half * shards + f) * fc_rows, fc_rows)] = tall(
+            pack_ref[pl.ds((2 * f + half) * fc_rows, fc_rows)] = tall(
                 ref, at_fc + f * fc_slot, fc_slot, fc_rows
             )
 
@@ -1243,7 +1248,7 @@
     )
 
     per, steps = split(PER_BACK_THREE)
-    p, t1, t3, duz, w3_local, fc2_local, norm3, corr_weight, corr_row, send = stream_call(
+    p, t1, t3, duz, keep_three, give_three, fc2_local, norm3, corr_weight, corr_row, send = stream_call(
         lambda step, *refs, per=per: back_three_kernel(step, per, *refs),
         per,
         steps,
@@ -1262,13 +1267,15 @@
             full(csum),
             full(att),
             full(fc_second),
+            core_in,
         ],
         [
             blocks_out(WIDTH, over=3),
             small(images, 2 * WIDTH),
             small(images, 2 * WIDTH),
             small(images, INTER),
-            small(WIDTH, C_IN),
+            small(WIDTH, C_IN // 2),
+            small(WIDTH, C_IN // 2),
             small(4 * INTER, 128),
             small(2, C_IN),
             ((WIDTH, WIDTH), BF16, whole((WIDTH, WIDTH))),
@@ -1312,21 +1319,9 @@
         name="back_att",
     )
     got_back_two = everyone(send)
-
     shards = lax.axis_size("fsdp")
     w3_rows = WIDTH // shards
-    fc_rows = packed.shape[0] // (2 * shards)
-    slot = (shards, 4 * w3_rows + fc_rows, 128)
-    keep, give = call(
-        pack_three_kernel,
-        1,
-        [core_in, full(w3_local), full(packed)],
-        [(slot, F32, whole(slot)), (slot, F32, whole(slot))],
-        flops=1000000,
-        moved=3000000,
-        name="pack_three",
-    )
-    three = slots(keep + other_core(give))
+    fc_rows = packed.shape[0] // devices
 
     per, steps = split(PER_BACK_TWO)
     dh2, u1, norm2, send = stream_call(
@@ -1350,12 +1345,13 @@
             full(full_two),
             gain_in,
             shift_in,
+            full(packed),
         ],
         [
             blocks_out(2 * WIDTH),
             blocks_out(WIDTH),
             small(2, 2 * WIDTH),
-            payload(2, WIDTH),
+            payload(4 + fc_rows, 128),
         ],
         [
             pltpu.VMEM((8, 2 * WIDTH), F32),
@@ -1366,7 +1362,6 @@
         moved=rows * WIDTH * 20,
         name="back_two",
     )
-    send, three, dh2 = lax.optimization_barrier((send, three, dh2))
     got_back_one = everyone(send)
 
     per, steps = split(PER_WEIGHT_TWO)
@@ -1419,8 +1414,8 @@
     )
 
     two_rows, one_rows = 9 * HALF // shards, C_IN // shards
-    two_slot, fc_slot, one_slot = slot_rows(two_rows, fc_rows, one_rows)
-    slot = (shards, two_slot + fc_slot + one_slot, WIDTH)
+    two_slot, fc_slot, one_slot, three_slot = slot_rows(two_rows, fc_rows, one_rows, w3_rows)
+    slot = (shards, two_slot + fc_slot + one_slot + three_slot, WIDTH)
     (parts,) = call(
         functools.partial(pack_last_kernel, fc_rows),
         1,
@@ -1429,7 +1424,9 @@
             near(other_core(give)),
             full(keep_one),
             near(other_core(give_one)),
-            near(three),
+            full(keep_three),
+            near(other_core(give_three)),
+            near(got_back_one),
         ],
         [(slot, BF16, whole(slot))],
         flops=1000000,
@@ -1453,11 +1450,11 @@
     )
 
     parts, input_grad = lax.optimization_barrier((parts, input_grad))
-    sums = (two_slot + one_slot + 2 * w3_rows + shards * fc_slot, WIDTH)
+    sums = (two_slot + one_slot + three_slot + shards * fc_slot, WIDTH)
     (mine,) = call(
-        functools.partial(sum_last_kernel, two_rows, fc_rows, one_rows),
+        functools.partial(sum_last_kernel, two_rows, fc_rows, one_rows, w3_rows),
         1,
-        [near(parts), near(three)],
+        [near(parts)],
         [(sums, F32, whole(sums), True)],
         flops=1000000,
         moved=2000000,

time: 314 us -> 311 us (level)
  starting transfers between devices: 59 us -> 48.1 us
  blocking collectives: 36.3 us -> 46.4 us
    all_to_all x2 -> x3, blocking collectives: 22.8 us -> 32.9 us  [everyone(): return lax.all_to_all(payload, AXES, 0, 0, tiled=True)]
    all_to_all x4 -> x3, waiting for transfers between devices: 18.1 us -> 23.6 us  [slots(): return lax.all_to_all(parts, 'fsdp', 0, 0, tiled=True)]
    all_to_all x4 -> x3, starting transfers between devices: 21.5 us -> 16.1 us  [slots(): return lax.all_to_all(parts, 'fsdp', 0, 0, tiled=True)]
    all_to_all x6 -> x5, starting transfers between devices: 27.7 us -> 22.8 us  [everyone(): return lax.all_to_all(payload, AXES, 0, 0, tiled=True)]
    all_to_all x6 -> x5, waiting for transfers between devices: 19.2 us -> 15.1 us  [everyone(): return lax.all_to_all(payload, AXES, 0, 0, tiled=True)]
    pallas_call x8 -> x7, Pallas kernels: 12.7 us -> 10.5 us  [call(): pl.pallas_call(kernel, grid=(grid,), in_specs=[spec for _, spec, *_ in in...]
  transfers between devices with their start and end apart: 17 -> 15, of which waited for: 10 -> 9; matrix products, arithmetic and copies ran while one was open for 1% -> 1% of each run, Pallas kernels for 35% -> 28%
where the time goes in v6:
time: 311 us; the launch traced here: 310 us
  Pallas kernels  170 us (55%)
  starting transfers between devices  48.1 us (15%)
  blocking collectives  46.4 us (15%)
  waiting for transfers between devices  41.7 us (13%)
    pallas_call x11, Pallas kernels, stream_call(): pl.pallas_call(whole_kernel, in_specs=in_specs, out_specs=out_specs, out_...  159 us
    all_to_all x3, blocking collectives, everyone(): return lax.all_to_all(payload, AXES, 0, 0, tiled=True)  32.9 us
    all_to_all x3, waiting for transfers between devices, slots(): return lax.all_to_all(parts, 'fsdp', 0, 0, tiled=True)  23.6 us
    all_to_all x5, starting transfers between devices, everyone(): return lax.all_to_all(payload, AXES, 0, 0, tiled=True)  22.8 us
    all_to_all x3, starting transfers between devices, slots(): return lax.all_to_all(parts, 'fsdp', 0, 0, tiled=True)  16.1 us
    all_to_all x5, waiting for transfers between devices, everyone(): return lax.all_to_all(payload, AXES, 0, 0, tiled=True)  15.1 us
    all_to_all x1, blocking collectives, slots(): return lax.all_to_all(parts, 'fsdp', 0, 0, tiled=True)  13.5 us
    pallas_call x7, Pallas kernels, call(): pl.pallas_call(kernel, grid=(grid,), in_specs=[spec for _, spec, *_ in in...  10.5 us
  transfers between devices with their start and end apart: 15, of which 9 were waited for; matrix products, arithmetic and copies ran while one was open for 1% of the time, Pallas kernels for 28%

profile of v6, /device:TPU:9, one launch (start us, length us, event | category | flops | bytes accessed | tf_op | source)
XLA Modules:
  0.0 309.7 jit_solution(12676721442858122065)
XLA Ops:
  0.6 2.0 pack.1
  2.6 13.5 %all_to_all.60.refs_3_ = bf16[16,64,128]{2,1,0:T(8,128)(2,1)S(1)} all-to-all(bf16[16,64,128]{2,1,0:T(8,128)(2,1)S(1)} %get-tuple-element.89), channel_id=1, replica_groups=mesh['fsdp'=16,'dp'=2] {'fsdp'}, dimensions={0} | all-to-all | bytes 524288 | tf_op jit(solution)/shard_map/all_to_all | solution.py:1048
  16.1 3.2 %collective-permute-start = (bf16[16,64,128]{2,1,0:T(8,128)(2,1)S(1)}, bf16[16,64,128]{2,1,0:T(8,128)(2,1)S(1)}, u32[]{:S(2)}, u32[]{:S(2)}) collective-permute-start(bf16[16,64,128]{2,1,0:T(8,128)(2,1)S(1)} %all_to_all.60.refs_3_), channel_id=1, source_target_pairs={{0,1},{1,0},{2,3},{3,2},{4,5},{5,4},{6,7},{7,6},{8,9},{9,8},{10,11... | collective-permute-start | bytes 786440 | tf_op jit(solution)/shard_map/ppermute | solution.py:1015
  19.3 1.2 collective-permute-done.refs_4_
  20.5 4.0 %all-to-all-start.1 = ((bf16[16,144,128]{2,1,0:T(8,128)(2,1)}), bf16[16,144,128]{2,1,0:T(8,128)(2,1)S(1)}, u32[]{:S(2)}, u32[]{:S(2)}) async-start(bf16[16,144,128]{2,1,0:T(8,128)(2,1)} %get-tuple-element.93), calls=%async_computation.1 | async-start | bytes 1179648 | tf_op jit(solution)/shard_map/all_to_all | solution.py:1048
  24.5 0.6 copy-done
  25.2 9.5 %conv_one.1 = (f32[6144,256]{1,0:T(8,128)}, bf16[1024,256]{1,0:T(8,128)(2,1)}, f32[32,4,256]{2,1,0:T(4,128)}) custom-call(s32[1]{0:T(128)} %bitcast.core_ref.refs_0_.refs_14_, s32[24]{0:T(128)S(1)} %copy-done, bf16[6144,1024]{1,0:T(8,128)(2,1)} %bitcast.7, bf16[16,64,128]{2,1,0:T(8,128)(2,1)S(1)} %all_to_all.60.refs_3_, ...), custom_call_target="tpu_custom_call" | custom-call | flops 3221225472 | bytes 18874368 | tf_op jit(solution)/shard_map/conv_one/pallas_call | solution.py:266
  34.7 5.1 %all-to-all-done.1.mine_ref = bf16[16,144,128]{2,1,0:T(8,128)(2,1)S(1)} async-done(((bf16[16,144,128]{2,1,0:T(8,128)(2,1)}), bf16[16,144,128]{2,1,0:T(8,128)(2,1)S(1)}, u32[]{:S(2)}, u32[]{:S(2)}) %all-to-all-start.1) | async-done | bytes 589856 | tf_op jit(solution)/shard_map/all_to_all | solution.py:1048
  39.7 1.9 collective-permute-start.1
  41.6 3.1 %all-to-all-start.2 = ((f32[32,4,256]{2,1,0:T(4,128)}), f32[32,4,256]{2,1,0:T(4,128)S(1)}, u32[]{:S(2)}, u32[]{:S(2)}) async-start(f32[32,4,256]{2,1,0:T(4,128)} %get-tuple-element.94), calls=%async_computation.2 | async-start | bytes 262144 | tf_op jit(solution)/shard_map/all_to_all | solution.py:1011
  44.8 0.0 copy-done.2
  44.8 0.6 reshape.55.refs_4_.refs_6_.refs_7_.gain_ref.refs_14_
  45.4 0.0 copy-done.3
  45.4 0.6 reshape.56.refs_5_.refs_7_.refs_8_.refs_15_
  46.0 0.0 collective-permute-done.1.other_ref
  46.0 1.4 unpack.2.refs_3_.refs_13_
  47.4 3.5 %all-to-all-done.2.refs_1_ = f32[32,4,256]{2,1,0:T(4,128)S(1)} async-done(((f32[32,4,256]{2,1,0:T(4,128)}), f32[32,4,256]{2,1,0:T(4,128)S(1)}, u32[]{:S(2)}, u32[]{:S(2)}) %all-to-all-start.2) | async-done | bytes 131104 | tf_op jit(solution)/shard_map/all_to_all | solution.py:1011
  50.9 5.5 %all-to-all-start.3 = ((bf16[16,64,128]{2,1,0:T(8,128)(2,1)}), bf16[16,64,128]{2,1,0:T(8,128)(2,1)S(1)}, u32[]{:S(2)}, u32[]{:S(2)}) async-start(bf16[16,64,128]{2,1,0:T(8,128)(2,1)} %get-tuple-element.102), calls=%async_computation.3 | async-start | bytes 524288 | tf_op jit(solution)/shard_map/all_to_all | solution.py:1048
  56.4 0.0 copy-done.1
  56.4 17.3 %conv_two.1 = (bf16[6144,256]{1,0:T(8,128)(2,1)}, f32[6144,512]{1,0:T(8,128)}, f32[8,256]{1,0:T(8,128)}, f32[32,2,512]{2,1,0:T(2,128)}) custom-call(s32[24]{0:T(128)S(1)} %copy-done.1, f32[32,4,256]{2,1,0:T(4,128)S(1)} %all-to-all-done.2.refs_1_, f32[6144,256]{1,0:T(8,128)} %get-tuple-element.98.refs_2_, bf16[1152,512]{1,0:T(8,128)(2,1)} %unpack.2.refs_3_.refs_13_, ...), custom_call_target="tpu_custom_call" | custom-call | flops 7247757312 | bytes 22020096 | tf_op jit(solution)/shard_map/conv_two/pallas_call | solution.py:266
  73.7 0.0 all-to-all-done.3.mine_ref
  73.7 6.0 %all-to-all-start.4 = ((f32[32,2,512]{2,1,0:T(2,128)}), f32[32,2,512]{2,1,0:T(2,128)S(1)}, u32[]{:S(2)}, u32[]{:S(2)}) async-start(f32[32,2,512]{2,1,0:T(2,128)} %get-tuple-element.103), calls=%async_computation.4 | async-start | bytes 262144 | tf_op jit(solution)/shard_map/all_to_all | solution.py:1011
  79.7 0.4 collective-permute-start.2
  80.1 5.7 %all-to-all-done.4.refs_2_ = f32[32,2,512]{2,1,0:T(2,128)S(1)} async-done(((f32[32,2,512]{2,1,0:T(2,128)}), f32[32,2,512]{2,1,0:T(2,128)S(1)}, u32[]{:S(2)}, u32[]{:S(2)}) %all-to-all-start.4) | async-done | bytes 131104 | tf_op jit(solution)/shard_map/all_to_all | solution.py:1011
  85.8 13.2 %act_two.1 = (bf16[6144,512]{1,0:T(8,128)(2,1)}, bf16[6144,512]{1,0:T(8,128)(2,1)}, bf16[6144,512]{1,0:T(8,128)(2,1)}, f32[24,256]{1,0:T(8,128)}, f32[24,128]{1,...) custom-call(s32[24]{0:T(128)S(1)} %copy-done.1, ...), custom_call_target="tpu_custom_call" | custom-call | flops 62914560 | bytes 31457280 | tf_op jit(solution)/shard_map/act_two/pallas_call | solution.py:266
  99.1 4.6 %all-to-all-start.5 = ((f32[32,2,128]{2,1,0:T(2,128)}), f32[32,2,128]{2,1,0:T(2,128)S(1)}, u32[]{:S(2)}, u32[]{:S(2)}) async-start(f32[32,2,128]{2,1,0:T(2,128)} %get-tuple-element.105), calls=%async_computation.5 | async-start | bytes 65536 | tf_op jit(solution)/shard_map/all_to_all | solution.py:1011
  103.7 0.0 collective-permute-done.2.other_ref
  103.7 0.9 unpack.3.refs_3_.refs_6_.refs_8_
  104.6 4.7 %all-to-all-done.5.refs_0_ = f32[32,2,128]{2,1,0:T(2,128)S(1)} async-done(((f32[32,2,128]{2,1,0:T(2,128)}), f32[32,2,128]{2,1,0:T(2,128)S(1)}, u32[]{:S(2)}, u32[]{:S(2)}) %all-to-all-start.5) | async-done | bytes 32800 | tf_op jit(solution)/shard_map/all_to_all | solution.py:1011
  109.3 7.1 %combine.1 = (f32[24,512]{1,0:T(8,128)}, bf16[6144,256]{1,0:T(8,128)(2,1)}, f32[256,1024]{1,0:T(8,128)}, f32[1,256]{1,0:T(1,128)}, f32[4,24,128]{2,1,0:T(8,128)}, /*index=5*/f32[32,2,1024]{2,1,0:T(2,128)S(1)}) custom-call(f32[32,2,128]{2,1,0:T(2,128)S(1)} %all-to-all-done.5.refs_0_, f32[24,128]{1,0:T(8,128)} %get-tuple-element.106.refs_1_, ...), custom_call_target="tpu_custom_call" | custom-call | flops 805306368 | bytes 9437184 | tf_op jit(solution)/shard_map/combine/pallas_call | solution.py:266
  116.5 12.1 %all_to_all.61.refs_2_ = f32[32,2,1024]{2,1,0:T(2,128)S(1)} all-to-all(f32[32,2,1024]{2,1,0:T(2,128)S(1)} %get-tuple-element.109), channel_id=1, replica_groups=mesh['fsdp'=16,'dp'=2] {'fsdp','dp'}, dimensions={0} | all-to-all | bytes 524288 | tf_op jit(solution)/shard_map/all_to_all | solution.py:1011
  128.5 24.8 %output.1 = (bf16[6144,1024]{1,0:T(8,128)(2,1)}, bf16[6144,1024]{1,0:T(8,128)(2,1)}, f32[8,1024]{1,0:T(8,128)}, f32[32,2,1024]{2,1,0:T(2,128)}) custom-call(s32[24]{0:T(128)S(1)} %copy-done.1, f32[8,256]{1,0:T(8,128)} %get-tuple-element.100.refs_1_.refs_2_, f32[32,2,1024]{2,1,0:T(2,128)S(1)} %all_to_all.61.refs_2_, ...), custom_call_target="tpu_custom_call" | custom-call | flops 3221225472 | bytes 50331648 | tf_op jit(solution)/shard_map/output/pallas_call | solution.py:266
  153.3 4.5 %all-to-all-start.7 = ((f32[32,2,1024]{2,1,0:T(2,128)}), f32[32,2,1024]{2,1,0:T(2,128)S(1)}, u32[]{:S(2)}, u32[]{:S(2)}) async-start(f32[32,2,1024]{2,1,0:T(2,128)} %get-tuple-element.114), calls=%async_computation.7 | async-start | bytes 524288 | tf_op jit(solution)/shard_map/all_to_all | solution.py:1011
  157.8 7.7 %outer_three.1.refs_9_ = f32[256,1024]{1,0:T(8,128)} custom-call(bf16[6144,256]{1,0:T(8,128)(2,1)} %get-tuple-element.110.refs_3_.refs_0_.refs_4_, bf16[6144,1024]{1,0:T(8,128)(2,1)} %get-tuple-element.116.refs_1_.refs_4_), custom_call_target="tpu_custom_call" | custom-call | flops 3221225472 | bytes 18874368 | tf_op jit(solution)/shard_map/outer_three/pallas_call | solution.py:266
  165.5 1.1 all-to-all-done.7.refs_1_
  166.6 18.5 %back_three.1 = (bf16[6144,256]{1,0:T(8,128)(2,1)}, f32[24,512]{1,0:T(8,128)}, f32[24,512]{1,0:T(8,128)}, f32[24,128]{1,0:T(8,128)}, f32[256,512]{1,0:T(8,128)},...) custom-call(f32[8,1024]{1,0:T(8,128)} %get-tuple-element.113.refs_0_, ...), custom_call_target="tpu_custom_call" | custom-call | flops 6442450944 | bytes 25165824 | tf_op jit(solution)/shard_map/back_three/pallas_call | solution.py:266
  185.1 10.8 %all_to_all.62.got_ref = f32[32,8,128]{2,1,0:T(8,128)S(1)} all-to-all(f32[32,8,128]{2,1,0:T(8,128)S(1)} %get-tuple-element.122), channel_id=1, replica_groups=mesh['fsdp'=16,'dp'=2] {'fsdp','dp'}, dimensions={0} | all-to-all | bytes 262144 | tf_op jit(solution)/shard_map/all_to_all | solution.py:1011
  195.9 2.3 back_att.1
  198.2 10.0 %all_to_all.63.refs_3_ = f32[32,2,512]{2,1,0:T(2,128)S(1)} all-to-all(f32[32,2,512]{2,1,0:T(2,128)S(1)} %get-tuple-element.130), channel_id=1, replica_groups=mesh['fsdp'=16,'dp'=2] {'fsdp','dp'}, dimensions={0} | all-to-all | bytes 262144 | tf_op jit(solution)/shard_map/all_to_all | solution.py:1011
  208.2 23.7 %back_two.1 = (bf16[6144,512]{1,0:T(8,128)(2,1)}, bf16[6144,256]{1,0:T(8,128)(2,1)}, f32[2,512]{1,0:T(2,128)}, f32[32,28,128]{2,1,0:T(8,128)}) custom-call(s32[24]{0:T(128)S(1)} %copy-done.1, f32[8,256]{1,0:T(8,128)} %get-tuple-element.100.refs_1_.refs_2_, f32[8,512]{1,0:T(8,128)} %get-tuple-element.112.refs_2_, f32[32,2,512]{2,1,0:T(2,128)S(1)} %all_to_all.63.refs_3_, ...), custom_call_target="tpu_custom_call" | custom-call | flops 7247757312 | bytes 31457280 | tf_op jit(solution)/shard_map/back_two/pallas_call | solution.py:266
  231.9 4.6 %all-to-all-start.10 = ((f32[32,28,128]{2,1,0:T(8,128)}), f32[32,28,128]{2,1,0:T(8,128)S(1)}, u32[]{:S(2)}, u32[]{:S(2)}) async-start(f32[32,28,128]{2,1,0:T(8,128)} %get-tuple-element.137), calls=%async_computation.10 | async-start | bytes 1048576 | tf_op jit(solution)/shard_map/all_to_all | solution.py:1011
  236.6 0.0 copy-start.6
  236.6 15.3 %weight_two.1 = (f32[1152,256]{1,0:T(8,128)}, f32[1152,256]{1,0:T(8,128)}) custom-call(s32[1]{0:T(128)} %bitcast.core_ref.refs_0_.refs_14_, s32[24]{0:T(128)S(1)} %copy-done.1, bf16[6144,256]{1,0:T(8,128)(2,1)} %get-tuple-element.134.refs_10_.refs_2_.refs_5_, bf16[6144,512]{1,0:T(8,128)(2,1)} %get-tuple-element.138.refs_3_, ...), custom_call_target="tpu_custom_call" | custom-call | flops 7247757312 | bytes 9437184 | tf_op jit(solution)/shard_map/weight_two/pallas_call | solution.py:266
  251.8 0.0 all-to-all-done.10.refs_3_.got_ref
  251.8 0.4 collective-permute-start.3
  252.3 0.0 copy-done.6
  252.3 0.1 collective-permute-start.5
  252.4 10.7 %back_one.1 = (bf16[6144,256]{1,0:T(8,128)(2,1)}, f32[1024,128]{1,0:T(8,128)}, f32[1024,128]{1,0:T(8,128)}, f32[1,1920]{1,0:T(1,128)}, f32[1,1920]{1,0:T(1,128)}) custom-call(s32[1]{0:T(128)} %bitcast.core_ref.refs_0_.refs_14_, s32[24]{0:T(128)S(1)} %copy-done.1, f32[8,256]{1,0:T(8,128)} %get-tuple-element.100.refs_1_.refs_2_, ...), custom_call_target="tpu_custom_call" | custom-call | flops 3221225472 | bytes 25165824 | tf_op jit(solution)/shard_map/back_one/pallas_call | solution.py:266
  263.1 0.5 collective-permute-start.4
  263.5 0.0 collective-permute-done.5.other3_ref
  263.5 1.7 collective-permute-done.4.other1_ref
  265.3 0.0 collective-permute-done.3.other2_ref
  265.3 2.9 pack_last.1
  268.2 6.5 %all-to-all-start.11 = ((bf16[16,160,256]{2,1,0:T(8,128)(2,1)}), bf16[16,160,256]{2,1,0:T(8,128)(2,1)S(1)}, u32[]{:S(2)}, u32[]{:S(2)}) async-start(bf16[16,160,256]{2,1,0:T(8,128)(2,1)} %pack_last.1), calls=%async_computation.11 | async-start | bytes 2621440 | tf_op jit(solution)/shard_map/all_to_all | solution.py:1048
  274.7 0.0 copy-start.4
  274.7 11.4 %input_grad.1 = bf16[6144,1024]{1,0:T(8,128)(2,1)} custom-call(bf16[6144,256]{1,0:T(8,128)(2,1)} %get-tuple-element.154.refs_0_, bf16[6144,1024]{1,0:T(8,128)(2,1)} %get-tuple-element.116.refs_1_.refs_4_, f32[8,1024]{1,0:T(8,128)} %get-tuple-element.113.refs_0_.refs_2_, bf16[1024,256]{1,0:T(8,128)(2,1)} %get-tuple-element.155.refs_3_), custom_call_target="tpu_custom_call" | custom-call | flops 3221225472 | bytes 31457280 | tf_op jit(solution)/shard_map/input_grad/pallas_call | solution.py:266
  286.1 18.5 %all-to-all-done.11.parts_ref = bf16[16,160,256]{2,1,0:T(8,128)(2,1)S(1)} async-done(((bf16[16,160,256]{2,1,0:T(8,128)(2,1)}), bf16[16,160,256]{2,1,0:T(8,128)(2,1)S(1)}, u32[]{:S(2)}, u32[]{:S(2)}) %all-to-all-start.11) | async-done | bytes 1310752 | tf_op jit(solution)/shard_map/all_to_all | solution.py:1048
  304.6 0.2 sum_last.1.mine_ref
  304.8 2.6 collective-permute-start.6
  307.4 0.0 copy-done.5
  307.4 0.6 reduce
  308.1 0.6 reduce.1
  308.7 0.1 collective-permute-done.6.other_ref
  308.8 0.9 finish.1
  (6 shorter events, 0.0 us)
Async XLA Ops:
  16.1 4.4 %collective-permute-start = (bf16[16,64,128]{2,1,0:T(8,128)(2,1)S(1)}, bf16[16,64,128]{2,1,0:T(8,128)(2,1)S(1)}, u32[]{:S(2)}, u32[]{:S(2)}) collective-permute-start(bf16[16,64,128]{2,1,0:T(8,128)(2,1)S(1)} %all_to_all.60.refs_3_), channel_id=1, source_target_pairs={{0,1},{1,0},{2,3},{3,2},{4,5},{5,4},{6,7},{7,6},{8,9},{9,8},{10,11... | collective-permute-start | bytes 786440 | tf_op jit(solution)/shard_map/ppermute | solution.py:1015
  20.5 19.2 %all-to-all-start.1 = ((bf16[16,144,128]{2,1,0:T(8,128)(2,1)}), bf16[16,144,128]{2,1,0:T(8,128)(2,1)S(1)}, u32[]{:S(2)}, u32[]{:S(2)}) async-start(bf16[16,144,128]{2,1,0:T(8,128)(2,1)} %get-tuple-element.93), calls=%async_computation.1 | async-start | bytes 1179648 | tf_op jit(solution)/shard_map/all_to_all | solution.py:1048
  24.5 0.7 copy-start
  25.2 19.6 %copy-start.2 = (f32[1920]{0:T(1024)S(1)}, f32[1920]{0:T(1024)}, u32[]{:S(2)}) copy-start(f32[1920]{0:T(1024)} %param.19) | copy-start | bytes 23044
  25.2 20.2 %copy-start.3 = (f32[1920]{0:T(1024)S(1)}, f32[1920]{0:T(1024)}, u32[]{:S(2)}) copy-start(f32[1920]{0:T(1024)} %param.20) | copy-start | bytes 23044
  25.2 31.2 %copy-start.1 = (s32[24]{0:T(128)S(1)}, s32[24]{0:T(128)}, u32[]{:S(2)}) copy-start(s32[24]{0:T(128)} %refs_1_.7) | copy-start | bytes 292
  39.7 6.3 %collective-permute-start.1 = (bf16[16,144,128]{2,1,0:T(8,128)(2,1)S(1)}, bf16[16,144,128]{2,1,0:T(8,128)(2,1)S(1)}, u32[]{:S(2)}, u32[]{:S(2)}) collective-permute-start(bf16[16,144,128]{2,1,0:T(8,128)(2,1)S(1)} %all-to-all-done.1.mine_ref), channel_id=1, source_target_pairs={{0,1},{1,0},{2,3},{3,2},{4,5},{5,4},{6,7},{7,6},{8,9},{9,8},{10,11... | collective-permute-start | bytes 1769480 | tf_op jit(solution)/shard_map/ppermute | solution.py:1015
  41.6 9.3 %all-to-all-start.2 = ((f32[32,4,256]{2,1,0:T(4,128)}), f32[32,4,256]{2,1,0:T(4,128)S(1)}, u32[]{:S(2)}, u32[]{:S(2)}) async-start(f32[32,4,256]{2,1,0:T(4,128)} %get-tuple-element.94), calls=%async_computation.2 | async-start | bytes 262144 | tf_op jit(solution)/shard_map/all_to_all | solution.py:1011
  50.9 22.8 %all-to-all-start.3 = ((bf16[16,64,128]{2,1,0:T(8,128)(2,1)}), bf16[16,64,128]{2,1,0:T(8,128)(2,1)S(1)}, u32[]{:S(2)}, u32[]{:S(2)}) async-start(bf16[16,64,128]{2,1,0:T(8,128)(2,1)} %get-tuple-element.102), calls=%async_computation.3 | async-start | bytes 524288 | tf_op jit(solution)/shard_map/all_to_all | solution.py:1048
  73.7 12.1 %all-to-all-start.4 = ((f32[32,2,512]{2,1,0:T(2,128)}), f32[32,2,512]{2,1,0:T(2,128)S(1)}, u32[]{:S(2)}, u32[]{:S(2)}) async-start(f32[32,2,512]{2,1,0:T(2,128)} %get-tuple-element.103), calls=%async_computation.4 | async-start | bytes 262144 | tf_op jit(solution)/shard_map/all_to_all | solution.py:1011
  79.7 24.0 %collective-permute-start.2 = (bf16[16,64,128]{2,1,0:T(8,128)(2,1)S(1)}, bf16[16,64,128]{2,1,0:T(8,128)(2,1)S(1)}, u32[]{:S(2)}, u32[]{:S(2)}) collective-permute-start(bf16[16,64,128]{2,1,0:T(8,128)(2,1)S(1)} %all-to-all-done.3.mine_ref), channel_id=1, source_target_pairs={{0,1},{1,0},{2,3},{3,2},{4,5},{5,4},{6,7},{7,6},{8,9},{9,8},{10,11... | collective-permute-start | bytes 786440 | tf_op jit(solution)/shard_map/ppermute | solution.py:1015
  99.1 10.3 %all-to-all-start.5 = ((f32[32,2,128]{2,1,0:T(2,128)}), f32[32,2,128]{2,1,0:T(2,128)S(1)}, u32[]{:S(2)}, u32[]{:S(2)}) async-start(f32[32,2,128]{2,1,0:T(2,128)} %get-tuple-element.105), calls=%async_computation.5 | async-start | bytes 65536 | tf_op jit(solution)/shard_map/all_to_all | solution.py:1011
  153.3 13.2 %all-to-all-start.7 = ((f32[32,2,1024]{2,1,0:T(2,128)}), f32[32,2,1024]{2,1,0:T(2,128)S(1)}, u32[]{:S(2)}, u32[]{:S(2)}) async-start(f32[32,2,1024]{2,1,0:T(2,128)} %get-tuple-element.114), calls=%async_computation.7 | async-start | bytes 524288 | tf_op jit(solution)/shard_map/all_to_all | solution.py:1011
  231.9 19.9 %all-to-all-start.10 = ((f32[32,28,128]{2,1,0:T(8,128)}), f32[32,28,128]{2,1,0:T(8,128)S(1)}, u32[]{:S(2)}, u32[]{:S(2)}) async-start(f32[32,28,128]{2,1,0:T(8,128)} %get-tuple-element.137), calls=%async_computation.10 | async-start | bytes 1048576 | tf_op jit(solution)/shard_map/all_to_all | solution.py:1011
  236.6 15.7 %copy-start.6 = (f32[256,512]{1,0:T(8,128)S(1)}, f32[256,512]{1,0:T(8,128)}, u32[]{:S(2)}) copy-start(f32[256,512]{1,0:T(8,128)} %get-tuple-element.152) | copy-start | bytes 1572868
  251.8 13.4 %collective-permute-start.3 = (f32[1152,256]{1,0:T(8,128)}, f32[1152,256]{1,0:T(8,128)S(1)}, u32[]{:S(2)}, u32[]{:S(2)}) collective-permute-start(f32[1152,256]{1,0:T(8,128)} %get-tuple-element.148), channel_id=1, source_target_pairs={{0,1},{1,0},{2,3},{3,2},{4,5},{5,4},{6,7},{7,6},{8,9},{9,8},{10,11... | collective-permute-start | bytes 3538952 | tf_op jit(solution)/shard_map/ppermute | solution.py:1015
  252.3 11.3 %collective-permute-start.5 = (f32[256,512]{1,0:T(8,128)S(1)}, f32[256,512]{1,0:T(8,128)S(1)}, u32[]{:S(2)}, u32[]{:S(2)}) collective-permute-start(f32[256,512]{1,0:T(8,128)S(1)} %copy-done.6), channel_id=1, source_target_pairs={{0,1},{1,0},{2,3},{3,2},{4,5},{5,4},{6,7},{7,6},{8,9},{9,8},{10,11... | collective-permute-start | bytes 1572872 | tf_op jit(solution)/shard_map/ppermute | solution.py:1015
  263.1 2.2 collective-permute-start.4
  268.2 36.5 %all-to-all-start.11 = ((bf16[16,160,256]{2,1,0:T(8,128)(2,1)}), bf16[16,160,256]{2,1,0:T(8,128)(2,1)S(1)}, u32[]{:S(2)}, u32[]{:S(2)}) async-start(bf16[16,160,256]{2,1,0:T(8,128)(2,1)} %pack_last.1), calls=%async_computation.11 | async-start | bytes 2621440 | tf_op jit(solution)/shard_map/all_to_all | solution.py:1048
  274.7 32.8 %copy-start.5 = (f32[1,1920]{1,0:T(1,128)S(1)}, f32[1,1920]{1,0:T(1,128)}, u32[]{:S(2)}) copy-start(f32[1,1920]{1,0:T(1,128)} %get-tuple-element.164) | copy-start | bytes 23044
  274.7 33.4 %copy-start.4 = (f32[1,1920]{1,0:T(1,128)S(1)}, f32[1,1920]{1,0:T(1,128)}, u32[]{:S(2)}) copy-start(f32[1,1920]{1,0:T(1,128)} %get-tuple-element.165) | copy-start | bytes 23044
  304.8 4.0 %collective-permute-start.6 = (f32[400,256]{1,0:T(8,128)S(1)}, f32[400,256]{1,0:T(8,128)S(1)}, u32[]{:S(2)}, u32[]{:S(2)}) collective-permute-start(f32[400,256]{1,0:T(8,128)S(1)} %sum_last.1.mine_ref), channel_id=1, source_target_pairs={{0,1},{1,0},{2,3},{3,2},{4,5},{5,4},{6,7},{7,6},{8,9},{9,8},{10,11... | collective-permute-start | bytes 1228808 | tf_op jit(solution)/shard_map/ppermute | solution.py:1015

commit v7 on v6

--- a/solution.py
+++ b/solution.py
@@ -23,7 +23,7 @@
 AHEAD = 4
 VMEM = 44
 CHUNK = 32
-PER_CONV_ONE = 4
+PER_CONV_ONE = 3
 PER_CONV_TWO = 3
 PER_ACT_TWO = 4
 PER_COMBINE = 6
@@ -1143,7 +1143,6 @@
     )
     send, mine_three = lax.optimization_barrier((send, mine_three))
     got_two = everyone(send)
-    full_three = join_weight(core, mine_three, (WIDTH, C_IN))
 
     per, steps = split(PER_ACT_TWO)
     hat2, a2, slope2, pooled, zin, t2, t4, stat2, send = stream_call(
@@ -1174,7 +1173,9 @@
         moved=rows * 2 * WIDTH * 10,
         name="act_two",
     )
+    send, mine_three = lax.optimization_barrier((send, mine_three))
     got_att = everyone(send)
+    full_three = join_weight(core, mine_three, (WIDTH, C_IN))
 
     per, steps = split(PER_COMBINE)
     att, comb, gw, csum, hid, send = stream_call(

time: 311 us -> 311 us (level)
  blocking collectives: 46.4 us -> 58.3 us
  starting transfers between devices: 48.1 us -> 41.8 us
  waiting for transfers between devices: 41.7 us -> 36.4 us
    all_to_all x3 -> x4, blocking collectives: 32.9 us -> 44.8 us  [everyone(): return lax.all_to_all(payload, AXES, 0, 0, tiled=True)]
    all_to_all x5 -> x4, starting transfers between devices: 22.8 us -> 15.7 us  [everyone(): return lax.all_to_all(payload, AXES, 0, 0, tiled=True)]
    all_to_all x5 -> x4, waiting for transfers between devices: 15.1 us -> 9.36 us  [everyone(): return lax.all_to_all(payload, AXES, 0, 0, tiled=True)]
  transfers between devices with their start and end apart: 15 -> 14, of which waited for: 9 -> 8; matrix products, arithmetic and copies ran while one was open for 1% -> 1% of each run, Pallas kernels for 28% -> 24%
where the time goes in v7:
time: 311 us; the launch traced here: 310 us
  Pallas kernels  169 us (54%)
  blocking collectives  58.3 us (19%)
  starting transfers between devices  41.8 us (13%)
  waiting for transfers between devices  36.4 us (12%)
    pallas_call x11, Pallas kernels, stream_call(): pl.pallas_call(whole_kernel, in_specs=in_specs, out_specs=out_specs, out_...  159 us
    all_to_all x4, blocking collectives, everyone(): return lax.all_to_all(payload, AXES, 0, 0, tiled=True)  44.8 us
    all_to_all x3, waiting for transfers between devices, slots(): return lax.all_to_all(parts, 'fsdp', 0, 0, tiled=True)  23.9 us
    all_to_all x3, starting transfers between devices, slots(): return lax.all_to_all(parts, 'fsdp', 0, 0, tiled=True)  16.1 us
    all_to_all x4, starting transfers between devices, everyone(): return lax.all_to_all(payload, AXES, 0, 0, tiled=True)  15.7 us
    all_to_all x1, blocking collectives, slots(): return lax.all_to_all(parts, 'fsdp', 0, 0, tiled=True)  13.5 us
    pallas_call x7, Pallas kernels, call(): pl.pallas_call(kernel, grid=(grid,), in_specs=[spec for _, spec, *_ in in...  10.5 us
    ppermute x7, starting transfers between devices, other_core(): return lax.ppermute(array, 'dp', [(0, 1), (1, 0)])  10.1 us
  transfers between devices with their start and end apart: 14, of which 8 were waited for; matrix products, arithmetic and copies ran while one was open for 1% of the time, Pallas kernels for 24%

profile of v7, /device:TPU:9, one launch (start us, length us, event | category | flops | bytes accessed | tf_op | source)
XLA Modules:
  0.0 309.6 jit_solution(6460820932947191282)
XLA Ops:
  0.6 2.0 pack.1
  2.6 13.5 %all_to_all.60.refs_3_ = bf16[16,64,128]{2,1,0:T(8,128)(2,1)S(1)} all-to-all(bf16[16,64,128]{2,1,0:T(8,128)(2,1)S(1)} %get-tuple-element.91), channel_id=1, replica_groups=mesh['fsdp'=16,'dp'=2] {'fsdp'}, dimensions={0} | all-to-all | bytes 524288 | tf_op jit(solution)/shard_map/all_to_all | solution.py:1048
  16.1 3.2 %collective-permute-start = (bf16[16,64,128]{2,1,0:T(8,128)(2,1)S(1)}, bf16[16,64,128]{2,1,0:T(8,128)(2,1)S(1)}, u32[]{:S(2)}, u32[]{:S(2)}) collective-permute-start(bf16[16,64,128]{2,1,0:T(8,128)(2,1)S(1)} %all_to_all.60.refs_3_), channel_id=1, source_target_pairs={{0,1},{1,0},{2,3},{3,2},{4,5},{5,4},{6,7},{7,6},{8,9},{9,8},{10,11... | collective-permute-start | bytes 786440 | tf_op jit(solution)/shard_map/ppermute | solution.py:1015
  19.3 1.2 collective-permute-done.refs_4_
  20.5 4.0 %all-to-all-start.1 = ((bf16[16,144,128]{2,1,0:T(8,128)(2,1)}), bf16[16,144,128]{2,1,0:T(8,128)(2,1)S(1)}, u32[]{:S(2)}, u32[]{:S(2)}) async-start(bf16[16,144,128]{2,1,0:T(8,128)(2,1)} %get-tuple-element.95), calls=%async_computation.1 | async-start | bytes 1179648 | tf_op jit(solution)/shard_map/all_to_all | solution.py:1048
  24.5 0.6 copy-done
  25.2 9.1 %conv_one.1 = (f32[6144,256]{1,0:T(8,128)}, bf16[1024,256]{1,0:T(8,128)(2,1)}, f32[32,4,256]{2,1,0:T(4,128)}) custom-call(s32[1]{0:T(128)} %bitcast.core_ref.refs_0_.refs_14_, s32[24]{0:T(128)S(1)} %copy-done, bf16[6144,1024]{1,0:T(8,128)(2,1)} %bitcast.7, bf16[16,64,128]{2,1,0:T(8,128)(2,1)S(1)} %all_to_all.60.refs_3_, ...), custom_call_target="tpu_custom_call" | custom-call | flops 3221225472 | bytes 18874368 | tf_op jit(solution)/shard_map/conv_one/pallas_call | solution.py:266
  34.3 5.4 %all-to-all-done.1.mine_ref = bf16[16,144,128]{2,1,0:T(8,128)(2,1)S(1)} async-done(((bf16[16,144,128]{2,1,0:T(8,128)(2,1)}), bf16[16,144,128]{2,1,0:T(8,128)(2,1)S(1)}, u32[]{:S(2)}, u32[]{:S(2)}) %all-to-all-start.1) | async-done | bytes 589856 | tf_op jit(solution)/shard_map/all_to_all | solution.py:1048
  39.7 1.9 collective-permute-start.1
  41.6 3.1 %all-to-all-start.2 = ((f32[32,4,256]{2,1,0:T(4,128)}), f32[32,4,256]{2,1,0:T(4,128)S(1)}, u32[]{:S(2)}, u32[]{:S(2)}) async-start(f32[32,4,256]{2,1,0:T(4,128)} %get-tuple-element.96), calls=%async_computation.2 | async-start | bytes 262144 | tf_op jit(solution)/shard_map/all_to_all | solution.py:1011
  44.8 0.0 copy-done.2
  44.8 0.6 reshape.55.refs_4_.refs_6_.refs_7_.gain_ref.refs_14_
  45.4 0.0 copy-done.3
  45.4 0.6 reshape.56.refs_5_.refs_7_.refs_8_.refs_15_
  46.0 0.0 collective-permute-done.1.other_ref
  46.0 1.4 unpack.2.refs_3_.refs_13_
  47.4 3.5 %all-to-all-done.2.refs_1_ = f32[32,4,256]{2,1,0:T(4,128)S(1)} async-done(((f32[32,4,256]{2,1,0:T(4,128)}), f32[32,4,256]{2,1,0:T(4,128)S(1)}, u32[]{:S(2)}, u32[]{:S(2)}) %all-to-all-start.2) | async-done | bytes 131104 | tf_op jit(solution)/shard_map/all_to_all | solution.py:1011
  50.9 5.5 %all-to-all-start.3 = ((bf16[16,64,128]{2,1,0:T(8,128)(2,1)}), bf16[16,64,128]{2,1,0:T(8,128)(2,1)S(1)}, u32[]{:S(2)}, u32[]{:S(2)}) async-start(bf16[16,64,128]{2,1,0:T(8,128)(2,1)} %get-tuple-element.104), calls=%async_computation.3 | async-start | bytes 524288 | tf_op jit(solution)/shard_map/all_to_all | solution.py:1048
  56.4 0.0 copy-done.1
  56.4 17.2 %conv_two.1 = (bf16[6144,256]{1,0:T(8,128)(2,1)}, f32[6144,512]{1,0:T(8,128)}, f32[8,256]{1,0:T(8,128)}, f32[32,2,512]{2,1,0:T(2,128)S(1)}) custom-call(s32[24]{0:T(128)S(1)} %copy-done.1, f32[32,4,256]{2,1,0:T(4,128)S(1)} %all-to-all-done.2.refs_1_, f32[6144,256]{1,0:T(8,128)} %get-tuple-element.100.refs_2_, bf16[1152,512]{1,0:T(8,128)(2,1)} %unpack.2.refs_3_.refs_13_, ...), custom_call_target="tpu_custom_call" | custom-call | flops 7247757312 | bytes 22020096 | tf_op jit(solution)/shard_map/conv_two/pallas_call | solution.py:266
  73.6 0.0 all-to-all-done.3.mine_ref
  73.6 12.0 %all_to_all.61.refs_2_ = f32[32,2,512]{2,1,0:T(2,128)S(1)} all-to-all(f32[32,2,512]{2,1,0:T(2,128)S(1)} %get-tuple-element.105), channel_id=1, replica_groups=mesh['fsdp'=16,'dp'=2] {'fsdp','dp'}, dimensions={0} | all-to-all | bytes 262144 | tf_op jit(solution)/shard_map/all_to_all | solution.py:1011
  85.6 13.2 %act_two.1 = (bf16[6144,512]{1,0:T(8,128)(2,1)}, bf16[6144,512]{1,0:T(8,128)(2,1)}, bf16[6144,512]{1,0:T(8,128)(2,1)}, f32[24,256]{1,0:T(8,128)}, f32[24,128]{1,...) custom-call(s32[24]{0:T(128)S(1)} %copy-done.1, ...), custom_call_target="tpu_custom_call" | custom-call | flops 62914560 | bytes 31457280 | tf_op jit(solution)/shard_map/act_two/pallas_call | solution.py:266
  98.8 1.4 collective-permute-start.2
  100.2 3.5 %all-to-all-start.5 = ((f32[32,2,128]{2,1,0:T(2,128)}), f32[32,2,128]{2,1,0:T(2,128)S(1)}, u32[]{:S(2)}, u32[]{:S(2)}) async-start(f32[32,2,128]{2,1,0:T(2,128)} %get-tuple-element.109), calls=%async_computation.5 | async-start | bytes 65536 | tf_op jit(solution)/shard_map/all_to_all | solution.py:1011
  103.7 0.0 collective-permute-done.2.other_ref
  103.7 0.9 unpack.3.refs_3_.refs_6_.refs_8_
  104.6 4.7 %all-to-all-done.5.refs_0_ = f32[32,2,128]{2,1,0:T(2,128)S(1)} async-done(((f32[32,2,128]{2,1,0:T(2,128)}), f32[32,2,128]{2,1,0:T(2,128)S(1)}, u32[]{:S(2)}, u32[]{:S(2)}) %all-to-all-start.5) | async-done | bytes 32800 | tf_op jit(solution)/shard_map/all_to_all | solution.py:1011
  109.3 7.1 %combine.1 = (f32[24,512]{1,0:T(8,128)}, bf16[6144,256]{1,0:T(8,128)(2,1)}, f32[256,1024]{1,0:T(8,128)}, f32[1,256]{1,0:T(1,128)}, f32[4,24,128]{2,1,0:T(8,128)}, /*index=5*/f32[32,2,1024]{2,1,0:T(2,128)S(1)}) custom-call(f32[32,2,128]{2,1,0:T(2,128)S(1)} %all-to-all-done.5.refs_0_, f32[24,128]{1,0:T(8,128)} %get-tuple-element.110.refs_1_, ...), custom_call_target="tpu_custom_call" | custom-call | flops 805306368 | bytes 9437184 | tf_op jit(solution)/shard_map/combine/pallas_call | solution.py:266
  116.5 12.1 %all_to_all.62.refs_2_ = f32[32,2,1024]{2,1,0:T(2,128)S(1)} all-to-all(f32[32,2,1024]{2,1,0:T(2,128)S(1)} %get-tuple-element.113), channel_id=1, replica_groups=mesh['fsdp'=16,'dp'=2] {'fsdp','dp'}, dimensions={0} | all-to-all | bytes 524288 | tf_op jit(solution)/shard_map/all_to_all | solution.py:1011
  128.5 24.8 %output.1 = (bf16[6144,1024]{1,0:T(8,128)(2,1)}, bf16[6144,1024]{1,0:T(8,128)(2,1)}, f32[8,1024]{1,0:T(8,128)}, f32[32,2,1024]{2,1,0:T(2,128)}) custom-call(s32[24]{0:T(128)S(1)} %copy-done.1, f32[8,256]{1,0:T(8,128)} %get-tuple-element.102.refs_1_.refs_2_, f32[32,2,1024]{2,1,0:T(2,128)S(1)} %all_to_all.62.refs_2_, ...), custom_call_target="tpu_custom_call" | custom-call | flops 3221225472 | bytes 50331648 | tf_op jit(solution)/shard_map/output/pallas_call | solution.py:266
  153.4 4.5 %all-to-all-start.7 = ((f32[32,2,1024]{2,1,0:T(2,128)}), f32[32,2,1024]{2,1,0:T(2,128)S(1)}, u32[]{:S(2)}, u32[]{:S(2)}) async-start(f32[32,2,1024]{2,1,0:T(2,128)} %get-tuple-element.118), calls=%async_computation.7 | async-start | bytes 524288 | tf_op jit(solution)/shard_map/all_to_all | solution.py:1011
  157.8 7.6 %outer_three.1.refs_9_ = f32[256,1024]{1,0:T(8,128)} custom-call(bf16[6144,256]{1,0:T(8,128)(2,1)} %get-tuple-element.114.refs_3_.refs_0_.refs_4_, bf16[6144,1024]{1,0:T(8,128)(2,1)} %get-tuple-element.120.refs_1_.refs_4_), custom_call_target="tpu_custom_call" | custom-call | flops 3221225472 | bytes 18874368 | tf_op jit(solution)/shard_map/outer_three/pallas_call | solution.py:266
  165.5 1.1 all-to-all-done.7.refs_1_
  166.6 18.6 %back_three.1 = (bf16[6144,256]{1,0:T(8,128)(2,1)}, f32[24,512]{1,0:T(8,128)}, f32[24,512]{1,0:T(8,128)}, f32[24,128]{1,0:T(8,128)}, f32[256,512]{1,0:T(8,128)},...) custom-call(f32[8,1024]{1,0:T(8,128)} %get-tuple-element.117.refs_0_, ...), custom_call_target="tpu_custom_call" | custom-call | flops 6442450944 | bytes 25165824 | tf_op jit(solution)/shard_map/back_three/pallas_call | solution.py:266
  185.1 10.8 %all_to_all.63.got_ref = f32[32,8,128]{2,1,0:T(8,128)S(1)} all-to-all(f32[32,8,128]{2,1,0:T(8,128)S(1)} %get-tuple-element.126), channel_id=1, replica_groups=mesh['fsdp'=16,'dp'=2] {'fsdp','dp'}, dimensions={0} | all-to-all | bytes 262144 | tf_op jit(solution)/shard_map/all_to_all | solution.py:1011
  195.9 2.3 back_att.1
  198.2 10.0 %all_to_all.64.refs_3_ = f32[32,2,512]{2,1,0:T(2,128)S(1)} all-to-all(f32[32,2,512]{2,1,0:T(2,128)S(1)} %get-tuple-element.134), channel_id=1, replica_groups=mesh['fsdp'=16,'dp'=2] {'fsdp','dp'}, dimensions={0} | all-to-all | bytes 262144 | tf_op jit(solution)/shard_map/all_to_all | solution.py:1011
  208.2 23.7 %back_two.1 = (bf16[6144,512]{1,0:T(8,128)(2,1)}, bf16[6144,256]{1,0:T(8,128)(2,1)}, f32[2,512]{1,0:T(2,128)}, f32[32,28,128]{2,1,0:T(8,128)}) custom-call(s32[24]{0:T(128)S(1)} %copy-done.1, f32[8,256]{1,0:T(8,128)} %get-tuple-element.102.refs_1_.refs_2_, f32[8,512]{1,0:T(8,128)} %get-tuple-element.116.refs_2_, f32[32,2,512]{2,1,0:T(2,128)S(1)} %all_to_all.64.refs_3_, ...), custom_call_target="tpu_custom_call" | custom-call | flops 7247757312 | bytes 31457280 | tf_op jit(solution)/shard_map/back_two/pallas_call | solution.py:266
  231.9 4.6 %all-to-all-start.10 = ((f32[32,28,128]{2,1,0:T(8,128)}), f32[32,28,128]{2,1,0:T(8,128)S(1)}, u32[]{:S(2)}, u32[]{:S(2)}) async-start(f32[32,28,128]{2,1,0:T(8,128)} %get-tuple-element.141), calls=%async_computation.10 | async-start | bytes 1048576 | tf_op jit(solution)/shard_map/all_to_all | solution.py:1011
  236.5 0.0 copy-start.6
  236.5 15.3 %weight_two.1 = (f32[1152,256]{1,0:T(8,128)}, f32[1152,256]{1,0:T(8,128)}) custom-call(s32[1]{0:T(128)} %bitcast.core_ref.refs_0_.refs_14_, s32[24]{0:T(128)S(1)} %copy-done.1, bf16[6144,256]{1,0:T(8,128)(2,1)} %get-tuple-element.138.refs_10_.refs_2_.refs_5_, bf16[6144,512]{1,0:T(8,128)(2,1)} %get-tuple-element.142.refs_3_, ...), custom_call_target="tpu_custom_call" | custom-call | flops 7247757312 | bytes 9437184 | tf_op jit(solution)/shard_map/weight_two/pallas_call | solution.py:266
  251.8 0.0 all-to-all-done.10.refs_3_.got_ref
  251.8 0.4 collective-permute-start.3
  252.2 0.0 copy-done.6
  252.2 0.2 collective-permute-start.5
  252.4 10.7 %back_one.1 = (bf16[6144,256]{1,0:T(8,128)(2,1)}, f32[1024,128]{1,0:T(8,128)}, f32[1024,128]{1,0:T(8,128)}, f32[1,1920]{1,0:T(1,128)}, f32[1,1920]{1,0:T(1,128)}) custom-call(s32[1]{0:T(128)} %bitcast.core_ref.refs_0_.refs_14_, s32[24]{0:T(128)S(1)} %copy-done.1, f32[8,256]{1,0:T(8,128)} %get-tuple-element.102.refs_1_.refs_2_, ...), custom_call_target="tpu_custom_call" | custom-call | flops 3221225472 | bytes 25165824 | tf_op jit(solution)/shard_map/back_one/pallas_call | solution.py:266
  263.1 0.4 collective-permute-start.4
  263.4 0.0 collective-permute-done.5.other3_ref
  263.4 1.8 collective-permute-done.4.other1_ref
  265.2 0.0 collective-permute-done.3.other2_ref
  265.2 2.9 pack_last.1
  268.1 6.5 %all-to-all-start.11 = ((bf16[16,160,256]{2,1,0:T(8,128)(2,1)}), bf16[16,160,256]{2,1,0:T(8,128)(2,1)S(1)}, u32[]{:S(2)}, u32[]{:S(2)}) async-start(bf16[16,160,256]{2,1,0:T(8,128)(2,1)} %pack_last.1), calls=%async_computation.11 | async-start | bytes 2621440 | tf_op jit(solution)/shard_map/all_to_all | solution.py:1048
  274.6 0.0 copy-start.4
  274.7 11.4 %input_grad.1 = bf16[6144,1024]{1,0:T(8,128)(2,1)} custom-call(bf16[6144,256]{1,0:T(8,128)(2,1)} %get-tuple-element.158.refs_0_, bf16[6144,1024]{1,0:T(8,128)(2,1)} %get-tuple-element.120.refs_1_.refs_4_, f32[8,1024]{1,0:T(8,128)} %get-tuple-element.117.refs_0_.refs_2_, bf16[1024,256]{1,0:T(8,128)(2,1)} %get-tuple-element.159.refs_3_), custom_call_target="tpu_custom_call" | custom-call | flops 3221225472 | bytes 31457280 | tf_op jit(solution)/shard_map/input_grad/pallas_call | solution.py:266
  286.0 18.5 %all-to-all-done.11.parts_ref = bf16[16,160,256]{2,1,0:T(8,128)(2,1)S(1)} async-done(((bf16[16,160,256]{2,1,0:T(8,128)(2,1)}), bf16[16,160,256]{2,1,0:T(8,128)(2,1)S(1)}, u32[]{:S(2)}, u32[]{:S(2)}) %all-to-all-start.11) | async-done | bytes 1310752 | tf_op jit(solution)/shard_map/all_to_all | solution.py:1048
  304.6 0.2 sum_last.1.mine_ref
  304.7 2.6 collective-permute-start.6
  307.4 0.0 copy-done.5
  307.4 0.6 reduce
  308.0 0.0 copy-done.4
  308.0 0.6 reduce.1
  308.6 0.1 collective-permute-done.6.other_ref
  308.7 0.9 finish.1
  (5 shorter events, 0.0 us)
Async XLA Ops:
  16.1 4.4 %collective-permute-start = (bf16[16,64,128]{2,1,0:T(8,128)(2,1)S(1)}, bf16[16,64,128]{2,1,0:T(8,128)(2,1)S(1)}, u32[]{:S(2)}, u32[]{:S(2)}) collective-permute-start(bf16[16,64,128]{2,1,0:T(8,128)(2,1)S(1)} %all_to_all.60.refs_3_), channel_id=1, source_target_pairs={{0,1},{1,0},{2,3},{3,2},{4,5},{5,4},{6,7},{7,6},{8,9},{9,8},{10,11... | collective-permute-start | bytes 786440 | tf_op jit(solution)/shard_map/ppermute | solution.py:1015
  20.5 19.2 %all-to-all-start.1 = ((bf16[16,144,128]{2,1,0:T(8,128)(2,1)}), bf16[16,144,128]{2,1,0:T(8,128)(2,1)S(1)}, u32[]{:S(2)}, u32[]{:S(2)}) async-start(bf16[16,144,128]{2,1,0:T(8,128)(2,1)} %get-tuple-element.95), calls=%async_computation.1 | async-start | bytes 1179648 | tf_op jit(solution)/shard_map/all_to_all | solution.py:1048
  24.5 0.7 copy-start
  25.2 19.6 %copy-start.2 = (f32[1920]{0:T(1024)S(1)}, f32[1920]{0:T(1024)}, u32[]{:S(2)}) copy-start(f32[1920]{0:T(1024)} %param.19) | copy-start | bytes 23044
  25.2 20.2 %copy-start.3 = (f32[1920]{0:T(1024)S(1)}, f32[1920]{0:T(1024)}, u32[]{:S(2)}) copy-start(f32[1920]{0:T(1024)} %param.20) | copy-start | bytes 23044
  25.2 31.2 %copy-start.1 = (s32[24]{0:T(128)S(1)}, s32[24]{0:T(128)}, u32[]{:S(2)}) copy-start(s32[24]{0:T(128)} %refs_1_.7) | copy-start | bytes 292
  39.7 6.3 %collective-permute-start.1 = (bf16[16,144,128]{2,1,0:T(8,128)(2,1)S(1)}, bf16[16,144,128]{2,1,0:T(8,128)(2,1)S(1)}, u32[]{:S(2)}, u32[]{:S(2)}) collective-permute-start(bf16[16,144,128]{2,1,0:T(8,128)(2,1)S(1)} %all-to-all-done.1.mine_ref), channel_id=1, source_target_pairs={{0,1},{1,0},{2,3},{3,2},{4,5},{5,4},{6,7},{7,6},{8,9},{9,8},{10,11... | collective-permute-start | bytes 1769480 | tf_op jit(solution)/shard_map/ppermute | solution.py:1015
  41.6 9.3 %all-to-all-start.2 = ((f32[32,4,256]{2,1,0:T(4,128)}), f32[32,4,256]{2,1,0:T(4,128)S(1)}, u32[]{:S(2)}, u32[]{:S(2)}) async-start(f32[32,4,256]{2,1,0:T(4,128)} %get-tuple-element.96), calls=%async_computation.2 | async-start | bytes 262144 | tf_op jit(solution)/shard_map/all_to_all | solution.py:1011
  50.9 22.7 %all-to-all-start.3 = ((bf16[16,64,128]{2,1,0:T(8,128)(2,1)}), bf16[16,64,128]{2,1,0:T(8,128)(2,1)S(1)}, u32[]{:S(2)}, u32[]{:S(2)}) async-start(bf16[16,64,128]{2,1,0:T(8,128)(2,1)} %get-tuple-element.104), calls=%async_computation.3 | async-start | bytes 524288 | tf_op jit(solution)/shard_map/all_to_all | solution.py:1048
  98.8 4.9 %collective-permute-start.2 = (bf16[16,64,128]{2,1,0:T(8,128)(2,1)S(1)}, bf16[16,64,128]{2,1,0:T(8,128)(2,1)S(1)}, u32[]{:S(2)}, u32[]{:S(2)}) collective-permute-start(bf16[16,64,128]{2,1,0:T(8,128)(2,1)S(1)} %all-to-all-done.3.mine_ref), channel_id=1, source_target_pairs={{0,1},{1,0},{2,3},{3,2},{4,5},{5,4},{6,7},{7,6},{8,9},{9,8},{10,11... | collective-permute-start | bytes 786440 | tf_op jit(solution)/shard_map/ppermute | solution.py:1015
  100.2 9.1 %all-to-all-start.5 = ((f32[32,2,128]{2,1,0:T(2,128)}), f32[32,2,128]{2,1,0:T(2,128)S(1)}, u32[]{:S(2)}, u32[]{:S(2)}) async-start(f32[32,2,128]{2,1,0:T(2,128)} %get-tuple-element.109), calls=%async_computation.5 | async-start | bytes 65536 | tf_op jit(solution)/shard_map/all_to_all | solution.py:1011
  153.4 13.2 %all-to-all-start.7 = ((f32[32,2,1024]{2,1,0:T(2,128)}), f32[32,2,1024]{2,1,0:T(2,128)S(1)}, u32[]{:S(2)}, u32[]{:S(2)}) async-start(f32[32,2,1024]{2,1,0:T(2,128)} %get-tuple-element.118), calls=%async_computation.7 | async-start | bytes 524288 | tf_op jit(solution)/shard_map/all_to_all | solution.py:1011
  231.9 19.9 %all-to-all-start.10 = ((f32[32,28,128]{2,1,0:T(8,128)}), f32[32,28,128]{2,1,0:T(8,128)S(1)}, u32[]{:S(2)}, u32[]{:S(2)}) async-start(f32[32,28,128]{2,1,0:T(8,128)} %get-tuple-element.141), calls=%async_computation.10 | async-start | bytes 1048576 | tf_op jit(solution)/shard_map/all_to_all | solution.py:1011
  236.5 15.7 %copy-start.6 = (f32[256,512]{1,0:T(8,128)S(1)}, f32[256,512]{1,0:T(8,128)}, u32[]{:S(2)}) copy-start(f32[256,512]{1,0:T(8,128)} %get-tuple-element.156) | copy-start | bytes 1572868
  251.8 13.5 %collective-permute-start.3 = (f32[1152,256]{1,0:T(8,128)}, f32[1152,256]{1,0:T(8,128)S(1)}, u32[]{:S(2)}, u32[]{:S(2)}) collective-permute-start(f32[1152,256]{1,0:T(8,128)} %get-tuple-element.152), channel_id=1, source_target_pairs={{0,1},{1,0},{2,3},{3,2},{4,5},{5,4},{6,7},{7,6},{8,9},{9,8},{10,11... | collective-permute-start | bytes 3538952 | tf_op jit(solution)/shard_map/ppermute | solution.py:1015
  252.2 11.2 %collective-permute-start.5 = (f32[256,512]{1,0:T(8,128)S(1)}, f32[256,512]{1,0:T(8,128)S(1)}, u32[]{:S(2)}, u32[]{:S(2)}) collective-permute-start(f32[256,512]{1,0:T(8,128)S(1)} %copy-done.6), channel_id=1, source_target_pairs={{0,1},{1,0},{2,3},{3,2},{4,5},{5,4},{6,7},{7,6},{8,9},{9,8},{10,11... | collective-permute-start | bytes 1572872 | tf_op jit(solution)/shard_map/ppermute | solution.py:1015
  263.1 2.2 collective-permute-start.4
  268.1 36.4 %all-to-all-start.11 = ((bf16[16,160,256]{2,1,0:T(8,128)(2,1)}), bf16[16,160,256]{2,1,0:T(8,128)(2,1)S(1)}, u32[]{:S(2)}, u32[]{:S(2)}) async-start(bf16[16,160,256]{2,1,0:T(8,128)(2,1)} %pack_last.1), calls=%async_computation.11 | async-start | bytes 2621440 | tf_op jit(solution)/shard_map/all_to_all | solution.py:1048
  274.6 32.7 %copy-start.5 = (f32[1,1920]{1,0:T(1,128)S(1)}, f32[1,1920]{1,0:T(1,128)}, u32[]{:S(2)}) copy-start(f32[1,1920]{1,0:T(1,128)} %get-tuple-element.168) | copy-start | bytes 23044
  274.6 33.3 %copy-start.4 = (f32[1,1920]{1,0:T(1,128)S(1)}, f32[1,1920]{1,0:T(1,128)}, u32[]{:S(2)}) copy-start(f32[1,1920]{1,0:T(1,128)} %get-tuple-element.169) | copy-start | bytes 23044
  304.7 4.0 %collective-permute-start.6 = (f32[400,256]{1,0:T(8,128)S(1)}, f32[400,256]{1,0:T(8,128)S(1)}, u32[]{:S(2)}, u32[]{:S(2)}) collective-permute-start(f32[400,256]{1,0:T(8,128)S(1)} %sum_last.1.mine_ref), channel_id=1, source_target_pairs={{0,1},{1,0},{2,3},{3,2},{4,5},{5,4},{6,7},{7,6},{8,9},{9,8},{10,11... | collective-permute-start | bytes 1228808 | tf_op jit(solution)/shard_map/ppermute | solution.py:1015

commit v8 on v7

--- a/solution.py
+++ b/solution.py
@@ -134,7 +134,7 @@
 def call(kernel, grid, ins, outs, scratch=(), vmem=VMEM, flops=0, moved=0, name=None):
     arrays = [
         array
-        if spec is SMEM_SPEC or near
+        if near
         else pltpu.with_memory_space_constraint(array, pltpu.HBM)
         for array, spec, *near in ins
     ]
@@ -181,7 +181,7 @@
             continue
         in_specs.append(spec)
         arrays.append(
-            array if spec is SMEM_SPEC else pltpu.with_memory_space_constraint(array, pltpu.HBM)
+            pltpu.with_memory_space_constraint(array, pltpu.HBM)
         )
     for at, (shape, dtype, spec, *near) in enumerate(outs):
         shapes.append(jax.ShapeDtypeStruct(shape, dtype) if near else pltpu.HBM(shape, dtype))

time: 311 us -> 311 us (level)
  no operation moved by 1% of the time
where the time goes in v8:
time: 311 us; the launch traced here: 310 us
  Pallas kernels  169 us (54%)
  blocking collectives  58.3 us (19%)
  starting transfers between devices  41.9 us (13%)
  waiting for transfers between devices  36.7 us (12%)
    pallas_call x11, Pallas kernels, stream_call(): pl.pallas_call(whole_kernel, in_specs=in_specs, out_specs=out_specs, out_...  159 us
    all_to_all x4, blocking collectives, everyone(): return lax.all_to_all(payload, AXES, 0, 0, tiled=True)  44.8 us
    all_to_all x3, waiting for transfers between devices, slots(): return lax.all_to_all(parts, 'fsdp', 0, 0, tiled=True)  24.3 us
    all_to_all x3, starting transfers between devices, slots(): return lax.all_to_all(parts, 'fsdp', 0, 0, tiled=True)  16.1 us
    all_to_all x4, starting transfers between devices, everyone(): return lax.all_to_all(payload, AXES, 0, 0, tiled=True)  15.7 us
    all_to_all x1, blocking collectives, slots(): return lax.all_to_all(parts, 'fsdp', 0, 0, tiled=True)  13.5 us
    pallas_call x7, Pallas kernels, call(): pl.pallas_call(kernel, grid=(grid,), in_specs=[spec for _, spec, *_ in in...  10.4 us
    ppermute x7, starting transfers between devices, other_core(): return lax.ppermute(array, 'dp', [(0, 1), (1, 0)])  10.1 us
  transfers between devices with their start and end apart: 14, of which 8 were waited for; matrix products, arithmetic and copies ran while one was open for 1% of the time, Pallas kernels for 24%

profile of v8, /device:TPU:9, one launch (start us, length us, event | category | flops | bytes accessed | tf_op | source)
XLA Modules:
  0.0 309.7 jit_solution(14906798730104092755)
XLA Ops:
  0.6 2.0 pack.1
  2.6 13.5 %all_to_all.60.refs_3_ = bf16[16,64,128]{2,1,0:T(8,128)(2,1)S(1)} all-to-all(bf16[16,64,128]{2,1,0:T(8,128)(2,1)S(1)} %get-tuple-element.91), channel_id=1, replica_groups=mesh['fsdp'=16,'dp'=2] {'fsdp'}, dimensions={0} | all-to-all | bytes 524288 | tf_op jit(solution)/shard_map/all_to_all | solution.py:1048
  16.1 3.2 %collective-permute-start = (bf16[16,64,128]{2,1,0:T(8,128)(2,1)S(1)}, bf16[16,64,128]{2,1,0:T(8,128)(2,1)S(1)}, u32[]{:S(2)}, u32[]{:S(2)}) collective-permute-start(bf16[16,64,128]{2,1,0:T(8,128)(2,1)S(1)} %all_to_all.60.refs_3_), channel_id=1, source_target_pairs={{0,1},{1,0},{2,3},{3,2},{4,5},{5,4},{6,7},{7,6},{8,9},{9,8},{10,11... | collective-permute-start | bytes 786440 | tf_op jit(solution)/shard_map/ppermute | solution.py:1015
  19.3 1.2 collective-permute-done.refs_4_
  20.5 4.0 %all-to-all-start.1 = ((bf16[16,144,128]{2,1,0:T(8,128)(2,1)}), bf16[16,144,128]{2,1,0:T(8,128)(2,1)S(1)}, u32[]{:S(2)}, u32[]{:S(2)}) async-start(bf16[16,144,128]{2,1,0:T(8,128)(2,1)} %get-tuple-element.95), calls=%async_computation.1 | async-start | bytes 1179648 | tf_op jit(solution)/shard_map/all_to_all | solution.py:1048
  24.5 0.0 copy-start
  24.5 0.0 copy-start.1
  24.6 9.4 %conv_one.1 = (f32[6144,256]{1,0:T(8,128)}, bf16[1024,256]{1,0:T(8,128)(2,1)}, f32[32,4,256]{2,1,0:T(4,128)}) custom-call(s32[1]{0:T(128)} %bitcast.core_ref.refs_0_.refs_14_, s32[24]{0:T(128)} %refs_1_.7, bf16[6144,1024]{1,0:T(8,128)(2,1)} %bitcast.7, bf16[16,64,128]{2,1,0:T(8,128)(2,1)S(1)} %all_to_all.60.refs_3_, ...), custom_call_target="tpu_custom_call" | custom-call | flops 3221225472 | bytes 18874368 | tf_op jit(solution)/shard_map/conv_one/pallas_call | solution.py:266
  34.0 5.8 %all-to-all-done.1.mine_ref = bf16[16,144,128]{2,1,0:T(8,128)(2,1)S(1)} async-done(((bf16[16,144,128]{2,1,0:T(8,128)(2,1)}), bf16[16,144,128]{2,1,0:T(8,128)(2,1)S(1)}, u32[]{:S(2)}, u32[]{:S(2)}) %all-to-all-start.1) | async-done | bytes 589856 | tf_op jit(solution)/shard_map/all_to_all | solution.py:1048
  39.7 1.9 collective-permute-start.1
  41.6 3.1 %all-to-all-start.2 = ((f32[32,4,256]{2,1,0:T(4,128)}), f32[32,4,256]{2,1,0:T(4,128)S(1)}, u32[]{:S(2)}, u32[]{:S(2)}) async-start(f32[32,4,256]{2,1,0:T(4,128)} %get-tuple-element.96), calls=%async_computation.2 | async-start | bytes 262144 | tf_op jit(solution)/shard_map/all_to_all | solution.py:1011
  44.8 0.0 copy-done
  44.8 0.6 reshape.55.refs_4_.refs_6_.refs_7_.gain_ref.refs_14_
  45.4 0.0 copy-done.1
  45.4 0.6 reshape.56.refs_5_.refs_7_.refs_8_.refs_15_
  46.0 0.0 collective-permute-done.1.other_ref
  46.0 1.4 unpack.2.refs_3_.refs_13_
  47.4 3.5 %all-to-all-done.2.refs_1_ = f32[32,4,256]{2,1,0:T(4,128)S(1)} async-done(((f32[32,4,256]{2,1,0:T(4,128)}), f32[32,4,256]{2,1,0:T(4,128)S(1)}, u32[]{:S(2)}, u32[]{:S(2)}) %all-to-all-start.2) | async-done | bytes 131104 | tf_op jit(solution)/shard_map/all_to_all | solution.py:1011
  50.9 5.5 %all-to-all-start.3 = ((bf16[16,64,128]{2,1,0:T(8,128)(2,1)}), bf16[16,64,128]{2,1,0:T(8,128)(2,1)S(1)}, u32[]{:S(2)}, u32[]{:S(2)}) async-start(bf16[16,64,128]{2,1,0:T(8,128)(2,1)} %get-tuple-element.104), calls=%async_computation.3 | async-start | bytes 524288 | tf_op jit(solution)/shard_map/all_to_all | solution.py:1048
  56.4 17.2 %conv_two.1 = (bf16[6144,256]{1,0:T(8,128)(2,1)}, f32[6144,512]{1,0:T(8,128)}, f32[8,256]{1,0:T(8,128)}, f32[32,2,512]{2,1,0:T(2,128)S(1)}) custom-call(s32[24]{0:T(128)} %refs_1_.7, f32[32,4,256]{2,1,0:T(4,128)S(1)} %all-to-all-done.2.refs_1_, f32[6144,256]{1,0:T(8,128)} %get-tuple-element.100.refs_2_, bf16[1152,512]{1,0:T(8,128)(2,1)} %unpack.2.refs_3_.refs_13_, ...), custom_call_target="tpu_custom_call" | custom-call | flops 7247757312 | bytes 22020096 | tf_op jit(solution)/shard_map/conv_two/pallas_call | solution.py:266
  73.6 0.0 all-to-all-done.3.mine_ref
  73.6 12.0 %all_to_all.61.refs_2_ = f32[32,2,512]{2,1,0:T(2,128)S(1)} all-to-all(f32[32,2,512]{2,1,0:T(2,128)S(1)} %get-tuple-element.105), channel_id=1, replica_groups=mesh['fsdp'=16,'dp'=2] {'fsdp','dp'}, dimensions={0} | all-to-all | bytes 262144 | tf_op jit(solution)/shard_map/all_to_all | solution.py:1011
  85.6 13.2 %act_two.1 = (bf16[6144,512]{1,0:T(8,128)(2,1)}, bf16[6144,512]{1,0:T(8,128)(2,1)}, bf16[6144,512]{1,0:T(8,128)(2,1)}, f32[24,256]{1,0:T(8,128)}, f32[24,128]{1,...) custom-call(s32[24]{0:T(128)} %refs_1_.7, ...), custom_call_target="tpu_custom_call" | custom-call | flops 62914560 | bytes 31457280 | tf_op jit(solution)/shard_map/act_two/pallas_call | solution.py:266
  98.8 1.4 collective-permute-start.2
  100.2 3.5 %all-to-all-start.5 = ((f32[32,2,128]{2,1,0:T(2,128)}), f32[32,2,128]{2,1,0:T(2,128)S(1)}, u32[]{:S(2)}, u32[]{:S(2)}) async-start(f32[32,2,128]{2,1,0:T(2,128)} %get-tuple-element.109), calls=%async_computation.5 | async-start | bytes 65536 | tf_op jit(solution)/shard_map/all_to_all | solution.py:1011
  103.7 0.0 collective-permute-done.2.other_ref
  103.7 0.9 unpack.3.refs_3_.refs_6_.refs_8_
  104.6 4.8 %all-to-all-done.5.refs_0_ = f32[32,2,128]{2,1,0:T(2,128)S(1)} async-done(((f32[32,2,128]{2,1,0:T(2,128)}), f32[32,2,128]{2,1,0:T(2,128)S(1)}, u32[]{:S(2)}, u32[]{:S(2)}) %all-to-all-start.5) | async-done | bytes 32800 | tf_op jit(solution)/shard_map/all_to_all | solution.py:1011
  109.3 7.2 %combine.1 = (f32[24,512]{1,0:T(8,128)}, bf16[6144,256]{1,0:T(8,128)(2,1)}, f32[256,1024]{1,0:T(8,128)}, f32[1,256]{1,0:T(1,128)}, f32[4,24,128]{2,1,0:T(8,128)}, /*index=5*/f32[32,2,1024]{2,1,0:T(2,128)S(1)}) custom-call(f32[32,2,128]{2,1,0:T(2,128)S(1)} %all-to-all-done.5.refs_0_, f32[24,128]{1,0:T(8,128)} %get-tuple-element.110.refs_1_, ...), custom_call_target="tpu_custom_call" | custom-call | flops 805306368 | bytes 9437184 | tf_op jit(solution)/shard_map/combine/pallas_call | solution.py:266
  116.5 12.1 %all_to_all.62.refs_2_ = f32[32,2,1024]{2,1,0:T(2,128)S(1)} all-to-all(f32[32,2,1024]{2,1,0:T(2,128)S(1)} %get-tuple-element.113), channel_id=1, replica_groups=mesh['fsdp'=16,'dp'=2] {'fsdp','dp'}, dimensions={0} | all-to-all | bytes 524288 | tf_op jit(solution)/shard_map/all_to_all | solution.py:1011
  128.5 24.8 %output.1 = (bf16[6144,1024]{1,0:T(8,128)(2,1)}, bf16[6144,1024]{1,0:T(8,128)(2,1)}, f32[8,1024]{1,0:T(8,128)}, f32[32,2,1024]{2,1,0:T(2,128)}) custom-call(s32[24]{0:T(128)} %refs_1_.7, f32[8,256]{1,0:T(8,128)} %get-tuple-element.102.refs_1_.refs_2_, f32[32,2,1024]{2,1,0:T(2,128)S(1)} %all_to_all.62.refs_2_, ...), custom_call_target="tpu_custom_call" | custom-call | flops 3221225472 | bytes 50331648 | tf_op jit(solution)/shard_map/output/pallas_call | solution.py:266
  153.4 4.5 %all-to-all-start.7 = ((f32[32,2,1024]{2,1,0:T(2,128)}), f32[32,2,1024]{2,1,0:T(2,128)S(1)}, u32[]{:S(2)}, u32[]{:S(2)}) async-start(f32[32,2,1024]{2,1,0:T(2,128)} %get-tuple-element.118), calls=%async_computation.7 | async-start | bytes 524288 | tf_op jit(solution)/shard_map/all_to_all | solution.py:1011
  157.8 7.7 %outer_three.1.refs_9_ = f32[256,1024]{1,0:T(8,128)} custom-call(bf16[6144,256]{1,0:T(8,128)(2,1)} %get-tuple-element.114.refs_3_.refs_0_.refs_4_, bf16[6144,1024]{1,0:T(8,128)(2,1)} %get-tuple-element.120.refs_1_.refs_4_), custom_call_target="tpu_custom_call" | custom-call | flops 3221225472 | bytes 18874368 | tf_op jit(solution)/shard_map/outer_three/pallas_call | solution.py:266
  165.5 1.1 all-to-all-done.7.refs_1_
  166.6 18.6 %back_three.1 = (bf16[6144,256]{1,0:T(8,128)(2,1)}, f32[24,512]{1,0:T(8,128)}, f32[24,512]{1,0:T(8,128)}, f32[24,128]{1,0:T(8,128)}, f32[256,512]{1,0:T(8,128)},...) custom-call(f32[8,1024]{1,0:T(8,128)} %get-tuple-element.117.refs_0_, ...), custom_call_target="tpu_custom_call" | custom-call | flops 6442450944 | bytes 25165824 | tf_op jit(solution)/shard_map/back_three/pallas_call | solution.py:266
  185.2 10.8 %all_to_all.63.got_ref = f32[32,8,128]{2,1,0:T(8,128)S(1)} all-to-all(f32[32,8,128]{2,1,0:T(8,128)S(1)} %get-tuple-element.126), channel_id=1, replica_groups=mesh['fsdp'=16,'dp'=2] {'fsdp','dp'}, dimensions={0} | all-to-all | bytes 262144 | tf_op jit(solution)/shard_map/all_to_all | solution.py:1011
  195.9 2.3 back_att.1
  198.2 10.0 %all_to_all.64.refs_3_ = f32[32,2,512]{2,1,0:T(2,128)S(1)} all-to-all(f32[32,2,512]{2,1,0:T(2,128)S(1)} %get-tuple-element.134), channel_id=1, replica_groups=mesh['fsdp'=16,'dp'=2] {'fsdp','dp'}, dimensions={0} | all-to-all | bytes 262144 | tf_op jit(solution)/shard_map/all_to_all | solution.py:1011
  208.2 23.7 %back_two.1 = (bf16[6144,512]{1,0:T(8,128)(2,1)}, bf16[6144,256]{1,0:T(8,128)(2,1)}, f32[2,512]{1,0:T(2,128)}, f32[32,28,128]{2,1,0:T(8,128)}) custom-call(s32[24]{0:T(128)} %refs_1_.7, f32[8,256]{1,0:T(8,128)} %get-tuple-element.102.refs_1_.refs_2_, f32[8,512]{1,0:T(8,128)} %get-tuple-element.116.refs_2_, f32[32,2,512]{2,1,0:T(2,128)S(1)} %all_to_all.64.refs_3_, ...), custom_call_target="tpu_custom_call" | custom-call | flops 7247757312 | bytes 31457280 | tf_op jit(solution)/shard_map/back_two/pallas_call | solution.py:266
  231.9 4.6 %all-to-all-start.10 = ((f32[32,28,128]{2,1,0:T(8,128)}), f32[32,28,128]{2,1,0:T(8,128)S(1)}, u32[]{:S(2)}, u32[]{:S(2)}) async-start(f32[32,28,128]{2,1,0:T(8,128)} %get-tuple-element.141), calls=%async_computation.10 | async-start | bytes 1048576 | tf_op jit(solution)/shard_map/all_to_all | solution.py:1011
  236.6 0.0 copy-start.4
  236.6 15.3 %weight_two.1 = (f32[1152,256]{1,0:T(8,128)}, f32[1152,256]{1,0:T(8,128)}) custom-call(s32[1]{0:T(128)} %bitcast.core_ref.refs_0_.refs_14_, s32[24]{0:T(128)} %refs_1_.7, bf16[6144,256]{1,0:T(8,128)(2,1)} %get-tuple-element.138.refs_10_.refs_2_.refs_5_, bf16[6144,512]{1,0:T(8,128)(2,1)} %get-tuple-element.142.refs_3_, ...), custom_call_target="tpu_custom_call" | custom-call | flops 7247757312 | bytes 9437184 | tf_op jit(solution)/shard_map/weight_two/pallas_call | solution.py:266
  251.9 0.0 all-to-all-done.10.refs_3_.got_ref
  251.9 0.4 collective-permute-start.3
  252.3 0.0 copy-done.4
  252.3 0.2 collective-permute-start.5
  252.4 10.7 %back_one.1 = (bf16[6144,256]{1,0:T(8,128)(2,1)}, f32[1024,128]{1,0:T(8,128)}, f32[1024,128]{1,0:T(8,128)}, f32[1,1920]{1,0:T(1,128)}, f32[1,1920]{1,0:T(1,128)}) custom-call(s32[1]{0:T(128)} %bitcast.core_ref.refs_0_.refs_14_, s32[24]{0:T(128)} %refs_1_.7, f32[8,256]{1,0:T(8,128)} %get-tuple-element.102.refs_1_.refs_2_, ...), custom_call_target="tpu_custom_call" | custom-call | flops 3221225472 | bytes 25165824 | tf_op jit(solution)/shard_map/back_one/pallas_call | solution.py:266
  263.2 0.4 collective-permute-start.4
  263.6 0.0 collective-permute-done.5.other3_ref
  263.6 1.8 collective-permute-done.4.other1_ref
  265.3 0.0 collective-permute-done.3.other2_ref
  265.3 2.9 pack_last.1
  268.2 6.5 %all-to-all-start.11 = ((bf16[16,160,256]{2,1,0:T(8,128)(2,1)}), bf16[16,160,256]{2,1,0:T(8,128)(2,1)S(1)}, u32[]{:S(2)}, u32[]{:S(2)}) async-start(bf16[16,160,256]{2,1,0:T(8,128)(2,1)} %pack_last.1), calls=%async_computation.11 | async-start | bytes 2621440 | tf_op jit(solution)/shard_map/all_to_all | solution.py:1048
  274.7 0.0 copy-start.2
  274.8 11.4 %input_grad.1 = bf16[6144,1024]{1,0:T(8,128)(2,1)} custom-call(bf16[6144,256]{1,0:T(8,128)(2,1)} %get-tuple-element.158.refs_0_, bf16[6144,1024]{1,0:T(8,128)(2,1)} %get-tuple-element.120.refs_1_.refs_4_, f32[8,1024]{1,0:T(8,128)} %get-tuple-element.117.refs_0_.refs_2_, bf16[1024,256]{1,0:T(8,128)(2,1)} %get-tuple-element.159.refs_3_), custom_call_target="tpu_custom_call" | custom-call | flops 3221225472 | bytes 31457280 | tf_op jit(solution)/shard_map/input_grad/pallas_call | solution.py:266
  286.1 18.5 %all-to-all-done.11.parts_ref = bf16[16,160,256]{2,1,0:T(8,128)(2,1)S(1)} async-done(((bf16[16,160,256]{2,1,0:T(8,128)(2,1)}), bf16[16,160,256]{2,1,0:T(8,128)(2,1)S(1)}, u32[]{:S(2)}, u32[]{:S(2)}) %all-to-all-start.11) | async-done | bytes 1310752 | tf_op jit(solution)/shard_map/all_to_all | solution.py:1048
  304.7 0.2 sum_last.1.mine_ref
  304.8 2.6 collective-permute-start.6
  307.5 0.0 copy-done.3
  307.5 0.6 reduce
  308.1 0.0 copy-done.2
  308.1 0.6 reduce.1
  308.7 0.1 collective-permute-done.6.other_ref
  308.8 0.9 finish.1
  (1 shorter events, 0.0 us)
Async XLA Ops:
  16.1 4.4 %collective-permute-start = (bf16[16,64,128]{2,1,0:T(8,128)(2,1)S(1)}, bf16[16,64,128]{2,1,0:T(8,128)(2,1)S(1)}, u32[]{:S(2)}, u32[]{:S(2)}) collective-permute-start(bf16[16,64,128]{2,1,0:T(8,128)(2,1)S(1)} %all_to_all.60.refs_3_), channel_id=1, source_target_pairs={{0,1},{1,0},{2,3},{3,2},{4,5},{5,4},{6,7},{7,6},{8,9},{9,8},{10,11... | collective-permute-start | bytes 786440 | tf_op jit(solution)/shard_map/ppermute | solution.py:1015
  20.5 19.2 %all-to-all-start.1 = ((bf16[16,144,128]{2,1,0:T(8,128)(2,1)}), bf16[16,144,128]{2,1,0:T(8,128)(2,1)S(1)}, u32[]{:S(2)}, u32[]{:S(2)}) async-start(bf16[16,144,128]{2,1,0:T(8,128)(2,1)} %get-tuple-element.95), calls=%async_computation.1 | async-start | bytes 1179648 | tf_op jit(solution)/shard_map/all_to_all | solution.py:1048
  24.5 20.3 %copy-start = (f32[1920]{0:T(1024)S(1)}, f32[1920]{0:T(1024)}, u32[]{:S(2)}) copy-start(f32[1920]{0:T(1024)} %param.19) | copy-start | bytes 23044
  24.5 20.9 %copy-start.1 = (f32[1920]{0:T(1024)S(1)}, f32[1920]{0:T(1024)}, u32[]{:S(2)}) copy-start(f32[1920]{0:T(1024)} %param.20) | copy-start | bytes 23044
  39.7 6.3 %collective-permute-start.1 = (bf16[16,144,128]{2,1,0:T(8,128)(2,1)S(1)}, bf16[16,144,128]{2,1,0:T(8,128)(2,1)S(1)}, u32[]{:S(2)}, u32[]{:S(2)}) collective-permute-start(bf16[16,144,128]{2,1,0:T(8,128)(2,1)S(1)} %all-to-all-done.1.mine_ref), channel_id=1, source_target_pairs={{0,1},{1,0},{2,3},{3,2},{4,5},{5,4},{6,7},{7,6},{8,9},{9,8},{10,11... | collective-permute-start | bytes 1769480 | tf_op jit(solution)/shard_map/ppermute | solution.py:1015
  41.6 9.3 %all-to-all-start.2 = ((f32[32,4,256]{2,1,0:T(4,128)}), f32[32,4,256]{2,1,0:T(4,128)S(1)}, u32[]{:S(2)}, u32[]{:S(2)}) async-start(f32[32,4,256]{2,1,0:T(4,128)} %get-tuple-element.96), calls=%async_computation.2 | async-start | bytes 262144 | tf_op jit(solution)/shard_map/all_to_all | solution.py:1011
  50.9 22.7 %all-to-all-start.3 = ((bf16[16,64,128]{2,1,0:T(8,128)(2,1)}), bf16[16,64,128]{2,1,0:T(8,128)(2,1)S(1)}, u32[]{:S(2)}, u32[]{:S(2)}) async-start(bf16[16,64,128]{2,1,0:T(8,128)(2,1)} %get-tuple-element.104), calls=%async_computation.3 | async-start | bytes 524288 | tf_op jit(solution)/shard_map/all_to_all | solution.py:1048
  98.8 4.9 %collective-permute-start.2 = (bf16[16,64,128]{2,1,0:T(8,128)(2,1)S(1)}, bf16[16,64,128]{2,1,0:T(8,128)(2,1)S(1)}, u32[]{:S(2)}, u32[]{:S(2)}) collective-permute-start(bf16[16,64,128]{2,1,0:T(8,128)(2,1)S(1)} %all-to-all-done.3.mine_ref), channel_id=1, source_target_pairs={{0,1},{1,0},{2,3},{3,2},{4,5},{5,4},{6,7},{7,6},{8,9},{9,8},{10,11... | collective-permute-start | bytes 786440 | tf_op jit(solution)/shard_map/ppermute | solution.py:1015
  100.2 9.1 %all-to-all-start.5 = ((f32[32,2,128]{2,1,0:T(2,128)}), f32[32,2,128]{2,1,0:T(2,128)S(1)}, u32[]{:S(2)}, u32[]{:S(2)}) async-start(f32[32,2,128]{2,1,0:T(2,128)} %get-tuple-element.109), calls=%async_computation.5 | async-start | bytes 65536 | tf_op jit(solution)/shard_map/all_to_all | solution.py:1011
  153.4 13.2 %all-to-all-start.7 = ((f32[32,2,1024]{2,1,0:T(2,128)}), f32[32,2,1024]{2,1,0:T(2,128)S(1)}, u32[]{:S(2)}, u32[]{:S(2)}) async-start(f32[32,2,1024]{2,1,0:T(2,128)} %get-tuple-element.118), calls=%async_computation.7 | async-start | bytes 524288 | tf_op jit(solution)/shard_map/all_to_all | solution.py:1011
  231.9 19.9 %all-to-all-start.10 = ((f32[32,28,128]{2,1,0:T(8,128)}), f32[32,28,128]{2,1,0:T(8,128)S(1)}, u32[]{:S(2)}, u32[]{:S(2)}) async-start(f32[32,28,128]{2,1,0:T(8,128)} %get-tuple-element.141), calls=%async_computation.10 | async-start | bytes 1048576 | tf_op jit(solution)/shard_map/all_to_all | solution.py:1011
  236.6 15.7 %copy-start.4 = (f32[256,512]{1,0:T(8,128)S(1)}, f32[256,512]{1,0:T(8,128)}, u32[]{:S(2)}) copy-start(f32[256,512]{1,0:T(8,128)} %get-tuple-element.156) | copy-start | bytes 1572868
  251.9 13.5 %collective-permute-start.3 = (f32[1152,256]{1,0:T(8,128)}, f32[1152,256]{1,0:T(8,128)S(1)}, u32[]{:S(2)}, u32[]{:S(2)}) collective-permute-start(f32[1152,256]{1,0:T(8,128)} %get-tuple-element.152), channel_id=1, source_target_pairs={{0,1},{1,0},{2,3},{3,2},{4,5},{5,4},{6,7},{7,6},{8,9},{9,8},{10,11... | collective-permute-start | bytes 3538952 | tf_op jit(solution)/shard_map/ppermute | solution.py:1015
  252.3 11.3 %collective-permute-start.5 = (f32[256,512]{1,0:T(8,128)S(1)}, f32[256,512]{1,0:T(8,128)S(1)}, u32[]{:S(2)}, u32[]{:S(2)}) collective-permute-start(f32[256,512]{1,0:T(8,128)S(1)} %copy-done.4), channel_id=1, source_target_pairs={{0,1},{1,0},{2,3},{3,2},{4,5},{5,4},{6,7},{7,6},{8,9},{9,8},{10,11... | collective-permute-start | bytes 1572872 | tf_op jit(solution)/shard_map/ppermute | solution.py:1015
  263.2 2.2 collective-permute-start.4
  268.2 36.5 %all-to-all-start.11 = ((bf16[16,160,256]{2,1,0:T(8,128)(2,1)}), bf16[16,160,256]{2,1,0:T(8,128)(2,1)S(1)}, u32[]{:S(2)}, u32[]{:S(2)}) async-start(bf16[16,160,256]{2,1,0:T(8,128)(2,1)} %pack_last.1), calls=%async_computation.11 | async-start | bytes 2621440 | tf_op jit(solution)/shard_map/all_to_all | solution.py:1048
  274.7 32.7 %copy-start.3 = (f32[1,1920]{1,0:T(1,128)S(1)}, f32[1,1920]{1,0:T(1,128)}, u32[]{:S(2)}) copy-start(f32[1,1920]{1,0:T(1,128)} %get-tuple-element.168) | copy-start | bytes 23044
  274.7 33.4 %copy-start.2 = (f32[1,1920]{1,0:T(1,128)S(1)}, f32[1,1920]{1,0:T(1,128)}, u32[]{:S(2)}) copy-start(f32[1,1920]{1,0:T(1,128)} %get-tuple-element.169) | copy-start | bytes 23044
  304.8 4.0 %collective-permute-start.6 = (f32[400,256]{1,0:T(8,128)S(1)}, f32[400,256]{1,0:T(8,128)S(1)}, u32[]{:S(2)}, u32[]{:S(2)}) collective-permute-start(f32[400,256]{1,0:T(8,128)S(1)} %sum_last.1.mine_ref), channel_id=1, source_target_pairs={{0,1},{1,0},{2,3},{3,2},{4,5},{5,4},{6,7},{7,6},{8,9},{9,8},{10,11... | collective-permute-start | bytes 1228808 | tf_op jit(solution)/shard_map/ppermute | solution.py:1015
